TPU v7x, 128 devices: a whole 4x4x4 slice. The times are simulated.
128 devices in a mesh: dp: 8 (over z, core), expert: 16 (over y, x).
Axes of the slice: x: 4, y: 4, z: 4, core: 2. Of those that a mesh axis runs over, the one named last changes fastest.
Arguments:
- tokens: bfloat16 [128, 2, 64, 1280], P(('dp', 'expert')), may hold values from -6 to 6
- expert_ids: int32 [128, 2, 64], P(('dp', 'expert')), may hold values from 0 to 31, as said below
- slots: int32 [128, 2, 64], P(('dp', 'expert')), may hold values from 0 to 5, as said below
- ln_gain: float32 [1280], replicated, may hold values from 0.5 to 1.5
- w_in: bfloat16 [32, 1280, 5120], P('expert', None, 'dp'), may hold values from -0.15625 to 0.15625
- w_out: bfloat16 [32, 5120, 1280], P('expert', 'dp'), may hold values from -0.078125 to 0.078125
Outputs:
- grad_tokens: bfloat16 [128, 2, 64, 1280], P(('dp', 'expert'))
- grad_w_in: float32 [32, 1280, 5120], P('expert', None, 'dp')
- grad_w_out: float32 [32, 5120, 1280], P('expert', 'dp')
Inputs may be any that keep to these rules, and one draw needn't show every extreme that they name: `expert_ids`: within each block of 128 tokens of one device, no expert is named more than 6 times, and in every draw one expert is named exactly 6 times in every block. Within each block, the tokens of one expert have distinct slots.
All inputs are finite; a program needn't handle non-finite values.
Results may differ from a plain program's by a relative error of at most 0.019.
Values may be sent and summed in bfloat16 or wider, within the bound.
No kernel may reach another device: no remote copies, remote signals or barrier semaphores. Data moves between devices by JAX's collectives and lax.ppermute only.
A program may use at most 128 MiB of HBM per device.

v0:
```python
import math

import jax
import jax.numpy as jnp
from jax import lax
from jax.sharding import PartitionSpec as P

norm_eps = 1e-06
objective_scale = 32.0


def layer_norm(values, gain_vector):
    centred = values - jnp.mean(values, axis=-1, keepdims=True)
    spread = jnp.mean(centred * centred, axis=-1, keepdims=True)
    return centred * lax.rsqrt(spread + norm_eps) * gain_vector


def gelu_tanh(values):
    return jax.nn.gelu(values, approximate=True)


def body(tokens, expert_ids, slots, ln_gain, w_in, w_out):
    pair_count = tokens.shape[0]
    tok_count = tokens.shape[2]
    model_width = tokens.shape[3]
    row_count = pair_count * 2 * tok_count
    expert_groups = lax.axis_size("expert")
    data_groups = lax.axis_size("dp")
    local_experts = w_in.shape[0]
    expert_total = local_experts * expert_groups
    capacity = max(2, 3 * row_count // (2 * expert_total))
    flat_tokens = tokens.reshape(row_count, model_width)
    position = expert_ids.reshape(row_count) * capacity + slots.reshape(row_count)
    normed_full, norm_back = jax.vjp(
        lambda values: layer_norm(values, ln_gain), flat_tokens.astype(jnp.float32)
    )
    normed = normed_full.astype(jnp.bfloat16)

    def dispatch(values):
        buffer = (
            jnp.zeros((expert_total * capacity, model_width), jnp.bfloat16).at[position].set(values)
        )
        return buffer.reshape(expert_groups, local_experts, capacity, model_width)

    def collect(buffer):
        shared = lax.all_gather(buffer[None], "dp", axis=0, tiled=True)
        routed = lax.all_to_all(shared, "expert", split_axis=1, concat_axis=1, tiled=True)
        return routed.reshape(data_groups * expert_groups, local_experts, capacity, model_width)

    def settle(partial_out):
        grouped = partial_out.astype(jnp.bfloat16).reshape(
            data_groups, expert_groups, local_experts, capacity, model_width
        )
        returned = lax.all_to_all(grouped, "expert", split_axis=1, concat_axis=1, tiled=True)
        summed = lax.psum_scatter(
            returned.astype(jnp.float32).astype(jnp.bfloat16), "dp", scatter_dimension=0, tiled=True
        ).astype(jnp.float32)[0]
        result = summed.astype(jnp.bfloat16)
        return result.reshape(expert_total * capacity, model_width)

    gathered = collect(dispatch(normed))
    hidden_pre = jnp.einsum("secd,edh->sech", gathered, w_in, preferred_element_type=jnp.float32)
    act_full, gelu_back = jax.vjp(gelu_tanh, hidden_pre)
    activation = act_full.astype(jnp.bfloat16)
    partial_out = jnp.einsum(
        "sech,ehd->secd", activation, w_out, preferred_element_type=jnp.float32
    )
    expert_rows = settle(partial_out)
    combined = expert_rows[position]
    mixed_rows = flat_tokens.astype(jnp.float32) + combined.astype(jnp.float32)
    pooled = jnp.mean(mixed_rows.reshape(pair_count, 2, tok_count, model_width), axis=2)
    image_emb = pooled[:, 0]
    text_emb = pooled[:, 1]
    logit_scale = tok_count / math.sqrt(model_width)
    all_image, all_text = (
        lax.all_gather(image_emb, ("dp", "expert"), axis=0, tiled=True),
        lax.all_gather(text_emb, ("dp", "expert"), axis=0, tiled=True),
    )
    pair_total = all_image.shape[0]
    first_pair = lax.axis_index(("dp", "expert")) * pair_count
    own_pairs = jnp.arange(pair_count, dtype=jnp.int32) + first_pair
    self_match = (own_pairs[:, None] == jnp.arange(pair_total, dtype=jnp.int32)[None, :]).astype(
        jnp.float32
    )
    highest = lax.Precision.HIGHEST
    row_logits = logit_scale * jnp.dot(image_emb, all_text.T, precision=highest)
    col_logits = logit_scale * jnp.dot(text_emb, all_image.T, precision=highest)
    row_grad = objective_scale * (jax.nn.softmax(row_logits, axis=1) - self_match)
    col_grad = objective_scale * (jax.nn.softmax(col_logits, axis=1) - self_match)
    image_far, text_far = (
        lax.psum_scatter(
            logit_scale * jnp.dot(col_grad.T, text_emb, precision=highest),
            ("dp", "expert"),
            scatter_dimension=0,
            tiled=True,
        ),
        lax.psum_scatter(
            logit_scale * jnp.dot(row_grad.T, image_emb, precision=highest),
            ("dp", "expert"),
            scatter_dimension=0,
            tiled=True,
        ),
    )
    grad_image = logit_scale * jnp.dot(row_grad, all_text, precision=highest) + image_far
    grad_text = logit_scale * jnp.dot(col_grad, all_image, precision=highest) + text_far
    grad_pooled = jnp.stack([grad_image, grad_text], axis=1) / tok_count
    grad_mixed = jnp.broadcast_to(
        grad_pooled[:, :, None, :], (pair_count, 2, tok_count, model_width)
    ).reshape(row_count, model_width)
    grad_sent = grad_mixed.astype(jnp.bfloat16)
    grad_gathered = collect(dispatch(grad_sent))
    grad_act = jnp.einsum(
        "secd,ehd->sech", grad_gathered, w_out, preferred_element_type=jnp.float32
    )
    grad_w_out = jnp.einsum(
        "sech,secd->ehd", activation, grad_gathered, preferred_element_type=jnp.float32
    )
    grad_pre = gelu_back(grad_act)[0].astype(jnp.bfloat16)
    grad_w_in = jnp.einsum("secd,sech->edh", gathered, grad_pre, preferred_element_type=jnp.float32)
    grad_partial = jnp.einsum("sech,edh->secd", grad_pre, w_in, preferred_element_type=jnp.float32)
    grad_normed = settle(grad_partial)[position]
    grad_flat = grad_mixed + norm_back(grad_normed.astype(jnp.float32))[0]
    return (grad_flat.astype(jnp.bfloat16).reshape(tokens.shape), grad_w_in, grad_w_out)


def solution(mesh):
    placed = (
        P(("dp", "expert"), None, None, None),
        P(("dp", "expert"), None, None),
        P(("dp", "expert"), None, None),
        P(),
        P("expert", None, "dp"),
        P("expert", "dp", None),
    )
    return jax.shard_map(
        body,
        mesh=mesh,
        in_specs=placed,
        out_specs=(
            P(("dp", "expert"), None, None, None),
            P("expert", None, "dp"),
            P("expert", "dp", None),
        ),
        check_vma=False,
    )
```

profile of v0, /device:TPU:0, one launch (start us, length us, event | category | flops | bytes accessed | tf_op | source)
XLA Modules:
  0.0 713.9 jit_solution(14207907442331191499)
XLA Ops:
  7.2 1.2 convert_reduce_fusion
  8.5 0.1 div.48
  8.6 1.2 multiply_reduce_fusion
  9.8 0.7 multiply_add_fusion.1
  10.5 0.1 add.75
  10.6 0.1 rsqrt.16
  10.7 1.9 fusion.31
  12.6 2.4 scatter_custom_fusion
  15.0 2.0 broadcast_in_dim_reshape.6
  17.0 2.0 copy.29
  19.1 33.8 %all-gather.5.cloned.1.call-done = bf16[8,16,2,6,1280]{4,1,3,2,0:T(8,128)(2,1)} async-done(((bf16[1,16,2,6,1280]{4,1,3,2,0:T(8,128)(2,1)}), bf16[8,16,2,6,1280]{4,1,3,2,0:T(8,128)(2,1)}) %all-gather.5.cloned.1.call-update) | async-done | bytes 3932176 | tf_op jit(solution)/shard_map/all_gather | solution.py:46
  52.9 4.3 copy.30
  57.2 55.1 %all_to_all.20 = bf16[8,16,2,6,1280]{4,0,3,2,1:T(8,128)(2,1)S(1)} all-to-all(bf16[8,16,2,6,1280]{4,0,3,2,1:T(8,128)(2,1)S(1)} %copy.30), channel_id=1, replica_groups=mesh['dp'=8,'expert'=16] {'expert'}, dimensions={1} | all-to-all | bytes 7864320 | tf_op jit(solution)/shard_map/all_to_all | solution.py:47
  112.2 2.2 copy.31
  114.4 1.9 copy-done.4
  116.3 3.2 fusion.12
  119.5 4.1 convolution_convert_fusion.1
  123.6 1.2 copy.32
  124.9 50.8 %all_to_all.21 = bf16[8,16,2,6,1280]{4,0,3,2,1:T(8,128)(2,1)S(1)} all-to-all(bf16[8,16,2,6,1280]{4,0,3,2,1:T(8,128)(2,1)S(1)} %copy.32), channel_id=1, replica_groups=mesh['dp'=8,'expert'=16] {'expert'}, dimensions={1} | all-to-all | bytes 7864320 | tf_op jit(solution)/shard_map/all_to_all | solution.py:54
  175.7 4.1 copy.33
  179.9 33.7 %reduce-scatter.3.cloned.1.call-done = bf16[1,16,2,6,1280]{4,1,3,2,0:T(8,128)(2,1)} async-done(((bf16[8,16,2,6,1280]{4,1,3,2,0:T(8,128)(2,1)}), bf16[1,16,2,6,1280]{4,1,3,2,0:T(8,128)(2,1)}) %reduce-scatter.3.cloned.1.call-update) | async-done | bytes 491536 | tf_op jit(solution)/shard_map/reduce_scatter | solution.py:55
  213.6 2.0 copy.34
  215.6 2.0 convert_element_type.105
  217.7 3.0 gather_fusion
  220.6 1.2 fusion.28
  221.9 58.5 %all-gather.1 = f32[128,1,1280]{2,1,0:T(1,128)S(1)} all-gather(f32[1,1,1280]{2,1,0:T(1,128)S(1)} %get-tuple-element.9), channel_id=3, replica_groups=mesh['dp'=8,'expert'=16] {'dp','expert'}, dimensions={0}, use_global_device_ids=true | all-gather | bytes 660480 | tf_op jit(solution)/shard_map/all_gather | solution.py:76
  280.4 0.8 copy-done.2
  281.2 1.2 fusion.57
  282.5 57.8 %all-gather = f32[128,1,1280]{2,1,0:T(1,128)S(1)} all-gather(f32[1,1,1280]{2,1,0:T(1,128)S(1)} %get-tuple-element.10), channel_id=2, replica_groups=mesh['dp'=8,'expert'=16] {'dp','expert'}, dimensions={0}, use_global_device_ids=true | all-gather | bytes 660480 | tf_op jit(solution)/shard_map/all_gather | solution.py:77
  340.3 0.9 copy-done.3
  341.1 1.2 fusion.56
  342.4 1.3 fusion.50
  343.7 1.2 fusion.49
  344.9 2.6 fusion.47
  347.5 0.9 multiply_multiply_fusion.2
  348.5 1.0 multiply_multiply_fusion.3
  349.5 1.5 convolution_reduce_fusion
  351.0 1.5 convolution_reduce_fusion.1
  352.5 143.4 %all-reduce.5.cloned.1.call-done = (f32[128,1280]{1,0:T(8,128)}, f32[128,1280]{1,0:T(8,128)}) async-done(((f32[128,1280]{1,0:T(8,128)}, f32[128,1280]{1,0:T(8,128)}), (f32[128,1280]{1,0:T(8,128)}, f32[128,1280]{1,0:T(8,128)})) %all-reduce.5.cloned.1.call-update) | async-done | bytes 1310736
  495.9 0.8 dynamic-slice_add_fusion.1
  496.7 0.8 dynamic-slice_add_fusion
  497.5 0.7 broadcast_in_dim.9
  498.3 2.4 scatter_custom_fusion.1
  500.7 2.0 broadcast_in_dim_reshape.7
  502.7 2.0 copy.35
  504.8 30.0 %all-gather.7.cloned.1.call-done = bf16[8,16,2,6,1280]{4,1,3,2,0:T(8,128)(2,1)} async-done(((bf16[1,16,2,6,1280]{4,1,3,2,0:T(8,128)(2,1)}), bf16[8,16,2,6,1280]{4,1,3,2,0:T(8,128)(2,1)}) %all-gather.7.cloned.1.call-update) | async-done | bytes 3932176 | tf_op jit(solution)/shard_map/all_gather | solution.py:46
  534.7 4.3 copy.36
  539.0 55.3 %all_to_all.22 = bf16[8,16,2,6,1280]{4,0,3,2,1:T(8,128)(2,1)S(1)} all-to-all(bf16[8,16,2,6,1280]{4,0,3,2,1:T(8,128)(2,1)S(1)} %copy.36), channel_id=1, replica_groups=mesh['dp'=8,'expert'=16] {'expert'}, dimensions={1} | all-to-all | bytes 7864320 | tf_op jit(solution)/shard_map/all_to_all | solution.py:47
  594.3 2.2 copy.37
  596.5 5.0 fusion.6
  601.6 3.5 convolution_convert_fusion
  605.1 1.2 copy.38
  606.3 50.9 %all_to_all.23 = bf16[8,16,2,6,1280]{4,0,3,2,1:T(8,128)(2,1)S(1)} all-to-all(bf16[8,16,2,6,1280]{4,0,3,2,1:T(8,128)(2,1)S(1)} %copy.38), channel_id=1, replica_groups=mesh['dp'=8,'expert'=16] {'expert'}, dimensions={1} | all-to-all | bytes 7864320 | tf_op jit(solution)/shard_map/all_to_all | solution.py:54
  657.2 4.1 copy.39
  661.3 1.5 copy-done.11
  662.8 8.3 %convolution_bitcast_fusion.1 = f32[2,1280,640]{2,1,0:T(8,128)} fusion(bf16[128,2,6,1280]{3,0,2,1:T(8,128)(2,1)} %bitcast.125, bf16[128,2,6,640]{3,0,2,1:T(8,128)(2,1)S(1)} %copy-done.11), kind=kOutput, calls=%fused_computation.7 | convolution fusion | flops 2516582400 | bytes 12451840 | tf_op jit(solution)/shard_map/secd,sech->edh/dot_general | solution.py:119
  671.1 5.0 convolution_bitcast_fusion
  676.2 19.0 %reduce-scatter.5.cloned.1.call-done = bf16[1,16,2,6,1280]{4,1,3,2,0:T(8,128)(2,1)} async-done(((bf16[8,16,2,6,1280]{4,1,3,2,0:T(8,128)(2,1)}), bf16[1,16,2,6,1280]{4,1,3,2,0:T(8,128)(2,1)}) %reduce-scatter.5.cloned.1.call-update) | async-done | bytes 491536 | tf_op jit(solution)/shard_map/reduce_scatter | solution.py:55
  695.1 2.0 copy.40
  697.1 2.0 convert_element_type.114
  699.2 2.9 gather_fusion.1
  702.1 1.3 fusion.27
  703.4 1.4 fusion.36
  704.8 2.1 add_convert_fusion
  (47 shorter events, 0.5 us)
Async XLA Ops:
  7.2 112.3 %copy-start = (bf16[2,640,1280]{2,1,0:T(8,128)(2,1)S(1)}, bf16[2,640,1280]{2,1,0:T(8,128)(2,1)}, u32[]{:S(2)}) copy-start(bf16[2,640,1280]{2,1,0:T(8,128)(2,1)} %param.11) | copy-start | bytes 9830404
  7.2 45.7 %all-gather.5.cloned.1.call-start = ((), (), s32[]{:S(2)}) async-start(), calls=%async_computation.6 | async-start | bytes 4423680 | tf_op jit(solution)/shard_map/all_gather | solution.py:46
  19.0 194.6 %reduce-scatter.3.cloned.1.call-start = ((), (), s32[]{:S(2)}) async-start(), calls=%async_computation.7 | async-start | bytes 4423680 | tf_op jit(solution)/shard_map/reduce_scatter | solution.py:55
  112.2 4.0 copy-start.8
  114.4 1.9 copy-start.4
  119.5 4.1 copy-start.12
  179.8 316.2 %all-reduce.5.cloned.1.call-start = ((), (), s32[]{:S(2)}) async-start(), calls=%async_computation.10 | async-start | bytes 2621440
  280.4 0.8 copy-start.2
  340.3 0.9 copy-start.3
  349.4 185.3 %all-gather.7.cloned.1.call-start = ((), (), s32[]{:S(2)}) async-start(), calls=%async_computation.8 | async-start | bytes 4423680 | tf_op jit(solution)/shard_map/all_gather | solution.py:46
  504.7 190.4 %reduce-scatter.5.cloned.1.call-start = ((), (), s32[]{:S(2)}) async-start(), calls=%async_computation.9 | async-start | bytes 4423680 | tf_op jit(solution)/shard_map/reduce_scatter | solution.py:55
  594.3 2.2 copy-start.13
  596.5 5.1 copy-start.5
  596.5 5.1 copy-start.9
  601.6 3.5 copy-start.10
  661.3 1.5 copy-start.11
  662.8 8.3 %copy-start.6 = (bf16[8,16,2,6,1280]{4,1,0,3,2:T(8,128)(2,1)S(1)}, bf16[8,16,2,6,1280]{4,1,0,3,2:T(8,128)(2,1)}, u32[]{:S(2)}) copy-start(bf16[8,16,2,6,1280]{4,1,0,3,2:T(8,128)(2,1)} %copy-done.5) | copy-start | bytes 11796484
  662.8 8.3 %copy-start.14 = (f32[2,128,6,640]{3,1,2,0:T(8,128)S(1)}, f32[2,128,6,640]{3,1,2,0:T(8,128)}, u32[]{:S(2)}) copy-start(f32[2,128,6,640]{3,1,2,0:T(8,128)} %copy-done.12) | copy-start | bytes 11796484
  671.1 35.8 %copy-start.1 = (bf16[2,640,1280]{2,1,0:T(8,128)(2,1)S(1)}, bf16[2,640,1280]{2,1,0:T(8,128)(2,1)}, u32[]{:S(2)}) copy-start(bf16[2,640,1280]{2,1,0:T(8,128)(2,1)} %param.11) | copy-start | bytes 9830404
  676.2 26.0 %copy-start.7 = (f32[1280]{0:T(1024)S(1)}, f32[1280]{0:T(1024)}, u32[]{:S(2)}) copy-start(f32[1280]{0:T(1024)} %param.9) | copy-start | bytes 15364
Sparse Core Ops, SparseCore 0:
  19.2 33.6 all-gather.4
  179.9 33.6 reduce-scatter.2
  349.5 146.3 all-reduce.4
  504.9 29.8 all-gather.6
  661.4 33.6 reduce-scatter.4
where the time goes:
time: 723 us; the launch traced here: 714 us
  blocking collectives  328 us (45%)
  waiting for transfers between devices  260 us (36%)
  local copies, waits for them, and re-layouts  56.4 us (8%)
  matrix products  34.7 us (5%)
  other arithmetic  19.8 us (3%)
  between operations  14.5 us (2%)
    unnamed x6, waiting for transfers between devices  143 us
    all_to_all x2, blocking collectives, collect(): lax.all_to_all(shared, 'expert', split_axis=1, concat_axis=1, tiled=True)  110 us
    all_to_all x2, blocking collectives, settle(): lax.all_to_all(grouped, 'expert', split_axis=1, concat_axis=1, tiled=True)  102 us
    all_gather x2, waiting for transfers between devices, collect(): shared = lax.all_gather(buffer[None], 'dp', axis=0, tiled=True)  63.8 us
    all_gather x1, blocking collectives, body(): lax.all_gather(image_emb, ('dp', 'expert'), axis=0, tiled=True)  58.5 us
    all_gather x1, blocking collectives, body(): lax.all_gather(text_emb, ('dp', 'expert'), axis=0, tiled=True)  57.8 us
    reduce_scatter x2, waiting for transfers between devices, settle(): lax.psum_scatter(returned.astype(jnp.float32).astype(jnp.bfloat16), 'dp',...  52.7 us
  transfers between devices with their start and end apart: 5, of which 5 were waited for; matrix products, arithmetic and copies ran while one was open for 2% of the time, Pallas kernels for 0%

commit v1 on v0

v1 whole, which is shorter than its diff:
```python
import math

import jax
import jax.numpy as jnp
from jax import lax
from jax.sharding import PartitionSpec as P

norm_eps = 1e-06
objective_scale = 32.0
bf16 = jnp.bfloat16
f32 = jnp.float32


def layer_norm(values, gain_vector):
    centred = values - jnp.mean(values, axis=-1, keepdims=True)
    spread = jnp.mean(centred * centred, axis=-1, keepdims=True)
    return centred * lax.rsqrt(spread + norm_eps) * gain_vector


def gelu_tanh(values):
    return jax.nn.gelu(values, approximate=True)


def mm(spec, a, b, out=f32):
    return jnp.einsum(spec, a, b, preferred_element_type=f32).astype(out)


def body(tokens, expert_ids, slots, ln_gain, w_in, w_out):
    tok_count = tokens.shape[2]
    width = tokens.shape[3]
    row_count = 2 * tok_count
    groups = lax.axis_size("expert")
    datas = lax.axis_size("dp")
    local = w_in.shape[0]
    total = local * groups
    cap = max(2, 3 * row_count // (2 * total))
    pairs = groups * datas
    everyone = ("dp", "expert")

    flat = tokens.reshape(row_count, width).astype(f32)
    position = expert_ids.reshape(row_count) * cap + slots.reshape(row_count)
    all_pos = lax.all_gather(position[None], everyone, axis=0, tiled=True)

    normed_full, norm_back = jax.vjp(lambda values: layer_norm(values, ln_gain), flat)
    normed = normed_full.astype(bf16)
    place = (jnp.arange(total * cap, dtype=jnp.int32)[:, None] == position[None, :]).astype(bf16)
    sent = mm("rt,td->rd", place, normed, bf16).reshape(groups, local, cap, width)
    routed = lax.all_to_all(sent, "expert", split_axis=0, concat_axis=0, tiled=True)
    routed = routed.transpose(1, 0, 2, 3).reshape(1, local, groups * cap, width)
    rows = lax.all_gather(routed, "dp", axis=0, tiled=True)

    first = lax.axis_index("expert") * (local * cap)
    held = jnp.arange(local * cap, dtype=jnp.int32)[None, :, None] + first
    named = (all_pos[:, None, :] == held).astype(f32).reshape(pairs, local * cap, 2, tok_count)
    kind = jnp.max(named, axis=3).reshape(datas, groups, local, cap, 2)
    eye = jnp.eye(groups, dtype=f32)
    pool = jnp.einsum("sglck,gf->slfkgc", kind, eye)
    pool = pool.reshape(datas, local, groups * 2, groups * cap).astype(bf16)

    hidden_pre = mm("slrd,ldh->slrh", rows, w_in)
    act_full, gelu_back = jax.vjp(gelu_tanh, hidden_pre)
    pooled_act = mm("slqr,slrh->slqh", pool, act_full.astype(bf16), bf16)
    partial = mm("slqh,lhd->sqd", pooled_act, w_out, bf16)
    partial = lax.all_to_all(
        partial.reshape(pairs, 2, width), everyone, split_axis=0, concat_axis=0, tiled=True
    )
    own = jnp.sum(partial.astype(f32), axis=0) + jnp.sum(
        flat.reshape(2, tok_count, width), axis=1
    )
    own = own / tok_count
    emb = lax.all_to_all(
        jnp.broadcast_to(own[None], (pairs, 2, width)),
        everyone,
        split_axis=0,
        concat_axis=0,
        tiled=True,
    )
    image_emb, text_emb = emb[:, 0], emb[:, 1]
    logit_scale = tok_count / math.sqrt(width)
    highest = lax.Precision.HIGHEST
    logits = logit_scale * jnp.dot(image_emb, text_emb.T, precision=highest)
    grad_logits = objective_scale * (
        jax.nn.softmax(logits, axis=1)
        + jax.nn.softmax(logits, axis=0)
        - 2.0 * jnp.eye(pairs, dtype=f32)
    )
    grad_image = logit_scale * jnp.dot(grad_logits, text_emb, precision=highest)
    grad_text = logit_scale * jnp.dot(grad_logits.T, image_emb, precision=highest)
    grad_pooled = jnp.stack([grad_image, grad_text], axis=1) / tok_count
    grad_rows = grad_pooled.astype(bf16).reshape(datas, groups * 2, width)
    me = lax.axis_index(everyone)
    grad_own = lax.dynamic_index_in_dim(grad_pooled, me, axis=0, keepdims=False)

    grad_pool = mm("sqd,lhd->slqh", grad_rows, w_out, bf16)
    grad_act = mm("slqr,slqh->slrh", pool, grad_pool)
    grad_pre = gelu_back(grad_act)[0].astype(bf16)
    grad_partial = mm("slrh,ldh->slrd", grad_pre, w_in, bf16)
    summed = lax.psum_scatter(
        grad_partial.reshape(datas * total * cap, width), "dp", scatter_dimension=0, tiled=True
    )
    grad_w_out = mm("slqh,sqd->lhd", pooled_act, grad_rows)
    grad_w_in = mm("slrd,slrh->ldh", rows, grad_pre)

    back = summed.reshape(local, groups, cap, width).transpose(1, 0, 2, 3)
    back = lax.all_to_all(back, "expert", split_axis=0, concat_axis=0, tiled=True)
    grad_normed = mm("rt,rd->td", place, back.reshape(total * cap, width))
    grad_flat = jnp.repeat(grad_own, tok_count, axis=0) + norm_back(grad_normed)[0]
    return (grad_flat.astype(bf16).reshape(tokens.shape), grad_w_in, grad_w_out)


def solution(mesh):
    placed = (
        P(("dp", "expert"), None, None, None),
        P(("dp", "expert"), None, None),
        P(("dp", "expert"), None, None),
        P(),
        P("expert", None, "dp"),
        P("expert", "dp", None),
    )
    return jax.shard_map(
        body,
        mesh=mesh,
        in_specs=placed,
        out_specs=(
            P(("dp", "expert"), None, None, None),
            P("expert", None, "dp"),
            P("expert", "dp", None),
        ),
        check_vma=False,
    )
```

time: 723 us -> 246 us (0.34); the launches traced: 714 us -> 245 us
  waiting for transfers between devices: 260 us -> 28.4 us
  blocking collectives: 328 us -> 114 us
  local copies, waits for them, and re-layouts: 56.4 us -> 31.2 us
  other arithmetic: 19.8 us -> 10.5 us
    all_to_all x4 -> x3, blocking collectives: 212 us -> 65.9 us  [the longest x1 26 us: body(): lax.all_to_all(jnp.broadcast_to(own[None], (pairs, 2, width)), everyone,...]
    unnamed x6 -> x2, waiting for transfers between devices: 143 us -> 0.03 us
    all_gather x2 -> x1, blocking collectives: 116 us -> 48.1 us  [body(): all_pos = lax.all_gather(position[None], everyone, axis=0, tiled=True)]
    all_gather x2 -> x1, waiting for transfers between devices: 63.8 us -> 0.02 us  [body(): rows = lax.all_gather(routed, 'dp', axis=0, tiled=True)]
    reduce_scatter x2 -> x1, waiting for transfers between devices: 52.7 us -> 23.5 us  [body(): lax.psum_scatter(grad_partial.reshape(datas * total * cap, width), 'dp',...]
    all_to_all x4 -> x1, local copies, waits for them, and re-layouts: 12.5 us -> 1.93 us  [body(): lax.all_to_all(back, 'expert', split_axis=0, concat_axis=0, tiled=True)]
    reshape x2 -> x8, local copies, waits for them, and re-layouts: 2.43 us -> 12.9 us  [the longest x2 3.49 us: body(): mm('rt,td->rd', place, normed, bf16).reshape(groups, local, cap, width)]
    all_gather x2 -> x1, local copies, waits for them, and re-layouts: 8.53 us -> 0.09 us  [body(): all_pos = lax.all_gather(position[None], everyone, axis=0, tiled=True)]
  transfers between devices with their start and end apart: 5 -> 3, of which waited for: 5 -> 2; matrix products, arithmetic and copies ran while one was open for 2% -> 9% of each run, Pallas kernels for 0% -> 0%
where the time goes in v1:
time: 246 us; the launch traced here: 245 us
  blocking collectives  114 us (46%)
  matrix products  39 us (16%)
  local copies, waits for them, and re-layouts  31.2 us (13%)
  waiting for transfers between devices  28.4 us (12%)
  between operations  14.3 us (6%)
  other arithmetic  10.5 us (4%)
  starting transfers between devices  7.08 us (3%)
    all_gather x1, blocking collectives, body(): all_pos = lax.all_gather(position[None], everyone, axis=0, tiled=True)  48.1 us
    dot_general x10, matrix products, mm(): return jnp.einsum(spec, a, b, preferred_element_type=f32).astype(out)  36.7 us
    all_to_all x1, blocking collectives, body(): lax.all_to_all(jnp.broadcast_to(own[None], (pairs, 2, width)), everyone,...  26 us
    reduce_scatter x1, waiting for transfers between devices, body(): lax.psum_scatter(grad_partial.reshape(datas * total * cap, width), 'dp',...  23.5 us
    all_to_all x1, blocking collectives, body(): lax.all_to_all(partial.reshape(pairs, 2, width), everyone, split_axis=0,...  21.8 us
    all_to_all x1, blocking collectives, body(): lax.all_to_all(sent, 'expert', split_axis=0, concat_axis=0, tiled=True)  18.1 us
    all_to_all x1, starting transfers between devices, body(): lax.all_to_all(back, 'expert', split_axis=0, concat_axis=0, tiled=True)  7 us
  transfers between devices with their start and end apart: 3, of which 2 were waited for; matrix products, arithmetic and copies ran while one was open for 9% of the time, Pallas kernels for 0%

profile of v1, /device:TPU:0, one launch (start us, length us, event | category | flops | bytes accessed | tf_op | source)
XLA Modules:
  0.0 244.7 jit_solution(15240730624935674204)
XLA Ops:
  7.2 0.0 copy-start
  7.2 0.0 all-gather.3.cloned.1.call-start
  7.2 1.3 convert_reduce_fusion.2
  8.5 0.1 div.49
  8.6 1.2 multiply_reduce_fusion.1
  9.8 0.7 multiply_add_fusion.1
  10.5 0.1 add.77
  10.6 0.1 add.80
  10.7 0.6 copy-done.3
  11.3 1.2 multiply_convert_fusion.1
  12.5 1.1 convolution_convert_fusion.1
  13.5 2.0 reshape.145
  15.6 1.5 copy.40
  17.0 18.1 %all_to_all.20 = bf16[16,2,6,1280]{3,1,2,0:T(2,128)(2,1)S(1)} all-to-all(bf16[16,2,6,1280]{3,1,2,0:T(2,128)(2,1)S(1)} %copy.40), channel_id=1, replica_groups=mesh['dp'=8,'expert'=16] {'expert'}, dimensions={0} | all-to-all | bytes 983040 | tf_op jit(solution)/shard_map/all_to_all | solution.py:48
  35.1 0.8 copy.41
  36.0 0.0 all-gather.3.cloned.1.call-update
  36.0 0.0 reduce-scatter.2.cloned.1.call-start
  36.0 0.0 copy-done.8
  36.1 0.1 reshape.154
  36.1 48.1 %all-gather = s32[128,1,128]{2,1,0:T(1,128)S(1)} all-gather(s32[1,1,128]{2,1,0:T(1,128)S(1)} %reshape.154), channel_id=1, replica_groups=mesh['dp'=8,'expert'=16] {'dp','expert'}, dimensions={0}, use_global_device_ids=true | all-gather | bytes 66048 | tf_op jit(solution)/shard_map/all_gather | solution.py:42
  84.3 0.1 copy.38
  84.4 0.2 convert_reduce_fusion.1
  84.6 0.7 reshape.143
  85.3 1.1 copy.39
  86.5 1.8 fusion.26
  88.3 3.5 %convert_element_type.74 = bf16[8,2,32,96]{3,2,1,0:T(8,128)(2,1)S(1)} reshape(bf16[8,2,16,2,16,6]{5,4,3,2,1,0:T(8,128)(2,1)} %fusion.26) | data formatting | bytes 196608 | tf_op jit(solution)/shard_map/convert_element_type | solution.py:58
  91.8 0.0 all-gather.3.cloned.1.call-done
  91.8 0.0 copy-start.7
  91.8 7.7 %fusion.9 = (bf16[8,2,96,640]{3,2,0,1:T(8,128)(2,1)S(1)}, f32[2,8,96,640]{3,2,1,0:T(8,128)}) fusion(bf16[8,2,96,1280]{3,2,0,1:T(8,128)(2,1)} %all-gather.3.cloned.1.call-done, bf16[2,1280,640]{2,1,0:T(8,128)(2,1)S(1)} %copy-done), kind=kOutput, calls=%fused_computation.17 | convolution fusion | flops 2525429760 | bytes 13107200 | tf_op jit(solution)/shard_map/slrd,ldh->slrh/dot_general | solution.py:25
  99.6 0.4 fusion.29
  100.0 0.8 copy-done.1
  100.8 1.9 fusion.21
  102.7 2.6 %reshape.147 = bf16[128,2,1280]{2,1,0:T(2,128)(2,1)} reshape(bf16[8,32,1280]{2,1,0:T(8,128)(2,1)} %fusion.21) | data formatting | bytes 1310720 | tf_op jit(solution)/shard_map/reshape | solution.py:65
  105.4 21.8 %all_to_all.21 = bf16[128,2,1280]{2,1,0:T(2,128)(2,1)S(1)} all-to-all(bf16[128,2,1280]{2,1,0:T(2,128)(2,1)} %reshape.147), channel_id=1, replica_groups=mesh['dp'=8,'expert'=16] {'dp','expert'}, dimensions={0} | all-to-all | bytes 1310720 | tf_op jit(solution)/shard_map/all_to_all | solution.py:64
  127.1 0.6 convert_reduce_fusion
  127.7 0.3 broadcast_in_dim.8
  128.1 26.0 %all_to_all.22 = f32[128,2,1280]{2,1,0:T(2,128)S(1)} all-to-all(f32[128,2,1280]{2,1,0:T(2,128)S(1)} %broadcast_in_dim.8), channel_id=1, replica_groups=mesh['dp'=8,'expert'=16] {'dp','expert'}, dimensions={0} | all-to-all | bytes 2621440 | tf_op jit(solution)/shard_map/all_to_all | solution.py:71
  154.1 1.0 fusion.59
  155.1 0.8 fusion.57
  155.9 0.2 fusion.51
  156.1 0.8 fusion.25
  156.9 0.8 fusion.24
  157.7 1.2 maximum_multiply_fusion
  158.9 1.5 copy.43
  160.4 2.7 %reshape.161 = bf16[8,32,1280,1]{2,1,0,3:T(8,128)(2,1)} reshape(bf16[128,2,1280]{2,1,0:T(2,128)(2,1)} %copy.43) | data formatting | bytes 1310720 | tf_op jit(solution)/shard_map/convert_element_type | solution.py:90
  163.1 3.3 %fusion.35 = bf16[8,2,32,640]{3,2,1,0:T(8,128)(2,1)S(1)} fusion(bf16[2,640,1280]{2,1,0:T(8,128)(2,1)} %param.11, bf16[8,32,1280,1]{2,1,0,3:T(8,128)(2,1)} %reshape.161), kind=kOutput, calls=%fused_computation.41 | convolution fusion | flops 839188480 | bytes 4587520 | tf_op jit(solution)/shard_map/sqd,lhd->slqh/dot_general | solution.py:25
  166.4 3.1 %fusion.6 = bf16[8,2,96,640]{3,2,0,1:T(8,128)(2,1)S(1)} fusion(f32[2,8,96,640]{3,2,1,0:T(8,128)S(1)} %copy-done.11, bf16[8,2,32,640]{3,2,1,0:T(8,128)(2,1)S(1)} %fusion.35, bf16[8,2,32,96]{3,2,1,0:T(8,128)(2,1)S(1)} %convert_element_type.74), kind=kOutput, calls=%fused_computation.12 | convolution fusion | flops 82575360 | bytes 6651904 | tf_op jit(solution)/shard_map/slqr,slqh->slrh/dot_general | solution.py:25
  169.5 3.7 %fusion.10 = bf16[8,2,96,1280]{3,2,0,1:T(8,128)(2,1)S(1)} fusion(bf16[8,2,96,640]{3,2,0,1:T(8,128)(2,1)S(1)} %fusion.6, bf16[2,1280,640]{2,1,0:T(8,128)(2,1)S(1)} %copy-done), kind=kOutput, calls=%fused_computation.18 | convolution fusion | flops 2518548480 | bytes 9175040 | tf_op jit(solution)/shard_map/slrh,ldh->slrd/dot_general | solution.py:25
  173.2 2.2 copy.46
  175.4 0.0 reduce-scatter.2.cloned.1.call-update
  175.5 0.9 constant_dynamic-slice_fusion
  176.4 8.8 %convolution_bitcast_fusion.1 = f32[2,1280,640]{2,1,0:T(8,128)} fusion(bf16[8,2,96,1280]{3,2,0,1:T(8,128)(2,1)} %all-gather.3.cloned.1.call-done, bf16[8,2,96,640]{3,2,0,1:T(8,128)(2,1)} %copy-done.10), kind=kOutput, calls=%fused_computation.3 | convolution fusion | flops 2516582400 | bytes 12451840 | tf_op jit(solution)/shard_map/slrd,slrh->ldh/dot_general | solution.py:25
  185.2 23.5 %reduce-scatter.2.cloned.1.call-done = bf16[192,1280]{1,0:T(8,128)(2,1)} async-done(((bf16[1536,1280]{1,0:T(8,128)(2,1)}), bf16[192,1280]{1,0:T(8,128)(2,1)}) %reduce-scatter.2.cloned.1.call-update) | async-done | bytes 491536 | tf_op jit(solution)/shard_map/reduce_scatter | solution.py:98
  208.7 2.0 reshape.150
  210.8 2.4 copy.47
  213.1 7.0 %all-to-all-start.3 = ((bf16[16,2,6,1280]{3,1,2,0:T(2,128)(2,1)}), bf16[16,2,6,1280]{3,1,2,0:T(2,128)(2,1)}, u32[]{:S(2)}, u32[]{:S(2)}) async-start(bf16[16,2,6,1280]{3,1,2,0:T(2,128)(2,1)} %copy.47), calls=%async_computation.4 | async-start | bytes 983040 | tf_op jit(solution)/shard_map/all_to_all | solution.py:105
  220.1 0.0 copy-start.2
  220.2 5.1 %convolution_bitcast_fusion = f32[2,640,1280]{2,1,0:T(8,128)} fusion(bf16[8,2,32,640]{3,2,1,0:T(8,128)(2,1)} %copy-done.1, bf16[8,32,1280,1]{2,1,0,3:T(8,128)(2,1)} %reshape.161), kind=kOutput, calls=%fused_computation.2 | convolution fusion | flops 838860800 | bytes 7864320 | tf_op jit(solution)/shard_map/slqh,sqd->lhd/dot_general | solution.py:25
  225.3 4.8 %all-to-all-done.3 = bf16[16,2,6,1280]{3,1,2,0:T(2,128)(2,1)} async-done(((bf16[16,2,6,1280]{3,1,2,0:T(2,128)(2,1)}), bf16[16,2,6,1280]{3,1,2,0:T(2,128)(2,1)}, u32[]{:S(2)}, u32[]{:S(2)}) %all-to-all-start.3) | async-done | bytes 491552 | tf_op jit(solution)/shard_map/all_to_all | solution.py:105
  230.2 1.9 copy.48
  232.1 2.0 reshape.151
  234.1 1.5 multiply_reduce_fusion
  235.7 1.3 fusion.58
  237.0 0.9 fusion.44
  (27 shorter events, 0.1 us)
Async XLA Ops:
  7.2 84.7 %copy-start = (bf16[2,1280,640]{2,1,0:T(8,128)(2,1)S(1)}, bf16[2,1280,640]{2,1,0:T(8,128)(2,1)}, u32[]{:S(2)}) copy-start(bf16[2,1280,640]{2,1,0:T(8,128)(2,1)} %param.10) | copy-start | bytes 9830404
  7.2 84.6 %all-gather.3.cloned.1.call-start = ((), (), s32[]{:S(2)}) async-start(), calls=%async_computation.5 | async-start | bytes 4423680 | tf_op jit(solution)/shard_map/all_gather | solution.py:50
  10.6 25.6 %copy-start.5 = (s32[128]{0:T(128)}, s32[128]{0:T(128)S(1)}, u32[]{:S(2)}) copy-start(s32[128]{0:T(128)S(1)} %add.77) | copy-start | bytes 1540
  10.7 25.4 %copy-start.8 = (f32[128]{0:T(128)}, f32[128]{0:T(128)S(1)}, u32[]{:S(2)}) copy-start(f32[128]{0:T(128)S(1)} %add.80) | copy-start | bytes 1540
  10.7 0.6 copy-start.3
  36.0 172.7 %reduce-scatter.2.cloned.1.call-start = ((), (), s32[]{:S(2)}) async-start(), calls=%async_computation.6 | async-start | bytes 4423680 | tf_op jit(solution)/shard_map/reduce_scatter | solution.py:98
  91.8 9.0 %copy-start.7 = (bf16[2,640,1280]{2,1,0:T(8,128)(2,1)S(1)}, bf16[2,640,1280]{2,1,0:T(8,128)(2,1)}, u32[]{:S(2)}) copy-start(bf16[2,640,1280]{2,1,0:T(8,128)(2,1)} %param.11) | copy-start | bytes 9830404
  100.0 0.8 copy-start.1
  163.1 3.3 %copy-start.11 = (f32[2,8,96,640]{3,2,1,0:T(8,128)S(1)}, f32[2,8,96,640]{3,2,1,0:T(8,128)}, u32[]{:S(2)}) copy-start(f32[2,8,96,640]{3,2,1,0:T(8,128)} %get-tuple-element.16) | copy-start | bytes 11796484
  169.5 3.8 %copy-start.10 = (bf16[8,2,96,640]{3,2,0,1:T(8,128)(2,1)}, bf16[8,2,96,640]{3,2,0,1:T(8,128)(2,1)S(1)}, u32[]{:S(2)}) copy-start(bf16[8,2,96,640]{3,2,0,1:T(8,128)(2,1)S(1)} %fusion.6) | copy-start | bytes 5898244
  213.1 17.0 %all-to-all-start.3 = ((bf16[16,2,6,1280]{3,1,2,0:T(2,128)(2,1)}), bf16[16,2,6,1280]{3,1,2,0:T(2,128)(2,1)}, u32[]{:S(2)}, u32[]{:S(2)}) async-start(bf16[16,2,6,1280]{3,1,2,0:T(2,128)(2,1)} %copy.47), calls=%async_computation.4 | async-start | bytes 983040 | tf_op jit(solution)/shard_map/all_to_all | solution.py:105
  220.1 14.0 %copy-start.2 = (f32[1280]{0:T(1024)S(1)}, f32[1280]{0:T(1024)}, u32[]{:S(2)}) copy-start(f32[1280]{0:T(1024)} %param.9) | copy-start | bytes 15364
  220.2 14.0 %copy-start.6 = (s32[128]{0:T(128)S(1)}, s32[128]{0:T(128)}, u32[]{:S(2)}) copy-start(s32[128]{0:T(128)} %copy-done.5) | copy-start | bytes 1540
  220.2 15.5 %copy-start.9 = (f32[128]{0:T(128)S(1)}, f32[128]{0:T(128)}, u32[]{:S(2)}) copy-start(f32[128]{0:T(128)} %copy-done.8) | copy-start | bytes 1540
  220.2 15.5 %copy-start.4 = (f32[128]{0:T(128)S(1)}, f32[128]{0:T(128)}, u32[]{:S(2)}) copy-start(f32[128]{0:T(128)} %copy-done.3) | copy-start | bytes 1540
Sparse Core Ops, SparseCore 0:
  36.1 29.7 all-gather.2
  175.6 33.1 reduce-scatter.1

commit v2 on v1

v2 whole, which is shorter than its diff:
```python
import functools
import math

import jax
import jax.numpy as jnp
from jax import lax
from jax.experimental import pallas as pl
from jax.experimental.pallas import tpu as pltpu
from jax.sharding import PartitionSpec as P

norm_eps = 1e-06
objective_scale = 32.0
bf16 = jnp.bfloat16
f32 = jnp.float32
i32 = jnp.int32

CAP = 6
HELD = 2
GROUP = HELD * CAP
PAD = 16
PEERS = 16
HALF = PEERS * CAP
KIND_ROWS = 16
POOLED = 2 * PEERS


def nn(a, b):
    return lax.dot_general(a, b, (((1,), (0,)), ((), ())), preferred_element_type=f32)


def nt(a, b, precision=None):
    return lax.dot_general(
        a, b, (((1,), (1,)), ((), ())), precision=precision, preferred_element_type=f32
    )


def tn(a, b, precision=None):
    return lax.dot_general(
        a, b, (((0,), (0,)), ((), ())), precision=precision, preferred_element_type=f32
    )


def iota(shape, dim):
    return lax.broadcasted_iota(i32, shape, dim)


def shape_of(*dims, dtype=bf16):
    return jax.ShapeDtypeStruct(dims, dtype)


def call(kernel, out, args, flops=0, nbytes=0, smem=(), scratch=(), vmem=40):
    specs = [
        pl.BlockSpec(memory_space=pltpu.SMEM if k in smem else pltpu.VMEM)
        for k in range(len(args))
    ]
    many = isinstance(out, (list, tuple))
    out_specs = [pl.BlockSpec(memory_space=pltpu.VMEM) for _ in (out if many else [out])]
    return pl.pallas_call(
        kernel,
        out_shape=out,
        in_specs=specs,
        out_specs=out_specs if many else out_specs[0],
        scratch_shapes=list(scratch),
        compiler_params=pltpu.CompilerParams(vmem_limit_bytes=vmem * 1024 * 1024),
        cost_estimate=pl.CostEstimate(flops=flops, bytes_accessed=nbytes, transcendentals=0),
    )(*args)


def normal_parts(x):
    centred = x - jnp.mean(x, axis=-1, keepdims=True)
    spread = jnp.mean(centred * centred, axis=-1, keepdims=True)
    scale = lax.rsqrt(spread + norm_eps)
    return centred * scale, scale


def slot_table(pos):
    tokens = pos.shape[1]
    row = iota((PEERS * PAD, tokens), 0)
    want = (row // PAD) * GROUP + row % PAD
    return jnp.where((want == pos) & (row % PAD < GROUP), 1.0, 0.0).astype(bf16)


def dispatch_kernel(me_ref, pos_ref, tok_ref, gain_ref, out_ref):
    pos = pos_ref[...]
    tokens = pos.shape[1]
    normed = normal_parts(tok_ref[...].astype(f32))[0] * gain_ref[...]
    normed = normed.astype(bf16)
    sent = nn(slot_table(pos), normed)
    row = iota((PEERS * PAD, tokens), 0)
    goes = jnp.where((row % PAD == GROUP) & (pos // GROUP == row // PAD), 1.0, 0.0).astype(bf16)
    place = pos % GROUP
    column = (place // CAP) * 128 + me_ref[0] * CAP + place % CAP
    lane = iota((2 * 128, tokens), 0)
    kind = jnp.where(iota((2 * 128, tokens), 1) < tokens // 2, 1.0, 2.0)
    kinds = nt(goes, jnp.where(lane == column, kind, 0.0).astype(bf16))
    width = sent.shape[1]
    first = sent[:, : 2 * 128] + kinds
    out_ref[:, :, : 2 * 128] = first.astype(bf16).reshape(PEERS, PAD, 2 * 128)
    out_ref[:, :, 2 * 128 :] = sent[:, 2 * 128 :].astype(bf16).reshape(
        PEERS, PAD, width - 2 * 128
    )


def repack_table(rows, back):
    shape = (PEERS * PAD, rows) if back else (rows, PEERS * PAD)
    r = iota(shape, 1 if back else 0)
    m = iota(shape, 0 if back else 1)
    held, rest = r // HALF, r % HALF
    from_slot = (rest // CAP) * PAD + held * CAP + rest % CAP
    hit = (r < 2 * HALF) & (m == from_slot)
    if not back:
        hit = hit | ((r == 2 * HALF) & (m % PAD == GROUP))
    return jnp.where(hit, 1.0, 0.0).astype(bf16)


def repack_kernel(in_ref, first_ref, second_ref):
    width = in_ref.shape[2]
    rows = 2 * HALF + KIND_ROWS
    out = nn(repack_table(rows, False), in_ref[...].reshape(PEERS * PAD, width)).astype(bf16)
    first_ref[...] = out[:HALF]
    second_ref[...] = out[HALF:]


def forward_kernel(count, *refs):
    firsts, seconds = refs[:count], refs[count : 2 * count]
    w_in, pooled_ref, slope_ref, pool_ref = refs[2 * count :]
    c0 = math.sqrt(2.0 / math.pi)
    c1 = 0.044715
    for k in range(count):
        for held in range(HELD):
            rows = firsts[k][...] if held == 0 else seconds[k][:HALF, :]
            h = nn(rows, w_in[held])
            h2 = h * h
            t = jnp.tanh(c0 * h * (1.0 + c1 * h2))
            half = 0.5 * (1.0 + t)
            act = (h * half).astype(bf16)
            slope = half + 0.5 * h * (1.0 - t * t) * (c0 * (1.0 + 3.0 * c1 * h2))
            kinds = seconds[k][HALF : HALF + KIND_ROWS, held * 128 : held * 128 + 128]
            kinds = kinds.astype(f32)[:1, :HALF]
            q = iota((POOLED, HALF), 0)
            r = iota((POOLED, HALF), 1)
            hit = (q % PEERS == r // CAP) & (kinds == (q // PEERS + 1).astype(f32))
            pool = jnp.where(hit, 1.0, 0.0).astype(bf16)
            pooled_ref[k, held] = nn(pool, act).astype(bf16)
            slope_ref[k, held] = slope.astype(bf16)
            pool_ref[k, held] = pool


def forward(firsts, seconds, w_in):
    count = len(firsts)
    hidden = w_in.shape[2]
    width = w_in.shape[1]
    return call(
        functools.partial(forward_kernel, count),
        [
            shape_of(count, HELD, POOLED, hidden),
            shape_of(count, HELD, HALF, hidden),
            shape_of(count, HELD, POOLED, HALF),
        ],
        [*firsts, *seconds, w_in],
        flops=count * 2 * 2 * HALF * width * hidden,
        nbytes=w_in.size * 2 + count * 2 * HALF * (width + hidden) * 2,
    )


def block_of(refs, k):
    if k < 2:
        return refs[0].at[k]
    if k < 6:
        return refs[1].at[k - 2]
    return refs[2].at[k - 6]


AROUND = (0, 4, 6, 2)


def out_kernel(a_ref, b_ref, c_ref, w_out, own_ref, other_ref):
    refs = (a_ref, b_ref, c_ref)
    for shift, out_ref in ((1, other_ref), (0, own_ref)):
        total = None
        for held in range(HELD):
            rows = jnp.concatenate([block_of(refs, k + shift)[held] for k in AROUND], axis=0)
            part = nn(rows, w_out[held])
            total = part if total is None else total + part
        out_ref[...] = total.astype(bf16).reshape(out_ref.shape)


def join_kernel(z_ref, own_ref, got_ref, out_ref):
    for ahead in range(4):
        to = lax.rem(z_ref[0] + ahead, 4)
        out_ref[to] = (own_ref[ahead].astype(f32) + got_ref[ahead].astype(f32)).astype(bf16)


def loss_kernel(z_ref, image_ref, text_ref, w_out, grad_ref, rows_ref, prod_ref, gi_ref, gt_ref):
    highest = lax.Precision.HIGHEST
    image, text = image_ref[...], text_ref[...]
    pairs, width = image.shape
    scale = PAIR_TOKENS / math.sqrt(width)
    logits = scale * nt(image, text, highest)

    def softmax(axis):
        top = jnp.exp(logits - jnp.max(logits, axis=axis, keepdims=True))
        return top / jnp.sum(top, axis=axis, keepdims=True)

    same = jnp.where(iota((pairs, pairs), 0) == iota((pairs, pairs), 1), 2.0, 0.0)
    grad_logits = objective_scale * (softmax(1) + softmax(0) - same)
    grad_image = (scale / PAIR_TOKENS) * lax.dot_general(
        grad_logits,
        text,
        (((1,), (0,)), ((), ())),
        precision=highest,
        preferred_element_type=f32,
    )
    grad_text = (scale / PAIR_TOKENS) * tn(grad_logits, image, highest)
    grad_ref[0] = grad_image
    grad_ref[1] = grad_text
    gi_ref[...] = grad_image.astype(bf16)
    gt_ref[...] = grad_text.astype(bf16)
    for at, k in enumerate(AROUND):
        for other in range(2):
            first = other * 4 * PEERS + lax.rem(z_ref[0] + at, 4) * PEERS
            span = pl.ds(pl.multiple_of(first, PEERS), PEERS)
            rows_ref[k + other, :PEERS, :] = gi_ref[span, :]
            rows_ref[k + other, PEERS:, :] = gt_ref[span, :]
    rows = rows_ref[...].reshape(8 * POOLED, width)
    for held in range(HELD):
        prod_ref[held] = nt(rows, w_out[held]).astype(bf16)


def backward_kernel(first, count, pool_ref, slope_ref, prod_ref, w_in, pre_ref, *outs):
    for k in range(count):
        for held in range(HELD):
            prod = prod_ref[held, (first + k) * POOLED : (first + k + 1) * POOLED, :]
            grad_act = tn(pool_ref[k, held], prod)
            pre = (grad_act * slope_ref[k, held].astype(f32)).astype(bf16)
            pre_ref[k, held] = pre
            outs[k][held * HALF : (held + 1) * HALF, :] = nt(pre, w_in[held]).astype(bf16)


def backward(first, pool, slope, prod, w_in):
    count = pool.shape[0]
    width, hidden = w_in.shape[1:]
    return call(
        functools.partial(backward_kernel, first, count),
        [shape_of(count, HELD, HALF, hidden)] + [shape_of(2 * HALF, width)] * count,
        [pool, slope, prod, w_in],
        flops=count * 2 * 2 * HALF * width * hidden,
        nbytes=w_in.size * 2 + count * 2 * HALF * (width + hidden) * 2,
    )


def grad_in_kernel(*refs):
    blocks, pres, out_ref, x_ref, p_ref = refs[:16], refs[16:19], refs[19], refs[20], refs[21]
    held = pl.program_id(0)

    def fill(which):
        for k in range(8):
            span = slice(k * HALF, (k + 1) * HALF)
            x_ref[span, :] = blocks[8 * which + k][:HALF, :]
            p_ref[span, :] = block_of(pres, k)[which]

    for which in range(HELD):
        pl.when(held == which)(functools.partial(fill, which))
    out_ref[0] = tn(x_ref[...], p_ref[...])


def grad_in(firsts, seconds, pres, width, hidden):
    whole = pl.BlockSpec(memory_space=pltpu.VMEM)
    return pl.pallas_call(
        grad_in_kernel,
        grid=(HELD,),
        out_shape=shape_of(HELD, width, hidden, dtype=f32),
        in_specs=[whole] * 19,
        out_specs=pl.BlockSpec((1, width, hidden), lambda i: (i, 0, 0)),
        scratch_shapes=[
            pltpu.VMEM((8 * HALF, width), bf16),
            pltpu.VMEM((8 * HALF, hidden), bf16),
        ],
        compiler_params=pltpu.CompilerParams(vmem_limit_bytes=44 * 1024 * 1024),
        cost_estimate=pl.CostEstimate(
            flops=2 * 2 * 8 * HALF * width * hidden, bytes_accessed=17_000_000, transcendentals=0
        ),
    )(*firsts, *seconds, *pres)


def grad_out_kernel(a_ref, b_ref, c_ref, rows_ref, out_ref):
    refs = (a_ref, b_ref, c_ref)
    held = pl.program_id(0)
    width = rows_ref.shape[2]
    pooled = jnp.concatenate([block_of(refs, k)[held] for k in range(8)], axis=0)
    out_ref[0] = tn(pooled, rows_ref[...].reshape(8 * POOLED, width))


def grad_out(pooled, rows, width, hidden):
    whole = pl.BlockSpec(memory_space=pltpu.VMEM)
    return pl.pallas_call(
        grad_out_kernel,
        grid=(HELD,),
        out_shape=shape_of(HELD, hidden, width, dtype=f32),
        in_specs=[whole] * 4,
        out_specs=pl.BlockSpec((1, hidden, width), lambda i: (i, 0, 0)),
        compiler_params=pltpu.CompilerParams(vmem_limit_bytes=32 * 1024 * 1024),
        cost_estimate=pl.CostEstimate(
            flops=2 * 2 * 8 * POOLED * width * hidden, bytes_accessed=9_000_000, transcendentals=0
        ),
    )(*pooled, rows)


def settle_kernel(own_ref, got_ref, la_ref, lb_ref, ra_ref, rb_ref, out_ref):
    width = own_ref.shape[1]
    total = own_ref[...].astype(f32) + got_ref[...].astype(f32)
    first = total[:HALF] + la_ref[...].astype(f32) + ra_ref[...].astype(f32)
    second = total[HALF:] + lb_ref[...].astype(f32) + rb_ref[...].astype(f32)
    table = repack_table(2 * HALF, True)
    rows = jnp.concatenate([first.astype(bf16), second.astype(bf16)], axis=0)
    out_ref[...] = nn(table, rows).astype(bf16).reshape(PEERS, PAD, width)


def tail_kernel(pos_ref, tok_ref, gain_ref, grad_ref, back_ref, out_ref):
    tokens, width = tok_ref.shape
    grad_normed = tn(slot_table(pos_ref[...]), back_ref[...].reshape(PEERS * PAD, width))
    unit, scale = normal_parts(tok_ref[...].astype(f32))
    grad = grad_normed * gain_ref[...]
    grad = scale * (
        grad
        - jnp.mean(grad, axis=-1, keepdims=True)
        - unit * jnp.mean(grad * unit, axis=-1, keepdims=True)
    )
    image = iota((tokens, width), 0) < tokens // 2
    mixed = jnp.where(image, grad_ref[0:1, :], grad_ref[1:2, :])
    out_ref[...] = (mixed + grad).astype(bf16)


PAIR_TOKENS = 64


def body(tokens, expert_ids, slots, ln_gain, w_in, w_out):
    width, hidden = w_in.shape[1:]
    row_count = tokens.shape[1] * tokens.shape[2]
    flat = tokens.reshape(row_count, width)
    gain = ln_gain.reshape(1, width)
    pos = (expert_ids * CAP + slots).reshape(1, row_count)
    data = lax.axis_index("dp")
    group = lax.axis_index("expert")
    z = (data // 2).reshape(1)
    everyone = ("dp", "expert")
    cores = [[d * PEERS + e for d in range(c, 8, 2) for e in range(PEERS)] for c in range(2)]

    def up(x):
        return lax.ppermute(x, "dp", [(i, (i + 2) % 8) for i in range(8)])

    def down(x):
        return lax.ppermute(x, "dp", [(i, (i + 6) % 8) for i in range(8)])

    def swap(x):
        return lax.ppermute(x, "dp", [(i, i ^ 1) for i in range(8)])

    def exchange(x):
        return lax.all_to_all(x, "expert", split_axis=0, concat_axis=0, tiled=True)

    def spread(x):
        return lax.all_to_all(
            x, everyone, split_axis=0, concat_axis=0, tiled=True, axis_index_groups=cores
        )

    sent = call(
        dispatch_kernel,
        shape_of(PEERS, PAD, width),
        [group.reshape(1), pos, flat, gain],
        smem=(0,),
    )
    first, second = call(
        repack_kernel,
        [shape_of(HALF, width), shape_of(HALF + KIND_ROWS, width)],
        [exchange(sent)],
    )

    a, b = [None] * 8, [None] * 8
    a[0], b[0] = first, second
    a[2] = up(first)
    b[4] = down(second)
    b[2] = up(second)
    a[4] = down(first)
    a[6] = up(a[2])
    b[6] = down(b[4])
    for k in (0, 2, 4, 6):
        a[k + 1] = swap(a[k])
        b[k + 1] = swap(b[k])
    made = [forward(a[i:j], b[i:j], w_in) for i, j in ((0, 2), (2, 6), (6, 8))]
    pooled = [m[0] for m in made]
    slope = [m[1] for m in made]
    pool = [m[2] for m in made]

    own, other = call(
        out_kernel,
        [shape_of(4, POOLED, width), shape_of(4, POOLED, width)],
        [*pooled, w_out],
        flops=2 * 8 * POOLED * width * hidden * HELD,
        nbytes=w_out.size * 2,
    )
    joined = call(
        join_kernel, shape_of(4, POOLED, width), [z, own, swap(other)], smem=(0,)
    )
    joined = joined.reshape(4, 2, PEERS, width).transpose(0, 2, 1, 3).reshape(-1, 2, width)
    parts = spread(joined)
    emb = jnp.sum(parts.astype(f32), axis=0) + jnp.sum(
        flat.reshape(2, PAIR_TOKENS, width).astype(f32), axis=1
    )
    emb = spread(jnp.broadcast_to((emb / PAIR_TOKENS)[None], (4 * PEERS, 2, width)))
    emb_other = swap(emb)
    image = jnp.concatenate([emb[:, 0], emb_other[:, 0]], axis=0)
    text = jnp.concatenate([emb[:, 1], emb_other[:, 1]], axis=0)
    grad_pooled, rows, prod = call(
        loss_kernel,
        [
            shape_of(2, 8 * PEERS, width, dtype=f32),
            shape_of(8, POOLED, width),
            shape_of(HELD, 8 * POOLED, hidden),
        ],
        [z, image, text, w_out],
        smem=(0,),
        scratch=[pltpu.VMEM((8 * PEERS, width), bf16), pltpu.VMEM((8 * PEERS, width), bf16)],
        flops=2 * 8 * POOLED * width * hidden * HELD,
        nbytes=w_out.size * 2,
    )
    grad_own = lax.dynamic_index_in_dim(
        grad_pooled, (data // 2) * PEERS + group, axis=1, keepdims=False
    )

    def plus(x, y):
        return (x.astype(f32) + y.astype(f32)).astype(bf16)

    pre_c, p6, p7 = backward(6, pool[2], slope[2], prod, w_in)
    r6 = plus(p6, swap(p7))
    from_below = up(r6[:HALF])
    from_above = down(r6[HALF:])
    pre_b, p2, p3, p4, p5 = backward(2, pool[1], slope[1], prod, w_in)
    r4 = plus(p4, swap(p5))
    r2 = plus(p2, swap(p3))
    low_b = up(r4[HALF:])
    high_a = down(r2[:HALF])
    low_a = up(plus(r4[:HALF], from_below))
    high_b = down(plus(r2[HALF:], from_above))
    pre_a, p0, p1 = backward(0, pool[0], slope[0], prod, w_in)
    got = swap(p1)
    grad_w_in = grad_in(a, b, [pre_a, pre_b, pre_c], width, hidden)
    grad_w_out = grad_out(pooled, rows, width, hidden)

    back = exchange(
        call(
            settle_kernel,
            shape_of(PEERS, PAD, width),
            [p0, got, low_a, low_b, high_a, high_b],
        )
    )
    grad_flat = call(
        tail_kernel, shape_of(row_count, width), [pos, flat, gain, grad_own, back]
    )
    return (grad_flat.reshape(tokens.shape), grad_w_in, grad_w_out)


def solution(mesh):
    placed = (
        P(("dp", "expert"), None, None, None),
        P(("dp", "expert"), None, None),
        P(("dp", "expert"), None, None),
        P(),
        P("expert", None, "dp"),
        P("expert", "dp", None),
    )
    return jax.shard_map(
        body,
        mesh=mesh,
        in_specs=placed,
        out_specs=(
            P(("dp", "expert"), None, None, None),
            P("expert", None, "dp"),
            P("expert", "dp", None),
        ),
        check_vma=False,
    )
```

time: 246 us -> 165 us (0.67)
  blocking collectives: 114 us -> 38.7 us
  matrix products: 39 us -> 0 us
  Pallas kernels: 0 us -> 36.5 us
  starting transfers between devices: 7.08 us -> 30.5 us
  local copies, waits for them, and re-layouts: 31.2 us -> 12.8 us
  between operations: 14.3 us -> 1.55 us
  waiting for transfers between devices: 28.4 us -> 40.8 us
  other arithmetic: 10.5 us -> 3.57 us
    all_gather x1 -> x0, blocking collectives: 48.1 us -> none  [body(): all_pos = lax.all_gather(position[None], everyone, axis=0, tiled=True)]
    dot_general x13 -> x0, matrix products: 39 us -> none  [the longest x10 36.7 us: mm(): return jnp.einsum(spec, a, b, preferred_element_type=f32).astype(out)]
    pallas_call x0 -> x15, Pallas kernels: none -> 36.5 us  [the longest x13 27 us: call(): pl.pallas_call(kernel, out_shape=out, in_specs=specs, out_specs=out_specs...]
    ppermute x0 -> x26, waiting for transfers between devices: none -> 29.1 us  [the longest x6 16.5 us: up(): return lax.ppermute(x, 'dp', [(i, (i + 2) % 8) for i in range(8)])]
    all_to_all x3 -> x2, blocking collectives: 65.9 us -> 38.7 us  [the longest x1 19.9 us: exchange(): return lax.all_to_all(x, 'expert', split_axis=0, concat_axis=0, tiled=True)]
    reduce_scatter x1 -> x0, waiting for transfers between devices: 23.5 us -> none  [body(): lax.psum_scatter(grad_partial.reshape(datas * total * cap, width), 'dp',...]
    ppermute x0 -> x26, starting transfers between devices: none -> 21.5 us  [the longest x6 15.5 us: down(): return lax.ppermute(x, 'dp', [(i, (i + 6) % 8) for i in range(8)])]
    reshape x8 -> x4, local copies, waits for them, and re-layouts: 12.9 us -> 1.87 us  [the longest x2 1.09 us: body(): joined.reshape(4, 2, PEERS, width).transpose(0, 2, 1, 3)]
  transfers between devices with their start and end apart: 3 -> 28, of which waited for: 2 -> 13; matrix products, arithmetic and copies ran while one was open for 9% -> 2% of each run, Pallas kernels for 0% -> 13%
where the time goes in v2:
time: 165 us; the launch traced here: 164 us
  waiting for transfers between devices  40.8 us (25%)
  blocking collectives  38.7 us (23%)
  Pallas kernels  36.5 us (22%)
  starting transfers between devices  30.5 us (18%)
  local copies, waits for them, and re-layouts  12.8 us (8%)
  other arithmetic  3.57 us (2%)
    pallas_call x13, Pallas kernels, call(): pl.pallas_call(kernel, out_shape=out, in_specs=specs, out_specs=out_specs...  27 us
    all_to_all x1, blocking collectives, exchange(): return lax.all_to_all(x, 'expert', split_axis=0, concat_axis=0, tiled=True)  19.9 us
    all_to_all x1, blocking collectives, spread(): lax.all_to_all(x, everyone, split_axis=0, concat_axis=0, tiled=True, axis...  18.9 us
    ppermute x6, waiting for transfers between devices, up(): return lax.ppermute(x, 'dp', [(i, (i + 2) % 8) for i in range(8)])  16.5 us
    ppermute x6, starting transfers between devices, down(): return lax.ppermute(x, 'dp', [(i, (i + 6) % 8) for i in range(8)])  15.5 us
    all_to_all x1, waiting for transfers between devices, spread(): lax.all_to_all(x, everyone, split_axis=0, concat_axis=0, tiled=True, axis...  10.9 us
    unnamed x131, local copies, waits for them, and re-layouts  9.66 us
    ppermute x6, waiting for transfers between devices, down(): return lax.ppermute(x, 'dp', [(i, (i + 6) % 8) for i in range(8)])  8.97 us
  transfers between devices with their start and end apart: 28, of which 13 were waited for; matrix products, arithmetic and copies ran while one was open for 2% of the time, Pallas kernels for 13%

profile of v2, /device:TPU:0, one launch (start us, length us, event | category | flops | bytes accessed | tf_op | source)
XLA Modules:
  0.0 164.5 jit_solution(8379654331915590809)
XLA Ops:
  0.6 0.7 multiply_add_fusion
  1.4 0.7 reshape.39.gain_ref
  2.1 1.0 copy-done.4
  3.1 0.6 shard_map.85
  3.7 19.9 %all_to_all.20.in_ref = bf16[16,16,1280]{2,1,0:T(8,128)(2,1)S(1)} all-to-all(bf16[16,16,1280]{2,1,0:T(8,128)(2,1)S(1)} %shard_map.85), channel_id=1, replica_groups=mesh['dp'=8,'expert'=16] {'expert'}, dimensions={0} | all-to-all | bytes 1310720 | tf_op jit(solution)/shard_map/all_to_all | solution.py:359
  23.6 0.4 shard_map.86
  24.0 4.1 %collective-permute-start.4 = (bf16[96,1280]{1,0:T(8,128)(2,1)S(1)}, bf16[96,1280]{1,0:T(8,128)(2,1)S(1)}, u32[]{:S(2)}, u32[]{:S(2)}) collective-permute-start(bf16[96,1280]{1,0:T(8,128)(2,1)S(1)} %get-tuple-element.30.refs_0_), channel_id=1, source_target_pairs={{0,96},{16,112},{32,0},{48,16},{64,32},{80,48},{96,64},{112,80},{1... | collective-permute-start | bytes 737288 | tf_op jit(solution)/shard_map/ppermute | solution.py:353
  28.1 0.4 collective-permute-start.8
  28.5 1.6 collective-permute-start.2
  30.1 4.3 %collective-permute-done.4.refs_2_.refs_4_ = bf16[96,1280]{1,0:T(8,128)(2,1)S(1)} collective-permute-done((bf16[96,1280]{1,0:T(8,128)(2,1)S(1)}, bf16[96,1280]{1,0:T(8,128)(2,1)S(1)}, u32[]{:S(2)}, u32[]{:S(2)}) %collective-permute-start.4) | collective-permute-done | bytes 245792 | tf_op jit(solution)/shard_map/ppermute | solution.py:353
  34.5 2.8 %collective-permute-done.2.refs_0_.refs_2_ = bf16[96,1280]{1,0:T(8,128)(2,1)S(1)} collective-permute-done((bf16[96,1280]{1,0:T(8,128)(2,1)S(1)}, bf16[96,1280]{1,0:T(8,128)(2,1)S(1)}, u32[]{:S(2)}, u32[]{:S(2)}) %collective-permute-start.2) | collective-permute-done | bytes 245792 | tf_op jit(solution)/shard_map/ppermute | solution.py:350
  37.3 0.7 collective-permute-done.8.refs_6_.refs_12_
  38.0 3.7 %collective-permute-start.12 = (bf16[112,1280]{1,0:T(8,128)(2,1)S(1)}, bf16[112,1280]{1,0:T(8,128)(2,1)S(1)}, u32[]{:S(2)}, u32[]{:S(2)}) collective-permute-start(bf16[112,1280]{1,0:T(8,128)(2,1)S(1)} %collective-permute-done.8.refs_6_.refs_12_), channel_id=1, source_target_pairs={{0,96},{16,112},{32,0},{48,16},{64,32},{80,48},{96,64},{112,80},{1... | collective-permute-start | bytes 860168 | tf_op jit(solution)/shard_map/ppermute | solution.py:353
  41.7 0.3 collective-permute-done.6.refs_4_.refs_10_
  42.0 0.5 collective-permute-start.7
  42.6 3.9 %collective-permute-done.12.refs_2_.refs_14_ = bf16[112,1280]{1,0:T(8,128)(2,1)S(1)} collective-permute-done((bf16[112,1280]{1,0:T(8,128)(2,1)S(1)}, bf16[112,1280]{1,0:T(8,128)(2,1)S(1)}, u32[]{:S(2)}, u32[]{:S(2)}) %collective-permute-start.12) | collective-permute-done | bytes 286752 | tf_op jit(solution)/shard_map/ppermute | solution.py:353
  46.6 2.5 %collective-permute-done.10.refs_0_.refs_6_ = bf16[96,1280]{1,0:T(8,128)(2,1)S(1)} collective-permute-done((bf16[96,1280]{1,0:T(8,128)(2,1)S(1)}, bf16[96,1280]{1,0:T(8,128)(2,1)S(1)}, u32[]{:S(2)}, u32[]{:S(2)}) %collective-permute-start.10) | collective-permute-done | bytes 245792 | tf_op jit(solution)/shard_map/ppermute | solution.py:350
  49.1 2.0 %copy-done = bf16[2,1280,640]{2,1,0:T(8,128)(2,1)S(1)} copy-done((bf16[2,1280,640]{2,1,0:T(8,128)(2,1)S(1)}, bf16[2,1280,640]{2,1,0:T(8,128)(2,1)}, u32[]{:S(2)}) %copy-start) | copy-done | bytes 3276824
  51.1 2.0 %shard_map.87 = (bf16[2,2,32,640]{3,2,1,0:T(8,128)(2,1)S(1)}, bf16[2,2,96,640]{3,2,1,0:T(8,128)(2,1)S(1)}, bf16[2,2,32,96]{3,2,1,0:T(8,128)(2,1)S(1)}) custom-call(bf16[96,1280]{1,0:T(8,128)(2,1)S(1)} %get-tuple-element.30.refs_0_, bf16[96,1280]{1,0:T(8,128)(2,1)S(1)} %collective-permute-done.refs_1_, ...), custom_call_target="tpu_custom_call" | custom-call | flops 629145600 | bytes 4751360 | tf_op jit(solution)/shard_map/pallas_call | solution.py:58
  53.2 0.8 copy-done.52
  53.9 0.6 copy-done.60
  54.6 3.9 %shard_map.88 = (bf16[4,2,32,640]{3,2,1,0:T(8,128)(2,1)S(1)}, bf16[4,2,96,640]{3,2,1,0:T(8,128)(2,1)S(1)}, bf16[4,2,32,96]{3,2,1,0:T(8,128)(2,1)S(1)}) custom-call(bf16[96,1280]{1,0:T(8,128)(2,1)S(1)} %collective-permute-done.2.refs_0_.refs_2_, bf16[96,1280]{1,0:T(8,128)(2,1)S(1)} %collective-permute-done.3.refs_1_.refs_3_, ...), custom_call_target="tpu_custom_call" | custom-call | flops 1258291200 | bytes 6225920 | tf_op jit(solution)/shard_map/pallas_call | solution.py:58
  58.6 0.9 copy-done.24
  59.6 2.0 %shard_map.89 = (bf16[2,2,32,640]{3,2,1,0:T(8,128)(2,1)S(1)}, bf16[2,2,96,640]{3,2,1,0:T(8,128)(2,1)S(1)}, bf16[2,2,32,96]{3,2,1,0:T(8,128)(2,1)S(1)}) custom-call(bf16[96,1280]{1,0:T(8,128)(2,1)S(1)} %collective-permute-done.10.refs_0_.refs_6_, bf16[96,1280]{1,0:T(8,128)(2,1)S(1)} %collective-permute-done.11.refs_1_.refs_7_, ...), custom_call_target="tpu_custom_call" | custom-call | flops 629145600 | bytes 4751360 | tf_op jit(solution)/shard_map/pallas_call | solution.py:58
  61.8 1.5 shard_map.90
  63.3 0.7 copy-done.56
  64.0 0.5 collective-permute-start.14
  64.5 1.6 collective-permute-done.14.got_ref
  66.1 1.0 copy-done.57
  67.1 1.1 shard_map.91
  68.2 1.1 copy.11
  69.3 5.5 %all-to-all-start.1 = ((bf16[64,2,1280]{2,1,0:T(2,128)(2,1)}), bf16[64,2,1280]{2,1,0:T(2,128)(2,1)}, u32[]{:S(2)}, u32[]{:S(2)}) async-start(bf16[64,2,1280]{2,1,0:T(2,128)(2,1)} %copy.11), calls=%async_computation.1 | async-start | bytes 655360 | tf_op jit(solution)/shard_map/all_to_all | solution.py:362
  74.7 1.0 convert_reduce_fusion
  75.8 10.9 %all-to-all-done.1 = bf16[64,2,1280]{2,1,0:T(2,128)(2,1)} async-done(((bf16[64,2,1280]{2,1,0:T(2,128)(2,1)}), bf16[64,2,1280]{2,1,0:T(2,128)(2,1)}, u32[]{:S(2)}, u32[]{:S(2)}) %all-to-all-start.1) | async-done | bytes 327712 | tf_op jit(solution)/shard_map/all_to_all | solution.py:362
  86.7 1.3 convert_reduce_fusion.1
  88.2 18.9 %all_to_all.21 = f32[64,2,1280]{2,1,0:T(2,128)S(1)} all-to-all(f32[64,2,1280]{2,1,0:T(2,128)S(1)} %broadcast_in_dim.2), channel_id=1, replica_groups={{0,1,2,3,4,5,6,7,8,9,10,11,12,13,14,15,32,33,34,35,36,37,38,39,40,41,42..., dimensions={0} | all-to-all | bytes 1310720 | tf_op jit(solution)/shard_map/all_to_all | solution.py:362
  107.1 0.3 collective-permute-start.15
  107.4 2.0 %collective-permute-done.15 = f32[64,2,1280]{2,0,1:T(8,128)S(1)} collective-permute-done((f32[64,2,1280]{2,0,1:T(8,128)S(1)}, f32[64,2,1280]{2,0,1:T(8,128)S(1)}, u32[]{:S(2)}, u32[]{:S(2)}) %collective-permute-start.15) | collective-permute-done | bytes 655392 | tf_op jit(solution)/shard_map/ppermute | solution.py:356
  109.7 4.1 %shard_map.92 = (f32[2,128,1280]{2,1,0:T(8,128)S(1)}, bf16[8,32,1280]{2,1,0:T(8,128)(2,1)S(1)}, bf16[2,256,640]{2,1,0:T(8,128)(2,1)S(1)}) custom-call(s32[1]{0:T(128)} %bitcast.1.z_ref, f32[128,1280]{1,0:T(8,128)S(1)} %get-tuple-element.63.image_ref, f32[128,1280]{1,0:T(8,128)S(1)} %get-tuple-element.64.text_ref, bf16[2,640,1280]{2,1,0:T(8,128)(2,1)S(1)} %copy-done.3), custom_call_target="tpu_custom_call" | custom-call | flops 838860800 | bytes 3276800 | tf_op jit(solution)/shard_map/pallas_call | solution.py:58
  113.8 2.2 %shard_map.95 = (bf16[2,2,96,640]{3,2,1,0:T(8,128)(2,1)S(1)}, bf16[192,1280]{1,0:T(8,128)(2,1)S(1)}, bf16[192,1280]{1,0:T(8,128)(2,1)S(1)}) custom-call(bf16[2,2,32,96]{3,2,1,0:T(8,128)(2,1)S(1)} %copy-done.63, bf16[2,2,96,640]{3,2,1,0:T(8,128)(2,1)S(1)} %copy-done.55, bf16[2,256,640]{2,1,0:T(8,128)(2,1)S(1)} %get-tuple-element.40.prod_ref, ...), custom_call_target="tpu_custom_call" | custom-call | flops 629145600 | bytes 4751360 | tf_op jit(solution)/shard_map/pallas_call | solution.py:58
  116.0 0.8 copy-done.48
  116.9 2.2 %shard_map.93 = (bf16[2,2,96,640]{3,2,1,0:T(8,128)(2,1)S(1)}, bf16[192,1280]{1,0:T(8,128)(2,1)S(1)}, bf16[192,1280]{1,0:T(8,128)(2,1)S(1)}) custom-call(bf16[2,2,32,96]{3,2,1,0:T(8,128)(2,1)S(1)} %copy-done.61, bf16[2,2,96,640]{3,2,1,0:T(8,128)(2,1)S(1)} %copy-done.53, bf16[2,256,640]{2,1,0:T(8,128)(2,1)S(1)} %get-tuple-element.40.prod_ref, ...), custom_call_target="tpu_custom_call" | custom-call | flops 629145600 | bytes 4751360 | tf_op jit(solution)/shard_map/pallas_call | solution.py:58
  119.2 0.8 copy-done.50
  120.0 0.4 collective-permute-start.16
  120.4 4.3 %shard_map.94 = (bf16[4,2,96,640]{3,2,1,0:T(8,128)(2,1)S(1)}, bf16[192,1280]{1,0:T(8,128)(2,1)S(1)}, bf16[192,1280]{1,0:T(8,128)(2,1)S(1)}, bf16[192,1280]{1,0:T(8,128)(2,1)S(1)}, bf16[192,1280]{1,0:T(8,128)(2,1)S(1)}) custom-call(bf16[4,2,32,96]{3,2,1,0:T(8,128)(2,1)S(1)} %copy-done.59, bf16[4,2,96,640]{3,2,1,0:T(8,128)(2,1)S(1)} %copy-done.25, ...), custom_call_target="tpu_custom_call" | custom-call | flops 1258291200 | bytes 6225920 | tf_op jit(solution)/shard_map/pallas_call | solution.py:58
  124.7 0.2 collective-permute-start.17
  124.9 0.4 collective-permute-start.22
  125.5 0.9 collective-permute-start.24
  126.4 1.1 collective-permute-start.19
  127.7 0.6 collective-permute-start.21
  128.5 3.1 %collective-permute-start.23 = (bf16[96,1280]{1,0:T(8,128)(2,1)S(1)}, bf16[96,1280]{1,0:T(8,128)(2,1)S(1)}, u32[]{:S(2)}, u32[]{:S(2)}) collective-permute-start(bf16[96,1280]{1,0:T(8,128)(2,1)S(1)} %slice.47), channel_id=1, source_target_pairs={{0,96},{16,112},{32,0},{48,16},{64,32},{80,48},{96,64},{112,80},{1... | collective-permute-start | bytes 737288 | tf_op jit(solution)/shard_map/ppermute | solution.py:353
  131.5 4.9 %collective-permute-done.19 = bf16[96,1280]{1,0:T(8,128)(2,1)S(1)} collective-permute-done((bf16[96,1280]{1,0:T(8,128)(2,1)S(1)}, bf16[96,1280]{1,0:T(8,128)(2,1)S(1)}, u32[]{:S(2)}, u32[]{:S(2)}) %collective-permute-start.19) | collective-permute-done | bytes 245792 | tf_op jit(solution)/shard_map/ppermute | solution.py:350
  136.7 3.3 %collective-permute-start.25 = (bf16[96,1280]{1,0:T(8,128)(2,1)S(1)}, bf16[96,1280]{1,0:T(8,128)(2,1)S(1)}, u32[]{:S(2)}, u32[]{:S(2)}) collective-permute-start(bf16[96,1280]{1,0:T(8,128)(2,1)S(1)} %add_convert_fusion.3), channel_id=1, source_target_pairs={{0,96},{16,112},{32,0},{48,16},{64,32},{80,48},{96,64},{112,80},{1... | collective-permute-start | bytes 737288 | tf_op jit(solution)/shard_map/ppermute | solution.py:353
  140.0 1.8 %collective-permute-done.21.lb_ref = bf16[96,1280]{1,0:T(8,128)(2,1)S(1)} collective-permute-done((bf16[96,1280]{1,0:T(8,128)(2,1)S(1)}, bf16[96,1280]{1,0:T(8,128)(2,1)S(1)}, u32[]{:S(2)}, u32[]{:S(2)}) %collective-permute-start.21) | collective-permute-done | bytes 245792 | tf_op jit(solution)/shard_map/ppermute | solution.py:350
  141.7 4.1 %collective-permute-done.20.la_ref = bf16[96,1280]{1,0:T(8,128)(2,1)S(1)} collective-permute-done((bf16[96,1280]{1,0:T(8,128)(2,1)S(1)}, bf16[96,1280]{1,0:T(8,128)(2,1)S(1)}, u32[]{:S(2)}, u32[]{:S(2)}) %collective-permute-start.20) | collective-permute-done | bytes 245792 | tf_op jit(solution)/shard_map/ppermute | solution.py:350
  145.9 1.3 shard_map.96
  147.2 3.6 %all-to-all-start.3 = ((bf16[16,16,1280]{2,1,0:T(8,128)(2,1)}), bf16[16,16,1280]{2,1,0:T(8,128)(2,1)S(1)}, u32[]{:S(2)}, u32[]{:S(2)}) async-start(bf16[16,16,1280]{2,1,0:T(8,128)(2,1)} %shard_map.96), calls=%async_computation.3 | async-start | bytes 1310720 | tf_op jit(solution)/shard_map/all_to_all | solution.py:359
  150.8 0.9 constant_dynamic-slice_fusion
  152.0 4.0 %shard_map.99 = f32[2,640,1280]{2,1,0:T(8,128)} custom-call(bf16[2,2,32,640]{3,2,1,0:T(8,128)(2,1)S(1)} %copy-done.45, bf16[4,2,32,640]{3,2,1,0:T(8,128)(2,1)S(1)} %copy-done.7, bf16[2,2,32,640]{3,2,1,0:T(8,128)(2,1)S(1)} %copy-done.47, bf16[8,32,1280]{2,1,0:T(8,128)(2,1)S(1)} %copy-done.43), custom_call_target="tpu_custom_call" | custom-call | flops 838860800 | bytes 9000000 | tf_op jit(solution)/shard_map/pallas_call | solution.py:296
  156.1 0.2 copy-done.49
  156.3 0.5 copy-done.51
  156.8 5.6 %shard_map.98 = f32[2,1280,640]{2,1,0:T(8,128)} custom-call(bf16[96,1280]{1,0:T(8,128)(2,1)S(1)} %get-tuple-element.30.refs_0_, bf16[96,1280]{1,0:T(8,128)(2,1)S(1)} %copy-done.29, bf16[96,1280]{1,0:T(8,128)(2,1)S(1)} %copy-done.37, bf16[96,1280]{1,0:T(8,128)(2,1)S(1)} %copy-done.41, bf16[96,1280]{1,0:T(8,128)(2,1)S(1)} %copy-done.35, ...), custom_call_target="tpu_custom_call" | custom-call | flops 2516582400 | bytes 17000000 | tf_op jit(solution)/shard_map/pallas_call | solution.py:269
  162.4 0.7 all-to-all-done.3.back_ref
  163.2 1.3 shard_map.97
  (162 shorter events, 1.8 us)
Async XLA Ops:
  24.0 30.6 %copy-start.8 = (bf16[112,1280]{1,0:T(8,128)(2,1)}, bf16[112,1280]{1,0:T(8,128)(2,1)S(1)}, u32[]{:S(2)}) copy-start(bf16[112,1280]{1,0:T(8,128)(2,1)S(1)} %get-tuple-element.31.refs_2_.refs_8_) | copy-start | bytes 860164
  24.0 10.5 %collective-permute-start.4 = (bf16[96,1280]{1,0:T(8,128)(2,1)S(1)}, bf16[96,1280]{1,0:T(8,128)(2,1)S(1)}, u32[]{:S(2)}, u32[]{:S(2)}) collective-permute-start(bf16[96,1280]{1,0:T(8,128)(2,1)S(1)} %get-tuple-element.30.refs_0_), channel_id=1, source_target_pairs={{0,96},{16,112},{32,0},{48,16},{64,32},{80,48},{96,64},{112,80},{1... | collective-permute-start | bytes 737288 | tf_op jit(solution)/shard_map/ppermute | solution.py:353
  28.1 9.9 %collective-permute-start.8 = (bf16[112,1280]{1,0:T(8,128)(2,1)S(1)}, bf16[112,1280]{1,0:T(8,128)(2,1)S(1)}, u32[]{:S(2)}, u32[]{:S(2)}) collective-permute-start(bf16[112,1280]{1,0:T(8,128)(2,1)S(1)} %get-tuple-element.31.refs_2_.refs_8_), channel_id=1, source_target_pairs={{0,96},{16,112},{32,0},{48,16},{64,32},{80,48},{96,64},{112,80},{1... | collective-permute-start | bytes 860168 | tf_op jit(solution)/shard_map/ppermute | solution.py:353
  28.5 8.8 %collective-permute-start.2 = (bf16[96,1280]{1,0:T(8,128)(2,1)S(1)}, bf16[96,1280]{1,0:T(8,128)(2,1)S(1)}, u32[]{:S(2)}, u32[]{:S(2)}) collective-permute-start(bf16[96,1280]{1,0:T(8,128)(2,1)S(1)} %get-tuple-element.30.refs_0_), channel_id=1, source_target_pairs={{0,32},{16,48},{32,64},{48,80},{64,96},{80,112},{96,0},{112,16},{1... | collective-permute-start | bytes 737288 | tf_op jit(solution)/shard_map/ppermute | solution.py:350
  30.1 11.6 %collective-permute-start = (bf16[96,1280]{1,0:T(8,128)(2,1)S(1)}, bf16[96,1280]{1,0:T(8,128)(2,1)S(1)}, u32[]{:S(2)}, u32[]{:S(2)}) collective-permute-start(bf16[96,1280]{1,0:T(8,128)(2,1)S(1)} %get-tuple-element.30.refs_0_), channel_id=1, source_target_pairs={{0,16},{16,0},{32,48},{48,32},{64,80},{80,64},{96,112},{112,96},{1... | collective-permute-start | bytes 737288 | tf_op jit(solution)/shard_map/ppermute | solution.py:356
  30.1 11.9 %collective-permute-start.6 = (bf16[112,1280]{1,0:T(8,128)(2,1)S(1)}, bf16[112,1280]{1,0:T(8,128)(2,1)S(1)}, u32[]{:S(2)}, u32[]{:S(2)}) collective-permute-start(bf16[112,1280]{1,0:T(8,128)(2,1)S(1)} %get-tuple-element.31.refs_2_.refs_8_), channel_id=1, source_target_pairs={{0,32},{16,48},{32,64},{48,80},{64,96},{80,112},{96,0},{112,16},{1... | collective-permute-start | bytes 860168 | tf_op jit(solution)/shard_map/ppermute | solution.py:350
  34.5 24.0 %copy-start.34 = (bf16[96,1280]{1,0:T(8,128)(2,1)}, bf16[96,1280]{1,0:T(8,128)(2,1)S(1)}, u32[]{:S(2)}) copy-start(bf16[96,1280]{1,0:T(8,128)(2,1)S(1)} %collective-permute-done.4.refs_2_.refs_4_) | copy-start | bytes 737284
  34.5 7.5 %collective-permute-start.1 = (bf16[112,1280]{1,0:T(8,128)(2,1)S(1)}, bf16[112,1280]{1,0:T(8,128)(2,1)S(1)}, u32[]{:S(2)}, u32[]{:S(2)}) collective-permute-start(bf16[112,1280]{1,0:T(8,128)(2,1)S(1)} %get-tuple-element.31.refs_2_.refs_8_), channel_id=1, source_target_pairs={{0,16},{16,0},{32,48},{48,32},{64,80},{80,64},{96,112},{112,96},{1... | collective-permute-start | bytes 860168 | tf_op jit(solution)/shard_map/ppermute | solution.py:356
  37.3 21.2 %copy-start.36 = (bf16[96,1280]{1,0:T(8,128)(2,1)}, bf16[96,1280]{1,0:T(8,128)(2,1)S(1)}, u32[]{:S(2)}) copy-start(bf16[96,1280]{1,0:T(8,128)(2,1)S(1)} %collective-permute-done.2.refs_0_.refs_2_) | copy-start | bytes 737284
  37.3 5.2 %collective-permute-start.5 = (bf16[96,1280]{1,0:T(8,128)(2,1)S(1)}, bf16[96,1280]{1,0:T(8,128)(2,1)S(1)}, u32[]{:S(2)}, u32[]{:S(2)}) collective-permute-start(bf16[96,1280]{1,0:T(8,128)(2,1)S(1)} %collective-permute-done.4.refs_2_.refs_4_), channel_id=1, source_target_pairs={{0,16},{16,0},{32,48},{48,32},{64,80},{80,64},{96,112},{112,96},{1... | collective-permute-start | bytes 737288 | tf_op jit(solution)/shard_map/ppermute | solution.py:356
  38.0 20.5 %copy-start.16 = (bf16[112,1280]{1,0:T(8,128)(2,1)}, bf16[112,1280]{1,0:T(8,128)(2,1)S(1)}, u32[]{:S(2)}) copy-start(bf16[112,1280]{1,0:T(8,128)(2,1)S(1)} %collective-permute-done.8.refs_6_.refs_12_) | copy-start | bytes 860164
  38.0 8.6 %collective-permute-start.12 = (bf16[112,1280]{1,0:T(8,128)(2,1)S(1)}, bf16[112,1280]{1,0:T(8,128)(2,1)S(1)}, u32[]{:S(2)}, u32[]{:S(2)}) collective-permute-start(bf16[112,1280]{1,0:T(8,128)(2,1)S(1)} %collective-permute-done.8.refs_6_.refs_12_), channel_id=1, source_target_pairs={{0,96},{16,112},{32,0},{48,16},{64,32},{80,48},{96,64},{112,80},{1... | collective-permute-start | bytes 860168 | tf_op jit(solution)/shard_map/ppermute | solution.py:353
  41.7 16.8 %copy-start.28 = (bf16[96,1280]{1,0:T(8,128)(2,1)}, bf16[96,1280]{1,0:T(8,128)(2,1)S(1)}, u32[]{:S(2)}) copy-start(bf16[96,1280]{1,0:T(8,128)(2,1)S(1)} %collective-permute-done.refs_1_) | copy-start | bytes 737284
  41.7 7.4 %collective-permute-start.10 = (bf16[96,1280]{1,0:T(8,128)(2,1)S(1)}, bf16[96,1280]{1,0:T(8,128)(2,1)S(1)}, u32[]{:S(2)}, u32[]{:S(2)}) collective-permute-start(bf16[96,1280]{1,0:T(8,128)(2,1)S(1)} %collective-permute-done.2.refs_0_.refs_2_), channel_id=1, source_target_pairs={{0,32},{16,48},{32,64},{48,80},{64,96},{80,112},{96,0},{112,16},{1... | collective-permute-start | bytes 737288 | tf_op jit(solution)/shard_map/ppermute | solution.py:350
  42.0 16.5 %copy-start.18 = (bf16[112,1280]{1,0:T(8,128)(2,1)}, bf16[112,1280]{1,0:T(8,128)(2,1)S(1)}, u32[]{:S(2)}) copy-start(bf16[112,1280]{1,0:T(8,128)(2,1)S(1)} %collective-permute-done.6.refs_4_.refs_10_) | copy-start | bytes 860164
  42.0 12.5 %collective-permute-start.9 = (bf16[112,1280]{1,0:T(8,128)(2,1)S(1)}, bf16[112,1280]{1,0:T(8,128)(2,1)S(1)}, u32[]{:S(2)}, u32[]{:S(2)}) collective-permute-start(bf16[112,1280]{1,0:T(8,128)(2,1)S(1)} %collective-permute-done.8.refs_6_.refs_12_), channel_id=1, source_target_pairs={{0,16},{16,0},{32,48},{48,32},{64,80},{80,64},{96,112},{112,96},{1... | collective-permute-start | bytes 860168 | tf_op jit(solution)/shard_map/ppermute | solution.py:356
  42.0 16.5 %copy-start.10 = (bf16[112,1280]{1,0:T(8,128)(2,1)}, bf16[112,1280]{1,0:T(8,128)(2,1)S(1)}, u32[]{:S(2)}) copy-start(bf16[112,1280]{1,0:T(8,128)(2,1)S(1)} %collective-permute-done.1.refs_3_.refs_9_) | copy-start | bytes 860164
  42.0 12.5 %collective-permute-start.7 = (bf16[112,1280]{1,0:T(8,128)(2,1)S(1)}, bf16[112,1280]{1,0:T(8,128)(2,1)S(1)}, u32[]{:S(2)}, u32[]{:S(2)}) collective-permute-start(bf16[112,1280]{1,0:T(8,128)(2,1)S(1)} %collective-permute-done.6.refs_4_.refs_10_), channel_id=1, source_target_pairs={{0,16},{16,0},{32,48},{48,32},{64,80},{80,64},{96,112},{112,96},{1... | collective-permute-start | bytes 860168 | tf_op jit(solution)/shard_map/ppermute | solution.py:356
  42.5 16.0 %copy-start.38 = (bf16[96,1280]{1,0:T(8,128)(2,1)}, bf16[96,1280]{1,0:T(8,128)(2,1)S(1)}, u32[]{:S(2)}) copy-start(bf16[96,1280]{1,0:T(8,128)(2,1)S(1)} %collective-permute-done.5.refs_3_.refs_5_) | copy-start | bytes 737284
  42.5 12.0 %collective-permute-start.3 = (bf16[96,1280]{1,0:T(8,128)(2,1)S(1)}, bf16[96,1280]{1,0:T(8,128)(2,1)S(1)}, u32[]{:S(2)}, u32[]{:S(2)}) collective-permute-start(bf16[96,1280]{1,0:T(8,128)(2,1)S(1)} %collective-permute-done.2.refs_0_.refs_2_), channel_id=1, source_target_pairs={{0,16},{16,0},{32,48},{48,32},{64,80},{80,64},{96,112},{112,96},{1... | collective-permute-start | bytes 737288 | tf_op jit(solution)/shard_map/ppermute | solution.py:356
  46.6 13.0 %copy-start.12 = (bf16[112,1280]{1,0:T(8,128)(2,1)}, bf16[112,1280]{1,0:T(8,128)(2,1)S(1)}, u32[]{:S(2)}) copy-start(bf16[112,1280]{1,0:T(8,128)(2,1)S(1)} %collective-permute-done.12.refs_2_.refs_14_) | copy-start | bytes 860164
  46.6 12.9 %collective-permute-start.13 = (bf16[112,1280]{1,0:T(8,128)(2,1)S(1)}, bf16[112,1280]{1,0:T(8,128)(2,1)S(1)}, u32[]{:S(2)}, u32[]{:S(2)}) collective-permute-start(bf16[112,1280]{1,0:T(8,128)(2,1)S(1)} %collective-permute-done.12.refs_2_.refs_14_), channel_id=1, source_target_pairs={{0,16},{16,0},{32,48},{48,32},{64,80},{80,64},{96,112},{112,96},{1... | collective-permute-start | bytes 860168 | tf_op jit(solution)/shard_map/ppermute | solution.py:356
  49.1 10.4 %copy-start.30 = (bf16[96,1280]{1,0:T(8,128)(2,1)}, bf16[96,1280]{1,0:T(8,128)(2,1)S(1)}, u32[]{:S(2)}) copy-start(bf16[96,1280]{1,0:T(8,128)(2,1)S(1)} %collective-permute-done.10.refs_0_.refs_6_) | copy-start | bytes 737284
  49.1 10.4 %collective-permute-start.11 = (bf16[96,1280]{1,0:T(8,128)(2,1)S(1)}, bf16[96,1280]{1,0:T(8,128)(2,1)S(1)}, u32[]{:S(2)}, u32[]{:S(2)}) collective-permute-start(bf16[96,1280]{1,0:T(8,128)(2,1)S(1)} %collective-permute-done.10.refs_0_.refs_6_), channel_id=1, source_target_pairs={{0,16},{16,0},{32,48},{48,32},{64,80},{80,64},{96,112},{112,96},{1... | collective-permute-start | bytes 737288 | tf_op jit(solution)/shard_map/ppermute | solution.py:356
  54.5 7.1 %copy-start.44 = (bf16[2,2,32,640]{3,2,1,0:T(8,128)(2,1)}, bf16[2,2,32,640]{3,2,1,0:T(8,128)(2,1)S(1)}, u32[]{:S(2)}) copy-start(bf16[2,2,32,640]{3,2,1,0:T(8,128)(2,1)S(1)} %get-tuple-element.32.a_ref) | copy-start | bytes 491524
  54.5 7.0 %copy-start.40 = (bf16[96,1280]{1,0:T(8,128)(2,1)}, bf16[96,1280]{1,0:T(8,128)(2,1)S(1)}, u32[]{:S(2)}) copy-start(bf16[96,1280]{1,0:T(8,128)(2,1)S(1)} %collective-permute-done.3.refs_1_.refs_3_) | copy-start | bytes 737284
  54.6 7.0 %copy-start.20 = (bf16[112,1280]{1,0:T(8,128)(2,1)}, bf16[112,1280]{1,0:T(8,128)(2,1)S(1)}, u32[]{:S(2)}) copy-start(bf16[112,1280]{1,0:T(8,128)(2,1)S(1)} %collective-permute-done.9.refs_7_.refs_13_) | copy-start | bytes 860164
  54.6 7.0 %copy-start.22 = (bf16[112,1280]{1,0:T(8,128)(2,1)}, bf16[112,1280]{1,0:T(8,128)(2,1)S(1)}, u32[]{:S(2)}) copy-start(bf16[112,1280]{1,0:T(8,128)(2,1)S(1)} %collective-permute-done.7.refs_5_.refs_11_) | copy-start | bytes 860164
  64.0 2.1 %collective-permute-start.14 = (bf16[4,32,1280]{2,1,0:T(8,128)(2,1)}, bf16[4,32,1280]{2,1,0:T(8,128)(2,1)}, u32[]{:S(2)}, u32[]{:S(2)}) collective-permute-start(bf16[4,32,1280]{2,1,0:T(8,128)(2,1)} %get-tuple-element.36), channel_id=1, source_target_pairs={{0,16},{16,0},{32,48},{48,32},{64,80},{80,64},{96,112},{112,96},{1... | collective-permute-start | bytes 983048 | tf_op jit(solution)/shard_map/ppermute | solution.py:356
  69.3 17.4 %all-to-all-start.1 = ((bf16[64,2,1280]{2,1,0:T(2,128)(2,1)}), bf16[64,2,1280]{2,1,0:T(2,128)(2,1)}, u32[]{:S(2)}, u32[]{:S(2)}) async-start(bf16[64,2,1280]{2,1,0:T(2,128)(2,1)} %copy.11), calls=%async_computation.1 | async-start | bytes 655360 | tf_op jit(solution)/shard_map/all_to_all | solution.py:362
  107.1 2.4 %collective-permute-start.15 = (f32[64,2,1280]{2,0,1:T(8,128)S(1)}, f32[64,2,1280]{2,0,1:T(8,128)S(1)}, u32[]{:S(2)}, u32[]{:S(2)}) collective-permute-start(f32[64,2,1280]{2,0,1:T(8,128)S(1)} %copy.12), channel_id=1, source_target_pairs={{0,16},{16,0},{32,48},{48,32},{64,80},{80,64},{96,112},{112,96},{1... | collective-permute-start | bytes 1966088 | tf_op jit(solution)/shard_map/ppermute | solution.py:356
  109.5 4.2 %copy-start.55 = (bf16[2,2,96,640]{3,2,1,0:T(8,128)(2,1)S(1)}, bf16[2,2,96,640]{3,2,1,0:T(8,128)(2,1)}, u32[]{:S(2)}) copy-start(bf16[2,2,96,640]{3,2,1,0:T(8,128)(2,1)} %copy-done.54) | copy-start | bytes 1474564
  109.5 4.2 %copy-start.63 = (bf16[2,2,32,96]{3,2,1,0:T(8,128)(2,1)S(1)}, bf16[2,2,32,96]{3,2,1,0:T(8,128)(2,1)}, u32[]{:S(2)}) copy-start(bf16[2,2,32,96]{3,2,1,0:T(8,128)(2,1)} %copy-done.62) | copy-start | bytes 73732
  113.7 5.5 %copy-start.42 = (bf16[8,32,1280]{2,1,0:T(8,128)(2,1)}, bf16[8,32,1280]{2,1,0:T(8,128)(2,1)S(1)}, u32[]{:S(2)}) copy-start(bf16[8,32,1280]{2,1,0:T(8,128)(2,1)S(1)} %get-tuple-element.56.rows_ref) | copy-start | bytes 1966084
  113.7 5.5 %copy-start.64 = (f32[2,128,1280]{2,1,0:T(8,128)}, f32[2,128,1280]{2,1,0:T(8,128)S(1)}, u32[]{:S(2)}) copy-start(f32[2,128,1280]{2,1,0:T(8,128)S(1)} %get-tuple-element.37) | copy-start | bytes 3932164
  116.8 8.5 %collective-permute-start.18 = (bf16[192,1280]{1,0:T(8,128)(2,1)S(1)}, bf16[192,1280]{1,0:T(8,128)(2,1)S(1)}, u32[]{:S(2)}, u32[]{:S(2)}) collective-permute-start(bf16[192,1280]{1,0:T(8,128)(2,1)S(1)} %get-tuple-element.50), channel_id=1, source_target_pairs={{0,16},{16,0},{32,48},{48,32},{64,80},{80,64},{96,112},{112,96},{1... | collective-permute-start | bytes 1474568 | tf_op jit(solution)/shard_map/ppermute | solution.py:356
  120.0 20.0 %collective-permute-start.16 = (bf16[192,1280]{1,0:T(8,128)(2,1)S(1)}, bf16[192,1280]{1,0:T(8,128)(2,1)S(1)}, u32[]{:S(2)}, u32[]{:S(2)}) collective-permute-start(bf16[192,1280]{1,0:T(8,128)(2,1)S(1)} %get-tuple-element.42), channel_id=1, source_target_pairs={{0,16},{16,0},{32,48},{48,32},{64,80},{80,64},{96,112},{112,96},{1... | collective-permute-start | bytes 1474568 | tf_op jit(solution)/shard_map/ppermute | solution.py:356
  124.7 11.8 %copy-start.26 = (bf16[4,2,96,640]{3,2,1,0:T(8,128)(2,1)}, bf16[4,2,96,640]{3,2,1,0:T(8,128)(2,1)S(1)}, u32[]{:S(2)}) copy-start(bf16[4,2,96,640]{3,2,1,0:T(8,128)(2,1)S(1)} %get-tuple-element.54.refs_17_) | copy-start | bytes 2949124
  124.7 2.9 %collective-permute-start.17 = (bf16[192,1280]{1,0:T(8,128)(2,1)S(1)}, bf16[192,1280]{1,0:T(8,128)(2,1)S(1)}, u32[]{:S(2)}, u32[]{:S(2)}) collective-permute-start(bf16[192,1280]{1,0:T(8,128)(2,1)S(1)} %get-tuple-element.46), channel_id=1, source_target_pairs={{0,16},{16,0},{32,48},{48,32},{64,80},{80,64},{96,112},{112,96},{1... | collective-permute-start | bytes 1474568 | tf_op jit(solution)/shard_map/ppermute | solution.py:356
  124.9 3.3 %collective-permute-start.22 = (bf16[192,1280]{1,0:T(8,128)(2,1)S(1)}, bf16[192,1280]{1,0:T(8,128)(2,1)S(1)}, u32[]{:S(2)}, u32[]{:S(2)}) collective-permute-start(bf16[192,1280]{1,0:T(8,128)(2,1)S(1)} %get-tuple-element.52), channel_id=1, source_target_pairs={{0,16},{16,0},{32,48},{48,32},{64,80},{80,64},{96,112},{112,96},{1... | collective-permute-start | bytes 1474568 | tf_op jit(solution)/shard_map/ppermute | solution.py:356
  125.5 11.2 %collective-permute-start.24 = (bf16[96,1280]{1,0:T(8,128)(2,1)S(1)}, bf16[96,1280]{1,0:T(8,128)(2,1)S(1)}, u32[]{:S(2)}, u32[]{:S(2)}) collective-permute-start(bf16[96,1280]{1,0:T(8,128)(2,1)S(1)} %get-tuple-element.61), channel_id=1, source_target_pairs={{0,96},{16,112},{32,0},{48,16},{64,32},{80,48},{96,64},{112,80},{1... | collective-permute-start | bytes 737288 | tf_op jit(solution)/shard_map/ppermute | solution.py:353
  126.4 10.0 %collective-permute-start.19 = (bf16[96,1280]{1,0:T(8,128)(2,1)S(1)}, bf16[96,1280]{1,0:T(8,128)(2,1)S(1)}, u32[]{:S(2)}, u32[]{:S(2)}) collective-permute-start(bf16[96,1280]{1,0:T(8,128)(2,1)S(1)} %get-tuple-element.62), channel_id=1, source_target_pairs={{0,32},{16,48},{32,64},{48,80},{64,96},{80,112},{96,0},{112,16},{1... | collective-permute-start | bytes 737288 | tf_op jit(solution)/shard_map/ppermute | solution.py:350
  127.7 14.0 %collective-permute-start.21 = (bf16[96,1280]{1,0:T(8,128)(2,1)S(1)}, bf16[96,1280]{1,0:T(8,128)(2,1)S(1)}, u32[]{:S(2)}, u32[]{:S(2)}) collective-permute-start(bf16[96,1280]{1,0:T(8,128)(2,1)S(1)} %slice.46), channel_id=1, source_target_pairs={{0,32},{16,48},{32,64},{48,80},{64,96},{80,112},{96,0},{112,16},{1... | collective-permute-start | bytes 737288 | tf_op jit(solution)/shard_map/ppermute | solution.py:350
  128.4 23.4 %copy-start.7 = (bf16[4,2,32,640]{3,2,1,0:T(8,128)(2,1)S(1)}, bf16[4,2,32,640]{3,2,1,0:T(8,128)(2,1)}, u32[]{:S(2)}) copy-start(bf16[4,2,32,640]{3,2,1,0:T(8,128)(2,1)} %copy-done.6) | copy-start | bytes 983044
  128.4 23.4 %copy-start.43 = (bf16[8,32,1280]{2,1,0:T(8,128)(2,1)S(1)}, bf16[8,32,1280]{2,1,0:T(8,128)(2,1)}, u32[]{:S(2)}) copy-start(bf16[8,32,1280]{2,1,0:T(8,128)(2,1)} %copy-done.42) | copy-start | bytes 1966084
  128.4 23.4 %copy-start.45 = (bf16[2,2,32,640]{3,2,1,0:T(8,128)(2,1)S(1)}, bf16[2,2,32,640]{3,2,1,0:T(8,128)(2,1)}, u32[]{:S(2)}) copy-start(bf16[2,2,32,640]{3,2,1,0:T(8,128)(2,1)} %copy-done.44) | copy-start | bytes 491524
  128.4 23.4 %copy-start.47 = (bf16[2,2,32,640]{3,2,1,0:T(8,128)(2,1)S(1)}, bf16[2,2,32,640]{3,2,1,0:T(8,128)(2,1)}, u32[]{:S(2)}) copy-start(bf16[2,2,32,640]{3,2,1,0:T(8,128)(2,1)} %copy-done.46) | copy-start | bytes 491524
  128.5 13.3 %collective-permute-start.23 = (bf16[96,1280]{1,0:T(8,128)(2,1)S(1)}, bf16[96,1280]{1,0:T(8,128)(2,1)S(1)}, u32[]{:S(2)}, u32[]{:S(2)}) collective-permute-start(bf16[96,1280]{1,0:T(8,128)(2,1)S(1)} %slice.47), channel_id=1, source_target_pairs={{0,96},{16,112},{32,0},{48,16},{64,32},{80,48},{96,64},{112,80},{1... | collective-permute-start | bytes 737288 | tf_op jit(solution)/shard_map/ppermute | solution.py:353
  136.5 9.3 %collective-permute-start.20 = (bf16[96,1280]{1,0:T(8,128)(2,1)S(1)}, bf16[96,1280]{1,0:T(8,128)(2,1)S(1)}, u32[]{:S(2)}, u32[]{:S(2)}) collective-permute-start(bf16[96,1280]{1,0:T(8,128)(2,1)S(1)} %add_convert_fusion.4), channel_id=1, source_target_pairs={{0,32},{16,48},{32,64},{48,80},{64,96},{80,112},{96,0},{112,16},{1... | collective-permute-start | bytes 737288 | tf_op jit(solution)/shard_map/ppermute | solution.py:350
  136.7 9.2 %collective-permute-start.25 = (bf16[96,1280]{1,0:T(8,128)(2,1)S(1)}, bf16[96,1280]{1,0:T(8,128)(2,1)S(1)}, u32[]{:S(2)}, u32[]{:S(2)}) collective-permute-start(bf16[96,1280]{1,0:T(8,128)(2,1)S(1)} %add_convert_fusion.3), channel_id=1, source_target_pairs={{0,96},{16,112},{32,0},{48,16},{64,32},{80,48},{96,64},{112,80},{1... | collective-permute-start | bytes 737288 | tf_op jit(solution)/shard_map/ppermute | solution.py:353
  147.2 15.9 %all-to-all-start.3 = ((bf16[16,16,1280]{2,1,0:T(8,128)(2,1)}), bf16[16,16,1280]{2,1,0:T(8,128)(2,1)S(1)}, u32[]{:S(2)}, u32[]{:S(2)}) async-start(bf16[16,16,1280]{2,1,0:T(8,128)(2,1)} %shard_map.96), calls=%async_computation.3 | async-start | bytes 1310720 | tf_op jit(solution)/shard_map/all_to_all | solution.py:359
  151.8 4.2 %copy-start.9 = (bf16[112,1280]{1,0:T(8,128)(2,1)S(1)}, bf16[112,1280]{1,0:T(8,128)(2,1)}, u32[]{:S(2)}) copy-start(bf16[112,1280]{1,0:T(8,128)(2,1)} %copy-done.8) | copy-start | bytes 860164
  151.8 4.1 %copy-start.11 = (bf16[112,1280]{1,0:T(8,128)(2,1)S(1)}, bf16[112,1280]{1,0:T(8,128)(2,1)}, u32[]{:S(2)}) copy-start(bf16[112,1280]{1,0:T(8,128)(2,1)} %copy-done.10) | copy-start | bytes 860164
  151.8 4.1 %copy-start.13 = (bf16[112,1280]{1,0:T(8,128)(2,1)S(1)}, bf16[112,1280]{1,0:T(8,128)(2,1)}, u32[]{:S(2)}) copy-start(bf16[112,1280]{1,0:T(8,128)(2,1)} %copy-done.12) | copy-start | bytes 860164
  151.8 4.1 %copy-start.15 = (bf16[112,1280]{1,0:T(8,128)(2,1)S(1)}, bf16[112,1280]{1,0:T(8,128)(2,1)}, u32[]{:S(2)}) copy-start(bf16[112,1280]{1,0:T(8,128)(2,1)} %copy-done.14) | copy-start | bytes 860164
  151.8 4.1 %copy-start.17 = (bf16[112,1280]{1,0:T(8,128)(2,1)S(1)}, bf16[112,1280]{1,0:T(8,128)(2,1)}, u32[]{:S(2)}) copy-start(bf16[112,1280]{1,0:T(8,128)(2,1)} %copy-done.16) | copy-start | bytes 860164
  151.9 4.1 %copy-start.19 = (bf16[112,1280]{1,0:T(8,128)(2,1)S(1)}, bf16[112,1280]{1,0:T(8,128)(2,1)}, u32[]{:S(2)}) copy-start(bf16[112,1280]{1,0:T(8,128)(2,1)} %copy-done.18) | copy-start | bytes 860164
  151.9 4.1 %copy-start.21 = (bf16[112,1280]{1,0:T(8,128)(2,1)S(1)}, bf16[112,1280]{1,0:T(8,128)(2,1)}, u32[]{:S(2)}) copy-start(bf16[112,1280]{1,0:T(8,128)(2,1)} %copy-done.20) | copy-start | bytes 860164
  151.9 4.1 %copy-start.23 = (bf16[112,1280]{1,0:T(8,128)(2,1)S(1)}, bf16[112,1280]{1,0:T(8,128)(2,1)}, u32[]{:S(2)}) copy-start(bf16[112,1280]{1,0:T(8,128)(2,1)} %copy-done.22) | copy-start | bytes 860164
  151.9 4.1 %copy-start.27 = (bf16[4,2,96,640]{3,2,1,0:T(8,128)(2,1)S(1)}, bf16[4,2,96,640]{3,2,1,0:T(8,128)(2,1)}, u32[]{:S(2)}) copy-start(bf16[4,2,96,640]{3,2,1,0:T(8,128)(2,1)} %copy-done.26) | copy-start | bytes 2949124
  151.9 4.1 %copy-start.29 = (bf16[96,1280]{1,0:T(8,128)(2,1)S(1)}, bf16[96,1280]{1,0:T(8,128)(2,1)}, u32[]{:S(2)}) copy-start(bf16[96,1280]{1,0:T(8,128)(2,1)} %copy-done.28) | copy-start | bytes 737284
  152.0 4.4 %copy-start.49 = (bf16[2,2,96,640]{3,2,1,0:T(8,128)(2,1)S(1)}, bf16[2,2,96,640]{3,2,1,0:T(8,128)(2,1)}, u32[]{:S(2)}) copy-start(bf16[2,2,96,640]{3,2,1,0:T(8,128)(2,1)} %copy-done.48) | copy-start | bytes 1474564
  152.0 4.8 %copy-start.51 = (bf16[2,2,96,640]{3,2,1,0:T(8,128)(2,1)S(1)}, bf16[2,2,96,640]{3,2,1,0:T(8,128)(2,1)}, u32[]{:S(2)}) copy-start(bf16[2,2,96,640]{3,2,1,0:T(8,128)(2,1)} %copy-done.50) | copy-start | bytes 1474564
  156.8 6.3 %copy-start.5 = (bf16[1,2,64,1280]{3,2,1,0:T(8,128)(2,1)S(1)}, bf16[1,2,64,1280]{3,2,1,0:T(8,128)(2,1)}, u32[]{:S(2)}) copy-start(bf16[1,2,64,1280]{3,2,1,0:T(8,128)(2,1)} %param.6) | copy-start | bytes 983044
  (29 other events, 77.7 us)

commit v3 on v2

--- a/solution.py
+++ b/solution.py
@@ -48,7 +48,7 @@
     return jax.ShapeDtypeStruct(dims, dtype)
 
 
-def call(kernel, out, args, flops=0, nbytes=0, smem=(), scratch=(), vmem=40):
+def call(kernel, out, args, flops=0, nbytes=0, smem=(), scratch=(), vmem=14):
     specs = [
         pl.BlockSpec(memory_space=pltpu.SMEM if k in smem else pltpu.VMEM)
         for k in range(len(args))
@@ -73,6 +73,10 @@
     return centred * scale, scale
 
 
+def place_of(ids_ref, slots_ref, half):
+    return ids_ref[half : half + 1, :] * CAP + slots_ref[half : half + 1, :]
+
+
 def slot_table(pos):
     tokens = pos.shape[1]
     row = iota((PEERS * PAD, tokens), 0)
@@ -80,20 +84,24 @@
     return jnp.where((want == pos) & (row % PAD < GROUP), 1.0, 0.0).astype(bf16)
 
 
-def dispatch_kernel(me_ref, pos_ref, tok_ref, gain_ref, out_ref):
-    pos = pos_ref[...]
-    tokens = pos.shape[1]
-    normed = normal_parts(tok_ref[...].astype(f32))[0] * gain_ref[...]
+def dispatch_kernel(me_ref, ids_ref, slots_ref, tok_ref, gain_ref, out_ref):
+    normed = normal_parts(tok_ref[...].astype(f32))[0] * gain_ref[...].reshape(1, -1)
     normed = normed.astype(bf16)
-    sent = nn(slot_table(pos), normed)
-    row = iota((PEERS * PAD, tokens), 0)
-    goes = jnp.where((row % PAD == GROUP) & (pos // GROUP == row // PAD), 1.0, 0.0).astype(bf16)
-    place = pos % GROUP
-    column = (place // CAP) * 128 + me_ref[0] * CAP + place % CAP
-    lane = iota((2 * 128, tokens), 0)
-    kind = jnp.where(iota((2 * 128, tokens), 1) < tokens // 2, 1.0, 2.0)
-    kinds = nt(goes, jnp.where(lane == column, kind, 0.0).astype(bf16))
-    width = sent.shape[1]
+    tokens, width = normed.shape
+    tokens = tokens // 2
+    sent = kinds = None
+    for half in range(2):
+        pos = place_of(ids_ref, slots_ref, half)
+        part = nn(slot_table(pos), normed[half * tokens : (half + 1) * tokens])
+        row = iota((PEERS * PAD, tokens), 0)
+        goes = (row % PAD == GROUP) & (pos // GROUP == row // PAD)
+        goes = jnp.where(goes, 1.0, 0.0).astype(bf16)
+        place = pos % GROUP
+        column = (place // CAP) * 128 + me_ref[0] * CAP + place % CAP
+        lane = iota((2 * 128, tokens), 0)
+        kind = nt(goes, jnp.where(lane == column, 1.0 + half, 0.0).astype(bf16))
+        sent = part if sent is None else sent + part
+        kinds = kind if kinds is None else kinds + kind
     first = sent[:, : 2 * 128] + kinds
     out_ref[:, :, : 2 * 128] = first.astype(bf16).reshape(PEERS, PAD, 2 * 128)
     out_ref[:, :, 2 * 128 :] = sent[:, 2 * 128 :].astype(bf16).reshape(
@@ -168,21 +176,20 @@
         return refs[0].at[k]
     if k < 6:
         return refs[1].at[k - 2]
-    return refs[2].at[k - 6]
+    return refs[k - 4].at[0]
 
 
 AROUND = (0, 4, 6, 2)
 
 
-def out_kernel(a_ref, b_ref, c_ref, w_out, own_ref, other_ref):
-    refs = (a_ref, b_ref, c_ref)
-    for shift, out_ref in ((1, other_ref), (0, own_ref)):
-        total = None
-        for held in range(HELD):
-            rows = jnp.concatenate([block_of(refs, k + shift)[held] for k in AROUND], axis=0)
-            part = nn(rows, w_out[held])
-            total = part if total is None else total + part
-        out_ref[...] = total.astype(bf16).reshape(out_ref.shape)
+def out_kernel(shift, *refs):
+    pooled, w_out, out_ref = refs[:-2], refs[-2], refs[-1]
+    total = None
+    for held in range(HELD):
+        rows = jnp.concatenate([block_of(pooled, k + shift)[held] for k in AROUND], axis=0)
+        part = nn(rows, w_out[held])
+        total = part if total is None else total + part
+    out_ref[...] = total.astype(bf16).reshape(out_ref.shape)
 
 
 def join_kernel(z_ref, own_ref, got_ref, out_ref):
@@ -191,9 +198,10 @@
         out_ref[to] = (own_ref[ahead].astype(f32) + got_ref[ahead].astype(f32)).astype(bf16)
 
 
-def loss_kernel(z_ref, image_ref, text_ref, w_out, grad_ref, rows_ref, prod_ref, gi_ref, gt_ref):
+def loss_kernel(z_ref, own_ref, other_ref, w_out, grad_ref, rows_ref, prod_ref, gi_ref, gt_ref):
     highest = lax.Precision.HIGHEST
-    image, text = image_ref[...], text_ref[...]
+    image = jnp.concatenate([own_ref[0], other_ref[0]], axis=0)
+    text = jnp.concatenate([own_ref[1], other_ref[1]], axis=0)
     pairs, width = image.shape
     scale = PAIR_TOKENS / math.sqrt(width)
     logits = scale * nt(image, text, highest)
@@ -227,37 +235,37 @@
         prod_ref[held] = nt(rows, w_out[held]).astype(bf16)
 
 
-def backward_kernel(first, count, pool_ref, slope_ref, prod_ref, w_in, pre_ref, *outs):
+def backward_kernel(first, at, count, pool_ref, slope_ref, prod_ref, w_in, pre_ref, *outs):
     for k in range(count):
         for held in range(HELD):
             prod = prod_ref[held, (first + k) * POOLED : (first + k + 1) * POOLED, :]
-            grad_act = tn(pool_ref[k, held], prod)
-            pre = (grad_act * slope_ref[k, held].astype(f32)).astype(bf16)
+            grad_act = tn(pool_ref[at + k, held], prod)
+            pre = (grad_act * slope_ref[at + k, held].astype(f32)).astype(bf16)
             pre_ref[k, held] = pre
             outs[k][held * HALF : (held + 1) * HALF, :] = nt(pre, w_in[held]).astype(bf16)
 
 
-def backward(first, pool, slope, prod, w_in):
-    count = pool.shape[0]
+def backward(first, at, count, made, prod, w_in):
     width, hidden = w_in.shape[1:]
     return call(
-        functools.partial(backward_kernel, first, count),
+        functools.partial(backward_kernel, first, at, count),
         [shape_of(count, HELD, HALF, hidden)] + [shape_of(2 * HALF, width)] * count,
-        [pool, slope, prod, w_in],
+        [made[2], made[1], prod, w_in],
         flops=count * 2 * 2 * HALF * width * hidden,
         nbytes=w_in.size * 2 + count * 2 * HALF * (width + hidden) * 2,
     )
 
 
 def grad_in_kernel(*refs):
-    blocks, pres, out_ref, x_ref, p_ref = refs[:16], refs[16:19], refs[19], refs[20], refs[21]
+    blocks, pres = refs[:16], refs[16:21]
+    out_ref, x_ref, p_ref = refs[21:]
     held = pl.program_id(0)
 
     def fill(which):
         for k in range(8):
             span = slice(k * HALF, (k + 1) * HALF)
             x_ref[span, :] = blocks[8 * which + k][:HALF, :]
-            p_ref[span, :] = block_of(pres, k)[which]
+            p_ref[span, :] = (pres[k // 2].at[k % 2] if k < 6 else pres[k - 3].at[0])[which]
 
     for which in range(HELD):
         pl.when(held == which)(functools.partial(fill, which))
@@ -270,21 +278,21 @@
         grad_in_kernel,
         grid=(HELD,),
         out_shape=shape_of(HELD, width, hidden, dtype=f32),
-        in_specs=[whole] * 19,
+        in_specs=[whole] * 21,
         out_specs=pl.BlockSpec((1, width, hidden), lambda i: (i, 0, 0)),
         scratch_shapes=[
             pltpu.VMEM((8 * HALF, width), bf16),
             pltpu.VMEM((8 * HALF, hidden), bf16),
         ],
-        compiler_params=pltpu.CompilerParams(vmem_limit_bytes=44 * 1024 * 1024),
+        compiler_params=pltpu.CompilerParams(vmem_limit_bytes=24 * 1024 * 1024),
         cost_estimate=pl.CostEstimate(
             flops=2 * 2 * 8 * HALF * width * hidden, bytes_accessed=17_000_000, transcendentals=0
         ),
     )(*firsts, *seconds, *pres)
 
 
-def grad_out_kernel(a_ref, b_ref, c_ref, rows_ref, out_ref):
-    refs = (a_ref, b_ref, c_ref)
+def grad_out_kernel(*args):
+    refs, rows_ref, out_ref = args[:-2], args[-2], args[-1]
     held = pl.program_id(0)
     width = rows_ref.shape[2]
     pooled = jnp.concatenate([block_of(refs, k)[held] for k in range(8)], axis=0)
@@ -297,9 +305,9 @@
         grad_out_kernel,
         grid=(HELD,),
         out_shape=shape_of(HELD, hidden, width, dtype=f32),
-        in_specs=[whole] * 4,
+        in_specs=[whole] * 5,
         out_specs=pl.BlockSpec((1, hidden, width), lambda i: (i, 0, 0)),
-        compiler_params=pltpu.CompilerParams(vmem_limit_bytes=32 * 1024 * 1024),
+        compiler_params=pltpu.CompilerParams(vmem_limit_bytes=18 * 1024 * 1024),
         cost_estimate=pl.CostEstimate(
             flops=2 * 2 * 8 * POOLED * width * hidden, bytes_accessed=9_000_000, transcendentals=0
         ),
@@ -316,19 +324,22 @@
     out_ref[...] = nn(table, rows).astype(bf16).reshape(PEERS, PAD, width)
 
 
-def tail_kernel(pos_ref, tok_ref, gain_ref, grad_ref, back_ref, out_ref):
-    tokens, width = tok_ref.shape
-    grad_normed = tn(slot_table(pos_ref[...]), back_ref[...].reshape(PEERS * PAD, width))
-    unit, scale = normal_parts(tok_ref[...].astype(f32))
-    grad = grad_normed * gain_ref[...]
-    grad = scale * (
-        grad
-        - jnp.mean(grad, axis=-1, keepdims=True)
-        - unit * jnp.mean(grad * unit, axis=-1, keepdims=True)
-    )
-    image = iota((tokens, width), 0) < tokens // 2
-    mixed = jnp.where(image, grad_ref[0:1, :], grad_ref[1:2, :])
-    out_ref[...] = (mixed + grad).astype(bf16)
+def tail_kernel(ids_ref, slots_ref, tok_ref, gain_ref, grad_ref, back_ref, out_ref):
+    width = tok_ref.shape[1]
+    tokens = tok_ref.shape[0] // 2
+    gain = gain_ref[...].reshape(1, -1)
+    back = back_ref[...].reshape(PEERS * PAD, width)
+    for half in range(2):
+        span = slice(half * tokens, (half + 1) * tokens)
+        grad_normed = tn(slot_table(place_of(ids_ref, slots_ref, half)), back)
+        unit, scale = normal_parts(tok_ref[span, :].astype(f32))
+        grad = grad_normed * gain
+        grad = scale * (
+            grad
+            - jnp.mean(grad, axis=-1, keepdims=True)
+            - unit * jnp.mean(grad * unit, axis=-1, keepdims=True)
+        )
+        out_ref[span, :] = (grad_ref[half : half + 1, :] + grad).astype(bf16)
 
 
 PAIR_TOKENS = 64
@@ -338,8 +349,7 @@
     width, hidden = w_in.shape[1:]
     row_count = tokens.shape[1] * tokens.shape[2]
     flat = tokens.reshape(row_count, width)
-    gain = ln_gain.reshape(1, width)
-    pos = (expert_ids * CAP + slots).reshape(1, row_count)
+    ids, places = expert_ids[0], slots[0]
     data = lax.axis_index("dp")
     group = lax.axis_index("expert")
     z = (data // 2).reshape(1)
@@ -355,6 +365,9 @@
     def swap(x):
         return lax.ppermute(x, "dp", [(i, i ^ 1) for i in range(8)])
 
+    def after(x, *tokens):
+        return lax.optimization_barrier((x, *tokens))[0]
+
     def exchange(x):
         return lax.all_to_all(x, "expert", split_axis=0, concat_axis=0, tiled=True)
 
@@ -366,7 +379,7 @@
     sent = call(
         dispatch_kernel,
         shape_of(PEERS, PAD, width),
-        [group.reshape(1), pos, flat, gain],
+        [group.reshape(1), ids, places, flat, ln_gain],
         smem=(0,),
     )
     first, second = call(
@@ -379,27 +392,41 @@
     a[0], b[0] = first, second
     a[2] = up(first)
     b[4] = down(second)
-    b[2] = up(second)
-    a[4] = down(first)
+    a[1], b[1] = swap(first), swap(second)
+    b[2] = up(after(second, a[1]))
+    a[4] = down(after(first, b[1]))
+    near = forward(a[0:2], b[0:2], w_in)
+    a[2], b[4] = after(a[2], near[0]), after(b[4], near[0])
     a[6] = up(a[2])
     b[6] = down(b[4])
-    for k in (0, 2, 4, 6):
+    for k in (2, 4):
         a[k + 1] = swap(a[k])
         b[k + 1] = swap(b[k])
-    made = [forward(a[i:j], b[i:j], w_in) for i, j in ((0, 2), (2, 6), (6, 8))]
+    mid = forward(a[2:6], b[2:6], w_in)
+    a[6], b[6] = after(a[6], mid[0]), after(b[6], mid[0])
+    a[7], b[7] = swap(a[6]), swap(b[6])
+    far = forward(a[6:7], b[6:7], w_in)
+    a[7] = after(a[7], far[0])
+    last = forward(a[7:8], b[7:8], w_in)
+    made = [near, mid, far, last]
     pooled = [m[0] for m in made]
     slope = [m[1] for m in made]
     pool = [m[2] for m in made]
 
-    own, other = call(
-        out_kernel,
-        [shape_of(4, POOLED, width), shape_of(4, POOLED, width)],
-        [*pooled, w_out],
-        flops=2 * 8 * POOLED * width * hidden * HELD,
-        nbytes=w_out.size * 2,
-    )
+    def product(shift, w_out):
+        return call(
+            functools.partial(out_kernel, shift),
+            shape_of(4, POOLED, width),
+            [*pooled, w_out],
+            flops=2 * 4 * POOLED * width * hidden * HELD,
+            nbytes=w_out.size * 2,
+        )
+
+    other = product(1, w_out)
+    got = swap(other)
+    own = product(0, after(w_out, other))
     joined = call(
-        join_kernel, shape_of(4, POOLED, width), [z, own, swap(other)], smem=(0,)
+        join_kernel, shape_of(4, POOLED, width), [z, own, after(got, own)], smem=(0,)
     )
     joined = joined.reshape(4, 2, PEERS, width).transpose(0, 2, 1, 3).reshape(-1, 2, width)
     parts = spread(joined)
@@ -407,9 +434,8 @@
         flat.reshape(2, PAIR_TOKENS, width).astype(f32), axis=1
     )
     emb = spread(jnp.broadcast_to((emb / PAIR_TOKENS)[None], (4 * PEERS, 2, width)))
+    emb = emb.transpose(1, 0, 2)
     emb_other = swap(emb)
-    image = jnp.concatenate([emb[:, 0], emb_other[:, 0]], axis=0)
-    text = jnp.concatenate([emb[:, 1], emb_other[:, 1]], axis=0)
     grad_pooled, rows, prod = call(
         loss_kernel,
         [
@@ -417,7 +443,7 @@
             shape_of(8, POOLED, width),
             shape_of(HELD, 8 * POOLED, hidden),
         ],
-        [z, image, text, w_out],
+        [z, emb, emb_other, w_out],
         smem=(0,),
         scratch=[pltpu.VMEM((8 * PEERS, width), bf16), pltpu.VMEM((8 * PEERS, width), bf16)],
         flops=2 * 8 * POOLED * width * hidden * HELD,
@@ -430,31 +456,36 @@
     def plus(x, y):
         return (x.astype(f32) + y.astype(f32)).astype(bf16)
 
-    pre_c, p6, p7 = backward(6, pool[2], slope[2], prod, w_in)
-    r6 = plus(p6, swap(p7))
+    pre7, p7 = backward(7, 0, 1, last, prod, w_in)
+    s7 = swap(p7)
+    pre6, p6 = backward(6, 0, 1, far, after(prod, p7), w_in)
+    pre4, p4, p5 = backward(4, 2, 2, mid, after(prod, p6), w_in)
+    s5 = swap(p5)
+    r6 = plus(p6, after(s7, p4))
     from_below = up(r6[:HALF])
     from_above = down(r6[HALF:])
-    pre_b, p2, p3, p4, p5 = backward(2, pool[1], slope[1], prod, w_in)
-    r4 = plus(p4, swap(p5))
-    r2 = plus(p2, swap(p3))
+    pre2, p2, p3 = backward(2, 0, 2, mid, after(prod, r6), w_in)
+    s3 = swap(p3)
+    r4 = plus(p4, after(s5, p2))
     low_b = up(r4[HALF:])
+    pre0, p0, p1 = backward(0, 0, 2, near, after(prod, r4), w_in)
+    s1 = swap(p1)
+    r2 = plus(p2, after(s3, p0))
     high_a = down(r2[:HALF])
     low_a = up(plus(r4[:HALF], from_below))
     high_b = down(plus(r2[HALF:], from_above))
-    pre_a, p0, p1 = backward(0, pool[0], slope[0], prod, w_in)
-    got = swap(p1)
-    grad_w_in = grad_in(a, b, [pre_a, pre_b, pre_c], width, hidden)
-    grad_w_out = grad_out(pooled, rows, width, hidden)
-
-    back = exchange(
-        call(
-            settle_kernel,
-            shape_of(PEERS, PAD, width),
-            [p0, got, low_a, low_b, high_a, high_b],
-        )
-    )
+    grad_w_in = grad_in(
+        a, b, [after(pre0, r2), pre2, pre4, pre6, pre7], width, hidden
+    )
+    settled = call(
+        settle_kernel,
+        shape_of(PEERS, PAD, width),
+        [after(p0, grad_w_in), s1, low_a, low_b, high_a, high_b],
+    )
+    back = exchange(settled)
+    grad_w_out = grad_out(pooled, after(rows, settled), width, hidden)
     grad_flat = call(
-        tail_kernel, shape_of(row_count, width), [pos, flat, gain, grad_own, back]
+        tail_kernel, shape_of(row_count, width), [ids, places, flat, ln_gain, grad_own, after(back, grad_w_out)]
     )
     return (grad_flat.reshape(tokens.shape), grad_w_in, grad_w_out)
 

time: 165 us -> 159 us (0.964)
  waiting for transfers between devices: 40.8 us -> 29.3 us
  local copies, waits for them, and re-layouts: 12.8 us -> 15.3 us
    ppermute x6, waiting for transfers between devices: 16.5 us -> 6.81 us  [up(): return lax.ppermute(x, 'dp', [(i, (i + 2) % 8) for i in range(8)])]
    all_to_all x1, waiting for transfers between devices: 0.73 us -> 6.42 us  [exchange(): return lax.all_to_all(x, 'expert', split_axis=0, concat_axis=0, tiled=True)]
    ppermute x6, waiting for transfers between devices: 8.97 us -> 3.59 us  [down(): return lax.ppermute(x, 'dp', [(i, (i + 6) % 8) for i in range(8)])]
    unnamed x131 -> x137, local copies, waits for them, and re-layouts: 9.66 us -> 13.1 us
    pallas_call x13 -> x17, Pallas kernels: 27 us -> 28.1 us  [call(): pl.pallas_call(kernel, out_shape=out, in_specs=specs, out_specs=out_specs...]
  transfers between devices with their start and end apart: 28 -> 28, of which waited for: 13 -> 9; matrix products, arithmetic and copies ran while one was open for 2% -> 2% of each run, Pallas kernels for 13% -> 16%
where the time goes in v3:
time: 159 us; the launch traced here: 157 us
  blocking collectives  38.4 us (24%)
  Pallas kernels  37.2 us (23%)
  starting transfers between devices  31.1 us (20%)
  waiting for transfers between devices  29.3 us (18%)
  local copies, waits for them, and re-layouts  15.3 us (10%)
  other arithmetic  4.23 us (3%)
  between operations  1.6 us (1%)
    pallas_call x17, Pallas kernels, call(): pl.pallas_call(kernel, out_shape=out, in_specs=specs, out_specs=out_specs...  28.1 us
    all_to_all x1, blocking collectives, exchange(): return lax.all_to_all(x, 'expert', split_axis=0, concat_axis=0, tiled=True)  19.9 us
    all_to_all x1, blocking collectives, spread(): lax.all_to_all(x, everyone, split_axis=0, concat_axis=0, tiled=True, axis...  18.6 us
    ppermute x6, starting transfers between devices, down(): return lax.ppermute(x, 'dp', [(i, (i + 6) % 8) for i in range(8)])  15.8 us
    unnamed x137, local copies, waits for them, and re-layouts  13.1 us
    all_to_all x1, waiting for transfers between devices, spread(): lax.all_to_all(x, everyone, split_axis=0, concat_axis=0, tiled=True, axis...  10 us
    ppermute x6, waiting for transfers between devices, up(): return lax.ppermute(x, 'dp', [(i, (i + 2) % 8) for i in range(8)])  6.81 us
    all_to_all x1, waiting for transfers between devices, exchange(): return lax.all_to_all(x, 'expert', split_axis=0, concat_axis=0, tiled=True)  6.42 us
  transfers between devices with their start and end apart: 28, of which 9 were waited for; matrix products, arithmetic and copies ran while one was open for 2% of the time, Pallas kernels for 16%

profile of v3, /device:TPU:0, one launch (start us, length us, event | category | flops | bytes accessed | tf_op | source)
XLA Modules:
  0.0 157.2 jit_solution(6216143606052358373)
XLA Ops:
  0.6 1.0 copy-done.7
  1.6 0.7 copy-done.57
  2.3 0.7 copy-done.63
  3.0 0.7 copy-done.65
  3.7 0.8 shard_map.85
  4.5 19.9 %all_to_all.20.in_ref = bf16[16,16,1280]{2,1,0:T(8,128)(2,1)S(1)} all-to-all(bf16[16,16,1280]{2,1,0:T(8,128)(2,1)S(1)} %shard_map.85), channel_id=1, replica_groups=mesh['dp'=8,'expert'=16] {'expert'}, dimensions={0} | all-to-all | bytes 1310720 | tf_op jit(solution)/shard_map/all_to_all | solution.py:372
  24.3 0.4 shard_map.86
  24.8 0.5 collective-permute-start.1
  25.3 1.9 %collective-permute-start.2 = (bf16[96,1280]{1,0:T(8,128)(2,1)S(1)}, bf16[96,1280]{1,0:T(8,128)(2,1)S(1)}, u32[]{:S(2)}, u32[]{:S(2)}) collective-permute-start(bf16[96,1280]{1,0:T(8,128)(2,1)S(1)} %get-tuple-element.57.refs_0_), channel_id=1, source_target_pairs={{0,32},{16,48},{32,64},{48,80},{64,96},{80,112},{96,0},{112,16},{1... | collective-permute-start | bytes 737288 | tf_op jit(solution)/shard_map/ppermute | solution.py:360
  27.2 2.1 %collective-permute-start.8 = (bf16[112,1280]{1,0:T(8,128)(2,1)S(1)}, bf16[112,1280]{1,0:T(8,128)(2,1)S(1)}, u32[]{:S(2)}, u32[]{:S(2)}) collective-permute-start(bf16[112,1280]{1,0:T(8,128)(2,1)S(1)} %get-tuple-element.58.refs_2_.refs_8_), channel_id=1, source_target_pairs={{0,96},{16,112},{32,0},{48,16},{64,32},{80,48},{96,64},{112,80},{1... | collective-permute-start | bytes 860168 | tf_op jit(solution)/shard_map/ppermute | solution.py:363
  29.4 3.2 %collective-permute-start.4 = (bf16[96,1280]{1,0:T(8,128)(2,1)S(1)}, bf16[96,1280]{1,0:T(8,128)(2,1)S(1)}, u32[]{:S(2)}, u32[]{:S(2)}) collective-permute-start(bf16[96,1280]{1,0:T(8,128)(2,1)S(1)} %get-tuple-element.57.refs_0_), channel_id=1, source_target_pairs={{0,96},{16,112},{32,0},{48,16},{64,32},{80,48},{96,64},{112,80},{1... | collective-permute-start | bytes 737288 | tf_op jit(solution)/shard_map/ppermute | solution.py:363
  32.6 1.9 %copy-done = bf16[2,1280,640]{2,1,0:T(8,128)(2,1)S(1)} copy-done((bf16[2,1280,640]{2,1,0:T(8,128)(2,1)S(1)}, bf16[2,1280,640]{2,1,0:T(8,128)(2,1)}, u32[]{:S(2)}) %copy-start) | copy-done | bytes 3276824
  34.5 2.0 %shard_map.87 = (bf16[2,2,32,640]{3,2,1,0:T(8,128)(2,1)S(1)}, bf16[2,2,96,640]{3,2,1,0:T(8,128)(2,1)S(1)}, bf16[2,2,32,96]{3,2,1,0:T(8,128)(2,1)S(1)}) custom-call(bf16[96,1280]{1,0:T(8,128)(2,1)S(1)} %get-tuple-element.57.refs_0_, bf16[96,1280]{1,0:T(8,128)(2,1)S(1)} %collective-permute-done.refs_1_, ...), custom_call_target="tpu_custom_call" | custom-call | flops 629145600 | bytes 4751360 | tf_op jit(solution)/shard_map/pallas_call | solution.py:58
  36.5 0.8 copy-done.49
  37.4 0.5 collective-permute-start.9
  37.9 3.9 %collective-permute-done.6.refs_4_.refs_10_ = bf16[112,1280]{1,0:T(8,128)(2,1)S(1)} collective-permute-done((bf16[112,1280]{1,0:T(8,128)(2,1)S(1)}, bf16[112,1280]{1,0:T(8,128)(2,1)S(1)}, u32[]{:S(2)}, u32[]{:S(2)}) %collective-permute-start.6) | collective-permute-done | bytes 286752 | tf_op jit(solution)/shard_map/ppermute | solution.py:360
  41.7 0.5 collective-permute-start.5
  42.2 2.4 %collective-permute-start.11 = (bf16[112,1280]{1,0:T(8,128)(2,1)S(1)}, bf16[112,1280]{1,0:T(8,128)(2,1)S(1)}, u32[]{:S(2)}, u32[]{:S(2)}) collective-permute-start(bf16[112,1280]{1,0:T(8,128)(2,1)S(1)} %collective-permute-done.8.refs_6_.refs_12_), channel_id=1, source_target_pairs={{0,96},{16,112},{32,0},{48,16},{64,32},{80,48},{96,64},{112,80},{1... | collective-permute-start | bytes 860168 | tf_op jit(solution)/shard_map/ppermute | solution.py:363
  44.8 3.8 %shard_map.88 = (bf16[4,2,32,640]{3,2,1,0:T(8,128)(2,1)S(1)}, bf16[4,2,96,640]{3,2,1,0:T(8,128)(2,1)S(1)}, bf16[4,2,32,96]{3,2,1,0:T(8,128)(2,1)S(1)}) custom-call(bf16[96,1280]{1,0:T(8,128)(2,1)S(1)} %collective-permute-done.2.refs_0_.refs_2_, bf16[96,1280]{1,0:T(8,128)(2,1)S(1)} %collective-permute-done.3.refs_1_.refs_3_, ...), custom_call_target="tpu_custom_call" | custom-call | flops 1258291200 | bytes 6225920 | tf_op jit(solution)/shard_map/pallas_call | solution.py:58
  48.6 0.9 copy-done.5
  49.6 0.6 copy-done.51
  50.2 1.2 collective-permute-done.11.refs_1_.refs_14_
  51.6 2.4 %collective-permute-done.10.refs_0_.refs_6_ = bf16[96,1280]{1,0:T(8,128)(2,1)S(1)} collective-permute-done((bf16[96,1280]{1,0:T(8,128)(2,1)S(1)}, bf16[96,1280]{1,0:T(8,128)(2,1)S(1)}, u32[]{:S(2)}, u32[]{:S(2)}) %collective-permute-start.10) | collective-permute-done | bytes 245792 | tf_op jit(solution)/shard_map/ppermute | solution.py:360
  54.0 1.1 shard_map.89
  55.2 0.4 collective-permute-done.12.refs_0_.refs_7_
  55.5 1.1 shard_map.90
  56.6 0.7 copy-done.55
  57.3 1.4 shard_map.91
  59.0 1.9 %copy-done.3 = bf16[2,640,1280]{2,1,0:T(8,128)(2,1)S(1)} copy-done((bf16[2,640,1280]{2,1,0:T(8,128)(2,1)S(1)}, bf16[2,640,1280]{2,1,0:T(8,128)(2,1)}, u32[]{:S(2)}) %copy-start.3) | copy-done | bytes 3276824
  60.9 1.0 copy-done.10
  61.9 0.9 copy-done.45
  62.8 0.7 shard_map.92.own_ref
  63.5 1.1 shard_map.93
  64.6 1.1 copy.11
  65.6 5.7 %all-to-all-start.1 = ((bf16[64,2,1280]{2,1,0:T(2,128)(2,1)}), bf16[64,2,1280]{2,1,0:T(2,128)(2,1)}, u32[]{:S(2)}, u32[]{:S(2)}) async-start(bf16[64,2,1280]{2,1,0:T(2,128)(2,1)} %copy.11), calls=%async_computation.1 | async-start | bytes 655360 | tf_op jit(solution)/shard_map/all_to_all | solution.py:375
  71.3 1.6 %convert_reduce_fusion = f32[2,1280]{1,0:T(2,128)} fusion(bf16[1,2,64,1280]{3,2,1,0:T(8,128)(2,1)} %param.6), kind=kLoop, calls=%fused_computation.4 | loop fusion | flops 325120 | bytes 337920 | tf_op jit(solution)/shard_map/reduce_sum | solution.py:433
  73.0 10.0 %all-to-all-done.1 = bf16[64,2,1280]{2,1,0:T(2,128)(2,1)} async-done(((bf16[64,2,1280]{2,1,0:T(2,128)(2,1)}), bf16[64,2,1280]{2,1,0:T(2,128)(2,1)}, u32[]{:S(2)}, u32[]{:S(2)}) %all-to-all-start.1) | async-done | bytes 327712 | tf_op jit(solution)/shard_map/all_to_all | solution.py:375
  83.0 1.4 convert_reduce_fusion.1
  84.5 0.7 add_multiply_fusion
  85.3 18.6 %all_to_all.21 = f32[64,2,1280]{2,1,0:T(2,128)S(1)} all-to-all(f32[64,2,1280]{2,1,0:T(2,128)S(1)} %broadcast_in_dim.2), channel_id=1, replica_groups={{0,1,2,3,4,5,6,7,8,9,10,11,12,13,14,15,32,33,34,35,36,37,38,39,40,41,42..., dimensions={0} | all-to-all | bytes 1310720 | tf_op jit(solution)/shard_map/all_to_all | solution.py:375
  104.1 2.1 %collective-permute-done.15.other_ref = f32[2,64,1280]{2,1,0:T(8,128)S(1)} collective-permute-done((f32[2,64,1280]{2,1,0:T(8,128)S(1)}, f32[2,64,1280]{2,1,0:T(8,128)S(1)}, u32[]{:S(2)}, u32[]{:S(2)}) %collective-permute-start.15) | collective-permute-done | bytes 655392 | tf_op jit(solution)/shard_map/ppermute | solution.py:366
  106.1 4.0 %shard_map.94 = (f32[2,128,1280]{2,1,0:T(8,128)S(1)}, bf16[8,32,1280]{2,1,0:T(8,128)(2,1)S(1)}, bf16[2,256,640]{2,1,0:T(8,128)(2,1)S(1)}) custom-call(s32[1]{0:T(128)} %bitcast.3.z_ref, f32[2,64,1280]{2,1,0:T(8,128)S(1)} %bitcast.19, f32[2,64,1280]{2,1,0:T(8,128)S(1)} %collective-permute-done.15.other_ref, bf16[2,640,1280]{2,1,0:T(8,128)(2,1)S(1)} %copy-done.4), custom_call_target="tpu_custom_call" | custom-call | flops 838860800 | bytes 3276800 | tf_op jit(solution)/shard_map/pallas_call | solution.py:58
  110.2 1.2 shard_map.95
  111.5 0.4 collective-permute-start.17
  111.9 1.2 shard_map.96
  113.2 2.2 %shard_map.97 = (bf16[2,2,96,640]{3,2,1,0:T(8,128)(2,1)S(1)}, bf16[192,1280]{1,0:T(8,128)(2,1)S(1)}, bf16[192,1280]{1,0:T(8,128)(2,1)S(1)}) custom-call(bf16[4,2,32,96]{3,2,1,0:T(8,128)(2,1)S(1)} %copy-done.52, bf16[4,2,96,640]{3,2,1,0:T(8,128)(2,1)S(1)} %copy-done.6, bf16[2,256,640]{2,1,0:T(8,128)(2,1)S(1)} %get-tuple-element.88.prod_ref, ...), custom_call_target="tpu_custom_call" | custom-call | flops 629145600 | bytes 4751360 | tf_op jit(solution)/shard_map/pallas_call | solution.py:58
  115.4 0.5 collective-permute-start.16
  116.0 0.6 collective-permute-start.20
  116.6 2.2 %shard_map.98 = (bf16[2,2,96,640]{3,2,1,0:T(8,128)(2,1)S(1)}, bf16[192,1280]{1,0:T(8,128)(2,1)S(1)}, bf16[192,1280]{1,0:T(8,128)(2,1)S(1)}) custom-call(bf16[4,2,32,96]{3,2,1,0:T(8,128)(2,1)S(1)} %copy-done.52, bf16[4,2,96,640]{3,2,1,0:T(8,128)(2,1)S(1)} %copy-done.6, bf16[2,256,640]{2,1,0:T(8,128)(2,1)S(1)} %get-tuple-element.88.prod_ref, ...), custom_call_target="tpu_custom_call" | custom-call | flops 629145600 | bytes 4751360 | tf_op jit(solution)/shard_map/pallas_call | solution.py:58
  119.0 2.8 %collective-permute-start.24 = (bf16[96,1280]{1,0:T(8,128)(2,1)S(1)}, bf16[96,1280]{1,0:T(8,128)(2,1)S(1)}, u32[]{:S(2)}, u32[]{:S(2)}) collective-permute-start(bf16[96,1280]{1,0:T(8,128)(2,1)S(1)} %get-tuple-element.103), channel_id=1, source_target_pairs={{0,96},{16,112},{32,0},{48,16},{64,32},{80,48},{96,64},{112,80},{1... | collective-permute-start | bytes 737288 | tf_op jit(solution)/shard_map/ppermute | solution.py:363
  122.0 2.2 %shard_map.99 = (bf16[2,2,96,640]{3,2,1,0:T(8,128)(2,1)S(1)}, bf16[192,1280]{1,0:T(8,128)(2,1)S(1)}, bf16[192,1280]{1,0:T(8,128)(2,1)S(1)}) custom-call(bf16[2,2,32,96]{3,2,1,0:T(8,128)(2,1)S(1)} %get-tuple-element.69.pool_ref, bf16[2,2,96,640]{3,2,1,0:T(8,128)(2,1)S(1)} %copy-done.50, bf16[2,256,640]{2,1,0:T(8,128)(2,1)S(1)} %get-tuple-element.88.prod_ref, ...), custom_call_target="tpu_custom_call" | custom-call | flops 629145600 | bytes 4751360 | tf_op jit(solution)/shard_map/pallas_call | solution.py:58
  124.2 0.6 collective-permute-start.19
  124.8 0.5 collective-permute-done.20
  125.6 3.3 %collective-permute-start.23 = (bf16[96,1280]{1,0:T(8,128)(2,1)S(1)}, bf16[96,1280]{1,0:T(8,128)(2,1)S(1)}, u32[]{:S(2)}, u32[]{:S(2)}) collective-permute-start(bf16[96,1280]{1,0:T(8,128)(2,1)S(1)} %slice.27), channel_id=1, source_target_pairs={{0,96},{16,112},{32,0},{48,16},{64,32},{80,48},{96,64},{112,80},{1... | collective-permute-start | bytes 737288 | tf_op jit(solution)/shard_map/ppermute | solution.py:363
  129.0 1.9 %collective-permute-start.25 = (bf16[96,1280]{1,0:T(8,128)(2,1)S(1)}, bf16[96,1280]{1,0:T(8,128)(2,1)S(1)}, u32[]{:S(2)}, u32[]{:S(2)}) collective-permute-start(bf16[96,1280]{1,0:T(8,128)(2,1)S(1)} %add_convert_fusion.3), channel_id=1, source_target_pairs={{0,96},{16,112},{32,0},{48,16},{64,32},{80,48},{96,64},{112,80},{1... | collective-permute-start | bytes 737288 | tf_op jit(solution)/shard_map/ppermute | solution.py:363
  131.0 5.7 %shard_map.100 = f32[2,1280,640]{2,1,0:T(8,128)} custom-call(bf16[96,1280]{1,0:T(8,128)(2,1)S(1)} %copy-done.29, bf16[96,1280]{1,0:T(8,128)(2,1)S(1)} %copy-done.31, bf16[96,1280]{1,0:T(8,128)(2,1)S(1)} %copy-done.33, bf16[96,1280]{1,0:T(8,128)(2,1)S(1)} %copy-done.37, bf16[96,1280]{1,0:T(8,128)(2,1)S(1)} %copy-done.35, bf16[96,1280]{1,0:T(8,128)(2,1)S(1)} %copy-done.39, ...), custom_call_target="tpu_custom_call" | custom-call | flops 2516582400 | bytes 17000000 | tf_op jit(solution)/shard_map/pallas_call | solution.py:277
  136.7 2.3 %collective-permute-done.25.rb_ref = bf16[96,1280]{1,0:T(8,128)(2,1)S(1)} collective-permute-done((bf16[96,1280]{1,0:T(8,128)(2,1)S(1)}, bf16[96,1280]{1,0:T(8,128)(2,1)S(1)}, u32[]{:S(2)}, u32[]{:S(2)}) %collective-permute-start.25) | collective-permute-done | bytes 245792 | tf_op jit(solution)/shard_map/ppermute | solution.py:363
  139.0 1.3 shard_map.101
  140.4 3.6 %all-to-all-start.3 = ((bf16[16,16,1280]{2,1,0:T(8,128)(2,1)}), bf16[16,16,1280]{2,1,0:T(8,128)(2,1)S(1)}, u32[]{:S(2)}, u32[]{:S(2)}) async-start(bf16[16,16,1280]{2,1,0:T(8,128)(2,1)} %shard_map.101), calls=%async_computation.3 | async-start | bytes 1310720 | tf_op jit(solution)/shard_map/all_to_all | solution.py:372
  144.0 0.9 constant_dynamic-slice_fusion
  144.9 1.1 copy-done.48
  146.0 3.5 %shard_map.102 = f32[2,640,1280]{2,1,0:T(8,128)} custom-call(bf16[2,2,32,640]{3,2,1,0:T(8,128)(2,1)S(1)} %get-tuple-element.55.refs_0_.args_0_, bf16[4,2,32,640]{3,2,1,0:T(8,128)(2,1)S(1)} %copy-done.11, bf16[1,2,32,640]{3,2,1,0:T(8,128)(2,1)S(1)} %get-tuple-element.63.refs_2_.args_2_, bf16[1,2,32,640]{3,2,1,0:T(8,128)(2,1)S(1)} %copy-done.46, ...), custom_call_target="tpu_custom_call" | custom-call | flops 838860800 | bytes 9000000 | tf_op jit(solution)/shard_map/pallas_call | solution.py:304
  149.5 6.4 %all-to-all-done.3.back_ref = bf16[16,16,1280]{2,1,0:T(8,128)(2,1)S(1)} async-done(((bf16[16,16,1280]{2,1,0:T(8,128)(2,1)}), bf16[16,16,1280]{2,1,0:T(8,128)(2,1)S(1)}, u32[]{:S(2)}, u32[]{:S(2)}) %all-to-all-start.3) | async-done | bytes 655392 | tf_op jit(solution)/shard_map/all_to_all | solution.py:372
  155.9 1.3 shard_map.103
  (166 shorter events, 1.7 us)
Async XLA Ops:
  24.7 20.0 %copy-start.28 = (bf16[96,1280]{1,0:T(8,128)(2,1)}, bf16[96,1280]{1,0:T(8,128)(2,1)S(1)}, u32[]{:S(2)}) copy-start(bf16[96,1280]{1,0:T(8,128)(2,1)S(1)} %get-tuple-element.57.refs_0_) | copy-start | bytes 737284
  24.7 23.9 %copy-start.12 = (bf16[112,1280]{1,0:T(8,128)(2,1)}, bf16[112,1280]{1,0:T(8,128)(2,1)S(1)}, u32[]{:S(2)}) copy-start(bf16[112,1280]{1,0:T(8,128)(2,1)S(1)} %get-tuple-element.58.refs_2_.refs_8_) | copy-start | bytes 860164
  24.7 4.6 %collective-permute-start = (bf16[96,1280]{1,0:T(8,128)(2,1)S(1)}, bf16[96,1280]{1,0:T(8,128)(2,1)S(1)}, u32[]{:S(2)}, u32[]{:S(2)}) collective-permute-start(bf16[96,1280]{1,0:T(8,128)(2,1)S(1)} %get-tuple-element.57.refs_0_), channel_id=1, source_target_pairs={{0,16},{16,0},{32,48},{48,32},{64,80},{80,64},{96,112},{112,96},{1... | collective-permute-start | bytes 737288 | tf_op jit(solution)/shard_map/ppermute | solution.py:366
  24.8 4.6 %collective-permute-start.1 = (bf16[112,1280]{1,0:T(8,128)(2,1)S(1)}, bf16[112,1280]{1,0:T(8,128)(2,1)S(1)}, u32[]{:S(2)}, u32[]{:S(2)}) collective-permute-start(bf16[112,1280]{1,0:T(8,128)(2,1)S(1)} %get-tuple-element.58.refs_2_.refs_8_), channel_id=1, source_target_pairs={{0,16},{16,0},{32,48},{48,32},{64,80},{80,64},{96,112},{112,96},{1... | collective-permute-start | bytes 860168 | tf_op jit(solution)/shard_map/ppermute | solution.py:366
  25.3 12.0 %collective-permute-start.2 = (bf16[96,1280]{1,0:T(8,128)(2,1)S(1)}, bf16[96,1280]{1,0:T(8,128)(2,1)S(1)}, u32[]{:S(2)}, u32[]{:S(2)}) collective-permute-start(bf16[96,1280]{1,0:T(8,128)(2,1)S(1)} %get-tuple-element.57.refs_0_), channel_id=1, source_target_pairs={{0,32},{16,48},{32,64},{48,80},{64,96},{80,112},{96,0},{112,16},{1... | collective-permute-start | bytes 737288 | tf_op jit(solution)/shard_map/ppermute | solution.py:360
  27.2 10.1 %collective-permute-start.8 = (bf16[112,1280]{1,0:T(8,128)(2,1)S(1)}, bf16[112,1280]{1,0:T(8,128)(2,1)S(1)}, u32[]{:S(2)}, u32[]{:S(2)}) collective-permute-start(bf16[112,1280]{1,0:T(8,128)(2,1)S(1)} %get-tuple-element.58.refs_2_.refs_8_), channel_id=1, source_target_pairs={{0,96},{16,112},{32,0},{48,16},{64,32},{80,48},{96,64},{112,80},{1... | collective-permute-start | bytes 860168 | tf_op jit(solution)/shard_map/ppermute | solution.py:363
  29.4 15.4 %copy-start.30 = (bf16[96,1280]{1,0:T(8,128)(2,1)}, bf16[96,1280]{1,0:T(8,128)(2,1)S(1)}, u32[]{:S(2)}) copy-start(bf16[96,1280]{1,0:T(8,128)(2,1)S(1)} %collective-permute-done.refs_1_) | copy-start | bytes 737284
  29.4 12.3 %collective-permute-start.6 = (bf16[112,1280]{1,0:T(8,128)(2,1)S(1)}, bf16[112,1280]{1,0:T(8,128)(2,1)S(1)}, u32[]{:S(2)}, u32[]{:S(2)}) collective-permute-start(bf16[112,1280]{1,0:T(8,128)(2,1)S(1)} %get-tuple-element.58.refs_2_.refs_8_), channel_id=1, source_target_pairs={{0,32},{16,48},{32,64},{48,80},{64,96},{80,112},{96,0},{112,16},{1... | collective-permute-start | bytes 860168 | tf_op jit(solution)/shard_map/ppermute | solution.py:360
  29.4 19.2 %copy-start.14 = (bf16[112,1280]{1,0:T(8,128)(2,1)}, bf16[112,1280]{1,0:T(8,128)(2,1)S(1)}, u32[]{:S(2)}) copy-start(bf16[112,1280]{1,0:T(8,128)(2,1)S(1)} %collective-permute-done.1.refs_3_.refs_9_) | copy-start | bytes 860164
  29.4 12.3 %collective-permute-start.4 = (bf16[96,1280]{1,0:T(8,128)(2,1)S(1)}, bf16[96,1280]{1,0:T(8,128)(2,1)S(1)}, u32[]{:S(2)}, u32[]{:S(2)}) collective-permute-start(bf16[96,1280]{1,0:T(8,128)(2,1)S(1)} %get-tuple-element.57.refs_0_), channel_id=1, source_target_pairs={{0,96},{16,112},{32,0},{48,16},{64,32},{80,48},{96,64},{112,80},{1... | collective-permute-start | bytes 737288 | tf_op jit(solution)/shard_map/ppermute | solution.py:363
  34.5 10.2 %copy-start.1 = (bf16[2,1280,640]{2,1,0:T(8,128)(2,1)S(1)}, bf16[2,1280,640]{2,1,0:T(8,128)(2,1)}, u32[]{:S(2)}) copy-start(bf16[2,1280,640]{2,1,0:T(8,128)(2,1)} %w_in.9) | copy-start | bytes 9830404
  37.3 17.8 %copy-start.32 = (bf16[96,1280]{1,0:T(8,128)(2,1)}, bf16[96,1280]{1,0:T(8,128)(2,1)S(1)}, u32[]{:S(2)}) copy-start(bf16[96,1280]{1,0:T(8,128)(2,1)S(1)} %collective-permute-done.2.refs_0_.refs_2_) | copy-start | bytes 737284
  37.3 7.3 %collective-permute-start.3 = (bf16[96,1280]{1,0:T(8,128)(2,1)S(1)}, bf16[96,1280]{1,0:T(8,128)(2,1)S(1)}, u32[]{:S(2)}, u32[]{:S(2)}) collective-permute-start(bf16[96,1280]{1,0:T(8,128)(2,1)S(1)} %collective-permute-done.2.refs_0_.refs_2_), channel_id=1, source_target_pairs={{0,16},{16,0},{32,48},{48,32},{64,80},{80,64},{96,112},{112,96},{1... | collective-permute-start | bytes 737288 | tf_op jit(solution)/shard_map/ppermute | solution.py:366
  37.4 17.8 %copy-start.16 = (bf16[112,1280]{1,0:T(8,128)(2,1)}, bf16[112,1280]{1,0:T(8,128)(2,1)S(1)}, u32[]{:S(2)}) copy-start(bf16[112,1280]{1,0:T(8,128)(2,1)S(1)} %collective-permute-done.8.refs_6_.refs_12_) | copy-start | bytes 860164
  37.4 7.3 %collective-permute-start.9 = (bf16[112,1280]{1,0:T(8,128)(2,1)S(1)}, bf16[112,1280]{1,0:T(8,128)(2,1)S(1)}, u32[]{:S(2)}, u32[]{:S(2)}) collective-permute-start(bf16[112,1280]{1,0:T(8,128)(2,1)S(1)} %collective-permute-done.8.refs_6_.refs_12_), channel_id=1, source_target_pairs={{0,16},{16,0},{32,48},{48,32},{64,80},{80,64},{96,112},{112,96},{1... | collective-permute-start | bytes 860168 | tf_op jit(solution)/shard_map/ppermute | solution.py:366
  41.7 13.4 %copy-start.18 = (bf16[112,1280]{1,0:T(8,128)(2,1)}, bf16[112,1280]{1,0:T(8,128)(2,1)S(1)}, u32[]{:S(2)}) copy-start(bf16[112,1280]{1,0:T(8,128)(2,1)S(1)} %collective-permute-done.6.refs_4_.refs_10_) | copy-start | bytes 860164
  41.7 3.0 %collective-permute-start.7 = (bf16[112,1280]{1,0:T(8,128)(2,1)S(1)}, bf16[112,1280]{1,0:T(8,128)(2,1)S(1)}, u32[]{:S(2)}, u32[]{:S(2)}) collective-permute-start(bf16[112,1280]{1,0:T(8,128)(2,1)S(1)} %collective-permute-done.6.refs_4_.refs_10_), channel_id=1, source_target_pairs={{0,16},{16,0},{32,48},{48,32},{64,80},{80,64},{96,112},{112,96},{1... | collective-permute-start | bytes 860168 | tf_op jit(solution)/shard_map/ppermute | solution.py:366
  41.7 13.4 %copy-start.34 = (bf16[96,1280]{1,0:T(8,128)(2,1)}, bf16[96,1280]{1,0:T(8,128)(2,1)S(1)}, u32[]{:S(2)}) copy-start(bf16[96,1280]{1,0:T(8,128)(2,1)S(1)} %collective-permute-done.4.refs_2_.refs_4_) | copy-start | bytes 737284
  41.7 3.0 %collective-permute-start.5 = (bf16[96,1280]{1,0:T(8,128)(2,1)S(1)}, bf16[96,1280]{1,0:T(8,128)(2,1)S(1)}, u32[]{:S(2)}, u32[]{:S(2)}) collective-permute-start(bf16[96,1280]{1,0:T(8,128)(2,1)S(1)} %collective-permute-done.4.refs_2_.refs_4_), channel_id=1, source_target_pairs={{0,16},{16,0},{32,48},{48,32},{64,80},{80,64},{96,112},{112,96},{1... | collective-permute-start | bytes 737288 | tf_op jit(solution)/shard_map/ppermute | solution.py:366
  42.2 9.2 %collective-permute-start.11 = (bf16[112,1280]{1,0:T(8,128)(2,1)S(1)}, bf16[112,1280]{1,0:T(8,128)(2,1)S(1)}, u32[]{:S(2)}, u32[]{:S(2)}) collective-permute-start(bf16[112,1280]{1,0:T(8,128)(2,1)S(1)} %collective-permute-done.8.refs_6_.refs_12_), channel_id=1, source_target_pairs={{0,96},{16,112},{32,0},{48,16},{64,32},{80,48},{96,64},{112,80},{1... | collective-permute-start | bytes 860168 | tf_op jit(solution)/shard_map/ppermute | solution.py:363
  44.7 9.3 %collective-permute-start.10 = (bf16[96,1280]{1,0:T(8,128)(2,1)S(1)}, bf16[96,1280]{1,0:T(8,128)(2,1)S(1)}, u32[]{:S(2)}, u32[]{:S(2)}) collective-permute-start(bf16[96,1280]{1,0:T(8,128)(2,1)S(1)} %collective-permute-done.2.refs_0_.refs_2_), channel_id=1, source_target_pairs={{0,32},{16,48},{32,64},{48,80},{64,96},{80,112},{96,0},{112,16},{1... | collective-permute-start | bytes 737288 | tf_op jit(solution)/shard_map/ppermute | solution.py:360
  44.7 9.2 %copy-start.38 = (bf16[96,1280]{1,0:T(8,128)(2,1)}, bf16[96,1280]{1,0:T(8,128)(2,1)S(1)}, u32[]{:S(2)}) copy-start(bf16[96,1280]{1,0:T(8,128)(2,1)S(1)} %collective-permute-done.5.refs_3_.refs_5_) | copy-start | bytes 737284
  50.2 7.1 %copy-start.9 = (bf16[4,2,32,640]{3,2,1,0:T(8,128)(2,1)}, bf16[4,2,32,640]{3,2,1,0:T(8,128)(2,1)S(1)}, u32[]{:S(2)}) copy-start(bf16[4,2,32,640]{3,2,1,0:T(8,128)(2,1)S(1)} %get-tuple-element.60.refs_1_.args_1_) | copy-start | bytes 983044
  51.5 4.0 %collective-permute-start.13 = (bf16[112,1280]{1,0:T(8,128)(2,1)S(1)}, bf16[112,1280]{1,0:T(8,128)(2,1)S(1)}, u32[]{:S(2)}, u32[]{:S(2)}) collective-permute-start(bf16[112,1280]{1,0:T(8,128)(2,1)S(1)} %collective-permute-done.11.refs_1_.refs_14_), channel_id=1, source_target_pairs={{0,16},{16,0},{32,48},{48,32},{64,80},{80,64},{96,112},{112,96},{1... | collective-permute-start | bytes 860168 | tf_op jit(solution)/shard_map/ppermute | solution.py:366
  54.0 1.5 collective-permute-start.12
  58.8 4.7 %collective-permute-start.14 = (bf16[4,32,1280]{2,1,0:T(8,128)(2,1)}, bf16[4,32,1280]{2,1,0:T(8,128)(2,1)}, u32[]{:S(2)}, u32[]{:S(2)}) collective-permute-start(bf16[4,32,1280]{2,1,0:T(8,128)(2,1)} %shard_map.91), channel_id=1, source_target_pairs={{0,16},{16,0},{32,48},{48,32},{64,80},{80,64},{96,112},{112,96},{1... | collective-permute-start | bytes 983048 | tf_op jit(solution)/shard_map/ppermute | solution.py:366
  65.6 17.4 %all-to-all-start.1 = ((bf16[64,2,1280]{2,1,0:T(2,128)(2,1)}), bf16[64,2,1280]{2,1,0:T(2,128)(2,1)}, u32[]{:S(2)}, u32[]{:S(2)}) async-start(bf16[64,2,1280]{2,1,0:T(2,128)(2,1)} %copy.11), calls=%async_computation.1 | async-start | bytes 655360 | tf_op jit(solution)/shard_map/all_to_all | solution.py:375
  83.0 23.1 %copy-start.4 = (bf16[2,640,1280]{2,1,0:T(8,128)(2,1)S(1)}, bf16[2,640,1280]{2,1,0:T(8,128)(2,1)}, u32[]{:S(2)}) copy-start(bf16[2,640,1280]{2,1,0:T(8,128)(2,1)} %w_out.1) | copy-start | bytes 9830404
  103.9 8.0 %copy-start.54 = (bf16[1,2,96,640]{3,2,1,0:T(8,128)(2,1)S(1)}, bf16[1,2,96,640]{3,2,1,0:T(8,128)(2,1)}, u32[]{:S(2)}) copy-start(bf16[1,2,96,640]{3,2,1,0:T(8,128)(2,1)} %copy-done.53) | copy-start | bytes 737284
  104.0 8.0 %copy-start.60 = (bf16[1,2,32,96]{3,2,1,0:T(8,128)(2,1)S(1)}, bf16[1,2,32,96]{3,2,1,0:T(8,128)(2,1)}, u32[]{:S(2)}) copy-start(bf16[1,2,32,96]{3,2,1,0:T(8,128)(2,1)} %copy-done.59) | copy-start | bytes 36868
  104.0 2.2 %collective-permute-start.15 = (f32[2,64,1280]{2,1,0:T(8,128)S(1)}, f32[2,64,1280]{2,1,0:T(8,128)S(1)}, u32[]{:S(2)}, u32[]{:S(2)}) collective-permute-start(f32[2,64,1280]{2,1,0:T(8,128)S(1)} %bitcast.18), channel_id=1, source_target_pairs={{0,16},{16,0},{32,48},{48,32},{64,80},{80,64},{96,112},{112,96},{1... | collective-permute-start | bytes 1966088 | tf_op jit(solution)/shard_map/ppermute | solution.py:366
  111.5 4.4 %collective-permute-start.17 = (bf16[192,1280]{1,0:T(8,128)(2,1)S(1)}, bf16[192,1280]{1,0:T(8,128)(2,1)S(1)}, u32[]{:S(2)}, u32[]{:S(2)}) collective-permute-start(bf16[192,1280]{1,0:T(8,128)(2,1)S(1)} %get-tuple-element.78), channel_id=1, source_target_pairs={{0,16},{16,0},{32,48},{48,32},{64,80},{80,64},{96,112},{112,96},{1... | collective-permute-start | bytes 1474568 | tf_op jit(solution)/shard_map/ppermute | solution.py:366
  115.4 3.4 %collective-permute-start.16 = (bf16[192,1280]{1,0:T(8,128)(2,1)S(1)}, bf16[192,1280]{1,0:T(8,128)(2,1)S(1)}, u32[]{:S(2)}, u32[]{:S(2)}) collective-permute-start(bf16[192,1280]{1,0:T(8,128)(2,1)S(1)} %get-tuple-element.83), channel_id=1, source_target_pairs={{0,16},{16,0},{32,48},{48,32},{64,80},{80,64},{96,112},{112,96},{1... | collective-permute-start | bytes 1474568 | tf_op jit(solution)/shard_map/ppermute | solution.py:366
  116.0 9.3 %collective-permute-start.20 = (bf16[96,1280]{1,0:T(8,128)(2,1)S(1)}, bf16[96,1280]{1,0:T(8,128)(2,1)S(1)}, u32[]{:S(2)}, u32[]{:S(2)}) collective-permute-start(bf16[96,1280]{1,0:T(8,128)(2,1)S(1)} %get-tuple-element.104), channel_id=1, source_target_pairs={{0,32},{16,48},{32,64},{48,80},{64,96},{80,112},{96,0},{112,16},{1... | collective-permute-start | bytes 737288 | tf_op jit(solution)/shard_map/ppermute | solution.py:360
  119.0 9.9 %collective-permute-start.24 = (bf16[96,1280]{1,0:T(8,128)(2,1)S(1)}, bf16[96,1280]{1,0:T(8,128)(2,1)S(1)}, u32[]{:S(2)}, u32[]{:S(2)}) collective-permute-start(bf16[96,1280]{1,0:T(8,128)(2,1)S(1)} %get-tuple-element.103), channel_id=1, source_target_pairs={{0,96},{16,112},{32,0},{48,16},{64,32},{80,48},{96,64},{112,80},{1... | collective-permute-start | bytes 737288 | tf_op jit(solution)/shard_map/ppermute | solution.py:363
  121.8 3.7 %collective-permute-start.18 = (bf16[192,1280]{1,0:T(8,128)(2,1)S(1)}, bf16[192,1280]{1,0:T(8,128)(2,1)S(1)}, u32[]{:S(2)}, u32[]{:S(2)}) collective-permute-start(bf16[192,1280]{1,0:T(8,128)(2,1)S(1)} %get-tuple-element.91), channel_id=1, source_target_pairs={{0,16},{16,0},{32,48},{48,32},{64,80},{80,64},{96,112},{112,96},{1... | collective-permute-start | bytes 1474568 | tf_op jit(solution)/shard_map/ppermute | solution.py:366
  121.8 14.9 %collective-permute-start.22 = (bf16[96,1280]{1,0:T(8,128)(2,1)S(1)}, bf16[96,1280]{1,0:T(8,128)(2,1)S(1)}, u32[]{:S(2)}, u32[]{:S(2)}) collective-permute-start(bf16[96,1280]{1,0:T(8,128)(2,1)S(1)} %slice.26), channel_id=1, source_target_pairs={{0,32},{16,48},{32,64},{48,80},{64,96},{80,112},{96,0},{112,16},{1... | collective-permute-start | bytes 737288 | tf_op jit(solution)/shard_map/ppermute | solution.py:360
  121.8 9.1 %copy-start.13 = (bf16[112,1280]{1,0:T(8,128)(2,1)S(1)}, bf16[112,1280]{1,0:T(8,128)(2,1)}, u32[]{:S(2)}) copy-start(bf16[112,1280]{1,0:T(8,128)(2,1)} %copy-done.12) | copy-start | bytes 860164
  121.8 9.0 %copy-start.15 = (bf16[112,1280]{1,0:T(8,128)(2,1)S(1)}, bf16[112,1280]{1,0:T(8,128)(2,1)}, u32[]{:S(2)}) copy-start(bf16[112,1280]{1,0:T(8,128)(2,1)} %copy-done.14) | copy-start | bytes 860164
  121.8 9.0 %copy-start.17 = (bf16[112,1280]{1,0:T(8,128)(2,1)S(1)}, bf16[112,1280]{1,0:T(8,128)(2,1)}, u32[]{:S(2)}) copy-start(bf16[112,1280]{1,0:T(8,128)(2,1)} %copy-done.16) | copy-start | bytes 860164
  121.8 9.0 %copy-start.19 = (bf16[112,1280]{1,0:T(8,128)(2,1)S(1)}, bf16[112,1280]{1,0:T(8,128)(2,1)}, u32[]{:S(2)}) copy-start(bf16[112,1280]{1,0:T(8,128)(2,1)} %copy-done.18) | copy-start | bytes 860164
  121.9 9.0 %copy-start.21 = (bf16[112,1280]{1,0:T(8,128)(2,1)S(1)}, bf16[112,1280]{1,0:T(8,128)(2,1)}, u32[]{:S(2)}) copy-start(bf16[112,1280]{1,0:T(8,128)(2,1)} %copy-done.20) | copy-start | bytes 860164
  121.9 9.0 %copy-start.23 = (bf16[112,1280]{1,0:T(8,128)(2,1)S(1)}, bf16[112,1280]{1,0:T(8,128)(2,1)}, u32[]{:S(2)}) copy-start(bf16[112,1280]{1,0:T(8,128)(2,1)} %copy-done.22) | copy-start | bytes 860164
  121.9 9.0 %copy-start.25 = (bf16[112,1280]{1,0:T(8,128)(2,1)S(1)}, bf16[112,1280]{1,0:T(8,128)(2,1)}, u32[]{:S(2)}) copy-start(bf16[112,1280]{1,0:T(8,128)(2,1)} %copy-done.24) | copy-start | bytes 860164
  121.9 9.0 %copy-start.27 = (bf16[112,1280]{1,0:T(8,128)(2,1)S(1)}, bf16[112,1280]{1,0:T(8,128)(2,1)}, u32[]{:S(2)}) copy-start(bf16[112,1280]{1,0:T(8,128)(2,1)} %copy-done.26) | copy-start | bytes 860164
  121.9 9.0 %copy-start.29 = (bf16[96,1280]{1,0:T(8,128)(2,1)S(1)}, bf16[96,1280]{1,0:T(8,128)(2,1)}, u32[]{:S(2)}) copy-start(bf16[96,1280]{1,0:T(8,128)(2,1)} %copy-done.28) | copy-start | bytes 737284
  121.9 9.0 %copy-start.31 = (bf16[96,1280]{1,0:T(8,128)(2,1)S(1)}, bf16[96,1280]{1,0:T(8,128)(2,1)}, u32[]{:S(2)}) copy-start(bf16[96,1280]{1,0:T(8,128)(2,1)} %copy-done.30) | copy-start | bytes 737284
  121.9 9.0 %copy-start.33 = (bf16[96,1280]{1,0:T(8,128)(2,1)S(1)}, bf16[96,1280]{1,0:T(8,128)(2,1)}, u32[]{:S(2)}) copy-start(bf16[96,1280]{1,0:T(8,128)(2,1)} %copy-done.32) | copy-start | bytes 737284
  121.9 9.0 %copy-start.35 = (bf16[96,1280]{1,0:T(8,128)(2,1)S(1)}, bf16[96,1280]{1,0:T(8,128)(2,1)}, u32[]{:S(2)}) copy-start(bf16[96,1280]{1,0:T(8,128)(2,1)} %copy-done.34) | copy-start | bytes 737284
  121.9 9.0 %copy-start.37 = (bf16[96,1280]{1,0:T(8,128)(2,1)S(1)}, bf16[96,1280]{1,0:T(8,128)(2,1)}, u32[]{:S(2)}) copy-start(bf16[96,1280]{1,0:T(8,128)(2,1)} %copy-done.36) | copy-start | bytes 737284
  121.9 9.0 %copy-start.39 = (bf16[96,1280]{1,0:T(8,128)(2,1)S(1)}, bf16[96,1280]{1,0:T(8,128)(2,1)}, u32[]{:S(2)}) copy-start(bf16[96,1280]{1,0:T(8,128)(2,1)} %copy-done.38) | copy-start | bytes 737284
  122.0 9.0 %copy-start.41 = (bf16[96,1280]{1,0:T(8,128)(2,1)S(1)}, bf16[96,1280]{1,0:T(8,128)(2,1)}, u32[]{:S(2)}) copy-start(bf16[96,1280]{1,0:T(8,128)(2,1)} %copy-done.40) | copy-start | bytes 737284
  122.0 9.0 %copy-start.43 = (bf16[96,1280]{1,0:T(8,128)(2,1)S(1)}, bf16[96,1280]{1,0:T(8,128)(2,1)}, u32[]{:S(2)}) copy-start(bf16[96,1280]{1,0:T(8,128)(2,1)} %copy-done.42) | copy-start | bytes 737284
  124.2 12.5 %collective-permute-start.19 = (bf16[192,1280]{1,0:T(8,128)(2,1)S(1)}, bf16[192,1280]{1,0:T(8,128)(2,1)S(1)}, u32[]{:S(2)}, u32[]{:S(2)}) collective-permute-start(bf16[192,1280]{1,0:T(8,128)(2,1)S(1)} %get-tuple-element.99), channel_id=1, source_target_pairs={{0,16},{16,0},{32,48},{48,32},{64,80},{80,64},{96,112},{112,96},{1... | collective-permute-start | bytes 1474568 | tf_op jit(solution)/shard_map/ppermute | solution.py:366
  125.4 11.3 %collective-permute-start.21 = (bf16[96,1280]{1,0:T(8,128)(2,1)S(1)}, bf16[96,1280]{1,0:T(8,128)(2,1)S(1)}, u32[]{:S(2)}, u32[]{:S(2)}) collective-permute-start(bf16[96,1280]{1,0:T(8,128)(2,1)S(1)} %add_convert_fusion.4), channel_id=1, source_target_pairs={{0,32},{16,48},{32,64},{48,80},{64,96},{80,112},{96,0},{112,16},{1... | collective-permute-start | bytes 737288 | tf_op jit(solution)/shard_map/ppermute | solution.py:360
  125.6 11.1 %collective-permute-start.23 = (bf16[96,1280]{1,0:T(8,128)(2,1)S(1)}, bf16[96,1280]{1,0:T(8,128)(2,1)S(1)}, u32[]{:S(2)}, u32[]{:S(2)}) collective-permute-start(bf16[96,1280]{1,0:T(8,128)(2,1)S(1)} %slice.27), channel_id=1, source_target_pairs={{0,96},{16,112},{32,0},{48,16},{64,32},{80,48},{96,64},{112,80},{1... | collective-permute-start | bytes 737288 | tf_op jit(solution)/shard_map/ppermute | solution.py:363
  129.0 10.1 %collective-permute-start.25 = (bf16[96,1280]{1,0:T(8,128)(2,1)S(1)}, bf16[96,1280]{1,0:T(8,128)(2,1)S(1)}, u32[]{:S(2)}, u32[]{:S(2)}) collective-permute-start(bf16[96,1280]{1,0:T(8,128)(2,1)S(1)} %add_convert_fusion.3), channel_id=1, source_target_pairs={{0,96},{16,112},{32,0},{48,16},{64,32},{80,48},{96,64},{112,80},{1... | collective-permute-start | bytes 737288 | tf_op jit(solution)/shard_map/ppermute | solution.py:363
  136.7 8.2 %copy-start.11 = (bf16[4,2,32,640]{3,2,1,0:T(8,128)(2,1)S(1)}, bf16[4,2,32,640]{3,2,1,0:T(8,128)(2,1)}, u32[]{:S(2)}) copy-start(bf16[4,2,32,640]{3,2,1,0:T(8,128)(2,1)} %copy-done.9) | copy-start | bytes 983044
  136.7 8.3 %copy-start.46 = (bf16[1,2,32,640]{3,2,1,0:T(8,128)(2,1)S(1)}, bf16[1,2,32,640]{3,2,1,0:T(8,128)(2,1)}, u32[]{:S(2)}) copy-start(bf16[1,2,32,640]{3,2,1,0:T(8,128)(2,1)} %copy-done.44) | copy-start | bytes 245764
  140.4 15.5 %all-to-all-start.3 = ((bf16[16,16,1280]{2,1,0:T(8,128)(2,1)}), bf16[16,16,1280]{2,1,0:T(8,128)(2,1)S(1)}, u32[]{:S(2)}, u32[]{:S(2)}) async-start(bf16[16,16,1280]{2,1,0:T(8,128)(2,1)} %shard_map.101), calls=%async_computation.3 | async-start | bytes 1310720 | tf_op jit(solution)/shard_map/all_to_all | solution.py:372
  146.0 9.9 %copy-start.8 = (bf16[1,2,64,1280]{3,2,1,0:T(8,128)(2,1)S(1)}, bf16[1,2,64,1280]{3,2,1,0:T(8,128)(2,1)}, u32[]{:S(2)}) copy-start(bf16[1,2,64,1280]{3,2,1,0:T(8,128)(2,1)} %param.6) | copy-start | bytes 983044
  146.0 9.9 %copy-start.58 = (f32[1280]{0:T(1024)S(1)}, f32[1280]{0:T(1024)}, u32[]{:S(2)}) copy-start(f32[1280]{0:T(1024)} %gain_ref.3) | copy-start | bytes 15364
  146.0 9.9 %copy-start.64 = (s32[1,2,64]{2,1,0:T(2,128)S(1)}, s32[1,2,64]{2,1,0:T(2,128)}, u32[]{:S(2)}) copy-start(s32[1,2,64]{2,1,0:T(2,128)} %param.7) | copy-start | bytes 1540
  146.0 9.9 %copy-start.66 = (s32[1,2,64]{2,1,0:T(2,128)S(1)}, s32[1,2,64]{2,1,0:T(2,128)}, u32[]{:S(2)}) copy-start(s32[1,2,64]{2,1,0:T(2,128)} %param.8) | copy-start | bytes 1540
  (32 other events, 93.4 us)

commit v4 on v1

v4 whole, which is shorter than its diff:
```python
import functools
import math

import jax
import jax.numpy as jnp
from jax import lax
from jax.experimental import pallas as pl
from jax.experimental.pallas import tpu as pltpu
from jax.sharding import PartitionSpec as P

norm_eps = 1e-06
objective_scale = 32.0
bf16 = jnp.bfloat16
f32 = jnp.float32
i32 = jnp.int32

CAP = 6
HELD = 2
GROUP = HELD * CAP
PEERS = 16
PLANES = 4
HALF = PEERS * CAP
ROWS = 2 * HALF + 16
POOLED = 2 * PEERS
LANES = 128
QUAD = 4 * GROUP
REST = 32
MESSAGE = 2 * QUAD + REST
PAIR_TOKENS = 64


def nn(a, b):
    return lax.dot_general(a, b, (((1,), (0,)), ((), ())), preferred_element_type=f32)


def nt(a, b, precision=None):
    return lax.dot_general(
        a, b, (((1,), (1,)), ((), ())), precision=precision, preferred_element_type=f32
    )


def tn(a, b, precision=None):
    return lax.dot_general(
        a, b, (((0,), (0,)), ((), ())), precision=precision, preferred_element_type=f32
    )


def iota(shape, dim):
    return lax.broadcasted_iota(i32, shape, dim)


def shape_of(*dims, dtype=bf16):
    return jax.ShapeDtypeStruct(dims, dtype)


def call(kernel, out, args, flops=0, nbytes=0, smem=(), scratch=(), vmem=14):
    specs = [
        pl.BlockSpec(memory_space=pltpu.SMEM if k in smem else pltpu.VMEM)
        for k in range(len(args))
    ]
    many = isinstance(out, (list, tuple))
    out_specs = [pl.BlockSpec(memory_space=pltpu.VMEM) for _ in (out if many else [out])]
    return pl.pallas_call(
        kernel,
        out_shape=out,
        in_specs=specs,
        out_specs=out_specs if many else out_specs[0],
        scratch_shapes=list(scratch),
        compiler_params=pltpu.CompilerParams(vmem_limit_bytes=vmem * 1024 * 1024),
        cost_estimate=pl.CostEstimate(flops=flops, bytes_accessed=nbytes, transcendentals=0),
    )(*args)


def normal_parts(x):
    centred = x - jnp.mean(x, axis=-1, keepdims=True)
    spread = jnp.mean(centred * centred, axis=-1, keepdims=True)
    scale = lax.rsqrt(spread + norm_eps)
    return centred * scale, scale


def places(ids_ref, slots_ref):
    pos = ids_ref[...] * CAP + slots_ref[...]
    return jnp.concatenate([pos[:1], pos[1:]], axis=1)


def one_hot(hit):
    return jnp.where(hit, 1.0, 0.0).astype(bf16)


def slot_table(pos, span, at):
    tokens = pos.shape[1]
    row = iota((PEERS * span, tokens), 0)
    inner = row % span - at
    return one_hot(((row // span) * GROUP + inner == pos) & (inner >= 0) & (inner < GROUP))


def dispatch_kernel(me_ref, ids_ref, slots_ref, tok_ref, gain_ref, out_ref):
    pos = places(ids_ref, slots_ref)
    tokens = pos.shape[1]
    normed = normal_parts(tok_ref[...].astype(f32))[0] * gain_ref[...].reshape(1, -1)
    normed = normed.astype(bf16)

    def column(j):
        return normed[:, j * LANES : (j + 1) * LANES]

    quads = None
    for at in range(4):
        both = jnp.concatenate([column(at), column(at + 4)], axis=1)
        part = nn(slot_table(pos, QUAD, at * GROUP), both)
        quads = part if quads is None else quads + part
    row = iota((PEERS * REST, tokens), 0)
    held = row % REST - 2 * GROUP
    goes = one_hot((pos // GROUP == row // REST) & ((pos % GROUP) // CAP == held))
    kind = jnp.where(iota((LANES, tokens), 1) < tokens // 2, 1.0, 2.0)
    lane = iota((LANES, tokens), 0)
    rest = nt(goes, jnp.where(lane == me_ref[0] * CAP + pos % CAP, kind, 0.0).astype(bf16))
    for at in range(2):
        rest = rest + nn(slot_table(pos, REST, at * GROUP), column(8 + at))
    first = quads[:, :LANES].astype(bf16).reshape(PEERS, QUAD, LANES)
    second = quads[:, LANES:].astype(bf16).reshape(PEERS, QUAD, LANES)
    rest = rest.astype(bf16).reshape(PEERS, REST, LANES)
    for plane in range(PLANES):
        to = slice(plane * PEERS, (plane + 1) * PEERS)
        out_ref[to, :QUAD, :] = first
        out_ref[to, QUAD : 2 * QUAD, :] = second
        out_ref[to, 2 * QUAD :, :] = rest


def row_table(span, at, back):
    shape = (PEERS * span, 2 * HALF) if back else (2 * HALF, PEERS * span)
    r = iota(shape, 1 if back else 0)
    inner = r % HALF
    want = (inner // CAP) * span + at + (r // HALF) * CAP + inner % CAP
    return one_hot(iota(shape, 0 if back else 1) == want)


def repack_kernel(in_ref, out_ref):
    quad = [row_table(QUAD, at * GROUP, False) for at in range(4)]
    rest = [row_table(REST, at * GROUP, False) for at in range(2)]
    row = iota((16, PEERS * REST), 0)
    kinds = one_hot(iota((16, PEERS * REST), 1) % REST - 2 * GROUP == row)
    kinds = jnp.where(row < HELD, kinds, jnp.zeros_like(kinds))
    for plane in range(PLANES):
        of = slice(plane * PEERS, (plane + 1) * PEERS)
        first = in_ref[of, :QUAD, :].reshape(PEERS * QUAD, LANES)
        second = in_ref[of, QUAD : 2 * QUAD, :].reshape(PEERS * QUAD, LANES)
        both = jnp.concatenate([first, second], axis=1)
        for at in range(4):
            got = nn(quad[at], both).astype(bf16)
            out_ref[plane, : 2 * HALF, at * LANES : (at + 1) * LANES] = got[:, :LANES]
            out_ref[plane, : 2 * HALF, (at + 4) * LANES : (at + 5) * LANES] = got[:, LANES:]
        last = in_ref[of, 2 * QUAD :, :].reshape(PEERS * REST, LANES)
        for at in range(2):
            got = nn(rest[at], last).astype(bf16)
            out_ref[plane, : 2 * HALF, (at + 8) * LANES : (at + 9) * LANES] = got
        out_ref[plane, 2 * HALF :, :LANES] = nn(kinds, last).astype(bf16)
        width = out_ref.shape[2]
        out_ref[plane, 2 * HALF :, LANES:] = jnp.zeros((16, width - LANES), bf16)


def forward_kernel(x_ref, w_in, pooled_ref, slope_ref, pool_ref):
    c0 = math.sqrt(2.0 / math.pi)
    c1 = c0 * 0.044715
    hidden = w_in.shape[2]
    for plane in range(PLANES):
        kinds = x_ref[plane, 2 * HALF :, :LANES].astype(f32)
        for held in range(HELD):
            rows = x_ref[plane, held * HALF : (held + 1) * HALF, :]
            q = iota((POOLED, HALF), 0)
            r = iota((POOLED, HALF), 1)
            kind = kinds[held : held + 1, :HALF]
            pool = one_hot((q % PEERS == r // CAP) & (kind == (q // PEERS + 1).astype(f32)))
            pool_ref[plane, held] = pool
            for at in range(0, hidden, 256):
                to = slice(at, min(at + 256, hidden))
                h = nn(rows, w_in[held, :, to])
                h2 = h * h
                t = jnp.tanh(h * (c0 + c1 * h2))
                half = 0.5 + 0.5 * t
                act = h * half
                slope = half + act * (1.0 - t) * (c0 + 3.0 * c1 * h2)
                pooled_ref[plane, held, :, to] = nn(pool, act.astype(bf16)).astype(bf16)
                slope_ref[plane, held, :, to] = slope.astype(bf16)


def forward(x, w_in):
    width, hidden = w_in.shape[1:]
    return call(
        forward_kernel,
        [
            shape_of(PLANES, HELD, POOLED, hidden),
            shape_of(PLANES, HELD, HALF, hidden),
            shape_of(PLANES, HELD, POOLED, HALF),
        ],
        [x, w_in],
        flops=PLANES * 2 * 2 * HALF * width * hidden,
        nbytes=w_in.size * 2 + PLANES * 2 * HALF * (width + hidden) * 2,
    )


def out_kernel(pooled_ref, w_out, out_ref):
    total = None
    for held in range(HELD):
        rows = jnp.concatenate([pooled_ref[k, held] for k in range(PLANES)], axis=0)
        part = nn(rows, w_out[held])
        total = part if total is None else total + part
    out_ref[...] = total.astype(bf16).reshape(out_ref.shape)


def loss_kernel(own_ref, other_ref, w_out, grad_ref, rows_ref, prod_ref):
    highest = lax.Precision.HIGHEST
    image = jnp.concatenate([own_ref[0], other_ref[0]], axis=0)
    text = jnp.concatenate([own_ref[1], other_ref[1]], axis=0)
    pairs, width = image.shape
    scale = PAIR_TOKENS / math.sqrt(width)
    logits = scale * nt(image, text, highest)

    def softmax(axis):
        top = jnp.exp(logits - jnp.max(logits, axis=axis, keepdims=True))
        return top / jnp.sum(top, axis=axis, keepdims=True)

    same = jnp.where(iota((pairs, pairs), 0) == iota((pairs, pairs), 1), 2.0, 0.0)
    grad_logits = objective_scale * (softmax(1) + softmax(0) - same)
    grad_image = (scale / PAIR_TOKENS) * lax.dot_general(
        grad_logits,
        text,
        (((1,), (0,)), ((), ())),
        precision=highest,
        preferred_element_type=f32,
    )
    grad_text = (scale / PAIR_TOKENS) * tn(grad_logits, image, highest)
    grad_ref[0] = grad_image
    grad_ref[1] = grad_text
    for core in range(2):
        for plane in range(PLANES):
            first = (core * PLANES + plane) * PEERS
            span = slice(first, first + PEERS)
            rows_ref[core, plane, :PEERS, :] = grad_image[span].astype(bf16)
            rows_ref[core, plane, PEERS:, :] = grad_text[span].astype(bf16)
    for core in range(2):
        rows = rows_ref[core].reshape(PLANES * POOLED, width)
        for held in range(HELD):
            prod_ref[core, held] = nt(rows, w_out[held]).astype(bf16)


def backward_kernel(core, pool_ref, slope_ref, prod_ref, w_in, pre_ref, out_ref):
    for held in range(HELD):
        for plane in range(PLANES):
            prod = prod_ref[core, held, plane * POOLED : (plane + 1) * POOLED, :]
            grad_act = tn(pool_ref[plane, held], prod)
            pre = (grad_act * slope_ref[plane, held].astype(f32)).astype(bf16)
            pre_ref[plane, held] = pre
        pre = pre_ref[:, held].reshape(PLANES * HALF, -1)
        part = nt(pre, w_in[held]).astype(bf16)
        for plane in range(PLANES):
            span = slice(plane * HALF, (plane + 1) * HALF)
            out_ref[plane, held * HALF : (held + 1) * HALF, :] = part[span]


def backward(core, made, prod, w_in):
    width, hidden = w_in.shape[1:]
    return call(
        functools.partial(backward_kernel, core),
        [shape_of(PLANES, HELD, HALF, hidden), shape_of(PLANES, 2 * HALF, width)],
        [made[2], made[1], prod, w_in],
        flops=PLANES * 2 * 2 * HALF * width * hidden,
        nbytes=w_in.size * 2 + PLANES * 2 * HALF * (width + hidden) * 2,
    )


def unpack_kernel(own_ref, got_ref, out_ref):
    quad = [row_table(QUAD, at * GROUP, True) for at in range(4)]
    rest = [row_table(REST, at * GROUP, True) for at in range(2)]
    for plane in range(PLANES):
        of = slice(plane * PEERS, (plane + 1) * PEERS)
        rows = (own_ref[plane].astype(f32) + got_ref[plane].astype(f32)).astype(bf16)

        def column(j):
            return rows[:, j * LANES : (j + 1) * LANES]

        total = None
        for at in range(4):
            both = jnp.concatenate([column(at), column(at + 4)], axis=1)
            part = nn(quad[at], both)
            total = part if total is None else total + part
        total = total.astype(bf16)
        out_ref[of, :QUAD, :] = total[:, :LANES].reshape(PEERS, QUAD, LANES)
        out_ref[of, QUAD : 2 * QUAD, :] = total[:, LANES:].reshape(PEERS, QUAD, LANES)
        last = nn(rest[0], column(8)) + nn(rest[1], column(9))
        out_ref[of, 2 * QUAD :, :] = last.astype(bf16).reshape(PEERS, REST, LANES)


def grad_in_kernel(own_ref, other_ref, own_pre, other_pre, out_ref, x_ref, p_ref):
    held = pl.program_id(0)

    def fill(which):
        for core, (x, pre) in enumerate(((own_ref, own_pre), (other_ref, other_pre))):
            for plane in range(PLANES):
                first = (core * PLANES + plane) * HALF
                x_ref[first : first + HALF, :] = x[plane, which * HALF : (which + 1) * HALF, :]
                p_ref[first : first + HALF, :] = pre[plane, which]

    for which in range(HELD):
        pl.when(held == which)(functools.partial(fill, which))
    out_ref[0] = tn(x_ref[...], p_ref[...])


def grad_in(own, other, own_pre, other_pre, width, hidden):
    whole = pl.BlockSpec(memory_space=pltpu.VMEM)
    return pl.pallas_call(
        grad_in_kernel,
        grid=(HELD,),
        out_shape=shape_of(HELD, width, hidden, dtype=f32),
        in_specs=[whole] * 4,
        out_specs=pl.BlockSpec((1, width, hidden), lambda i: (i, 0, 0)),
        scratch_shapes=[
            pltpu.VMEM((8 * HALF, width), bf16),
            pltpu.VMEM((8 * HALF, hidden), bf16),
        ],
        compiler_params=pltpu.CompilerParams(vmem_limit_bytes=26 * 1024 * 1024),
        cost_estimate=pl.CostEstimate(
            flops=2 * 2 * 8 * HALF * width * hidden, bytes_accessed=17_000_000, transcendentals=0
        ),
    )(own, other, own_pre, other_pre)


def grad_out_kernel(own_ref, other_ref, rows_ref, out_ref):
    held = pl.program_id(0)
    width = rows_ref.shape[3]
    pooled = [ref[k, held] for ref in (own_ref, other_ref) for k in range(PLANES)]
    rows = rows_ref[...].reshape(8 * POOLED, width)
    out_ref[0] = tn(jnp.concatenate(pooled, axis=0), rows)


def grad_out(own, other, rows, width, hidden):
    whole = pl.BlockSpec(memory_space=pltpu.VMEM)
    return pl.pallas_call(
        grad_out_kernel,
        grid=(HELD,),
        out_shape=shape_of(HELD, hidden, width, dtype=f32),
        in_specs=[whole] * 3,
        out_specs=pl.BlockSpec((1, hidden, width), lambda i: (i, 0, 0)),
        compiler_params=pltpu.CompilerParams(vmem_limit_bytes=18 * 1024 * 1024),
        cost_estimate=pl.CostEstimate(
            flops=2 * 2 * 8 * POOLED * width * hidden, bytes_accessed=9_000_000, transcendentals=0
        ),
    )(own, other, rows)


def tail_kernel(ids_ref, slots_ref, tok_ref, gain_ref, grad_ref, back_ref, out_ref, sum_ref):
    tokens = tok_ref.shape[0]
    pos = places(ids_ref, slots_ref)
    for peer in range(0, PEERS, 4):
        total = None
        for plane in range(PLANES):
            first = plane * PEERS + peer
            part = back_ref[first : first + 4].astype(f32)
            total = part if total is None else total + part
        sum_ref[peer : peer + 4] = total.astype(bf16)
    first = sum_ref[:, :QUAD, :].reshape(PEERS * QUAD, LANES)
    second = sum_ref[:, QUAD : 2 * QUAD, :].reshape(PEERS * QUAD, LANES)
    both = jnp.concatenate([first, second], axis=1)
    quads = [tn(slot_table(pos, QUAD, at * GROUP), both) for at in range(4)]
    last = sum_ref[:, 2 * QUAD :, :].reshape(PEERS * REST, LANES)
    ends = [tn(slot_table(pos, REST, at * GROUP), last) for at in range(2)]
    grad = jnp.concatenate(
        [g[:, :LANES] for g in quads] + [g[:, LANES:] for g in quads] + ends, axis=1
    )
    unit, scale = normal_parts(tok_ref[...].astype(f32))
    grad = grad * gain_ref[...].reshape(1, -1)
    grad = scale * (
        grad
        - jnp.mean(grad, axis=-1, keepdims=True)
        - unit * jnp.mean(grad * unit, axis=-1, keepdims=True)
    )
    for half in range(2):
        span = slice(half * (tokens // 2), (half + 1) * (tokens // 2))
        out_ref[span, :] = (grad_ref[half : half + 1, :] + grad[span]).astype(bf16)


def body(tokens, expert_ids, slots, ln_gain, w_in, w_out):
    width, hidden = w_in.shape[1:]
    row_count = tokens.shape[1] * tokens.shape[2]
    flat = tokens.reshape(row_count, width)
    ids, slot = expert_ids[0], slots[0]
    data = lax.axis_index("dp")
    group = lax.axis_index("expert")
    everyone = ("dp", "expert")
    chips = PLANES * PEERS
    cores = [[d * PEERS + e for d in range(c, 8, 2) for e in range(PEERS)] for c in range(2)]

    def swap(x):
        return lax.ppermute(x, "dp", [(i, i ^ 1) for i in range(8)])

    def after(x, *tokens):
        return lax.optimization_barrier((x, *tokens))[0]

    def spread(x):
        return lax.all_to_all(
            x, everyone, split_axis=0, concat_axis=0, tiled=True, axis_index_groups=cores
        )

    sent = call(
        dispatch_kernel,
        shape_of(chips, MESSAGE, LANES),
        [group.reshape(1), ids, slot, flat, ln_gain],
        smem=(0,),
    )
    x_own = call(repack_kernel, shape_of(PLANES, ROWS, width), [spread(sent)])
    x_other = swap(x_own)
    made_own = forward(x_own, w_in)

    def product(made, w_out):
        return call(
            out_kernel,
            shape_of(PLANES, POOLED, width),
            [made[0], w_out],
            flops=2 * 4 * POOLED * width * hidden * HELD,
            nbytes=w_out.size * 2,
        )

    own = product(made_own, w_out)
    made_other = forward(after(x_other, own), w_in)
    got = swap(product(made_other, w_out))
    joined = (own.astype(f32) + got.astype(f32)).astype(bf16)
    joined = joined.reshape(PLANES, 2, PEERS, width).transpose(0, 2, 1, 3)
    parts = spread(joined.reshape(chips, 2, width))
    emb = jnp.sum(parts.astype(f32), axis=0) + jnp.sum(
        flat.reshape(2, PAIR_TOKENS, width).astype(f32), axis=1
    )
    emb = spread(jnp.broadcast_to((emb / PAIR_TOKENS)[None], (chips, 2, width)))
    emb = emb.transpose(1, 0, 2)
    grad_pooled, rows, prod = call(
        loss_kernel,
        [
            shape_of(2, 2 * chips, width, dtype=f32),
            shape_of(2, PLANES, POOLED, width),
            shape_of(2, HELD, PLANES * POOLED, hidden),
        ],
        [emb, swap(emb), w_out],
        flops=2 * 8 * POOLED * width * hidden * HELD,
        nbytes=w_out.size * 2,
    )
    grad_own = lax.dynamic_index_in_dim(
        grad_pooled, (data // 2) * PEERS + group, axis=1, keepdims=False
    )
    pre_other, p_other = backward(1, made_other, prod, w_in)
    p_got = swap(p_other)
    pre_own, p_own = backward(0, made_own, after(prod, p_other), w_in)
    packed = call(unpack_kernel, shape_of(chips, MESSAGE, LANES), [p_own, p_got])
    back = spread(packed)
    grad_w_in = grad_in(x_own, x_other, after(pre_own, packed), pre_other, width, hidden)
    grad_w_out = grad_out(
        made_own[0], made_other[0], after(rows, packed), width, hidden
    )
    grad_flat = call(
        tail_kernel,
        shape_of(row_count, width),
        [ids, slot, flat, ln_gain, grad_own, after(back, grad_w_in, grad_w_out)],
        scratch=[pltpu.VMEM((PEERS, MESSAGE, LANES), bf16)],
    )
    return (grad_flat.reshape(tokens.shape), grad_w_in, grad_w_out)


def solution(mesh):
    placed = (
        P(("dp", "expert"), None, None, None),
        P(("dp", "expert"), None, None),
        P(("dp", "expert"), None, None),
        P(),
        P("expert", None, "dp"),
        P("expert", "dp", None),
    )
    return jax.shard_map(
        body,
        mesh=mesh,
        in_specs=placed,
        out_specs=(
            P(("dp", "expert"), None, None, None),
            P("expert", None, "dp"),
            P("expert", "dp", None),
        ),
        check_vma=False,
    )
```

time: 246 us -> 159 us (0.65)
  blocking collectives: 114 us -> 59.8 us
  Pallas kernels: 0 us -> 39.9 us
  matrix products: 39 us -> 0 us
  local copies, waits for them, and re-layouts: 31.2 us -> 9.19 us
  between operations: 14.3 us -> 1 us
  other arithmetic: 10.5 us -> 2.55 us
  starting transfers between devices: 7.08 us -> 12.5 us
  waiting for transfers between devices: 28.4 us -> 33.2 us
    all_gather x1 -> x0, blocking collectives: 48.1 us -> none  [body(): all_pos = lax.all_gather(position[None], everyone, axis=0, tiled=True)]
    pallas_call x0 -> x13, Pallas kernels: none -> 39.9 us  [the longest x11 30.3 us: call(): pl.pallas_call(kernel, out_shape=out, in_specs=specs, out_specs=out_specs...]
    dot_general x13 -> x0, matrix products: 39 us -> none  [the longest x10 36.7 us: mm(): return jnp.einsum(spec, a, b, preferred_element_type=f32).astype(out)]
    all_to_all x1 -> x2, waiting for transfers between devices: 4.84 us -> 29.3 us  [spread(): lax.all_to_all(x, everyone, split_axis=0, concat_axis=0, tiled=True, axis...]
    reduce_scatter x1 -> x0, waiting for transfers between devices: 23.5 us -> none  [body(): lax.psum_scatter(grad_partial.reshape(datas * total * cap, width), 'dp',...]
    reshape x8 -> x2, local copies, waits for them, and re-layouts: 12.9 us -> 1.09 us  [the longest x1 1.06 us: body(): parts = spread(joined.reshape(chips, 2, width))]
    convert_element_type x4 -> x0, local copies, waits for them, and re-layouts: 9.9 us -> none  [the longest x2 4.22 us: body(): grad_rows = grad_pooled.astype(bf16).reshape(datas, groups * 2, width)]
    all_to_all x3 -> x2, blocking collectives: 65.9 us -> 59.8 us  [spread(): lax.all_to_all(x, everyone, split_axis=0, concat_axis=0, tiled=True, axis...]
  transfers between devices with their start and end apart: 3 -> 6, of which waited for: 2 -> 5; matrix products, arithmetic and copies ran while one was open for 9% -> 1% of each run, Pallas kernels for 0% -> 11%
where the time goes in v4:
time: 159 us; the launch traced here: 158 us
  blocking collectives  59.8 us (38%)
  Pallas kernels  39.9 us (25%)
  waiting for transfers between devices  33.2 us (21%)
  starting transfers between devices  12.5 us (8%)
  local copies, waits for them, and re-layouts  9.19 us (6%)
  other arithmetic  2.55 us (2%)
    all_to_all x2, blocking collectives, spread(): lax.all_to_all(x, everyone, split_axis=0, concat_axis=0, tiled=True, axis...  59.8 us
    pallas_call x11, Pallas kernels, call(): pl.pallas_call(kernel, out_shape=out, in_specs=specs, out_specs=out_specs...  30.3 us
    all_to_all x2, waiting for transfers between devices, spread(): lax.all_to_all(x, everyone, split_axis=0, concat_axis=0, tiled=True, axis...  29.3 us
    all_to_all x2, starting transfers between devices, spread(): lax.all_to_all(x, everyone, split_axis=0, concat_axis=0, tiled=True, axis...  11.2 us
    unnamed x61, local copies, waits for them, and re-layouts  6.99 us
    pallas_call x1, Pallas kernels, grad_in(): pl.pallas_call(grad_in_kernel, grid=(HELD,), out_shape=shape_of(HELD, wid...  5.64 us
    pallas_call x1, Pallas kernels, grad_out(): pl.pallas_call(grad_out_kernel, grid=(HELD,), out_shape=shape_of(HELD, hi...  4 us
    ppermute x4, waiting for transfers between devices, swap(): return lax.ppermute(x, 'dp', [(i, i ^ 1) for i in range(8)])  3.85 us
  transfers between devices with their start and end apart: 6, of which 5 were waited for; matrix products, arithmetic and copies ran while one was open for 1% of the time, Pallas kernels for 11%

profile of v4, /device:TPU:0, one launch (start us, length us, event | category | flops | bytes accessed | tf_op | source)
XLA Modules:
  0.0 158.2 jit_solution(7428751021322748584)
XLA Ops:
  0.6 0.0 copy-start.7
  0.6 1.0 copy-done.7
  1.6 0.7 copy-done.23
  2.3 0.7 copy-done.25
  3.0 0.7 copy-done.27
  3.7 1.1 shard_map.85
  4.8 41.3 %all_to_all.20.in_ref = bf16[64,128,128]{2,1,0:T(8,128)(2,1)S(1)} all-to-all(bf16[64,128,128]{2,1,0:T(8,128)(2,1)S(1)} %shard_map.85), channel_id=1, replica_groups={{0,1,2,3,4,5,6,7,8,9,10,11,12,13,14,15,32,33,34,35,36,37,38,39,40,41,42..., dimensions={0} | all-to-all | bytes 4194304 | tf_op jit(solution)/shard_map/all_to_all | solution.py:399
  46.0 2.1 %shard_map.86.x_ref.own_ref = bf16[4,208,1280]{2,1,0:T(8,128)(2,1)S(1)} custom-call(bf16[64,128,128]{2,1,0:T(8,128)(2,1)S(1)} %all_to_all.20.in_ref), custom_call_target="tpu_custom_call" | custom-call | tf_op jit(solution)/shard_map/pallas_call | solution.py:63
  48.1 0.0 copy-start.3
  48.2 0.0 copy-start.1
  48.2 0.3 collective-permute-start
  48.4 0.0 copy-done
  48.4 5.1 %shard_map.87 = (bf16[4,2,32,640]{3,2,1,0:T(8,128)(2,1)S(1)}, bf16[4,2,96,640]{3,2,1,0:T(8,128)(2,1)S(1)}, bf16[4,2,32,96]{3,2,1,0:T(8,128)(2,1)S(1)}) custom-call(bf16[4,208,1280]{2,1,0:T(8,128)(2,1)S(1)} %shard_map.86.x_ref.own_ref, bf16[2,1280,640]{2,1,0:T(8,128)(2,1)S(1)} %copy-done), custom_call_target="tpu_custom_call" | custom-call | flops 1258291200 | bytes 6225920 | tf_op jit(solution)/shard_map/pallas_call | solution.py:63
  53.6 0.0 copy-done.3
  53.6 1.0 copy-done.13
  54.6 0.0 copy-done.1
  54.6 0.7 shard_map.88
  55.2 0.0 collective-permute-done.x_ref.other_ref
  55.2 0.0 copy-start.5
  55.3 5.1 %shard_map.89 = (bf16[4,2,32,640]{3,2,1,0:T(8,128)(2,1)S(1)}, bf16[4,2,96,640]{3,2,1,0:T(8,128)(2,1)S(1)}, bf16[4,2,32,96]{3,2,1,0:T(8,128)(2,1)S(1)}) custom-call(bf16[4,208,1280]{2,1,0:T(8,128)(2,1)S(1)} %collective-permute-done.x_ref.other_ref, bf16[2,1280,640]{2,1,0:T(8,128)(2,1)S(1)} %copy-done), custom_call_target="tpu_custom_call" | custom-call | flops 1258291200 | bytes 6225920 | tf_op jit(solution)/shard_map/pallas_call | solution.py:63
  60.4 0.0 copy-done.9
  60.4 0.0 copy-done.5
  60.4 0.0 copy-start.15
  60.4 0.7 shard_map.90
  61.1 0.6 collective-permute-start.1
  61.6 1.3 collective-permute-done.1
  62.9 0.1 add_convert_fusion
  63.0 0.0 copy-done.11
  63.0 0.0 copy-done.15
  63.0 1.1 copy.11
  64.1 6.1 %all-to-all-start.1 = ((bf16[64,2,1280]{2,1,0:T(2,128)(2,1)}), bf16[64,2,1280]{2,1,0:T(2,128)(2,1)}, u32[]{:S(2)}, u32[]{:S(2)}) async-start(bf16[64,2,1280]{2,1,0:T(2,128)(2,1)} %copy.11), calls=%async_computation.1 | async-start | bytes 655360 | tf_op jit(solution)/shard_map/all_to_all | solution.py:399
  70.2 1.0 convert_reduce_fusion
  71.3 10.6 %all-to-all-done.1 = bf16[64,2,1280]{2,1,0:T(2,128)(2,1)} async-done(((bf16[64,2,1280]{2,1,0:T(2,128)(2,1)}), bf16[64,2,1280]{2,1,0:T(2,128)(2,1)}, u32[]{:S(2)}, u32[]{:S(2)}) %all-to-all-start.1) | async-done | bytes 327712 | tf_op jit(solution)/shard_map/all_to_all | solution.py:399
  81.9 1.4 convert_reduce_fusion.1
  83.3 0.2 broadcast_in_dim.2
  83.5 18.6 %all_to_all.21 = f32[64,2,1280]{2,1,0:T(2,128)S(1)} all-to-all(f32[64,2,1280]{2,1,0:T(2,128)S(1)} %broadcast_in_dim.2), channel_id=1, replica_groups={{0,1,2,3,4,5,6,7,8,9,10,11,12,13,14,15,32,33,34,35,36,37,38,39,40,41,42..., dimensions={0} | all-to-all | bytes 1310720 | tf_op jit(solution)/shard_map/all_to_all | solution.py:399
  102.1 0.0 copy-start.16
  102.1 0.3 collective-permute-start.2
  102.4 2.1 %collective-permute-done.2.other_ref = f32[2,64,1280]{2,1,0:T(8,128)S(1)} collective-permute-done((f32[2,64,1280]{2,1,0:T(8,128)S(1)}, f32[2,64,1280]{2,1,0:T(8,128)S(1)}, u32[]{:S(2)}, u32[]{:S(2)}) %collective-permute-start.2) | collective-permute-done | bytes 655392 | tf_op jit(solution)/shard_map/ppermute | solution.py:393
  104.5 0.0 copy-done.2
  104.5 4.8 %shard_map.91 = (f32[2,128,1280]{2,1,0:T(8,128)S(1)}, bf16[2,4,32,1280]{3,2,1,0:T(8,128)(2,1)S(1)}, bf16[2,2,128,640]{3,2,1,0:T(8,128)(2,1)S(1)}) custom-call(f32[2,64,1280]{2,1,0:T(8,128)S(1)} %bitcast.18, f32[2,64,1280]{2,1,0:T(8,128)S(1)} %collective-permute-done.2.other_ref, bf16[2,640,1280]{2,1,0:T(8,128)(2,1)S(1)} %copy-done.2), custom_call_target="tpu_custom_call" | custom-call | flops 838860800 | bytes 3276800 | tf_op jit(solution)/shard_map/pallas_call | solution.py:63
  109.3 0.0 copy-start.21
  109.3 0.8 copy-done.21
  110.1 0.0 copy-done.16
  110.1 2.3 %shard_map.92 = (bf16[4,2,96,640]{3,2,1,0:T(8,128)(2,1)S(1)}, bf16[4,192,1280]{2,1,0:T(8,128)(2,1)S(1)}) custom-call(bf16[4,2,32,96]{3,2,1,0:T(8,128)(2,1)S(1)} %get-tuple-element.28.pool_ref, bf16[4,2,96,640]{3,2,1,0:T(8,128)(2,1)S(1)} %copy-done.16, bf16[2,2,128,640]{3,2,1,0:T(8,128)(2,1)S(1)} %get-tuple-element.31.prod_ref, bf16[2,1280,640]{2,1,0:T(8,128)(2,1)S(1)} %copy-done), custom_call_target="tpu_custom_call" | custom-call | flops 1258291200 | bytes 6225920 | tf_op jit(solution)/shard_map/pallas_call | solution.py:63
  112.5 0.0 copy-done.29
  112.5 0.0 copy-start.17
  112.5 0.2 collective-permute-start.3
  112.7 0.0 copy-done.14
  112.7 2.3 %shard_map.93 = (bf16[4,2,96,640]{3,2,1,0:T(8,128)(2,1)S(1)}, bf16[4,192,1280]{2,1,0:T(8,128)(2,1)S(1)}) custom-call(bf16[4,2,32,96]{3,2,1,0:T(8,128)(2,1)S(1)} %get-tuple-element.25.pool_ref, bf16[4,2,96,640]{3,2,1,0:T(8,128)(2,1)S(1)} %copy-done.14, bf16[2,2,128,640]{3,2,1,0:T(8,128)(2,1)S(1)} %get-tuple-element.31.prod_ref, bf16[2,1280,640]{2,1,0:T(8,128)(2,1)S(1)} %copy-done), custom_call_target="tpu_custom_call" | custom-call | flops 1258291200 | bytes 6225920 | tf_op jit(solution)/shard_map/pallas_call | solution.py:63
  115.1 0.0 copy-done.17
  115.1 1.0 copy-done.19
  116.0 0.5 collective-permute-done.3.got_ref
  116.5 3.7 %shard_map.94 = bf16[64,128,128]{2,1,0:T(8,128)(2,1)} custom-call(bf16[4,192,1280]{2,1,0:T(8,128)(2,1)S(1)} %get-tuple-element.32.own_ref, bf16[4,192,1280]{2,1,0:T(8,128)(2,1)S(1)} %collective-permute-done.3.got_ref), custom_call_target="tpu_custom_call" | custom-call | tf_op jit(solution)/shard_map/pallas_call | solution.py:63
  120.3 5.1 %all-to-all-start.3 = ((bf16[64,128,128]{2,1,0:T(8,128)(2,1)}), bf16[64,128,128]{2,1,0:T(8,128)(2,1)S(1)}, u32[]{:S(2)}, u32[]{:S(2)}) async-start(bf16[64,128,128]{2,1,0:T(8,128)(2,1)} %shard_map.94), calls=%async_computation.3 | async-start | bytes 4194304 | tf_op jit(solution)/shard_map/all_to_all | solution.py:399
  125.4 0.9 constant_dynamic-slice_fusion
  126.3 0.0 copy-start.4
  126.4 4.0 %shard_map.96 = f32[2,640,1280]{2,1,0:T(8,128)} custom-call(bf16[4,2,32,640]{3,2,1,0:T(8,128)(2,1)S(1)} %copy-done.10, bf16[4,2,32,640]{3,2,1,0:T(8,128)(2,1)S(1)} %copy-done.12, bf16[2,4,32,1280]{3,2,1,0:T(8,128)(2,1)S(1)} %copy-done.22), custom_call_target="tpu_custom_call" | custom-call | flops 838860800 | bytes 9000000 | tf_op jit(solution)/shard_map/pallas_call | solution.py:337
  130.4 0.6 copy-done.18
  131.0 0.5 copy-done.20
  131.5 5.6 %shard_map.95 = f32[2,1280,640]{2,1,0:T(8,128)} custom-call(bf16[4,208,1280]{2,1,0:T(8,128)(2,1)S(1)} %copy-done.4, bf16[4,208,1280]{2,1,0:T(8,128)(2,1)S(1)} %copy-done.6, bf16[4,2,96,640]{3,2,1,0:T(8,128)(2,1)S(1)} %copy-done.20, bf16[4,2,96,640]{3,2,1,0:T(8,128)(2,1)S(1)} %copy-done.18), custom_call_target="tpu_custom_call" | custom-call | flops 2516582400 | bytes 17000000 | tf_op jit(solution)/shard_map/pallas_call | solution.py:310
  137.1 18.7 %all-to-all-done.3.back_ref = bf16[64,128,128]{2,1,0:T(8,128)(2,1)S(1)} async-done(((bf16[64,128,128]{2,1,0:T(8,128)(2,1)}), bf16[64,128,128]{2,1,0:T(8,128)(2,1)S(1)}, u32[]{:S(2)}, u32[]{:S(2)}) %all-to-all-start.3) | async-done | bytes 2097184 | tf_op jit(solution)/shard_map/all_to_all | solution.py:399
  155.8 0.0 copy-done.26
  155.8 2.3 %shard_map.97 = bf16[128,1280]{1,0:T(8,128)(2,1)} custom-call(s32[2,64]{1,0:T(2,128)S(1)} %bitcast.21, s32[2,64]{1,0:T(2,128)S(1)} %bitcast.23, bf16[128,1280]{1,0:T(8,128)(2,1)S(1)} %bitcast.16, f32[1280]{0:T(1024)S(1)} %copy-done.24, f32[2,1280]{1,0:T(2,128)S(1)} %bitcast.19, bf16[64,128,128]{2,1,0:T(8,128)(2,1)S(1)} %all-to-all-done.3.back_ref), custom_call_target="tpu_custom_call" | custom-call | tf_op jit(solution)/shard_map/pallas_call | solution.py:63
  (33 shorter events, 0.1 us)
Async XLA Ops:
  0.6 1.0 copy-start.7
  1.6 0.7 copy-start.23
  2.3 0.7 copy-start.25
  3.0 0.7 copy-start.27
  46.0 2.4 %copy-start = (bf16[2,1280,640]{2,1,0:T(8,128)(2,1)S(1)}, bf16[2,1280,640]{2,1,0:T(8,128)(2,1)}, u32[]{:S(2)}) copy-start(bf16[2,1280,640]{2,1,0:T(8,128)(2,1)} %w_in.7) | copy-start | bytes 9830404
  48.1 5.4 %copy-start.3 = (bf16[4,208,1280]{2,1,0:T(8,128)(2,1)}, bf16[4,208,1280]{2,1,0:T(8,128)(2,1)S(1)}, u32[]{:S(2)}) copy-start(bf16[4,208,1280]{2,1,0:T(8,128)(2,1)S(1)} %shard_map.86.x_ref.own_ref) | copy-start | bytes 6389764
  48.2 6.4 %copy-start.1 = (bf16[2,640,1280]{2,1,0:T(8,128)(2,1)S(1)}, bf16[2,640,1280]{2,1,0:T(8,128)(2,1)}, u32[]{:S(2)}) copy-start(bf16[2,640,1280]{2,1,0:T(8,128)(2,1)} %w_out.5) | copy-start | bytes 9830404
  48.2 7.1 %collective-permute-start = (bf16[4,208,1280]{2,1,0:T(8,128)(2,1)S(1)}, bf16[4,208,1280]{2,1,0:T(8,128)(2,1)S(1)}, u32[]{:S(2)}, u32[]{:S(2)}) collective-permute-start(bf16[4,208,1280]{2,1,0:T(8,128)(2,1)S(1)} %shard_map.86.x_ref.own_ref), channel_id=1, source_target_pairs={{0,16},{16,0},{32,48},{48,32},{64,80},{80,64},{96,112},{112,96},{1... | collective-permute-start | bytes 6389768 | tf_op jit(solution)/shard_map/ppermute | solution.py:393
  53.6 1.0 copy-start.13
  54.6 5.8 %copy-start.9 = (bf16[4,2,32,640]{3,2,1,0:T(8,128)(2,1)}, bf16[4,2,32,640]{3,2,1,0:T(8,128)(2,1)S(1)}, u32[]{:S(2)}) copy-start(bf16[4,2,32,640]{3,2,1,0:T(8,128)(2,1)S(1)} %get-tuple-element.21.pooled_ref.own_ref) | copy-start | bytes 983044
  55.2 5.1 %copy-start.5 = (bf16[4,208,1280]{2,1,0:T(8,128)(2,1)}, bf16[4,208,1280]{2,1,0:T(8,128)(2,1)S(1)}, u32[]{:S(2)}) copy-start(bf16[4,208,1280]{2,1,0:T(8,128)(2,1)S(1)} %collective-permute-done.x_ref.other_ref) | copy-start | bytes 6389764
  60.4 2.6 %copy-start.11 = (bf16[4,2,32,640]{3,2,1,0:T(8,128)(2,1)}, bf16[4,2,32,640]{3,2,1,0:T(8,128)(2,1)S(1)}, u32[]{:S(2)}) copy-start(bf16[4,2,32,640]{3,2,1,0:T(8,128)(2,1)S(1)} %get-tuple-element.23.pooled_ref.other_ref) | copy-start | bytes 983044
  60.4 2.6 %copy-start.15 = (bf16[4,2,96,640]{3,2,1,0:T(8,128)(2,1)}, bf16[4,2,96,640]{3,2,1,0:T(8,128)(2,1)S(1)}, u32[]{:S(2)}) copy-start(bf16[4,2,96,640]{3,2,1,0:T(8,128)(2,1)S(1)} %get-tuple-element.29.slope_ref) | copy-start | bytes 2949124
  61.1 1.8 %collective-permute-start.1 = (bf16[4,32,1280]{2,1,0:T(8,128)(2,1)S(1)}, bf16[4,32,1280]{2,1,0:T(8,128)(2,1)S(1)}, u32[]{:S(2)}, u32[]{:S(2)}) collective-permute-start(bf16[4,32,1280]{2,1,0:T(8,128)(2,1)S(1)} %shard_map.90), channel_id=1, source_target_pairs={{0,16},{16,0},{32,48},{48,32},{64,80},{80,64},{96,112},{112,96},{1... | collective-permute-start | bytes 983048 | tf_op jit(solution)/shard_map/ppermute | solution.py:393
  64.1 17.8 %all-to-all-start.1 = ((bf16[64,2,1280]{2,1,0:T(2,128)(2,1)}), bf16[64,2,1280]{2,1,0:T(2,128)(2,1)}, u32[]{:S(2)}, u32[]{:S(2)}) async-start(bf16[64,2,1280]{2,1,0:T(2,128)(2,1)} %copy.11), calls=%async_computation.1 | async-start | bytes 655360 | tf_op jit(solution)/shard_map/all_to_all | solution.py:399
  81.9 22.6 %copy-start.2 = (bf16[2,640,1280]{2,1,0:T(8,128)(2,1)S(1)}, bf16[2,640,1280]{2,1,0:T(8,128)(2,1)}, u32[]{:S(2)}) copy-start(bf16[2,640,1280]{2,1,0:T(8,128)(2,1)} %w_out.5) | copy-start | bytes 9830404
  102.1 8.0 %copy-start.16 = (bf16[4,2,96,640]{3,2,1,0:T(8,128)(2,1)S(1)}, bf16[4,2,96,640]{3,2,1,0:T(8,128)(2,1)}, u32[]{:S(2)}) copy-start(bf16[4,2,96,640]{3,2,1,0:T(8,128)(2,1)} %copy-done.15) | copy-start | bytes 2949124
  102.1 2.4 %collective-permute-start.2 = (f32[2,64,1280]{2,1,0:T(8,128)S(1)}, f32[2,64,1280]{2,1,0:T(8,128)S(1)}, u32[]{:S(2)}, u32[]{:S(2)}) collective-permute-start(f32[2,64,1280]{2,1,0:T(8,128)S(1)} %bitcast.17), channel_id=1, source_target_pairs={{0,16},{16,0},{32,48},{48,32},{64,80},{80,64},{96,112},{112,96},{1... | collective-permute-start | bytes 1966088 | tf_op jit(solution)/shard_map/ppermute | solution.py:393
  109.3 0.8 copy-start.21
  110.1 2.3 %copy-start.29 = (f32[2,128,1280]{2,1,0:T(8,128)}, f32[2,128,1280]{2,1,0:T(8,128)S(1)}, u32[]{:S(2)}) copy-start(f32[2,128,1280]{2,1,0:T(8,128)S(1)} %get-tuple-element.24) | copy-start | bytes 3932164
  110.1 2.6 %copy-start.14 = (bf16[4,2,96,640]{3,2,1,0:T(8,128)(2,1)S(1)}, bf16[4,2,96,640]{3,2,1,0:T(8,128)(2,1)}, u32[]{:S(2)}) copy-start(bf16[4,2,96,640]{3,2,1,0:T(8,128)(2,1)} %copy-done.13) | copy-start | bytes 2949124
  112.5 2.6 %copy-start.17 = (bf16[4,2,96,640]{3,2,1,0:T(8,128)(2,1)}, bf16[4,2,96,640]{3,2,1,0:T(8,128)(2,1)S(1)}, u32[]{:S(2)}) copy-start(bf16[4,2,96,640]{3,2,1,0:T(8,128)(2,1)S(1)} %get-tuple-element.35.other_pre) | copy-start | bytes 2949124
  112.5 4.1 %collective-permute-start.3 = (bf16[4,192,1280]{2,1,0:T(8,128)(2,1)S(1)}, bf16[4,192,1280]{2,1,0:T(8,128)(2,1)S(1)}, u32[]{:S(2)}, u32[]{:S(2)}) collective-permute-start(bf16[4,192,1280]{2,1,0:T(8,128)(2,1)S(1)} %get-tuple-element.30), channel_id=1, source_target_pairs={{0,16},{16,0},{32,48},{48,32},{64,80},{80,64},{96,112},{112,96},{1... | collective-permute-start | bytes 5898248 | tf_op jit(solution)/shard_map/ppermute | solution.py:393
  115.1 1.0 copy-start.19
  120.3 6.0 %copy-start.10 = (bf16[4,2,32,640]{3,2,1,0:T(8,128)(2,1)S(1)}, bf16[4,2,32,640]{3,2,1,0:T(8,128)(2,1)}, u32[]{:S(2)}) copy-start(bf16[4,2,32,640]{3,2,1,0:T(8,128)(2,1)} %copy-done.9) | copy-start | bytes 983044
  120.3 6.0 %copy-start.12 = (bf16[4,2,32,640]{3,2,1,0:T(8,128)(2,1)S(1)}, bf16[4,2,32,640]{3,2,1,0:T(8,128)(2,1)}, u32[]{:S(2)}) copy-start(bf16[4,2,32,640]{3,2,1,0:T(8,128)(2,1)} %copy-done.11) | copy-start | bytes 983044
  120.3 6.1 %copy-start.22 = (bf16[2,4,32,1280]{3,2,1,0:T(8,128)(2,1)S(1)}, bf16[2,4,32,1280]{3,2,1,0:T(8,128)(2,1)}, u32[]{:S(2)}) copy-start(bf16[2,4,32,1280]{3,2,1,0:T(8,128)(2,1)} %copy-done.21) | copy-start | bytes 1966084
  120.3 35.5 %all-to-all-start.3 = ((bf16[64,128,128]{2,1,0:T(8,128)(2,1)}), bf16[64,128,128]{2,1,0:T(8,128)(2,1)S(1)}, u32[]{:S(2)}, u32[]{:S(2)}) async-start(bf16[64,128,128]{2,1,0:T(8,128)(2,1)} %shard_map.94), calls=%async_computation.3 | async-start | bytes 4194304 | tf_op jit(solution)/shard_map/all_to_all | solution.py:399
  126.3 4.0 %copy-start.4 = (bf16[4,208,1280]{2,1,0:T(8,128)(2,1)S(1)}, bf16[4,208,1280]{2,1,0:T(8,128)(2,1)}, u32[]{:S(2)}) copy-start(bf16[4,208,1280]{2,1,0:T(8,128)(2,1)} %copy-done.3) | copy-start | bytes 6389764
  126.4 4.0 %copy-start.6 = (bf16[4,208,1280]{2,1,0:T(8,128)(2,1)S(1)}, bf16[4,208,1280]{2,1,0:T(8,128)(2,1)}, u32[]{:S(2)}) copy-start(bf16[4,208,1280]{2,1,0:T(8,128)(2,1)} %copy-done.5) | copy-start | bytes 6389764
  126.4 4.6 %copy-start.18 = (bf16[4,2,96,640]{3,2,1,0:T(8,128)(2,1)S(1)}, bf16[4,2,96,640]{3,2,1,0:T(8,128)(2,1)}, u32[]{:S(2)}) copy-start(bf16[4,2,96,640]{3,2,1,0:T(8,128)(2,1)} %copy-done.17) | copy-start | bytes 2949124
  126.4 5.1 %copy-start.20 = (bf16[4,2,96,640]{3,2,1,0:T(8,128)(2,1)S(1)}, bf16[4,2,96,640]{3,2,1,0:T(8,128)(2,1)}, u32[]{:S(2)}) copy-start(bf16[4,2,96,640]{3,2,1,0:T(8,128)(2,1)} %copy-done.19) | copy-start | bytes 2949124
  131.5 24.3 %copy-start.8 = (bf16[1,2,64,1280]{3,2,1,0:T(8,128)(2,1)S(1)}, bf16[1,2,64,1280]{3,2,1,0:T(8,128)(2,1)}, u32[]{:S(2)}) copy-start(bf16[1,2,64,1280]{3,2,1,0:T(8,128)(2,1)} %param.6) | copy-start | bytes 983044
  131.5 24.3 %copy-start.24 = (f32[1280]{0:T(1024)S(1)}, f32[1280]{0:T(1024)}, u32[]{:S(2)}) copy-start(f32[1280]{0:T(1024)} %gain_ref.3) | copy-start | bytes 15364
  131.5 24.3 %copy-start.26 = (s32[1,2,64]{2,1,0:T(2,128)S(1)}, s32[1,2,64]{2,1,0:T(2,128)}, u32[]{:S(2)}) copy-start(s32[1,2,64]{2,1,0:T(2,128)} %param.7) | copy-start | bytes 1540
  131.5 24.3 %copy-start.28 = (s32[1,2,64]{2,1,0:T(2,128)S(1)}, s32[1,2,64]{2,1,0:T(2,128)}, u32[]{:S(2)}) copy-start(s32[1,2,64]{2,1,0:T(2,128)} %param.8) | copy-start | bytes 1540

commit v5 on v3

v5 whole, which is shorter than its diff:
```python
import functools
import math

import jax
import jax.numpy as jnp
from jax import lax
from jax.experimental import pallas as pl
from jax.experimental.pallas import tpu as pltpu
from jax.sharding import PartitionSpec as P

norm_eps = 1e-06
objective_scale = 32.0
bf16 = jnp.bfloat16
f32 = jnp.float32
i32 = jnp.int32

CAP = 6
HELD = 2
GROUP = HELD * CAP
PAD = 16
PEERS = 16
HALF = PEERS * CAP
KIND_ROWS = 16
POOLED = 2 * PEERS
PAIR_TOKENS = 64
LANES = 128
AROUND = (0, 4, 6, 2)


def nn(a, b):
    return lax.dot_general(a, b, (((1,), (0,)), ((), ())), preferred_element_type=f32)


def nt(a, b, precision=None):
    return lax.dot_general(
        a, b, (((1,), (1,)), ((), ())), precision=precision, preferred_element_type=f32
    )


def tn(a, b, precision=None):
    return lax.dot_general(
        a, b, (((0,), (0,)), ((), ())), precision=precision, preferred_element_type=f32
    )


def iota(shape, dim):
    return lax.broadcasted_iota(i32, shape, dim)


def shape_of(*dims, dtype=bf16):
    return jax.ShapeDtypeStruct(dims, dtype)


def one_hot(hit):
    return jnp.where(hit, 1.0, 0.0).astype(bf16)


def call(kernel, out, args, smem=(), hbm=(), scratch=(), vmem=14, cost=None):
    def space(k):
        return pltpu.SMEM if k in smem else pltpu.HBM if k in hbm else pltpu.VMEM

    many = isinstance(out, (list, tuple))
    out_specs = [pl.BlockSpec(memory_space=pltpu.VMEM) for _ in (out if many else [out])]
    return pl.pallas_call(
        kernel,
        out_shape=out,
        in_specs=[pl.BlockSpec(memory_space=space(k)) for k in range(len(args))],
        out_specs=out_specs if many else out_specs[0],
        scratch_shapes=list(scratch),
        compiler_params=pltpu.CompilerParams(vmem_limit_bytes=vmem * 1024 * 1024),
        cost_estimate=cost,
    )(*args)


def normal_parts(x):
    centred = x - jnp.mean(x, axis=-1, keepdims=True)
    spread = jnp.mean(centred * centred, axis=-1, keepdims=True)
    scale = lax.rsqrt(spread + norm_eps)
    return centred * scale, scale


def places(ids_ref, slots_ref):
    pos = ids_ref[...] * CAP + slots_ref[...]
    return jnp.concatenate([pos[:1], pos[1:]], axis=1)


def slot_table(pos):
    tokens = pos.shape[1]
    row = iota((PEERS * PAD, tokens), 0)
    want = (row // PAD) * GROUP + row % PAD
    return one_hot((want == pos) & (row % PAD < GROUP))


def fetch(sources, refs, sems):
    copies = [pltpu.make_async_copy(a, b, sems.at[k]) for k, (a, b) in enumerate(zip(sources, refs))]
    for copy in copies:
        copy.start()
    return copies


def input_scratch(tokens, width):
    return [
        pltpu.VMEM((2, tokens // 2), i32),
        pltpu.VMEM((2, tokens // 2), i32),
        pltpu.VMEM((tokens, width), bf16),
        pltpu.VMEM((width,), f32),
        pltpu.SemaphoreType.DMA((4,)),
    ]


def dispatch_kernel(ids, slots, toks, gain, out_ref, sum_ref, ids_ref, slots_ref, tok_ref, gain_ref, sems):
    copies = fetch((ids, slots, toks, gain), (ids_ref, slots_ref, tok_ref, gain_ref), sems)
    for copy in copies:
        copy.wait()
    pos = places(ids_ref, slots_ref)
    tokens = pos.shape[1]
    x = tok_ref[...].astype(f32)
    normed = normal_parts(x)[0] * gain_ref[...].reshape(1, -1)
    normed = normed.astype(bf16)
    sent = nn(slot_table(pos), normed)
    row = iota((PEERS * PAD, tokens), 0)
    goes = one_hot((row % PAD == GROUP) & (pos // GROUP == row // PAD))
    place = pos % GROUP
    column = (place // CAP) * 128 + lax.axis_index("expert") * CAP + place % CAP
    lane = iota((2 * 128, tokens), 0)
    kind = jnp.where(iota((2 * 128, tokens), 1) < tokens // 2, 1.0, 2.0)
    kinds = nt(goes, jnp.where(lane == column, kind, 0.0).astype(bf16))
    width = sent.shape[1]
    first = sent[:, : 2 * 128] + kinds
    out_ref[:, :, : 2 * 128] = first.astype(bf16).reshape(PEERS, PAD, 2 * 128)
    out_ref[:, :, 2 * 128 :] = sent[:, 2 * 128 :].astype(bf16).reshape(
        PEERS, PAD, width - 2 * 128
    )
    sum_ref[0:1, :] = jnp.sum(x[: tokens // 2], axis=0, keepdims=True)
    sum_ref[1:2, :] = jnp.sum(x[tokens // 2 :], axis=0, keepdims=True)


def repack_table(rows, back):
    shape = (PEERS * PAD, rows) if back else (rows, PEERS * PAD)
    r = iota(shape, 1 if back else 0)
    m = iota(shape, 0 if back else 1)
    held, rest = r // HALF, r % HALF
    from_slot = (rest // CAP) * PAD + held * CAP + rest % CAP
    hit = (r < 2 * HALF) & (m == from_slot)
    if not back:
        hit = hit | ((r == 2 * HALF) & (m % PAD == GROUP))
    return one_hot(hit)


def repack_kernel(in_ref, first_ref, second_ref):
    width = in_ref.shape[2]
    rows = 2 * HALF + KIND_ROWS
    out = nn(repack_table(rows, False), in_ref[...].reshape(PEERS * PAD, width)).astype(bf16)
    first_ref[...] = out[:HALF]
    second_ref[...] = out[HALF:]


def pool_table(seconds, held, wide_ref):
    count = len(seconds)
    wide_ref[...] = jnp.zeros_like(wide_ref)
    q = iota((POOLED, LANES), 0)
    r = iota((POOLED, LANES), 1)
    for k in range(count):
        kinds = seconds[k][HALF : HALF + KIND_ROWS, held * LANES : (held + 1) * LANES]
        kinds = kinds.astype(f32)[:1]
        hit = (q % PEERS == r // CAP) & (kinds == (q // PEERS + 1).astype(f32)) & (r < HALF)
        wide_ref[k * POOLED : (k + 1) * POOLED, k * LANES : (k + 1) * LANES] = one_hot(hit)


def forward_kernel(count, *refs):
    halves = refs[:count], refs[count : 2 * count]
    w_in, pooled_ref, slope_ref, wide_ref, act_ref = refs[2 * count :]
    c0 = math.sqrt(2.0 / math.pi)
    c1 = c0 * 0.044715
    hidden = w_in.shape[2]
    for held in range(HELD):
        pool_table(halves[1], held, wide_ref)
        rows = jnp.concatenate([ref[:HALF, :] for ref in halves[held]], axis=0)
        for at in range(0, hidden, 256):
            to = slice(at, min(at + 256, hidden))
            full = nn(rows, w_in[held, :, to])
            for k in range(count):
                h = full[k * HALF : (k + 1) * HALF]
                h2 = h * h
                t = jnp.tanh(h * (c0 + c1 * h2))
                half = 0.5 + 0.5 * t
                act = h * half
                slope = half + act * (1.0 - t) * (c0 + 3.0 * c1 * h2)
                slope_ref[k, held, :, to] = slope.astype(bf16)
                act_ref[k * LANES : k * LANES + HALF, to] = act.astype(bf16)
        for k in range(count):
            act_ref[k * LANES + HALF : (k + 1) * LANES, :] = jnp.zeros(
                (LANES - HALF, hidden), bf16
            )
        pooled = nn(wide_ref[...], act_ref[...]).astype(bf16)
        for k in range(count):
            pooled_ref[k, held] = pooled[k * POOLED : (k + 1) * POOLED]


def forward(firsts, seconds, w_in):
    count = len(firsts)
    hidden = w_in.shape[2]
    return call(
        functools.partial(forward_kernel, count),
        [
            shape_of(count, HELD, POOLED, hidden),
            shape_of(count, HELD, HALF, hidden),
        ],
        [*firsts, *seconds, w_in],
        scratch=[
            pltpu.VMEM((count * POOLED, count * LANES), bf16),
            pltpu.VMEM((count * LANES, hidden), bf16),
        ],
    )


def part_of(parts, k):
    if k < 2:
        return parts[0], k
    if k < 6:
        return parts[1], k - 2
    return parts[2], k - 6


def out_kernel(shift, a_ref, b_ref, c_ref, w_out, out_ref):
    total = None
    for held in range(HELD):
        rows = []
        for k in AROUND:
            ref, at = part_of((a_ref, b_ref, c_ref), k + shift)
            rows.append(ref[at, held])
        part = nn(jnp.concatenate(rows, axis=0), w_out[held])
        total = part if total is None else total + part
    out_ref[...] = total.astype(bf16).reshape(out_ref.shape)


def join_kernel(own_ref, got_ref, out_ref):
    for ahead in range(4):
        to = lax.rem(lax.axis_index("dp") // 2 + ahead, 4)
        out_ref[to] = (own_ref[ahead].astype(f32) + got_ref[ahead].astype(f32)).astype(bf16)


def mean_kernel(part_ref, sum_ref, out_ref):
    total = sum_ref[...]
    for first in range(0, part_ref.shape[0], 8):
        total = total + jnp.sum(part_ref[first : first + 8].astype(f32), axis=0)
    out_ref[...] = jnp.broadcast_to((total * (1.0 / PAIR_TOKENS))[None], out_ref.shape)


def split(x):
    high = x.astype(bf16)
    return high, (x - high.astype(f32)).astype(bf16)


def loss_kernel(own_ref, other_ref, w_out, grad_ref, rows_ref, prod_ref, gi_ref, gt_ref):
    image = jnp.concatenate([own_ref[0], other_ref[0]], axis=0)
    text = jnp.concatenate([own_ref[1], other_ref[1]], axis=0)
    pairs, width = image.shape
    scale = PAIR_TOKENS / math.sqrt(width)
    logits = scale * nt(image, text, lax.Precision.HIGHEST)

    def softmax(axis):
        top = jnp.exp(logits - jnp.max(logits, axis=axis, keepdims=True))
        return top / jnp.sum(top, axis=axis, keepdims=True)

    same = jnp.where(iota((pairs, pairs), 0) == iota((pairs, pairs), 1), 2.0, 0.0)
    grad_logits = (objective_scale * scale / PAIR_TOKENS) * (softmax(1) + softmax(0) - same)

    def thrice(g, x):
        (g0, g1), (x0, x1) = split(g), split(x)
        return nn(g0, x0) + (nn(g0, x1) + nn(g1, x0))

    grad_image = thrice(grad_logits, text)
    grad_text = thrice(grad_logits.T, image)
    grad_ref[0] = grad_image
    grad_ref[1] = grad_text
    gi_ref[...] = grad_image.astype(bf16)
    gt_ref[...] = grad_text.astype(bf16)
    for at, k in enumerate(AROUND):
        for other in range(2):
            first = other * 4 * PEERS + lax.rem(lax.axis_index("dp") // 2 + at, 4) * PEERS
            span = pl.ds(pl.multiple_of(first, PEERS), PEERS)
            rows_ref[k + other, :PEERS, :] = gi_ref[span, :]
            rows_ref[k + other, PEERS:, :] = gt_ref[span, :]
    rows = rows_ref[...].reshape(8 * POOLED, width)
    for held in range(HELD):
        prod_ref[held] = nt(rows, w_out[held]).astype(bf16)


def backward_kernel(blocks, *refs):
    count = len(blocks)
    seconds, slopes = refs[:count], refs[count : 2 * count]
    prod_ref, w_in, pre_ref = refs[2 * count : 2 * count + 3]
    outs = refs[2 * count + 3 : 3 * count + 3]
    wide_ref, prods_ref = refs[3 * count + 3 :]
    for held in range(HELD):
        pool_table(seconds, held, wide_ref)
        for k, block in enumerate(blocks):
            prods_ref[k * POOLED : (k + 1) * POOLED, :] = prod_ref[
                held, block * POOLED : (block + 1) * POOLED, :
            ]
        grad_act = tn(wide_ref[...], prods_ref[...])
        for k, block in enumerate(blocks):
            slope = slopes[k][part_of((None,) * 3, block)[1], held].astype(f32)
            pre_ref[k, held] = (grad_act[k * LANES : k * LANES + HALF] * slope).astype(bf16)
        pre = jnp.concatenate([pre_ref[k, held] for k in range(count)], axis=0)
        part = nt(pre, w_in[held]).astype(bf16)
        for k in range(count):
            outs[k][held * HALF : (held + 1) * HALF, :] = part[k * HALF : (k + 1) * HALF]


def backward(blocks, seconds, made, prod, w_in):
    count = len(blocks)
    width, hidden = w_in.shape[1:]
    of = [part_of(made, block)[0] for block in blocks]
    return call(
        functools.partial(backward_kernel, blocks),
        [shape_of(count, HELD, HALF, hidden)] + [shape_of(2 * HALF, width)] * count,
        [*[seconds[block] for block in blocks], *[m[1] for m in of], prod, w_in],
        scratch=[
            pltpu.VMEM((count * POOLED, count * LANES), bf16),
            pltpu.VMEM((count * POOLED, hidden), bf16),
        ],
    )


PAIRED = {7: (0, 0), 5: (0, 1), 6: (1, 0), 4: (1, 1), 3: (2, 0), 1: (2, 1), 2: (3, 0), 0: (3, 1)}


def grad_in_kernel(*refs):
    blocks, pres = refs[:16], refs[16:20]
    out_ref, x_ref, p_ref = refs[20:]
    held = pl.program_id(0)

    def fill(which):
        for k in range(8):
            span = slice(k * HALF, (k + 1) * HALF)
            x_ref[span, :] = blocks[8 * which + k][:HALF, :]
            pair, at = PAIRED[k]
            p_ref[span, :] = pres[pair][at, which]

    for which in range(HELD):
        pl.when(held == which)(functools.partial(fill, which))
    out_ref[0] = tn(x_ref[...], p_ref[...])


def grad_in(firsts, seconds, pres, width, hidden):
    whole = pl.BlockSpec(memory_space=pltpu.VMEM)
    return pl.pallas_call(
        grad_in_kernel,
        grid=(HELD,),
        out_shape=shape_of(HELD, width, hidden, dtype=f32),
        in_specs=[whole] * 20,
        out_specs=pl.BlockSpec((1, width, hidden), lambda i: (i, 0, 0)),
        scratch_shapes=[
            pltpu.VMEM((8 * HALF, width), bf16),
            pltpu.VMEM((8 * HALF, hidden), bf16),
        ],
        compiler_params=pltpu.CompilerParams(vmem_limit_bytes=26 * 1024 * 1024),
    )(*firsts, *seconds, *pres)


def grad_out_kernel(a_ref, b_ref, c_ref, rows_ref, out_ref):
    held = pl.program_id(0)
    width = rows_ref.shape[2]
    pooled = []
    for k in range(8):
        ref, at = part_of((a_ref, b_ref, c_ref), k)
        pooled.append(ref[at, held])
    out_ref[0] = tn(jnp.concatenate(pooled, axis=0), rows_ref[...].reshape(8 * POOLED, width))


def grad_out(pooled, rows, width, hidden):
    whole = pl.BlockSpec(memory_space=pltpu.VMEM)
    return pl.pallas_call(
        grad_out_kernel,
        grid=(HELD,),
        out_shape=shape_of(HELD, hidden, width, dtype=f32),
        in_specs=[whole] * 4,
        out_specs=pl.BlockSpec((1, hidden, width), lambda i: (i, 0, 0)),
        compiler_params=pltpu.CompilerParams(vmem_limit_bytes=18 * 1024 * 1024),
    )(*pooled, rows)


def plus_kernel(own_ref, got_ref, first_ref, second_ref):
    total = (own_ref[...].astype(f32) + got_ref[...].astype(f32)).astype(bf16)
    first_ref[...] = total[:HALF]
    second_ref[...] = total[HALF:]


def settle_kernel(own_ref, got_ref, la_ref, lb_ref, ra_ref, rb_ref, out_ref):
    width = own_ref.shape[1]
    total = own_ref[...].astype(f32) + got_ref[...].astype(f32)
    first = total[:HALF] + la_ref[...].astype(f32) + ra_ref[...].astype(f32)
    second = total[HALF:] + lb_ref[...].astype(f32) + rb_ref[...].astype(f32)
    table = repack_table(2 * HALF, True)
    rows = jnp.concatenate([first.astype(bf16), second.astype(bf16)], axis=0)
    out_ref[...] = nn(table, rows).astype(bf16).reshape(PEERS, PAD, width)


def tail_kernel(ids, slots, toks, gain, grads, back_ref, out_ref, ids_ref, slots_ref, tok_ref, gain_ref, sems, near_ref, near_sem):
    copies = fetch((ids, slots, toks, gain), (ids_ref, slots_ref, tok_ref, gain_ref), sems)
    at = (lax.axis_index("dp") // 2) * PEERS + lax.axis_index("expert")
    first = pl.multiple_of(at // 8 * 8, 8)
    near = pltpu.make_async_copy(grads.at[:, pl.ds(first, 8), :], near_ref, near_sem)
    near.start()
    for copy in copies:
        copy.wait()
    near.wait()
    width = tok_ref.shape[1]
    tokens = tok_ref.shape[0]
    back = back_ref[...].reshape(PEERS * PAD, width)
    grad_normed = tn(slot_table(places(ids_ref, slots_ref)), back)
    unit, scale = normal_parts(tok_ref[...].astype(f32))
    grad = grad_normed * gain_ref[...].reshape(1, -1)
    grad = scale * (
        grad
        - jnp.mean(grad, axis=-1, keepdims=True)
        - unit * jnp.mean(grad * unit, axis=-1, keepdims=True)
    )
    for half in range(2):
        span = slice(half * (tokens // 2), (half + 1) * (tokens // 2))
        rows = near_ref[half]
        own = jnp.where(iota(rows.shape, 0) == at % 8, rows, 0.0)
        own = jnp.sum(own, axis=0, keepdims=True)
        out_ref[span, :] = (own + grad[span]).astype(bf16)


def body(tokens, expert_ids, slots, ln_gain, w_in, w_out):
    width, hidden = w_in.shape[1:]
    row_count = tokens.shape[1] * tokens.shape[2]
    flat = tokens.reshape(row_count, width)
    ids, slot = expert_ids[0], slots[0]
    everyone = ("dp", "expert")
    chips = 4 * PEERS
    cores = [[d * PEERS + e for d in range(c, 8, 2) for e in range(PEERS)] for c in range(2)]

    def up(x):
        return lax.ppermute(x, "dp", [(i, (i + 2) % 8) for i in range(8)])

    def down(x):
        return lax.ppermute(x, "dp", [(i, (i + 6) % 8) for i in range(8)])

    def swap(x):
        return lax.ppermute(x, "dp", [(i, i ^ 1) for i in range(8)])

    def after(x, *tokens):
        return lax.optimization_barrier((x, *tokens))[0]

    def exchange(x):
        return lax.all_to_all(x, "expert", split_axis=0, concat_axis=0, tiled=True)

    def spread(x):
        return lax.all_to_all(
            x, everyone, split_axis=0, concat_axis=0, tiled=True, axis_index_groups=cores
        )

    sent, token_sum = call(
        dispatch_kernel,
        [shape_of(PEERS, PAD, width), shape_of(2, width, dtype=f32)],
        [ids, slot, flat, ln_gain],
        hbm=(0, 1, 2, 3),
        scratch=input_scratch(row_count, width),
        vmem=60,
    )
    first, second = call(
        repack_kernel,
        [shape_of(HALF, width), shape_of(HALF + KIND_ROWS, width)],
        [exchange(sent)],
    )

    a, b = [None] * 8, [None] * 8
    a[0], b[0] = first, second
    a[2] = up(first)
    b[4] = down(second)
    a[1], b[1] = swap(first), swap(second)
    b[2] = up(after(second, a[1], b[1]))
    a[4] = down(after(first, a[1], b[1]))
    a[6] = up(a[2])
    b[6] = down(b[4])
    near = forward(a[0:2], b[0:2], w_in)
    a[3], b[5] = swap(after(a[2], near[0])), swap(after(b[4], near[0]))
    a[5], b[3] = swap(a[4]), swap(b[2])
    mid = forward(a[2:6], b[2:6], w_in)
    a[6], b[6] = after(a[6], mid[0]), after(b[6], mid[0])
    a[7], b[7] = swap(a[6]), swap(b[6])
    far = forward(a[6:8], b[6:8], w_in)
    made = [near, mid, far]
    pooled = [m[0] for m in made]

    def product(shift, w_out):
        return call(
            functools.partial(out_kernel, shift),
            shape_of(4, POOLED, width),
            [*pooled, w_out],
        )

    other = product(1, w_out)
    got = swap(other)
    own = product(0, after(w_out, other))
    joined = call(join_kernel, shape_of(4, POOLED, width), [own, after(got, own)])
    joined = joined.reshape(4, 2, PEERS, width).transpose(0, 2, 1, 3).reshape(chips, 2, width)
    emb = call(
        mean_kernel, shape_of(chips, 2, width, dtype=f32), [spread(joined), token_sum]
    )
    emb = spread(emb).transpose(1, 0, 2)
    grad_pooled, rows, prod = call(
        loss_kernel,
        [
            shape_of(2, 8 * PEERS, width, dtype=f32),
            shape_of(8, POOLED, width),
            shape_of(HELD, 8 * POOLED, hidden),
        ],
        [emb, swap(emb), w_out],
        scratch=[pltpu.VMEM((8 * PEERS, width), bf16), pltpu.VMEM((8 * PEERS, width), bf16)],
    )

    def plus(x, y):
        return call(plus_kernel, [shape_of(HALF, width), shape_of(HALF, width)], [x, y])

    pre75, p7, p5 = backward((7, 5), b, made, prod, w_in)
    s7, s5 = swap(p7), swap(p5)
    pre64, p6, p4 = backward((6, 4), b, made, after(prod, p7), w_in)
    r6a, r6b = plus(p6, s7)
    from_below, from_above = up(r6a), down(r6b)
    r4a, r4b = plus(p4, after(s5, r6a))
    low_b = up(r4b)
    pre31, p3, p1 = backward((3, 1), b, made, after(prod, r4a), w_in)
    s3, s1 = swap(p3), swap(p1)
    pre20, p2, p0 = backward((2, 0), b, made, after(prod, p3), w_in)
    r2a, r2b = plus(p2, s3)
    high_a = down(r2a)

    def add(x, y):
        return (x.astype(f32) + y.astype(f32)).astype(bf16)

    grad_w_out = grad_out(pooled, after(rows, r2a), width, hidden)
    low_a = up(add(r4a, after(from_below, grad_w_out)))
    high_b = down(add(r2b, after(from_above, grad_w_out)))
    grad_w_in = grad_in(
        a, b, [pre75, pre64, pre31, after(pre20, grad_w_out)], width, hidden
    )
    settled = call(
        settle_kernel,
        shape_of(PEERS, PAD, width),
        [after(p0, grad_w_in), s1, low_a, low_b, high_a, high_b],
    )
    grad_flat = call(
        tail_kernel,
        shape_of(row_count, width),
        [ids, slot, flat, ln_gain, grad_pooled, exchange(settled)],
        hbm=(0, 1, 2, 3, 4),
        scratch=input_scratch(row_count, width)
        + [pltpu.VMEM((2, 8, width), f32), pltpu.SemaphoreType.DMA],
    )
    return (grad_flat.reshape(tokens.shape), grad_w_in, grad_w_out)


def solution(mesh):
    placed = (
        P(("dp", "expert"), None, None, None),
        P(("dp", "expert"), None, None),
        P(("dp", "expert"), None, None),
        P(),
        P("expert", None, "dp"),
        P("expert", "dp", None),
    )
    return jax.shard_map(
        body,
        mesh=mesh,
        in_specs=placed,
        out_specs=(
            P(("dp", "expert"), None, None, None),
            P("expert", None, "dp"),
            P("expert", "dp", None),
        ),
        check_vma=False,
    )
```

time: 159 us -> 143 us (0.90); the launches traced: 157 us -> 143 us
  blocking collectives: 38.4 us -> 70.1 us
  local copies, waits for them, and re-layouts: 15.3 us -> 2.25 us
  waiting for transfers between devices: 29.3 us -> 17.4 us
  starting transfers between devices: 31.1 us -> 20.2 us
  Pallas kernels: 37.2 us -> 31.7 us
  other arithmetic: 4.23 us -> 0.12 us
    all_to_all x2 -> x0, waiting for transfers between devices: 16.5 us -> none  [the longest x1 10 us: spread(): lax.all_to_all(x, everyone, split_axis=0, concat_axis=0, tiled=True, axis...]
    all_to_all x1 -> x2, blocking collectives: 18.6 us -> 34.6 us  [spread(): lax.all_to_all(x, everyone, split_axis=0, concat_axis=0, tiled=True, axis...]
    all_to_all x1 -> x2, blocking collectives: 19.9 us -> 35.5 us  [exchange(): return lax.all_to_all(x, 'expert', split_axis=0, concat_axis=0, tiled=True)]
    unnamed x137 -> x16, local copies, waits for them, and re-layouts: 13.1 us -> 1.96 us
    all_to_all x2 -> x0, starting transfers between devices: 9.3 us -> none  [the longest x1 5.71 us: spread(): lax.all_to_all(x, everyone, split_axis=0, concat_axis=0, tiled=True, axis...]
    pallas_call x17 -> x19, Pallas kernels: 28.1 us -> 22.7 us  [call(): pl.pallas_call(kernel, out_shape=out, in_specs=[pl.BlockSpec(memory_space...]
    ppermute x14, waiting for transfers between devices: 2.47 us -> 5.83 us  [swap(): return lax.ppermute(x, 'dp', [(i, i ^ 1) for i in range(8)])]
    reduce_sum x2 -> x0, other arithmetic: 3.05 us -> none  [the longest x1 1.64 us: body(): jnp.sum(flat.reshape(2, PAIR_TOKENS, width).astype(f32), axis=1)]
  transfers between devices with their start and end apart: 28 -> 26, of which waited for: 9 -> 11; matrix products, arithmetic and copies ran while one was open for 2% -> 0% of each run, Pallas kernels for 16% -> 12%
where the time goes in v5:
time: 143 us
  blocking collectives  70.1 us (49%)
  Pallas kernels  31.7 us (22%)
  starting transfers between devices  20.2 us (14%)
  waiting for transfers between devices  17.4 us (12%)
  local copies, waits for them, and re-layouts  2.25 us (2%)
    all_to_all x2, blocking collectives, exchange(): return lax.all_to_all(x, 'expert', split_axis=0, concat_axis=0, tiled=True)  35.5 us
    all_to_all x2, blocking collectives, spread(): lax.all_to_all(x, everyone, split_axis=0, concat_axis=0, tiled=True, axis...  34.6 us
    pallas_call x19, Pallas kernels, call(): pl.pallas_call(kernel, out_shape=out, in_specs=[pl.BlockSpec(memory_space...  22.7 us
    ppermute x6, starting transfers between devices, down(): return lax.ppermute(x, 'dp', [(i, (i + 6) % 8) for i in range(8)])  14.1 us
    ppermute x6, waiting for transfers between devices, up(): return lax.ppermute(x, 'dp', [(i, (i + 2) % 8) for i in range(8)])  7.87 us
    ppermute x14, waiting for transfers between devices, swap(): return lax.ppermute(x, 'dp', [(i, i ^ 1) for i in range(8)])  5.83 us
    pallas_call x1, Pallas kernels, grad_in(): pl.pallas_call(grad_in_kernel, grid=(HELD,), out_shape=shape_of(HELD, wid...  5.62 us
    ppermute x6, starting transfers between devices, up(): return lax.ppermute(x, 'dp', [(i, (i + 2) % 8) for i in range(8)])  3.9 us
  transfers between devices with their start and end apart: 26, of which 11 were waited for; matrix products, arithmetic and copies ran while one was open for 0% of the time, Pallas kernels for 12%

profile of v5, /device:TPU:0, one launch (start us, length us, event | category | flops | bytes accessed | tf_op | source)
XLA Modules:
  0.0 142.8 jit_solution(15312791683074185263)
XLA Ops:
  0.6 2.5 %shard_map.85 = (bf16[16,16,1280]{2,1,0:T(8,128)(2,1)}, f32[2,1280]{1,0:T(2,128)}) custom-call(s32[2,64]{1,0:T(2,128)} %bitcast.16, s32[2,64]{1,0:T(2,128)} %bitcast.18, bf16[128,1280]{1,0:T(8,128)(2,1)} %bitcast.13, f32[1280]{0:T(1024)} %gain.3), custom_call_target="tpu_custom_call" | custom-call | tf_op jit(solution)/shard_map/pallas_call | solution.py:64
  3.1 20.1 %all_to_all.20.in_ref = bf16[16,16,1280]{2,1,0:T(8,128)(2,1)S(1)} all-to-all(bf16[16,16,1280]{2,1,0:T(8,128)(2,1)} %get-tuple-element.51), channel_id=1, replica_groups=mesh['dp'=8,'expert'=16] {'expert'}, dimensions={0} | all-to-all | bytes 1310720 | tf_op jit(solution)/shard_map/all_to_all | solution.py:451
  23.2 0.4 shard_map.86
  23.6 0.1 collective-permute-start.1
  23.7 0.5 collective-permute-start
  24.2 1.9 %collective-permute-start.2 = (bf16[96,1280]{1,0:T(8,128)(2,1)S(1)}, bf16[96,1280]{1,0:T(8,128)(2,1)S(1)}, u32[]{:S(2)}, u32[]{:S(2)}) collective-permute-start(bf16[96,1280]{1,0:T(8,128)(2,1)S(1)} %get-tuple-element.56.refs_0_), channel_id=1, source_target_pairs={{0,32},{16,48},{32,64},{48,80},{64,96},{80,112},{96,0},{112,16},{1... | collective-permute-start | bytes 737288 | tf_op jit(solution)/shard_map/ppermute | solution.py:439
  26.1 2.1 %collective-permute-start.8 = (bf16[112,1280]{1,0:T(8,128)(2,1)S(1)}, bf16[112,1280]{1,0:T(8,128)(2,1)S(1)}, u32[]{:S(2)}, u32[]{:S(2)}) collective-permute-start(bf16[112,1280]{1,0:T(8,128)(2,1)S(1)} %get-tuple-element.57.refs_2_.refs_1_.refs_8_), channel_id=1, source_target_pairs={{0,96},{16,112},{32,0},{48,16},{64,32},{80,48},{96,64},{112,80},{1... | collective-permute-start | bytes 860168 | tf_op jit(solution)/shard_map/ppermute | solution.py:442
  28.2 3.2 %collective-permute-start.4 = (bf16[96,1280]{1,0:T(8,128)(2,1)S(1)}, bf16[96,1280]{1,0:T(8,128)(2,1)S(1)}, u32[]{:S(2)}, u32[]{:S(2)}) collective-permute-start(bf16[96,1280]{1,0:T(8,128)(2,1)S(1)} %get-tuple-element.56.refs_0_), channel_id=1, source_target_pairs={{0,96},{16,112},{32,0},{48,16},{64,32},{80,48},{96,64},{112,80},{1... | collective-permute-start | bytes 737288 | tf_op jit(solution)/shard_map/ppermute | solution.py:442
  31.4 1.9 %copy-done = bf16[2,1280,640]{2,1,0:T(8,128)(2,1)S(1)} copy-done((bf16[2,1280,640]{2,1,0:T(8,128)(2,1)S(1)}, bf16[2,1280,640]{2,1,0:T(8,128)(2,1)}, u32[]{:S(2)}) %copy-start) | copy-done | bytes 3276824
  33.4 1.5 %shard_map.87 = (bf16[2,2,32,640]{3,2,1,0:T(8,128)(2,1)S(1)}, bf16[2,2,96,640]{3,2,1,0:T(8,128)(2,1)S(1)}) custom-call(bf16[96,1280]{1,0:T(8,128)(2,1)S(1)} %get-tuple-element.56.refs_0_, bf16[96,1280]{1,0:T(8,128)(2,1)S(1)} %collective-permute-done.refs_1_, bf16[112,1280]{1,0:T(8,128)(2,1)S(1)} %get-tuple-element.57.refs_2_.refs_1_.refs_8_, ...), custom_call_target="tpu_custom_call" | custom-call | tf_op jit(solution)/shard_map/pallas_call | solution.py:64
  34.9 0.0 collective-permute-done.2.refs_0_.refs_2_
  34.9 0.1 collective-permute-start.3
  35.0 0.8 collective-permute-done.8.refs_6_.refs_1_.refs_12_
  35.8 4.8 %collective-permute-done.6.refs_4_.refs_0_.refs_10_ = bf16[112,1280]{1,0:T(8,128)(2,1)S(1)} collective-permute-done((bf16[112,1280]{1,0:T(8,128)(2,1)S(1)}, bf16[112,1280]{1,0:T(8,128)(2,1)S(1)}, u32[]{:S(2)}, u32[]{:S(2)}) %collective-permute-start.6) | collective-permute-done | bytes 286752 | tf_op jit(solution)/shard_map/ppermute | solution.py:439
  40.5 1.7 %collective-permute-start.12 = (bf16[112,1280]{1,0:T(8,128)(2,1)S(1)}, bf16[112,1280]{1,0:T(8,128)(2,1)S(1)}, u32[]{:S(2)}, u32[]{:S(2)}) collective-permute-start(bf16[112,1280]{1,0:T(8,128)(2,1)S(1)} %collective-permute-done.8.refs_6_.refs_1_.refs_12_), channel_id=1, source_target_pairs={{0,96},{16,112},{32,0},{48,16},{64,32},{80,48},{96,64},{112,80},{1... | collective-permute-start | bytes 860168 | tf_op jit(solution)/shard_map/ppermute | solution.py:442
  42.3 0.2 collective-permute-start.5
  42.5 0.3 collective-permute-start.10
  42.8 1.0 collective-permute-done.5.refs_3_.refs_5_
  43.8 3.1 %shard_map.88 = (bf16[4,2,32,640]{3,2,1,0:T(8,128)(2,1)S(1)}, bf16[4,2,96,640]{3,2,1,0:T(8,128)(2,1)S(1)}) custom-call(bf16[96,1280]{1,0:T(8,128)(2,1)S(1)} %collective-permute-done.2.refs_0_.refs_2_, bf16[96,1280]{1,0:T(8,128)(2,1)S(1)} %collective-permute-done.3.refs_1_.refs_3_, bf16[96,1280]{1,0:T(8,128)(2,1)S(1)} %collective-permute-done.4.refs_2_.refs_4_, ...), custom_call_target="tpu_custom_call" | custom-call | tf_op jit(solution)/shard_map/pallas_call | solution.py:64
  46.9 0.0 copy-start.2
  46.9 2.9 %collective-permute-done.12.refs_2_.refs_0_.refs_14_ = bf16[112,1280]{1,0:T(8,128)(2,1)S(1)} collective-permute-done((bf16[112,1280]{1,0:T(8,128)(2,1)S(1)}, bf16[112,1280]{1,0:T(8,128)(2,1)S(1)}, u32[]{:S(2)}, u32[]{:S(2)}) %collective-permute-start.12) | collective-permute-done | bytes 286752 | tf_op jit(solution)/shard_map/ppermute | solution.py:442
  49.8 2.1 %collective-permute-done.10.refs_0_.refs_6_ = bf16[96,1280]{1,0:T(8,128)(2,1)S(1)} collective-permute-done((bf16[96,1280]{1,0:T(8,128)(2,1)S(1)}, bf16[96,1280]{1,0:T(8,128)(2,1)S(1)}, u32[]{:S(2)}, u32[]{:S(2)}) %collective-permute-start.10) | collective-permute-done | bytes 245792 | tf_op jit(solution)/shard_map/ppermute | solution.py:439
  51.9 1.5 %collective-permute-done.11.refs_1_.refs_7_ = bf16[96,1280]{1,0:T(8,128)(2,1)S(1)} collective-permute-done((bf16[96,1280]{1,0:T(8,128)(2,1)S(1)}, bf16[96,1280]{1,0:T(8,128)(2,1)S(1)}, u32[]{:S(2)}, u32[]{:S(2)}) %collective-permute-start.11) | collective-permute-done | bytes 245792 | tf_op jit(solution)/shard_map/ppermute | solution.py:445
  53.4 1.5 %shard_map.89 = (bf16[2,2,32,640]{3,2,1,0:T(8,128)(2,1)S(1)}, bf16[2,2,96,640]{3,2,1,0:T(8,128)(2,1)S(1)}) custom-call(bf16[96,1280]{1,0:T(8,128)(2,1)S(1)} %collective-permute-done.10.refs_0_.refs_6_, bf16[96,1280]{1,0:T(8,128)(2,1)S(1)} %collective-permute-done.11.refs_1_.refs_7_, bf16[112,1280]{1,0:T(8,128)(2,1)S(1)} %collective-permute-done.12.refs_2_.refs_0_.refs_14_, ...), custom_call_target="tpu_custom_call" | custom-call | tf_op jit(solution)/shard_map/pallas_call | solution.py:64
  54.9 0.7 shard_map.90
  55.6 0.0 copy-start.5
  55.6 0.4 collective-permute-start.14
  56.0 0.7 shard_map.91.own_ref
  56.7 0.8 collective-permute-done.14.got_ref
  57.5 0.1 shard_map.92
  57.6 0.3 copy.11
  57.8 16.3 %all_to_all.21.part_ref = bf16[64,2,1280]{2,1,0:T(2,128)(2,1)S(1)} all-to-all(bf16[64,2,1280]{2,1,0:T(2,128)(2,1)S(1)} %bitcast.20), channel_id=1, replica_groups={{0,1,2,3,4,5,6,7,8,9,10,11,12,13,14,15,32,33,34,35,36,37,38,39,40,41,42..., dimensions={0} | all-to-all | bytes 655360 | tf_op jit(solution)/shard_map/all_to_all | solution.py:454
  74.1 0.3 shard_map.93
  74.5 18.3 %all_to_all.22 = f32[64,2,1280]{2,1,0:T(2,128)S(1)} all-to-all(f32[64,2,1280]{2,1,0:T(2,128)S(1)} %shard_map.93), channel_id=1, replica_groups={{0,1,2,3,4,5,6,7,8,9,10,11,12,13,14,15,32,33,34,35,36,37,38,39,40,41,42..., dimensions={0} | all-to-all | bytes 1310720 | tf_op jit(solution)/shard_map/all_to_all | solution.py:454
  92.8 0.1 collective-permute-start.15
  92.9 2.1 %collective-permute-done.15.other_ref = f32[2,64,1280]{2,1,0:T(8,128)S(1)} collective-permute-done((f32[2,64,1280]{2,1,0:T(8,128)S(1)}, f32[2,64,1280]{2,1,0:T(8,128)S(1)}, u32[]{:S(2)}, u32[]{:S(2)}) %collective-permute-start.15) | collective-permute-done | bytes 655392 | tf_op jit(solution)/shard_map/ppermute | solution.py:445
  95.0 3.5 %shard_map.94 = (f32[2,128,1280]{2,1,0:T(8,128)S(1)}, bf16[8,32,1280]{2,1,0:T(8,128)(2,1)S(1)}, bf16[2,256,640]{2,1,0:T(8,128)(2,1)S(1)}) custom-call(f32[2,64,1280]{2,1,0:T(8,128)S(1)} %bitcast.12, f32[2,64,1280]{2,1,0:T(8,128)S(1)} %collective-permute-done.15.other_ref, bf16[2,640,1280]{2,1,0:T(8,128)(2,1)S(1)} %copy-done.2), custom_call_target="tpu_custom_call" | custom-call | tf_op jit(solution)/shard_map/pallas_call | solution.py:64
  98.5 1.5 %shard_map.95 = (bf16[2,2,96,640]{3,2,1,0:T(8,128)(2,1)S(1)}, bf16[192,1280]{1,0:T(8,128)(2,1)S(1)}, bf16[192,1280]{1,0:T(8,128)(2,1)S(1)}) custom-call(bf16[112,1280]{1,0:T(8,128)(2,1)S(1)} %collective-permute-done.13.refs_3_.refs_0_.refs_15_, bf16[112,1280]{1,0:T(8,128)(2,1)S(1)} %collective-permute-done.9.refs_7_.refs_1_.refs_13_, ...), custom_call_target="tpu_custom_call" | custom-call | tf_op jit(solution)/shard_map/pallas_call | solution.py:64
  100.0 0.2 collective-permute-start.17
  100.3 0.4 collective-permute-start.16
  100.6 1.5 %shard_map.96 = (bf16[2,2,96,640]{3,2,1,0:T(8,128)(2,1)S(1)}, bf16[192,1280]{1,0:T(8,128)(2,1)S(1)}, bf16[192,1280]{1,0:T(8,128)(2,1)S(1)}) custom-call(bf16[112,1280]{1,0:T(8,128)(2,1)S(1)} %collective-permute-done.12.refs_2_.refs_0_.refs_14_, bf16[112,1280]{1,0:T(8,128)(2,1)S(1)} %collective-permute-done.8.refs_6_.refs_1_.refs_12_, ...), custom_call_target="tpu_custom_call" | custom-call | tf_op jit(solution)/shard_map/pallas_call | solution.py:64
  102.2 0.1 shard_map.97
  102.3 0.4 collective-permute-done.16.got_ref
  102.7 0.1 shard_map.98
  102.8 1.5 %shard_map.99 = (bf16[2,2,96,640]{3,2,1,0:T(8,128)(2,1)S(1)}, bf16[192,1280]{1,0:T(8,128)(2,1)S(1)}, bf16[192,1280]{1,0:T(8,128)(2,1)S(1)}) custom-call(bf16[112,1280]{1,0:T(8,128)(2,1)S(1)} %collective-permute-done.7.refs_5_.refs_0_.refs_11_, bf16[112,1280]{1,0:T(8,128)(2,1)S(1)} %collective-permute-done.1.refs_3_.refs_1_.refs_9_, ...), custom_call_target="tpu_custom_call" | custom-call | tf_op jit(solution)/shard_map/pallas_call | solution.py:64
  104.3 0.2 collective-permute-start.18
  104.5 0.9 collective-permute-start.24
  105.4 1.2 collective-permute-start.20
  106.6 0.5 collective-permute-start.22
  107.1 0.0 collective-permute-start.19
  107.1 1.5 %shard_map.100 = (bf16[2,2,96,640]{3,2,1,0:T(8,128)(2,1)S(1)}, bf16[192,1280]{1,0:T(8,128)(2,1)S(1)}, bf16[192,1280]{1,0:T(8,128)(2,1)S(1)}) custom-call(bf16[112,1280]{1,0:T(8,128)(2,1)S(1)} %collective-permute-done.6.refs_4_.refs_0_.refs_10_, bf16[112,1280]{1,0:T(8,128)(2,1)S(1)} %get-tuple-element.57.refs_2_.refs_1_.refs_8_, ...), custom_call_target="tpu_custom_call" | custom-call | tf_op jit(solution)/shard_map/pallas_call | solution.py:64
  108.6 0.1 shard_map.101
  108.7 2.8 %collective-permute-start.23 = (bf16[96,1280]{1,0:T(8,128)(2,1)S(1)}, bf16[96,1280]{1,0:T(8,128)(2,1)S(1)}, u32[]{:S(2)}, u32[]{:S(2)}) collective-permute-start(bf16[96,1280]{1,0:T(8,128)(2,1)S(1)} %get-tuple-element.89), channel_id=1, source_target_pairs={{0,96},{16,112},{32,0},{48,16},{64,32},{80,48},{96,64},{112,80},{1... | collective-permute-start | bytes 737288 | tf_op jit(solution)/shard_map/ppermute | solution.py:442
  111.5 3.4 %shard_map.102 = f32[2,640,1280]{2,1,0:T(8,128)} custom-call(bf16[2,2,32,640]{3,2,1,0:T(8,128)(2,1)S(1)} %get-tuple-element.54.a_ref, bf16[4,2,32,640]{3,2,1,0:T(8,128)(2,1)S(1)} %get-tuple-element.59.b_ref, bf16[2,2,32,640]{3,2,1,0:T(8,128)(2,1)S(1)} %get-tuple-element.62.c_ref, bf16[8,32,1280]{2,1,0:T(8,128)(2,1)S(1)} %get-tuple-element.90.rows_ref), custom_call_target="tpu_custom_call" | custom-call | tf_op jit(solution)/shard_map/pallas_call | solution.py:375
  115.0 0.5 collective-permute-done.20
  115.5 0.1 add_convert_fusion.1
  115.5 0.1 collective-permute-start.21
  115.6 0.1 add_convert_fusion
  115.7 3.3 %collective-permute-start.25 = (bf16[96,1280]{1,0:T(8,128)(2,1)S(1)}, bf16[96,1280]{1,0:T(8,128)(2,1)S(1)}, u32[]{:S(2)}, u32[]{:S(2)}) collective-permute-start(bf16[96,1280]{1,0:T(8,128)(2,1)S(1)} %add_convert_fusion), channel_id=1, source_target_pairs={{0,96},{16,112},{32,0},{48,16},{64,32},{80,48},{96,64},{112,80},{1... | collective-permute-start | bytes 737288 | tf_op jit(solution)/shard_map/ppermute | solution.py:442
  119.0 5.6 %shard_map.103 = f32[2,1280,640]{2,1,0:T(8,128)} custom-call(bf16[96,1280]{1,0:T(8,128)(2,1)S(1)} %get-tuple-element.56.refs_0_, bf16[96,1280]{1,0:T(8,128)(2,1)S(1)} %collective-permute-done.refs_1_, bf16[96,1280]{1,0:T(8,128)(2,1)S(1)} %collective-permute-done.2.refs_0_.refs_2_, bf16[96,1280]{1,0:T(8,128)(2,1)S(1)} %collective-permute-done.3.refs_1_.refs_3_, ...), custom_call_target="tpu_custom_call" | custom-call | tf_op jit(solution)/shard_map/pallas_call | solution.py:349
  124.6 0.5 collective-permute-done.21.la_ref
  125.1 0.5 shard_map.104
  125.6 15.4 %all_to_all.23.back_ref = bf16[16,16,1280]{2,1,0:T(8,128)(2,1)S(1)} all-to-all(bf16[16,16,1280]{2,1,0:T(8,128)(2,1)S(1)} %shard_map.104), channel_id=1, replica_groups=mesh['dp'=8,'expert'=16] {'expert'}, dimensions={0} | all-to-all | bytes 1310720 | tf_op jit(solution)/shard_map/all_to_all | solution.py:451
  141.1 1.6 %shard_map.105 = bf16[128,1280]{1,0:T(8,128)(2,1)} custom-call(s32[2,64]{1,0:T(2,128)S(1)} %bitcast.17, s32[2,64]{1,0:T(2,128)S(1)} %bitcast.19, bf16[128,1280]{1,0:T(8,128)(2,1)S(1)} %bitcast.14, f32[1280]{0:T(1024)S(1)} %copy-done.4, f32[2,128,1280]{2,1,0:T(8,128)S(1)} %get-tuple-element.66.grads, bf16[16,16,1280]{2,1,0:T(8,128)(2,1)S(1)} %all_to_all.23.back_ref), custom_call_target="tpu_custom_call" | custom-call | tf_op jit(solution)/shard_map/pallas_call | solution.py:64
  (33 shorter events, 0.1 us)
Async XLA Ops:
  23.6 4.6 %collective-permute-start.1 = (bf16[112,1280]{1,0:T(8,128)(2,1)S(1)}, bf16[112,1280]{1,0:T(8,128)(2,1)S(1)}, u32[]{:S(2)}, u32[]{:S(2)}) collective-permute-start(bf16[112,1280]{1,0:T(8,128)(2,1)S(1)} %get-tuple-element.57.refs_2_.refs_1_.refs_8_), channel_id=1, source_target_pairs={{0,16},{16,0},{32,48},{48,32},{64,80},{80,64},{96,112},{112,96},{1... | collective-permute-start | bytes 860168 | tf_op jit(solution)/shard_map/ppermute | solution.py:445
  23.7 4.5 %collective-permute-start = (bf16[96,1280]{1,0:T(8,128)(2,1)S(1)}, bf16[96,1280]{1,0:T(8,128)(2,1)S(1)}, u32[]{:S(2)}, u32[]{:S(2)}) collective-permute-start(bf16[96,1280]{1,0:T(8,128)(2,1)S(1)} %get-tuple-element.56.refs_0_), channel_id=1, source_target_pairs={{0,16},{16,0},{32,48},{48,32},{64,80},{80,64},{96,112},{112,96},{1... | collective-permute-start | bytes 737288 | tf_op jit(solution)/shard_map/ppermute | solution.py:445
  24.2 10.8 %collective-permute-start.2 = (bf16[96,1280]{1,0:T(8,128)(2,1)S(1)}, bf16[96,1280]{1,0:T(8,128)(2,1)S(1)}, u32[]{:S(2)}, u32[]{:S(2)}) collective-permute-start(bf16[96,1280]{1,0:T(8,128)(2,1)S(1)} %get-tuple-element.56.refs_0_), channel_id=1, source_target_pairs={{0,32},{16,48},{32,64},{48,80},{64,96},{80,112},{96,0},{112,16},{1... | collective-permute-start | bytes 737288 | tf_op jit(solution)/shard_map/ppermute | solution.py:439
  26.1 9.7 %collective-permute-start.8 = (bf16[112,1280]{1,0:T(8,128)(2,1)S(1)}, bf16[112,1280]{1,0:T(8,128)(2,1)S(1)}, u32[]{:S(2)}, u32[]{:S(2)}) collective-permute-start(bf16[112,1280]{1,0:T(8,128)(2,1)S(1)} %get-tuple-element.57.refs_2_.refs_1_.refs_8_), channel_id=1, source_target_pairs={{0,96},{16,112},{32,0},{48,16},{64,32},{80,48},{96,64},{112,80},{1... | collective-permute-start | bytes 860168 | tf_op jit(solution)/shard_map/ppermute | solution.py:442
  28.2 12.3 %collective-permute-start.6 = (bf16[112,1280]{1,0:T(8,128)(2,1)S(1)}, bf16[112,1280]{1,0:T(8,128)(2,1)S(1)}, u32[]{:S(2)}, u32[]{:S(2)}) collective-permute-start(bf16[112,1280]{1,0:T(8,128)(2,1)S(1)} %get-tuple-element.57.refs_2_.refs_1_.refs_8_), channel_id=1, source_target_pairs={{0,32},{16,48},{32,64},{48,80},{64,96},{80,112},{96,0},{112,16},{1... | collective-permute-start | bytes 860168 | tf_op jit(solution)/shard_map/ppermute | solution.py:439
  28.2 14.1 %collective-permute-start.4 = (bf16[96,1280]{1,0:T(8,128)(2,1)S(1)}, bf16[96,1280]{1,0:T(8,128)(2,1)S(1)}, u32[]{:S(2)}, u32[]{:S(2)}) collective-permute-start(bf16[96,1280]{1,0:T(8,128)(2,1)S(1)} %get-tuple-element.56.refs_0_), channel_id=1, source_target_pairs={{0,96},{16,112},{32,0},{48,16},{64,32},{80,48},{96,64},{112,80},{1... | collective-permute-start | bytes 737288 | tf_op jit(solution)/shard_map/ppermute | solution.py:442
  31.4 1.9 %copy-start = (bf16[2,1280,640]{2,1,0:T(8,128)(2,1)S(1)}, bf16[2,1280,640]{2,1,0:T(8,128)(2,1)}, u32[]{:S(2)}) copy-start(bf16[2,1280,640]{2,1,0:T(8,128)(2,1)} %refs_5_.7) | copy-start | bytes 9830404
  33.4 10.4 %copy-start.1 = (bf16[2,1280,640]{2,1,0:T(8,128)(2,1)S(1)}, bf16[2,1280,640]{2,1,0:T(8,128)(2,1)}, u32[]{:S(2)}) copy-start(bf16[2,1280,640]{2,1,0:T(8,128)(2,1)} %refs_5_.7) | copy-start | bytes 9830404
  34.9 7.6 %collective-permute-start.3 = (bf16[96,1280]{1,0:T(8,128)(2,1)S(1)}, bf16[96,1280]{1,0:T(8,128)(2,1)S(1)}, u32[]{:S(2)}, u32[]{:S(2)}) collective-permute-start(bf16[96,1280]{1,0:T(8,128)(2,1)S(1)} %collective-permute-done.2.refs_0_.refs_2_), channel_id=1, source_target_pairs={{0,16},{16,0},{32,48},{48,32},{64,80},{80,64},{96,112},{112,96},{1... | collective-permute-start | bytes 737288 | tf_op jit(solution)/shard_map/ppermute | solution.py:445
  35.8 7.0 %collective-permute-start.9 = (bf16[112,1280]{1,0:T(8,128)(2,1)S(1)}, bf16[112,1280]{1,0:T(8,128)(2,1)S(1)}, u32[]{:S(2)}, u32[]{:S(2)}) collective-permute-start(bf16[112,1280]{1,0:T(8,128)(2,1)S(1)} %collective-permute-done.8.refs_6_.refs_1_.refs_12_), channel_id=1, source_target_pairs={{0,16},{16,0},{32,48},{48,32},{64,80},{80,64},{96,112},{112,96},{1... | collective-permute-start | bytes 860168 | tf_op jit(solution)/shard_map/ppermute | solution.py:445
  40.5 3.3 %collective-permute-start.7 = (bf16[112,1280]{1,0:T(8,128)(2,1)S(1)}, bf16[112,1280]{1,0:T(8,128)(2,1)S(1)}, u32[]{:S(2)}, u32[]{:S(2)}) collective-permute-start(bf16[112,1280]{1,0:T(8,128)(2,1)S(1)} %collective-permute-done.6.refs_4_.refs_0_.refs_10_), channel_id=1, source_target_pairs={{0,16},{16,0},{32,48},{48,32},{64,80},{80,64},{96,112},{112,96},{1... | collective-permute-start | bytes 860168 | tf_op jit(solution)/shard_map/ppermute | solution.py:445
  40.5 9.2 %collective-permute-start.12 = (bf16[112,1280]{1,0:T(8,128)(2,1)S(1)}, bf16[112,1280]{1,0:T(8,128)(2,1)S(1)}, u32[]{:S(2)}, u32[]{:S(2)}) collective-permute-start(bf16[112,1280]{1,0:T(8,128)(2,1)S(1)} %collective-permute-done.8.refs_6_.refs_1_.refs_12_), channel_id=1, source_target_pairs={{0,96},{16,112},{32,0},{48,16},{64,32},{80,48},{96,64},{112,80},{1... | collective-permute-start | bytes 860168 | tf_op jit(solution)/shard_map/ppermute | solution.py:442
  42.3 1.5 %collective-permute-start.5 = (bf16[96,1280]{1,0:T(8,128)(2,1)S(1)}, bf16[96,1280]{1,0:T(8,128)(2,1)S(1)}, u32[]{:S(2)}, u32[]{:S(2)}) collective-permute-start(bf16[96,1280]{1,0:T(8,128)(2,1)S(1)} %collective-permute-done.4.refs_2_.refs_4_), channel_id=1, source_target_pairs={{0,16},{16,0},{32,48},{48,32},{64,80},{80,64},{96,112},{112,96},{1... | collective-permute-start | bytes 737288 | tf_op jit(solution)/shard_map/ppermute | solution.py:445
  42.5 9.4 %collective-permute-start.10 = (bf16[96,1280]{1,0:T(8,128)(2,1)S(1)}, bf16[96,1280]{1,0:T(8,128)(2,1)S(1)}, u32[]{:S(2)}, u32[]{:S(2)}) collective-permute-start(bf16[96,1280]{1,0:T(8,128)(2,1)S(1)} %collective-permute-done.2.refs_0_.refs_2_), channel_id=1, source_target_pairs={{0,32},{16,48},{32,64},{48,80},{64,96},{80,112},{96,0},{112,16},{1... | collective-permute-start | bytes 737288 | tf_op jit(solution)/shard_map/ppermute | solution.py:439
  46.9 8.0 %copy-start.2 = (bf16[2,640,1280]{2,1,0:T(8,128)(2,1)S(1)}, bf16[2,640,1280]{2,1,0:T(8,128)(2,1)}, u32[]{:S(2)}) copy-start(bf16[2,640,1280]{2,1,0:T(8,128)(2,1)} %w_out.4) | copy-start | bytes 9830404
  49.8 3.6 %collective-permute-start.13 = (bf16[112,1280]{1,0:T(8,128)(2,1)S(1)}, bf16[112,1280]{1,0:T(8,128)(2,1)S(1)}, u32[]{:S(2)}, u32[]{:S(2)}) collective-permute-start(bf16[112,1280]{1,0:T(8,128)(2,1)S(1)} %collective-permute-done.12.refs_2_.refs_0_.refs_14_), channel_id=1, source_target_pairs={{0,16},{16,0},{32,48},{48,32},{64,80},{80,64},{96,112},{112,96},{1... | collective-permute-start | bytes 860168 | tf_op jit(solution)/shard_map/ppermute | solution.py:445
  51.9 1.5 %collective-permute-start.11 = (bf16[96,1280]{1,0:T(8,128)(2,1)S(1)}, bf16[96,1280]{1,0:T(8,128)(2,1)S(1)}, u32[]{:S(2)}, u32[]{:S(2)}) collective-permute-start(bf16[96,1280]{1,0:T(8,128)(2,1)S(1)} %collective-permute-done.10.refs_0_.refs_6_), channel_id=1, source_target_pairs={{0,16},{16,0},{32,48},{48,32},{64,80},{80,64},{96,112},{112,96},{1... | collective-permute-start | bytes 737288 | tf_op jit(solution)/shard_map/ppermute | solution.py:445
  55.6 18.5 %copy-start.5 = (f32[2,1280]{1,0:T(2,128)S(1)}, f32[2,1280]{1,0:T(2,128)}, u32[]{:S(2)}) copy-start(f32[2,1280]{1,0:T(2,128)} %get-tuple-element.65.sum_ref) | copy-start | bytes 30724
  55.6 1.9 %collective-permute-start.14 = (bf16[4,32,1280]{2,1,0:T(8,128)(2,1)S(1)}, bf16[4,32,1280]{2,1,0:T(8,128)(2,1)S(1)}, u32[]{:S(2)}, u32[]{:S(2)}) collective-permute-start(bf16[4,32,1280]{2,1,0:T(8,128)(2,1)S(1)} %shard_map.90), channel_id=1, source_target_pairs={{0,16},{16,0},{32,48},{48,32},{64,80},{80,64},{96,112},{112,96},{1... | collective-permute-start | bytes 983048 | tf_op jit(solution)/shard_map/ppermute | solution.py:445
  92.8 2.2 %collective-permute-start.15 = (f32[2,64,1280]{2,1,0:T(8,128)S(1)}, f32[2,64,1280]{2,1,0:T(8,128)S(1)}, u32[]{:S(2)}, u32[]{:S(2)}) collective-permute-start(f32[2,64,1280]{2,1,0:T(8,128)S(1)} %bitcast.11), channel_id=1, source_target_pairs={{0,16},{16,0},{32,48},{48,32},{64,80},{80,64},{96,112},{112,96},{1... | collective-permute-start | bytes 1966088 | tf_op jit(solution)/shard_map/ppermute | solution.py:445
  100.0 2.1 %collective-permute-start.17 = (bf16[192,1280]{1,0:T(8,128)(2,1)S(1)}, bf16[192,1280]{1,0:T(8,128)(2,1)S(1)}, u32[]{:S(2)}, u32[]{:S(2)}) collective-permute-start(bf16[192,1280]{1,0:T(8,128)(2,1)S(1)} %get-tuple-element.71), channel_id=1, source_target_pairs={{0,16},{16,0},{32,48},{48,32},{64,80},{80,64},{96,112},{112,96},{1... | collective-permute-start | bytes 1474568 | tf_op jit(solution)/shard_map/ppermute | solution.py:445
  100.3 2.4 %collective-permute-start.16 = (bf16[192,1280]{1,0:T(8,128)(2,1)S(1)}, bf16[192,1280]{1,0:T(8,128)(2,1)S(1)}, u32[]{:S(2)}, u32[]{:S(2)}) collective-permute-start(bf16[192,1280]{1,0:T(8,128)(2,1)S(1)} %get-tuple-element.74), channel_id=1, source_target_pairs={{0,16},{16,0},{32,48},{48,32},{64,80},{80,64},{96,112},{112,96},{1... | collective-permute-start | bytes 1474568 | tf_op jit(solution)/shard_map/ppermute | solution.py:445
  104.3 4.2 %collective-permute-start.18 = (bf16[192,1280]{1,0:T(8,128)(2,1)S(1)}, bf16[192,1280]{1,0:T(8,128)(2,1)S(1)}, u32[]{:S(2)}, u32[]{:S(2)}) collective-permute-start(bf16[192,1280]{1,0:T(8,128)(2,1)S(1)} %get-tuple-element.80), channel_id=1, source_target_pairs={{0,16},{16,0},{32,48},{48,32},{64,80},{80,64},{96,112},{112,96},{1... | collective-permute-start | bytes 1474568 | tf_op jit(solution)/shard_map/ppermute | solution.py:445
  104.5 10.4 %collective-permute-start.24 = (bf16[96,1280]{1,0:T(8,128)(2,1)S(1)}, bf16[96,1280]{1,0:T(8,128)(2,1)S(1)}, u32[]{:S(2)}, u32[]{:S(2)}) collective-permute-start(bf16[96,1280]{1,0:T(8,128)(2,1)S(1)} %get-tuple-element.97), channel_id=1, source_target_pairs={{0,96},{16,112},{32,0},{48,16},{64,32},{80,48},{96,64},{112,80},{1... | collective-permute-start | bytes 737288 | tf_op jit(solution)/shard_map/ppermute | solution.py:442
  105.4 10.0 %collective-permute-start.20 = (bf16[96,1280]{1,0:T(8,128)(2,1)S(1)}, bf16[96,1280]{1,0:T(8,128)(2,1)S(1)}, u32[]{:S(2)}, u32[]{:S(2)}) collective-permute-start(bf16[96,1280]{1,0:T(8,128)(2,1)S(1)} %get-tuple-element.76), channel_id=1, source_target_pairs={{0,32},{16,48},{32,64},{48,80},{64,96},{80,112},{96,0},{112,16},{1... | collective-permute-start | bytes 737288 | tf_op jit(solution)/shard_map/ppermute | solution.py:439
  106.6 18.0 %collective-permute-start.22 = (bf16[96,1280]{1,0:T(8,128)(2,1)S(1)}, bf16[96,1280]{1,0:T(8,128)(2,1)S(1)}, u32[]{:S(2)}, u32[]{:S(2)}) collective-permute-start(bf16[96,1280]{1,0:T(8,128)(2,1)S(1)} %get-tuple-element.95), channel_id=1, source_target_pairs={{0,32},{16,48},{32,64},{48,80},{64,96},{80,112},{96,0},{112,16},{1... | collective-permute-start | bytes 737288 | tf_op jit(solution)/shard_map/ppermute | solution.py:439
  107.1 17.5 %collective-permute-start.19 = (bf16[192,1280]{1,0:T(8,128)(2,1)S(1)}, bf16[192,1280]{1,0:T(8,128)(2,1)S(1)}, u32[]{:S(2)}, u32[]{:S(2)}) collective-permute-start(bf16[192,1280]{1,0:T(8,128)(2,1)S(1)} %get-tuple-element.93), channel_id=1, source_target_pairs={{0,16},{16,0},{32,48},{48,32},{64,80},{80,64},{96,112},{112,96},{1... | collective-permute-start | bytes 1474568 | tf_op jit(solution)/shard_map/ppermute | solution.py:445
  108.7 15.9 %collective-permute-start.23 = (bf16[96,1280]{1,0:T(8,128)(2,1)S(1)}, bf16[96,1280]{1,0:T(8,128)(2,1)S(1)}, u32[]{:S(2)}, u32[]{:S(2)}) collective-permute-start(bf16[96,1280]{1,0:T(8,128)(2,1)S(1)} %get-tuple-element.89), channel_id=1, source_target_pairs={{0,96},{16,112},{32,0},{48,16},{64,32},{80,48},{96,64},{112,80},{1... | collective-permute-start | bytes 737288 | tf_op jit(solution)/shard_map/ppermute | solution.py:442
  115.5 9.6 %collective-permute-start.21 = (bf16[96,1280]{1,0:T(8,128)(2,1)S(1)}, bf16[96,1280]{1,0:T(8,128)(2,1)S(1)}, u32[]{:S(2)}, u32[]{:S(2)}) collective-permute-start(bf16[96,1280]{1,0:T(8,128)(2,1)S(1)} %add_convert_fusion.1), channel_id=1, source_target_pairs={{0,32},{16,48},{32,64},{48,80},{64,96},{80,112},{96,0},{112,16},{1... | collective-permute-start | bytes 737288 | tf_op jit(solution)/shard_map/ppermute | solution.py:439
  115.7 9.5 %collective-permute-start.25 = (bf16[96,1280]{1,0:T(8,128)(2,1)S(1)}, bf16[96,1280]{1,0:T(8,128)(2,1)S(1)}, u32[]{:S(2)}, u32[]{:S(2)}) collective-permute-start(bf16[96,1280]{1,0:T(8,128)(2,1)S(1)} %add_convert_fusion), channel_id=1, source_target_pairs={{0,96},{16,112},{32,0},{48,16},{64,32},{80,48},{96,64},{112,80},{1... | collective-permute-start | bytes 737288 | tf_op jit(solution)/shard_map/ppermute | solution.py:442
  124.6 16.5 %copy-start.3 = (bf16[1,2,64,1280]{3,2,1,0:T(8,128)(2,1)S(1)}, bf16[1,2,64,1280]{3,2,1,0:T(8,128)(2,1)}, u32[]{:S(2)}) copy-start(bf16[1,2,64,1280]{3,2,1,0:T(8,128)(2,1)} %param.6) | copy-start | bytes 983044
  124.6 16.5 %copy-start.4 = (f32[1280]{0:T(1024)S(1)}, f32[1280]{0:T(1024)}, u32[]{:S(2)}) copy-start(f32[1280]{0:T(1024)} %gain.3) | copy-start | bytes 15364
  124.6 16.5 %copy-start.6 = (s32[1,2,64]{2,1,0:T(2,128)S(1)}, s32[1,2,64]{2,1,0:T(2,128)}, u32[]{:S(2)}) copy-start(s32[1,2,64]{2,1,0:T(2,128)} %param.7) | copy-start | bytes 1540
  124.6 16.5 %copy-start.7 = (s32[1,2,64]{2,1,0:T(2,128)S(1)}, s32[1,2,64]{2,1,0:T(2,128)}, u32[]{:S(2)}) copy-start(s32[1,2,64]{2,1,0:T(2,128)} %param.8) | copy-start | bytes 1540

commit v6 on v5

--- a/solution.py
+++ b/solution.py
@@ -20,7 +20,7 @@
 PAD = 16
 PEERS = 16
 HALF = PEERS * CAP
-KIND_ROWS = 16
+KIND_ROWS = 8
 POOLED = 2 * PEERS
 PAIR_TOKENS = 64
 LANES = 128
@@ -55,7 +55,11 @@
     return jnp.where(hit, 1.0, 0.0).astype(bf16)
 
 
-def call(kernel, out, args, smem=(), hbm=(), scratch=(), vmem=14, cost=None):
+FREE = pl.CostEstimate(flops=1, bytes_accessed=1, transcendentals=0)
+DEAR = pl.CostEstimate(flops=10**11, bytes_accessed=10**8, transcendentals=0)
+
+
+def call(kernel, out, args, smem=(), hbm=(), scratch=(), vmem=14, cost=FREE):
     def space(k):
         return pltpu.SMEM if k in smem else pltpu.HBM if k in hbm else pltpu.VMEM
 
@@ -110,26 +114,27 @@
 
 def dispatch_kernel(ids, slots, toks, gain, out_ref, sum_ref, ids_ref, slots_ref, tok_ref, gain_ref, sems):
     copies = fetch((ids, slots, toks, gain), (ids_ref, slots_ref, tok_ref, gain_ref), sems)
-    for copy in copies:
-        copy.wait()
+    copies[0].wait()
+    copies[1].wait()
     pos = places(ids_ref, slots_ref)
-    tokens = pos.shape[1]
-    x = tok_ref[...].astype(f32)
-    normed = normal_parts(x)[0] * gain_ref[...].reshape(1, -1)
-    normed = normed.astype(bf16)
-    sent = nn(slot_table(pos), normed)
+    tokens, width = tok_ref.shape
+    table = slot_table(pos)
     row = iota((PEERS * PAD, tokens), 0)
     goes = one_hot((row % PAD == GROUP) & (pos // GROUP == row // PAD))
     place = pos % GROUP
-    column = (place // CAP) * 128 + lax.axis_index("expert") * CAP + place % CAP
-    lane = iota((2 * 128, tokens), 0)
-    kind = jnp.where(iota((2 * 128, tokens), 1) < tokens // 2, 1.0, 2.0)
+    column = (place // CAP) * LANES + lax.axis_index("expert") * CAP + place % CAP
+    lane = iota((2 * LANES, tokens), 0)
+    kind = jnp.where(iota((2 * LANES, tokens), 1) < tokens // 2, 1.0, 2.0)
     kinds = nt(goes, jnp.where(lane == column, kind, 0.0).astype(bf16))
-    width = sent.shape[1]
-    first = sent[:, : 2 * 128] + kinds
-    out_ref[:, :, : 2 * 128] = first.astype(bf16).reshape(PEERS, PAD, 2 * 128)
-    out_ref[:, :, 2 * 128 :] = sent[:, 2 * 128 :].astype(bf16).reshape(
-        PEERS, PAD, width - 2 * 128
+    copies[2].wait()
+    copies[3].wait()
+    x = tok_ref[...].astype(f32)
+    normed = normal_parts(x)[0] * gain_ref[...].reshape(1, -1)
+    sent = nn(table, normed.astype(bf16))
+    first = sent[:, : 2 * LANES] + kinds
+    out_ref[:, :, : 2 * LANES] = first.astype(bf16).reshape(PEERS, PAD, 2 * LANES)
+    out_ref[:, :, 2 * LANES :] = sent[:, 2 * LANES :].astype(bf16).reshape(
+        PEERS, PAD, width - 2 * LANES
     )
     sum_ref[0:1, :] = jnp.sum(x[: tokens // 2], axis=0, keepdims=True)
     sum_ref[1:2, :] = jnp.sum(x[tokens // 2 :], axis=0, keepdims=True)
@@ -147,35 +152,34 @@
     return one_hot(hit)
 
 
-def repack_kernel(in_ref, first_ref, second_ref):
+def repack_kernel(in_ref, out_ref):
     width = in_ref.shape[2]
-    rows = 2 * HALF + KIND_ROWS
-    out = nn(repack_table(rows, False), in_ref[...].reshape(PEERS * PAD, width)).astype(bf16)
-    first_ref[...] = out[:HALF]
-    second_ref[...] = out[HALF:]
+    table = repack_table(out_ref.shape[0], False)
+    out_ref[...] = nn(table, in_ref[...].reshape(PEERS * PAD, width)).astype(bf16)
 
 
 def pool_table(seconds, held, wide_ref):
-    count = len(seconds)
     wide_ref[...] = jnp.zeros_like(wide_ref)
     q = iota((POOLED, LANES), 0)
     r = iota((POOLED, LANES), 1)
-    for k in range(count):
-        kinds = seconds[k][HALF : HALF + KIND_ROWS, held * LANES : (held + 1) * LANES]
+    for k, ref in enumerate(seconds):
+        kinds = ref[2 * HALF : 2 * HALF + KIND_ROWS, held * LANES : (held + 1) * LANES]
         kinds = kinds.astype(f32)[:1]
         hit = (q % PEERS == r // CAP) & (kinds == (q // PEERS + 1).astype(f32)) & (r < HALF)
         wide_ref[k * POOLED : (k + 1) * POOLED, k * LANES : (k + 1) * LANES] = one_hot(hit)
 
 
-def forward_kernel(count, *refs):
-    halves = refs[:count], refs[count : 2 * count]
-    w_in, pooled_ref, slope_ref, wide_ref, act_ref = refs[2 * count :]
+def forward_kernel(*refs):
+    blocks = refs[:-5]
+    count = len(blocks)
+    w_in, pooled_ref, slope_ref, wide_ref, act_ref = refs[-5:]
     c0 = math.sqrt(2.0 / math.pi)
     c1 = c0 * 0.044715
     hidden = w_in.shape[2]
     for held in range(HELD):
-        pool_table(halves[1], held, wide_ref)
-        rows = jnp.concatenate([ref[:HALF, :] for ref in halves[held]], axis=0)
+        pool_table(blocks, held, wide_ref)
+        rows = [block[held * HALF : (held + 1) * HALF, :] for block in blocks]
+        rows = jnp.concatenate(rows, axis=0)
         for at in range(0, hidden, 256):
             to = slice(at, min(at + 256, hidden))
             full = nn(rows, w_in[held, :, to])
@@ -197,16 +201,16 @@
             pooled_ref[k, held] = pooled[k * POOLED : (k + 1) * POOLED]
 
 
-def forward(firsts, seconds, w_in):
-    count = len(firsts)
+def forward(arrays, w_in):
+    count = len(arrays)
     hidden = w_in.shape[2]
     return call(
-        functools.partial(forward_kernel, count),
+        forward_kernel,
         [
             shape_of(count, HELD, POOLED, hidden),
             shape_of(count, HELD, HALF, hidden),
         ],
-        [*firsts, *seconds, w_in],
+        [*arrays, w_in],
         scratch=[
             pltpu.VMEM((count * POOLED, count * LANES), bf16),
             pltpu.VMEM((count * LANES, hidden), bf16),
@@ -214,20 +218,31 @@
     )
 
 
+def pick_kernel(x2_ref, x4_ref, first_ref, second_ref):
+    first_ref[...] = x2_ref[:HALF, :]
+    second_ref[...] = x4_ref[HALF:, :]
+
+
+def stack_kernel(first_ref, second_ref, out_ref):
+    out_ref[:HALF, :] = first_ref[...]
+    out_ref[HALF:, :] = second_ref[...]
+
+
+PARTS = {0: (0, 0), 1: (1, 0), 2: (1, 1), 4: (1, 2), 3: (2, 0), 5: (2, 1), 6: (3, 0), 7: (3, 1)}
+
+
 def part_of(parts, k):
-    if k < 2:
-        return parts[0], k
-    if k < 6:
-        return parts[1], k - 2
-    return parts[2], k - 6
-
-
-def out_kernel(shift, a_ref, b_ref, c_ref, w_out, out_ref):
+    which, at = PARTS[k]
+    return parts[which], at
+
+
+def out_kernel(shift, *refs):
+    parts, (w_out, out_ref) = refs[:4], refs[4:]
     total = None
     for held in range(HELD):
         rows = []
         for k in AROUND:
-            ref, at = part_of((a_ref, b_ref, c_ref), k + shift)
+            ref, at = part_of(parts, k + shift)
             rows.append(ref[at, held])
         part = nn(jnp.concatenate(rows, axis=0), w_out[held])
         total = part if total is None else total + part
@@ -257,7 +272,8 @@
     text = jnp.concatenate([own_ref[1], other_ref[1]], axis=0)
     pairs, width = image.shape
     scale = PAIR_TOKENS / math.sqrt(width)
-    logits = scale * nt(image, text, lax.Precision.HIGHEST)
+    (i0, i1), (t0, t1) = split(image), split(text)
+    logits = scale * (nt(i0, t0) + (nt(i0, t1) + nt(i1, t0)))
 
     def softmax(axis):
         top = jnp.exp(logits - jnp.max(logits, axis=axis, keepdims=True))
@@ -266,12 +282,12 @@
     same = jnp.where(iota((pairs, pairs), 0) == iota((pairs, pairs), 1), 2.0, 0.0)
     grad_logits = (objective_scale * scale / PAIR_TOKENS) * (softmax(1) + softmax(0) - same)
 
-    def thrice(g, x):
-        (g0, g1), (x0, x1) = split(g), split(x)
+    def thrice(g, x0, x1):
+        g0, g1 = split(g)
         return nn(g0, x0) + (nn(g0, x1) + nn(g1, x0))
 
-    grad_image = thrice(grad_logits, text)
-    grad_text = thrice(grad_logits.T, image)
+    grad_image = thrice(grad_logits, t0, t1)
+    grad_text = thrice(grad_logits.T, i0, i1)
     grad_ref[0] = grad_image
     grad_ref[1] = grad_text
     gi_ref[...] = grad_image.astype(bf16)
@@ -291,8 +307,7 @@
     count = len(blocks)
     seconds, slopes = refs[:count], refs[count : 2 * count]
     prod_ref, w_in, pre_ref = refs[2 * count : 2 * count + 3]
-    outs = refs[2 * count + 3 : 3 * count + 3]
-    wide_ref, prods_ref = refs[3 * count + 3 :]
+    outs, (wide_ref, prods_ref) = refs[2 * count + 3 : -2], refs[-2:]
     for held in range(HELD):
         pool_table(seconds, held, wide_ref)
         for k, block in enumerate(blocks):
@@ -301,22 +316,28 @@
             ]
         grad_act = tn(wide_ref[...], prods_ref[...])
         for k, block in enumerate(blocks):
-            slope = slopes[k][part_of((None,) * 3, block)[1], held].astype(f32)
+            slope = slopes[k][PARTS[block][1], held].astype(f32)
             pre_ref[k, held] = (grad_act[k * LANES : k * LANES + HALF] * slope).astype(bf16)
         pre = jnp.concatenate([pre_ref[k, held] for k in range(count)], axis=0)
         part = nt(pre, w_in[held]).astype(bf16)
         for k in range(count):
-            outs[k][held * HALF : (held + 1) * HALF, :] = part[k * HALF : (k + 1) * HALF]
-
-
-def backward(blocks, seconds, made, prod, w_in):
+            rows = part[k * HALF : (k + 1) * HALF]
+            outs[k // 2][k % 2, held * HALF : (held + 1) * HALF, :] = rows
+
+
+def backward(blocks, rows, made, prod, w_in):
     count = len(blocks)
     width, hidden = w_in.shape[1:]
-    of = [part_of(made, block)[0] for block in blocks]
     return call(
         functools.partial(backward_kernel, blocks),
-        [shape_of(count, HELD, HALF, hidden)] + [shape_of(2 * HALF, width)] * count,
-        [*[seconds[block] for block in blocks], *[m[1] for m in of], prod, w_in],
+        [shape_of(count, HELD, HALF, hidden)]
+        + [shape_of(2, 2 * HALF, width)] * (count // 2),
+        [
+            *[rows[block] for block in blocks],
+            *[made[PARTS[block][0]][1] for block in blocks],
+            prod,
+            w_in,
+        ],
         scratch=[
             pltpu.VMEM((count * POOLED, count * LANES), bf16),
             pltpu.VMEM((count * POOLED, hidden), bf16),
@@ -324,18 +345,18 @@
     )
 
 
-PAIRED = {7: (0, 0), 5: (0, 1), 6: (1, 0), 4: (1, 1), 3: (2, 0), 1: (2, 1), 2: (3, 0), 0: (3, 1)}
+PAIRED = {7: (0, 0), 5: (0, 1), 6: (1, 0), 4: (1, 1), 3: (2, 0), 1: (2, 1), 2: (2, 2), 0: (2, 3)}
 
 
 def grad_in_kernel(*refs):
-    blocks, pres = refs[:16], refs[16:20]
-    out_ref, x_ref, p_ref = refs[20:]
+    rows, pres = refs[:8], refs[8:11]
+    out_ref, x_ref, p_ref = refs[11:]
     held = pl.program_id(0)
 
     def fill(which):
         for k in range(8):
             span = slice(k * HALF, (k + 1) * HALF)
-            x_ref[span, :] = blocks[8 * which + k][:HALF, :]
+            x_ref[span, :] = rows[k][which * HALF : (which + 1) * HALF, :]
             pair, at = PAIRED[k]
             p_ref[span, :] = pres[pair][at, which]
 
@@ -344,28 +365,30 @@
     out_ref[0] = tn(x_ref[...], p_ref[...])
 
 
-def grad_in(firsts, seconds, pres, width, hidden):
+def grad_in(rows, pres, width, hidden):
     whole = pl.BlockSpec(memory_space=pltpu.VMEM)
     return pl.pallas_call(
         grad_in_kernel,
         grid=(HELD,),
         out_shape=shape_of(HELD, width, hidden, dtype=f32),
-        in_specs=[whole] * 20,
+        in_specs=[whole] * 11,
         out_specs=pl.BlockSpec((1, width, hidden), lambda i: (i, 0, 0)),
         scratch_shapes=[
             pltpu.VMEM((8 * HALF, width), bf16),
             pltpu.VMEM((8 * HALF, hidden), bf16),
         ],
         compiler_params=pltpu.CompilerParams(vmem_limit_bytes=26 * 1024 * 1024),
-    )(*firsts, *seconds, *pres)
-
-
-def grad_out_kernel(a_ref, b_ref, c_ref, rows_ref, out_ref):
+        cost_estimate=FREE,
+    )(*rows, *pres)
+
+
+def grad_out_kernel(*refs):
+    parts, (rows_ref, out_ref) = refs[:4], refs[4:]
     held = pl.program_id(0)
     width = rows_ref.shape[2]
     pooled = []
     for k in range(8):
-        ref, at = part_of((a_ref, b_ref, c_ref), k)
+        ref, at = part_of(parts, k)
         pooled.append(ref[at, held])
     out_ref[0] = tn(jnp.concatenate(pooled, axis=0), rows_ref[...].reshape(8 * POOLED, width))
 
@@ -376,26 +399,37 @@
         grad_out_kernel,
         grid=(HELD,),
         out_shape=shape_of(HELD, hidden, width, dtype=f32),
-        in_specs=[whole] * 4,
+        in_specs=[whole] * 5,
         out_specs=pl.BlockSpec((1, hidden, width), lambda i: (i, 0, 0)),
         compiler_params=pltpu.CompilerParams(vmem_limit_bytes=18 * 1024 * 1024),
+        cost_estimate=FREE,
     )(*pooled, rows)
 
 
-def plus_kernel(own_ref, got_ref, first_ref, second_ref):
-    total = (own_ref[...].astype(f32) + got_ref[...].astype(f32)).astype(bf16)
-    first_ref[...] = total[:HALF]
-    second_ref[...] = total[HALF:]
-
-
-def settle_kernel(own_ref, got_ref, la_ref, lb_ref, ra_ref, rb_ref, out_ref):
-    width = own_ref.shape[1]
-    total = own_ref[...].astype(f32) + got_ref[...].astype(f32)
-    first = total[:HALF] + la_ref[...].astype(f32) + ra_ref[...].astype(f32)
-    second = total[HALF:] + lb_ref[...].astype(f32) + rb_ref[...].astype(f32)
-    table = repack_table(2 * HALF, True)
+def plus_kernel(own_ref, got_ref, *outs):
+    for k in range(len(outs) // 2):
+        total = (own_ref[k].astype(f32) + got_ref[k].astype(f32)).astype(bf16)
+        outs[2 * k][...] = total[:HALF]
+        outs[2 * k + 1][...] = total[HALF:]
+
+
+def add_kernel(x_ref, y_ref, out_ref):
+    out_ref[...] = (x_ref[...].astype(f32) + y_ref[...].astype(f32)).astype(bf16)
+
+
+def below_kernel(own_ref, got_ref, above_ref, first_ref, second_ref):
+    total = own_ref[0].astype(f32) + got_ref[0].astype(f32)
+    first_ref[...] = total[:HALF].astype(bf16)
+    second_ref[...] = (total[HALF:] + above_ref[...].astype(f32)).astype(bf16)
+
+
+def settle_kernel(own_ref, got_ref, la_ref, lb_ref, ha_ref, hb_ref, out_ref):
+    width = own_ref.shape[2]
+    total = own_ref[1].astype(f32) + got_ref[1].astype(f32)
+    first = total[:HALF] + la_ref[...].astype(f32) + ha_ref[...].astype(f32)
+    second = total[HALF:] + lb_ref[...].astype(f32) + hb_ref[...].astype(f32)
     rows = jnp.concatenate([first.astype(bf16), second.astype(bf16)], axis=0)
-    out_ref[...] = nn(table, rows).astype(bf16).reshape(PEERS, PAD, width)
+    out_ref[...] = nn(repack_table(2 * HALF, True), rows).astype(bf16).reshape(PEERS, PAD, width)
 
 
 def tail_kernel(ids, slots, toks, gain, grads, back_ref, out_ref, ids_ref, slots_ref, tok_ref, gain_ref, sems, near_ref, near_sem):
@@ -463,30 +497,24 @@
         scratch=input_scratch(row_count, width),
         vmem=60,
     )
+    rows_shape = shape_of(2 * HALF + KIND_ROWS, width)
+    x0 = call(repack_kernel, rows_shape, [exchange(sent)])
+    x2, x4, x1 = up(x0), down(x0), swap(x0)
+    made = [forward([x0], w_in)]
     first, second = call(
-        repack_kernel,
+        pick_kernel,
         [shape_of(HALF, width), shape_of(HALF + KIND_ROWS, width)],
-        [exchange(sent)],
-    )
-
-    a, b = [None] * 8, [None] * 8
-    a[0], b[0] = first, second
-    a[2] = up(first)
-    b[4] = down(second)
-    a[1], b[1] = swap(first), swap(second)
-    b[2] = up(after(second, a[1], b[1]))
-    a[4] = down(after(first, a[1], b[1]))
-    a[6] = up(a[2])
-    b[6] = down(b[4])
-    near = forward(a[0:2], b[0:2], w_in)
-    a[3], b[5] = swap(after(a[2], near[0])), swap(after(b[4], near[0]))
-    a[5], b[3] = swap(a[4]), swap(b[2])
-    mid = forward(a[2:6], b[2:6], w_in)
-    a[6], b[6] = after(a[6], mid[0]), after(b[6], mid[0])
-    a[7], b[7] = swap(a[6]), swap(b[6])
-    far = forward(a[6:8], b[6:8], w_in)
-    made = [near, mid, far]
+        [after(x2, made[0][0]), x4],
+    )
+    a6, b6 = up(first), down(second)
+    made.append(forward([x1, after(x2, first), x4], w_in))
+    x3, x5 = swap(after(x2, made[1][0])), swap(after(x4, made[1][0]))
+    x6 = call(stack_kernel, rows_shape, [after(a6, made[1][0]), b6])
+    x7 = swap(x6)
+    made.append(forward([after(x3, x6), x5], w_in))
+    made.append(forward([x6, after(x7, made[2][0])], w_in))
     pooled = [m[0] for m in made]
+    block_rows = [x0, x1, x2, x3, x4, x5, x6, x7]
 
     def product(shift, w_out):
         return call(
@@ -515,35 +543,27 @@
         scratch=[pltpu.VMEM((8 * PEERS, width), bf16), pltpu.VMEM((8 * PEERS, width), bf16)],
     )
 
-    def plus(x, y):
-        return call(plus_kernel, [shape_of(HALF, width), shape_of(HALF, width)], [x, y])
-
-    pre75, p7, p5 = backward((7, 5), b, made, prod, w_in)
-    s7, s5 = swap(p7), swap(p5)
-    pre64, p6, p4 = backward((6, 4), b, made, after(prod, p7), w_in)
-    r6a, r6b = plus(p6, s7)
+    pre75, p75 = backward((7, 5), block_rows, made, prod, w_in)
+    s75 = swap(p75)
+    pre64, p64 = backward((6, 4), block_rows, made, after(prod, p75), w_in)
+    half = shape_of(HALF, width)
+    r6a, r6b, r4a, r4b = call(plus_kernel, [half] * 4, [p64, s75])
     from_below, from_above = up(r6a), down(r6b)
-    r4a, r4b = plus(p4, after(s5, r6a))
     low_b = up(r4b)
-    pre31, p3, p1 = backward((3, 1), b, made, after(prod, r4a), w_in)
-    s3, s1 = swap(p3), swap(p1)
-    pre20, p2, p0 = backward((2, 0), b, made, after(prod, p3), w_in)
-    r2a, r2b = plus(p2, s3)
-    high_a = down(r2a)
-
-    def add(x, y):
-        return (x.astype(f32) + y.astype(f32)).astype(bf16)
-
+    rest, p31, p20 = backward((3, 1, 2, 0), block_rows, made, after(prod, r6a), w_in)
+    s31 = swap(p31)
+    low_a = call(add_kernel, half, [after(r4a, p20), from_below], cost=DEAR)
+    r2a, r2b = call(below_kernel, [half, half], [p20, after(s31, low_a), from_above])
+    high_a, high_b = down(r2a), down(r2b)
     grad_w_out = grad_out(pooled, after(rows, r2a), width, hidden)
-    low_a = up(add(r4a, after(from_below, grad_w_out)))
-    high_b = down(add(r2b, after(from_above, grad_w_out)))
     grad_w_in = grad_in(
-        a, b, [pre75, pre64, pre31, after(pre20, grad_w_out)], width, hidden
-    )
+        block_rows, [pre75, pre64, after(rest, grad_w_out)], width, hidden
+    )
+    low_a = up(low_a)
     settled = call(
         settle_kernel,
         shape_of(PEERS, PAD, width),
-        [after(p0, grad_w_in), s1, low_a, low_b, high_a, high_b],
+        [after(p20, grad_w_in), s31, low_a, low_b, high_a, high_b],
     )
     grad_flat = call(
         tail_kernel,

time: 143 us -> 139 us (0.972)
  starting transfers between devices: 20.2 us -> 15.5 us
  waiting for transfers between devices: 17.4 us -> 20.1 us
  blocking collectives: 70.1 us -> 68.4 us
    ppermute x6 -> x5, waiting for transfers between devices: 7.87 us -> 16 us  [up(): return lax.ppermute(x, 'dp', [(i, (i + 2) % 8) for i in range(8)])]
    ppermute x6 -> x5, waiting for transfers between devices: 3.65 us -> 0.01 us  [down(): return lax.ppermute(x, 'dp', [(i, (i + 6) % 8) for i in range(8)])]
    ppermute x6 -> x5, starting transfers between devices: 14.1 us -> 11.6 us  [down(): return lax.ppermute(x, 'dp', [(i, (i + 6) % 8) for i in range(8)])]
    ppermute x14 -> x8, waiting for transfers between devices: 5.83 us -> 4.11 us  [swap(): return lax.ppermute(x, 'dp', [(i, i ^ 1) for i in range(8)])]
    all_to_all x2, blocking collectives: 35.5 us -> 34 us  [exchange(): return lax.all_to_all(x, 'expert', split_axis=0, concat_axis=0, tiled=True)]
    ppermute x6 -> x5, starting transfers between devices: 3.9 us -> 2.6 us  [up(): return lax.ppermute(x, 'dp', [(i, (i + 2) % 8) for i in range(8)])]
    pallas_call x19 -> x21, Pallas kernels: 22.7 us -> 21.8 us  [call(): pl.pallas_call(kernel, out_shape=out, in_specs=[pl.BlockSpec(memory_space...]
  transfers between devices with their start and end apart: 26 -> 18, of which waited for: 11 -> 7; matrix products, arithmetic and copies ran while one was open for 0% -> 0% of each run, Pallas kernels for 12% -> 14%
where the time goes in v6:
time: 139 us; the launch traced here: 138 us
  blocking collectives  68.4 us (49%)
  Pallas kernels  30.9 us (22%)
  waiting for transfers between devices  20.1 us (14%)
  starting transfers between devices  15.5 us (11%)
  local copies, waits for them, and re-layouts  2.25 us (2%)
    all_to_all x2, blocking collectives, spread(): lax.all_to_all(x, everyone, split_axis=0, concat_axis=0, tiled=True, axis...  34.4 us
    all_to_all x2, blocking collectives, exchange(): return lax.all_to_all(x, 'expert', split_axis=0, concat_axis=0, tiled=True)  34 us
    pallas_call x21, Pallas kernels, call(): pl.pallas_call(kernel, out_shape=out, in_specs=[pl.BlockSpec(memory_space...  21.8 us
    ppermute x5, waiting for transfers between devices, up(): return lax.ppermute(x, 'dp', [(i, (i + 2) % 8) for i in range(8)])  16 us
    ppermute x5, starting transfers between devices, down(): return lax.ppermute(x, 'dp', [(i, (i + 6) % 8) for i in range(8)])  11.6 us
    pallas_call x1, Pallas kernels, grad_in(): pl.pallas_call(grad_in_kernel, grid=(HELD,), out_shape=shape_of(HELD, wid...  5.6 us
    ppermute x8, waiting for transfers between devices, swap(): return lax.ppermute(x, 'dp', [(i, i ^ 1) for i in range(8)])  4.11 us
    pallas_call x1, Pallas kernels, grad_out(): pl.pallas_call(grad_out_kernel, grid=(HELD,), out_shape=shape_of(HELD, hi...  3.43 us
  transfers between devices with their start and end apart: 18, of which 7 were waited for; matrix products, arithmetic and copies ran while one was open for 0% of the time, Pallas kernels for 14%

profile of v6, /device:TPU:0, one launch (start us, length us, event | category | flops | bytes accessed | tf_op | source)
XLA Modules:
  0.0 138.3 jit_solution(14083585841253628424)
XLA Ops:
  0.6 2.5 %shard_map.85 = (bf16[16,16,1280]{2,1,0:T(8,128)(2,1)}, f32[2,1280]{1,0:T(2,128)}) custom-call(s32[2,64]{1,0:T(2,128)} %bitcast.16, s32[2,64]{1,0:T(2,128)} %bitcast.18, bf16[128,1280]{1,0:T(8,128)(2,1)} %bitcast.13, f32[1280]{0:T(1024)} %gain.3), custom_call_target="tpu_custom_call" | custom-call | flops 1 | bytes 1 | tf_op jit(solution)/shard_map/pallas_call | solution.py:68
  3.1 20.1 %all_to_all.20.in_ref = bf16[16,16,1280]{2,1,0:T(8,128)(2,1)S(1)} all-to-all(bf16[16,16,1280]{2,1,0:T(8,128)(2,1)} %get-tuple-element.47), channel_id=1, replica_groups=mesh['dp'=8,'expert'=16] {'expert'}, dimensions={0} | all-to-all | bytes 1310720 | tf_op jit(solution)/shard_map/all_to_all | solution.py:485
  23.2 0.4 shard_map.86.refs_0_.refs_3_
  23.6 2.0 %collective-permute-start.1 = (bf16[200,1280]{1,0:T(8,128)(2,1)S(1)}, bf16[200,1280]{1,0:T(8,128)(2,1)S(1)}, u32[]{:S(2)}, u32[]{:S(2)}) collective-permute-start(bf16[200,1280]{1,0:T(8,128)(2,1)S(1)} %shard_map.86.refs_0_.refs_3_), channel_id=1, source_target_pairs={{0,32},{16,48},{32,64},{48,80},{64,96},{80,112},{96,0},{112,16},{1... | collective-permute-start | bytes 1536008 | tf_op jit(solution)/shard_map/ppermute | solution.py:473
  25.6 2.2 %collective-permute-start.2 = (bf16[200,1280]{1,0:T(8,128)(2,1)S(1)}, bf16[200,1280]{1,0:T(8,128)(2,1)S(1)}, u32[]{:S(2)}, u32[]{:S(2)}) collective-permute-start(bf16[200,1280]{1,0:T(8,128)(2,1)S(1)} %shard_map.86.refs_0_.refs_3_), channel_id=1, source_target_pairs={{0,96},{16,112},{32,0},{48,16},{64,32},{80,48},{96,64},{112,80},{1... | collective-permute-start | bytes 1536008 | tf_op jit(solution)/shard_map/ppermute | solution.py:476
  27.8 0.0 collective-permute-start
  27.8 1.9 %copy-done = bf16[2,1280,640]{2,1,0:T(8,128)(2,1)S(1)} copy-done((bf16[2,1280,640]{2,1,0:T(8,128)(2,1)S(1)}, bf16[2,1280,640]{2,1,0:T(8,128)(2,1)}, u32[]{:S(2)}) %copy-start) | copy-done | bytes 3276824
  29.7 1.1 shard_map.87
  30.8 7.2 %collective-permute-done.1.x2_ref.refs_1_.refs_2_ = bf16[200,1280]{1,0:T(8,128)(2,1)S(1)} collective-permute-done((bf16[200,1280]{1,0:T(8,128)(2,1)S(1)}, bf16[200,1280]{1,0:T(8,128)(2,1)S(1)}, u32[]{:S(2)}, u32[]{:S(2)}) %collective-permute-start.1) | collective-permute-done | bytes 512032 | tf_op jit(solution)/shard_map/ppermute | solution.py:473
  37.9 0.0 collective-permute-done.2.x4_ref.refs_2_.refs_1_.refs_4_
  38.0 3.1 %collective-permute-start.5 = (bf16[104,1280]{1,0:T(8,128)(2,1)S(1)}, bf16[104,1280]{1,0:T(8,128)(2,1)S(1)}, u32[]{:S(2)}, u32[]{:S(2)}) collective-permute-start(bf16[104,1280]{1,0:T(8,128)(2,1)S(1)} %get-tuple-element.55), channel_id=1, source_target_pairs={{0,96},{16,112},{32,0},{48,16},{64,32},{80,48},{96,64},{112,80},{1... | collective-permute-start | bytes 798728 | tf_op jit(solution)/shard_map/ppermute | solution.py:476
  41.1 0.0 collective-permute-start.4
  41.1 0.0 collective-permute-done.refs_0_.refs_1_
  41.1 2.4 %shard_map.89 = (bf16[3,2,32,640]{3,2,1,0:T(8,128)(2,1)S(1)}, bf16[3,2,96,640]{3,2,1,0:T(8,128)(2,1)S(1)}) custom-call(bf16[200,1280]{1,0:T(8,128)(2,1)S(1)} %collective-permute-done.refs_0_.refs_1_, bf16[200,1280]{1,0:T(8,128)(2,1)S(1)} %collective-permute-done.1.x2_ref.refs_1_.refs_2_, ...), custom_call_target="tpu_custom_call" | custom-call | flops 1 | bytes 1 | tf_op jit(solution)/shard_map/pallas_call | solution.py:68
  43.5 0.1 collective-permute-start.3
  43.6 0.5 collective-permute-start.6
  44.1 4.4 %collective-permute-done.4.first_ref = bf16[96,1280]{1,0:T(8,128)(2,1)S(1)} collective-permute-done((bf16[96,1280]{1,0:T(8,128)(2,1)S(1)}, bf16[96,1280]{1,0:T(8,128)(2,1)S(1)}, u32[]{:S(2)}, u32[]{:S(2)}) %collective-permute-start.4) | collective-permute-done | bytes 245792 | tf_op jit(solution)/shard_map/ppermute | solution.py:473
  48.5 0.0 collective-permute-done.5.second_ref
  48.5 0.0 copy-start.2
  48.5 0.1 collective-permute-start.7
  48.6 0.0 collective-permute-done.3.refs_0_.refs_3_
  48.6 0.0 collective-permute-done.6.refs_1_.refs_5_
  48.6 1.5 %shard_map.91 = (bf16[2,2,32,640]{3,2,1,0:T(8,128)(2,1)S(1)}, bf16[2,2,96,640]{3,2,1,0:T(8,128)(2,1)S(1)}) custom-call(bf16[200,1280]{1,0:T(8,128)(2,1)S(1)} %collective-permute-done.3.refs_0_.refs_3_, bf16[200,1280]{1,0:T(8,128)(2,1)S(1)} %collective-permute-done.6.refs_1_.refs_5_, bf16[2,1280,640]{2,1,0:T(8,128)(2,1)S(1)} %copy-done.1), custom_call_target="tpu_custom_call" | custom-call | flops 1 | bytes 1 | tf_op jit(solution)/shard_map/pallas_call | solution.py:68
  50.2 0.3 collective-permute-done.7.refs_1_.refs_0_.refs_7_
  50.5 1.5 %shard_map.92 = (bf16[2,2,32,640]{3,2,1,0:T(8,128)(2,1)S(1)}, bf16[2,2,96,640]{3,2,1,0:T(8,128)(2,1)S(1)}) custom-call(bf16[200,1280]{1,0:T(8,128)(2,1)S(1)} %shard_map.90.refs_0_.refs_6_, bf16[200,1280]{1,0:T(8,128)(2,1)S(1)} %collective-permute-done.7.refs_1_.refs_0_.refs_7_, bf16[2,1280,640]{2,1,0:T(8,128)(2,1)S(1)} %copy-done.1), custom_call_target="tpu_custom_call" | custom-call | flops 1 | bytes 1 | tf_op jit(solution)/shard_map/pallas_call | solution.py:68
  52.0 0.7 shard_map.93
  52.7 0.0 copy-start.5
  52.7 0.3 collective-permute-start.8
  53.0 0.7 shard_map.94.own_ref
  53.7 0.8 collective-permute-done.8.got_ref
  54.4 0.1 shard_map.95
  54.5 0.3 copy.11
  54.8 15.8 %all_to_all.21.part_ref = bf16[64,2,1280]{2,1,0:T(2,128)(2,1)S(1)} all-to-all(bf16[64,2,1280]{2,1,0:T(2,128)(2,1)S(1)} %bitcast.20), channel_id=1, replica_groups={{0,1,2,3,4,5,6,7,8,9,10,11,12,13,14,15,32,33,34,35,36,37,38,39,40,41,42..., dimensions={0} | all-to-all | bytes 655360 | tf_op jit(solution)/shard_map/all_to_all | solution.py:488
  70.6 0.3 shard_map.96
  70.9 18.5 %all_to_all.22 = f32[64,2,1280]{2,1,0:T(2,128)S(1)} all-to-all(f32[64,2,1280]{2,1,0:T(2,128)S(1)} %shard_map.96), channel_id=1, replica_groups={{0,1,2,3,4,5,6,7,8,9,10,11,12,13,14,15,32,33,34,35,36,37,38,39,40,41,42..., dimensions={0} | all-to-all | bytes 1310720 | tf_op jit(solution)/shard_map/all_to_all | solution.py:488
  89.5 0.1 collective-permute-start.9
  89.6 2.1 %collective-permute-done.9.other_ref = f32[2,64,1280]{2,1,0:T(8,128)S(1)} collective-permute-done((f32[2,64,1280]{2,1,0:T(8,128)S(1)}, f32[2,64,1280]{2,1,0:T(8,128)S(1)}, u32[]{:S(2)}, u32[]{:S(2)}) %collective-permute-start.9) | collective-permute-done | bytes 655392 | tf_op jit(solution)/shard_map/ppermute | solution.py:479
  91.7 2.9 %shard_map.97 = (f32[2,128,1280]{2,1,0:T(8,128)S(1)}, bf16[8,32,1280]{2,1,0:T(8,128)(2,1)S(1)}, bf16[2,256,640]{2,1,0:T(8,128)(2,1)S(1)}) custom-call(f32[2,64,1280]{2,1,0:T(8,128)S(1)} %bitcast.12, f32[2,64,1280]{2,1,0:T(8,128)S(1)} %collective-permute-done.9.other_ref, bf16[2,640,1280]{2,1,0:T(8,128)(2,1)S(1)} %copy-done.2), custom_call_target="tpu_custom_call" | custom-call | flops 1 | bytes 1 | tf_op jit(solution)/shard_map/pallas_call | solution.py:68
  94.6 1.5 %shard_map.98 = (bf16[2,2,96,640]{3,2,1,0:T(8,128)(2,1)S(1)}, bf16[2,192,1280]{2,1,0:T(8,128)(2,1)S(1)}) custom-call(bf16[200,1280]{1,0:T(8,128)(2,1)S(1)} %collective-permute-done.7.refs_1_.refs_0_.refs_7_, bf16[200,1280]{1,0:T(8,128)(2,1)S(1)} %collective-permute-done.6.refs_1_.refs_5_, bf16[2,2,96,640]{3,2,1,0:T(8,128)(2,1)S(1)} %get-tuple-element.69.refs_2_, ...), custom_call_target="tpu_custom_call" | custom-call | flops 1 | bytes 1 | tf_op jit(solution)/shard_map/pallas_call | solution.py:68
  96.1 0.2 collective-permute-start.10
  96.3 1.5 %shard_map.99 = (bf16[2,2,96,640]{3,2,1,0:T(8,128)(2,1)S(1)}, bf16[2,192,1280]{2,1,0:T(8,128)(2,1)S(1)}) custom-call(bf16[200,1280]{1,0:T(8,128)(2,1)S(1)} %shard_map.90.refs_0_.refs_6_, bf16[200,1280]{1,0:T(8,128)(2,1)S(1)} %collective-permute-done.2.x4_ref.refs_2_.refs_1_.refs_4_, bf16[2,2,96,640]{3,2,1,0:T(8,128)(2,1)S(1)} %get-tuple-element.69.refs_2_, ...), custom_call_target="tpu_custom_call" | custom-call | flops 1 | bytes 1 | tf_op jit(solution)/shard_map/pallas_call | solution.py:68
  97.8 0.9 collective-permute-done.10.got_ref
  98.8 0.2 shard_map.100
  99.0 0.5 collective-permute-start.12
  99.5 2.8 %collective-permute-start.13 = (bf16[96,1280]{1,0:T(8,128)(2,1)S(1)}, bf16[96,1280]{1,0:T(8,128)(2,1)S(1)}, u32[]{:S(2)}, u32[]{:S(2)}) collective-permute-start(bf16[96,1280]{1,0:T(8,128)(2,1)S(1)} %get-tuple-element.84), channel_id=1, source_target_pairs={{0,96},{16,112},{32,0},{48,16},{64,32},{80,48},{96,64},{112,80},{1... | collective-permute-start | bytes 737288 | tf_op jit(solution)/shard_map/ppermute | solution.py:476
  102.3 0.0 collective-permute-start.15
  102.3 2.3 %shard_map.101 = (bf16[4,2,96,640]{3,2,1,0:T(8,128)(2,1)S(1)}, bf16[2,192,1280]{2,1,0:T(8,128)(2,1)S(1)}, bf16[2,192,1280]{2,1,0:T(8,128)(2,1)S(1)}) custom-call(bf16[200,1280]{1,0:T(8,128)(2,1)S(1)} %collective-permute-done.3.refs_0_.refs_3_, bf16[200,1280]{1,0:T(8,128)(2,1)S(1)} %collective-permute-done.refs_0_.refs_1_, ...), custom_call_target="tpu_custom_call" | custom-call | flops 1 | bytes 1 | tf_op jit(solution)/shard_map/pallas_call | solution.py:68
  104.6 0.1 collective-permute-start.11
  104.7 4.4 %collective-permute-done.12.y_ref = bf16[96,1280]{1,0:T(8,128)(2,1)S(1)} collective-permute-done((bf16[96,1280]{1,0:T(8,128)(2,1)S(1)}, bf16[96,1280]{1,0:T(8,128)(2,1)S(1)}, u32[]{:S(2)}, u32[]{:S(2)}) %collective-permute-start.12) | collective-permute-done | bytes 245792 | tf_op jit(solution)/shard_map/ppermute | solution.py:473
  109.1 0.1 shard_map.102
  109.1 0.1 collective-permute-start.14
  109.2 0.0 collective-permute-done.11.got_ref
  109.2 0.0 collective-permute-done.13.above_ref
  109.2 0.1 shard_map.103
  109.4 3.3 %collective-permute-start.17 = (bf16[96,1280]{1,0:T(8,128)(2,1)S(1)}, bf16[96,1280]{1,0:T(8,128)(2,1)S(1)}, u32[]{:S(2)}, u32[]{:S(2)}) collective-permute-start(bf16[96,1280]{1,0:T(8,128)(2,1)S(1)} %get-tuple-element.90), channel_id=1, source_target_pairs={{0,96},{16,112},{32,0},{48,16},{64,32},{80,48},{96,64},{112,80},{1... | collective-permute-start | bytes 737288 | tf_op jit(solution)/shard_map/ppermute | solution.py:476
  112.7 0.3 collective-permute-start.16
  113.0 3.4 %shard_map.104 = f32[2,640,1280]{2,1,0:T(8,128)} custom-call(bf16[1,2,32,640]{3,2,1,0:T(8,128)(2,1)S(1)} %get-tuple-element.48.refs_0_, bf16[3,2,32,640]{3,2,1,0:T(8,128)(2,1)S(1)} %get-tuple-element.52.refs_1_, bf16[2,2,32,640]{3,2,1,0:T(8,128)(2,1)S(1)} %get-tuple-element.58.refs_2_, bf16[2,2,32,640]{3,2,1,0:T(8,128)(2,1)S(1)} %get-tuple-element.60.refs_3_, ...), custom_call_target="tpu_custom_call" | custom-call | flops 1 | bytes 1 | tf_op jit(solution)/shard_map/pallas_call | solution.py:398
  116.4 5.6 %shard_map.105 = f32[2,1280,640]{2,1,0:T(8,128)} custom-call(bf16[200,1280]{1,0:T(8,128)(2,1)S(1)} %shard_map.86.refs_0_.refs_3_, bf16[200,1280]{1,0:T(8,128)(2,1)S(1)} %collective-permute-done.refs_0_.refs_1_, bf16[200,1280]{1,0:T(8,128)(2,1)S(1)} %collective-permute-done.1.x2_ref.refs_1_.refs_2_, ...), custom_call_target="tpu_custom_call" | custom-call | flops 1 | bytes 1 | tf_op jit(solution)/shard_map/pallas_call | solution.py:370
  122.0 0.0 collective-permute-done.15.lb_ref
  122.0 0.0 collective-permute-done.14.la_ref
  122.0 0.0 collective-permute-done.16.ha_ref
  122.1 0.5 shard_map.106
  122.6 13.9 %all_to_all.23.back_ref = bf16[16,16,1280]{2,1,0:T(8,128)(2,1)S(1)} all-to-all(bf16[16,16,1280]{2,1,0:T(8,128)(2,1)S(1)} %shard_map.106), channel_id=1, replica_groups=mesh['dp'=8,'expert'=16] {'expert'}, dimensions={0} | all-to-all | bytes 1310720 | tf_op jit(solution)/shard_map/all_to_all | solution.py:485
  136.5 1.6 %shard_map.107 = bf16[128,1280]{1,0:T(8,128)(2,1)} custom-call(s32[2,64]{1,0:T(2,128)S(1)} %bitcast.17, s32[2,64]{1,0:T(2,128)S(1)} %bitcast.19, bf16[128,1280]{1,0:T(8,128)(2,1)S(1)} %bitcast.14, f32[1280]{0:T(1024)S(1)} %copy-done.4, f32[2,128,1280]{2,1,0:T(8,128)S(1)} %get-tuple-element.64.grads, bf16[16,16,1280]{2,1,0:T(8,128)(2,1)S(1)} %all_to_all.23.back_ref), custom_call_target="tpu_custom_call" | custom-call | flops 1 | bytes 1 | tf_op jit(solution)/shard_map/pallas_call | solution.py:68
  (17 shorter events, 0.1 us)
Async XLA Ops:
  23.6 14.3 %collective-permute-start.1 = (bf16[200,1280]{1,0:T(8,128)(2,1)S(1)}, bf16[200,1280]{1,0:T(8,128)(2,1)S(1)}, u32[]{:S(2)}, u32[]{:S(2)}) collective-permute-start(bf16[200,1280]{1,0:T(8,128)(2,1)S(1)} %shard_map.86.refs_0_.refs_3_), channel_id=1, source_target_pairs={{0,32},{16,48},{32,64},{48,80},{64,96},{80,112},{96,0},{112,16},{1... | collective-permute-start | bytes 1536008 | tf_op jit(solution)/shard_map/ppermute | solution.py:473
  25.6 12.4 %collective-permute-start.2 = (bf16[200,1280]{1,0:T(8,128)(2,1)S(1)}, bf16[200,1280]{1,0:T(8,128)(2,1)S(1)}, u32[]{:S(2)}, u32[]{:S(2)}) collective-permute-start(bf16[200,1280]{1,0:T(8,128)(2,1)S(1)} %shard_map.86.refs_0_.refs_3_), channel_id=1, source_target_pairs={{0,96},{16,112},{32,0},{48,16},{64,32},{80,48},{96,64},{112,80},{1... | collective-permute-start | bytes 1536008 | tf_op jit(solution)/shard_map/ppermute | solution.py:476
  27.8 13.3 %collective-permute-start = (bf16[200,1280]{1,0:T(8,128)(2,1)S(1)}, bf16[200,1280]{1,0:T(8,128)(2,1)S(1)}, u32[]{:S(2)}, u32[]{:S(2)}) collective-permute-start(bf16[200,1280]{1,0:T(8,128)(2,1)S(1)} %shard_map.86.refs_0_.refs_3_), channel_id=1, source_target_pairs={{0,16},{16,0},{32,48},{48,32},{64,80},{80,64},{96,112},{112,96},{1... | collective-permute-start | bytes 1536008 | tf_op jit(solution)/shard_map/ppermute | solution.py:479
  27.8 1.9 %copy-start = (bf16[2,1280,640]{2,1,0:T(8,128)(2,1)S(1)}, bf16[2,1280,640]{2,1,0:T(8,128)(2,1)}, u32[]{:S(2)}) copy-start(bf16[2,1280,640]{2,1,0:T(8,128)(2,1)} %refs_9_.1) | copy-start | bytes 9830404
  29.7 11.4 %copy-start.1 = (bf16[2,1280,640]{2,1,0:T(8,128)(2,1)S(1)}, bf16[2,1280,640]{2,1,0:T(8,128)(2,1)}, u32[]{:S(2)}) copy-start(bf16[2,1280,640]{2,1,0:T(8,128)(2,1)} %refs_9_.1) | copy-start | bytes 9830404
  38.0 10.5 %collective-permute-start.5 = (bf16[104,1280]{1,0:T(8,128)(2,1)S(1)}, bf16[104,1280]{1,0:T(8,128)(2,1)S(1)}, u32[]{:S(2)}, u32[]{:S(2)}) collective-permute-start(bf16[104,1280]{1,0:T(8,128)(2,1)S(1)} %get-tuple-element.55), channel_id=1, source_target_pairs={{0,96},{16,112},{32,0},{48,16},{64,32},{80,48},{96,64},{112,80},{1... | collective-permute-start | bytes 798728 | tf_op jit(solution)/shard_map/ppermute | solution.py:476
  41.1 7.4 %collective-permute-start.4 = (bf16[96,1280]{1,0:T(8,128)(2,1)S(1)}, bf16[96,1280]{1,0:T(8,128)(2,1)S(1)}, u32[]{:S(2)}, u32[]{:S(2)}) collective-permute-start(bf16[96,1280]{1,0:T(8,128)(2,1)S(1)} %get-tuple-element.50), channel_id=1, source_target_pairs={{0,32},{16,48},{32,64},{48,80},{64,96},{80,112},{96,0},{112,16},{1... | collective-permute-start | bytes 737288 | tf_op jit(solution)/shard_map/ppermute | solution.py:473
  43.5 5.2 %collective-permute-start.3 = (bf16[200,1280]{1,0:T(8,128)(2,1)S(1)}, bf16[200,1280]{1,0:T(8,128)(2,1)S(1)}, u32[]{:S(2)}, u32[]{:S(2)}) collective-permute-start(bf16[200,1280]{1,0:T(8,128)(2,1)S(1)} %collective-permute-done.1.x2_ref.refs_1_.refs_2_), channel_id=1, source_target_pairs={{0,16},{16,0},{32,48},{48,32},{64,80},{80,64},{96,112},{112,96},{1... | collective-permute-start | bytes 1536008 | tf_op jit(solution)/shard_map/ppermute | solution.py:479
  43.6 5.1 %collective-permute-start.6 = (bf16[200,1280]{1,0:T(8,128)(2,1)S(1)}, bf16[200,1280]{1,0:T(8,128)(2,1)S(1)}, u32[]{:S(2)}, u32[]{:S(2)}) collective-permute-start(bf16[200,1280]{1,0:T(8,128)(2,1)S(1)} %collective-permute-done.2.x4_ref.refs_2_.refs_1_.refs_4_), channel_id=1, source_target_pairs={{0,16},{16,0},{32,48},{48,32},{64,80},{80,64},{96,112},{112,96},{1... | collective-permute-start | bytes 1536008 | tf_op jit(solution)/shard_map/ppermute | solution.py:479
  48.5 3.5 %copy-start.2 = (bf16[2,640,1280]{2,1,0:T(8,128)(2,1)S(1)}, bf16[2,640,1280]{2,1,0:T(8,128)(2,1)}, u32[]{:S(2)}) copy-start(bf16[2,640,1280]{2,1,0:T(8,128)(2,1)} %w_out.1) | copy-start | bytes 9830404
  48.5 2.0 %collective-permute-start.7 = (bf16[200,1280]{1,0:T(8,128)(2,1)S(1)}, bf16[200,1280]{1,0:T(8,128)(2,1)S(1)}, u32[]{:S(2)}, u32[]{:S(2)}) collective-permute-start(bf16[200,1280]{1,0:T(8,128)(2,1)S(1)} %shard_map.90.refs_0_.refs_6_), channel_id=1, source_target_pairs={{0,16},{16,0},{32,48},{48,32},{64,80},{80,64},{96,112},{112,96},{1... | collective-permute-start | bytes 1536008 | tf_op jit(solution)/shard_map/ppermute | solution.py:479
  52.7 17.9 %copy-start.5 = (f32[2,1280]{1,0:T(2,128)S(1)}, f32[2,1280]{1,0:T(2,128)}, u32[]{:S(2)}) copy-start(f32[2,1280]{1,0:T(2,128)} %get-tuple-element.63.sum_ref) | copy-start | bytes 30724
  52.7 1.7 %collective-permute-start.8 = (bf16[4,32,1280]{2,1,0:T(8,128)(2,1)S(1)}, bf16[4,32,1280]{2,1,0:T(8,128)(2,1)S(1)}, u32[]{:S(2)}, u32[]{:S(2)}) collective-permute-start(bf16[4,32,1280]{2,1,0:T(8,128)(2,1)S(1)} %shard_map.93), channel_id=1, source_target_pairs={{0,16},{16,0},{32,48},{48,32},{64,80},{80,64},{96,112},{112,96},{1... | collective-permute-start | bytes 983048 | tf_op jit(solution)/shard_map/ppermute | solution.py:479
  89.5 2.2 %collective-permute-start.9 = (f32[2,64,1280]{2,1,0:T(8,128)S(1)}, f32[2,64,1280]{2,1,0:T(8,128)S(1)}, u32[]{:S(2)}, u32[]{:S(2)}) collective-permute-start(f32[2,64,1280]{2,1,0:T(8,128)S(1)} %bitcast.11), channel_id=1, source_target_pairs={{0,16},{16,0},{32,48},{48,32},{64,80},{80,64},{96,112},{112,96},{1... | collective-permute-start | bytes 1966088 | tf_op jit(solution)/shard_map/ppermute | solution.py:479
  96.1 2.6 %collective-permute-start.10 = (bf16[2,192,1280]{2,1,0:T(8,128)(2,1)S(1)}, bf16[2,192,1280]{2,1,0:T(8,128)(2,1)S(1)}, u32[]{:S(2)}, u32[]{:S(2)}) collective-permute-start(bf16[2,192,1280]{2,1,0:T(8,128)(2,1)S(1)} %get-tuple-element.70), channel_id=1, source_target_pairs={{0,16},{16,0},{32,48},{48,32},{64,80},{80,64},{96,112},{112,96},{1... | collective-permute-start | bytes 2949128 | tf_op jit(solution)/shard_map/ppermute | solution.py:479
  99.0 10.1 %collective-permute-start.12 = (bf16[96,1280]{1,0:T(8,128)(2,1)S(1)}, bf16[96,1280]{1,0:T(8,128)(2,1)S(1)}, u32[]{:S(2)}, u32[]{:S(2)}) collective-permute-start(bf16[96,1280]{1,0:T(8,128)(2,1)S(1)} %get-tuple-element.73), channel_id=1, source_target_pairs={{0,32},{16,48},{32,64},{48,80},{64,96},{80,112},{96,0},{112,16},{1... | collective-permute-start | bytes 737288 | tf_op jit(solution)/shard_map/ppermute | solution.py:473
  99.5 9.7 %collective-permute-start.13 = (bf16[96,1280]{1,0:T(8,128)(2,1)S(1)}, bf16[96,1280]{1,0:T(8,128)(2,1)S(1)}, u32[]{:S(2)}, u32[]{:S(2)}) collective-permute-start(bf16[96,1280]{1,0:T(8,128)(2,1)S(1)} %get-tuple-element.84), channel_id=1, source_target_pairs={{0,96},{16,112},{32,0},{48,16},{64,32},{80,48},{96,64},{112,80},{1... | collective-permute-start | bytes 737288 | tf_op jit(solution)/shard_map/ppermute | solution.py:476
  102.3 19.7 %collective-permute-start.15 = (bf16[96,1280]{1,0:T(8,128)(2,1)S(1)}, bf16[96,1280]{1,0:T(8,128)(2,1)S(1)}, u32[]{:S(2)}, u32[]{:S(2)}) collective-permute-start(bf16[96,1280]{1,0:T(8,128)(2,1)S(1)} %get-tuple-element.89), channel_id=1, source_target_pairs={{0,32},{16,48},{32,64},{48,80},{64,96},{80,112},{96,0},{112,16},{1... | collective-permute-start | bytes 737288 | tf_op jit(solution)/shard_map/ppermute | solution.py:473
  104.6 4.7 %collective-permute-start.11 = (bf16[2,192,1280]{2,1,0:T(8,128)(2,1)S(1)}, bf16[2,192,1280]{2,1,0:T(8,128)(2,1)S(1)}, u32[]{:S(2)}, u32[]{:S(2)}) collective-permute-start(bf16[2,192,1280]{2,1,0:T(8,128)(2,1)S(1)} %get-tuple-element.80), channel_id=1, source_target_pairs={{0,16},{16,0},{32,48},{48,32},{64,80},{80,64},{96,112},{112,96},{1... | collective-permute-start | bytes 2949128 | tf_op jit(solution)/shard_map/ppermute | solution.py:479
  109.1 12.9 %collective-permute-start.14 = (bf16[96,1280]{1,0:T(8,128)(2,1)S(1)}, bf16[96,1280]{1,0:T(8,128)(2,1)S(1)}, u32[]{:S(2)}, u32[]{:S(2)}) collective-permute-start(bf16[96,1280]{1,0:T(8,128)(2,1)S(1)} %shard_map.102), channel_id=1, source_target_pairs={{0,32},{16,48},{32,64},{48,80},{64,96},{80,112},{96,0},{112,16},{1... | collective-permute-start | bytes 737288 | tf_op jit(solution)/shard_map/ppermute | solution.py:473
  109.4 12.6 %collective-permute-start.17 = (bf16[96,1280]{1,0:T(8,128)(2,1)S(1)}, bf16[96,1280]{1,0:T(8,128)(2,1)S(1)}, u32[]{:S(2)}, u32[]{:S(2)}) collective-permute-start(bf16[96,1280]{1,0:T(8,128)(2,1)S(1)} %get-tuple-element.90), channel_id=1, source_target_pairs={{0,96},{16,112},{32,0},{48,16},{64,32},{80,48},{96,64},{112,80},{1... | collective-permute-start | bytes 737288 | tf_op jit(solution)/shard_map/ppermute | solution.py:476
  112.7 9.4 %collective-permute-start.16 = (bf16[96,1280]{1,0:T(8,128)(2,1)S(1)}, bf16[96,1280]{1,0:T(8,128)(2,1)S(1)}, u32[]{:S(2)}, u32[]{:S(2)}) collective-permute-start(bf16[96,1280]{1,0:T(8,128)(2,1)S(1)} %get-tuple-element.85), channel_id=1, source_target_pairs={{0,96},{16,112},{32,0},{48,16},{64,32},{80,48},{96,64},{112,80},{1... | collective-permute-start | bytes 737288 | tf_op jit(solution)/shard_map/ppermute | solution.py:476
  122.0 14.5 %copy-start.3 = (bf16[1,2,64,1280]{3,2,1,0:T(8,128)(2,1)S(1)}, bf16[1,2,64,1280]{3,2,1,0:T(8,128)(2,1)}, u32[]{:S(2)}) copy-start(bf16[1,2,64,1280]{3,2,1,0:T(8,128)(2,1)} %param.6) | copy-start | bytes 983044
  122.0 14.5 %copy-start.4 = (f32[1280]{0:T(1024)S(1)}, f32[1280]{0:T(1024)}, u32[]{:S(2)}) copy-start(f32[1280]{0:T(1024)} %gain.3) | copy-start | bytes 15364
  122.0 14.5 %copy-start.6 = (s32[1,2,64]{2,1,0:T(2,128)S(1)}, s32[1,2,64]{2,1,0:T(2,128)}, u32[]{:S(2)}) copy-start(s32[1,2,64]{2,1,0:T(2,128)} %param.7) | copy-start | bytes 1540
  122.0 14.5 %copy-start.7 = (s32[1,2,64]{2,1,0:T(2,128)S(1)}, s32[1,2,64]{2,1,0:T(2,128)}, u32[]{:S(2)}) copy-start(s32[1,2,64]{2,1,0:T(2,128)} %param.8) | copy-start | bytes 1540

commit v7 on v6

--- a/solution.py
+++ b/solution.py
@@ -322,7 +322,7 @@
         part = nt(pre, w_in[held]).astype(bf16)
         for k in range(count):
             rows = part[k * HALF : (k + 1) * HALF]
-            outs[k // 2][k % 2, held * HALF : (held + 1) * HALF, :] = rows
+            outs[k][held * HALF : (held + 1) * HALF, :] = rows
 
 
 def backward(blocks, rows, made, prod, w_in):
@@ -331,7 +331,7 @@
     return call(
         functools.partial(backward_kernel, blocks),
         [shape_of(count, HELD, HALF, hidden)]
-        + [shape_of(2, 2 * HALF, width)] * (count // 2),
+        + [shape_of(2 * HALF, width)] * count,
         [
             *[rows[block] for block in blocks],
             *[made[PARTS[block][0]][1] for block in blocks],
@@ -345,7 +345,7 @@
     )
 
 
-PAIRED = {7: (0, 0), 5: (0, 1), 6: (1, 0), 4: (1, 1), 3: (2, 0), 1: (2, 1), 2: (2, 2), 0: (2, 3)}
+PAIRED = {7: (0, 0), 6: (1, 0), 5: (1, 1), 4: (1, 2), 3: (2, 0), 1: (2, 1), 2: (2, 2), 0: (2, 3)}
 
 
 def grad_in_kernel(*refs):
@@ -406,11 +406,10 @@
     )(*pooled, rows)
 
 
-def plus_kernel(own_ref, got_ref, *outs):
-    for k in range(len(outs) // 2):
-        total = (own_ref[k].astype(f32) + got_ref[k].astype(f32)).astype(bf16)
-        outs[2 * k][...] = total[:HALF]
-        outs[2 * k + 1][...] = total[HALF:]
+def plus_kernel(own_ref, got_ref, first_ref, second_ref):
+    total = (own_ref[...].astype(f32) + got_ref[...].astype(f32)).astype(bf16)
+    first_ref[...] = total[:HALF]
+    second_ref[...] = total[HALF:]
 
 
 def add_kernel(x_ref, y_ref, out_ref):
@@ -418,29 +417,23 @@
 
 
 def below_kernel(own_ref, got_ref, above_ref, first_ref, second_ref):
-    total = own_ref[0].astype(f32) + got_ref[0].astype(f32)
+    total = own_ref[...].astype(f32) + got_ref[...].astype(f32)
     first_ref[...] = total[:HALF].astype(bf16)
     second_ref[...] = (total[HALF:] + above_ref[...].astype(f32)).astype(bf16)
 
 
 def settle_kernel(own_ref, got_ref, la_ref, lb_ref, ha_ref, hb_ref, out_ref):
-    width = own_ref.shape[2]
-    total = own_ref[1].astype(f32) + got_ref[1].astype(f32)
+    width = own_ref.shape[1]
+    total = own_ref[...].astype(f32) + got_ref[...].astype(f32)
     first = total[:HALF] + la_ref[...].astype(f32) + ha_ref[...].astype(f32)
     second = total[HALF:] + lb_ref[...].astype(f32) + hb_ref[...].astype(f32)
     rows = jnp.concatenate([first.astype(bf16), second.astype(bf16)], axis=0)
     out_ref[...] = nn(repack_table(2 * HALF, True), rows).astype(bf16).reshape(PEERS, PAD, width)
 
 
-def tail_kernel(ids, slots, toks, gain, grads, back_ref, out_ref, ids_ref, slots_ref, tok_ref, gain_ref, sems, near_ref, near_sem):
-    copies = fetch((ids, slots, toks, gain), (ids_ref, slots_ref, tok_ref, gain_ref), sems)
+def tail_kernel(ids_ref, slots_ref, tok_ref, gain_ref, grads_ref, back_ref, out_ref):
     at = (lax.axis_index("dp") // 2) * PEERS + lax.axis_index("expert")
-    first = pl.multiple_of(at // 8 * 8, 8)
-    near = pltpu.make_async_copy(grads.at[:, pl.ds(first, 8), :], near_ref, near_sem)
-    near.start()
-    for copy in copies:
-        copy.wait()
-    near.wait()
+    near = pl.ds(pl.multiple_of(at // 8 * 8, 8), 8)
     width = tok_ref.shape[1]
     tokens = tok_ref.shape[0]
     back = back_ref[...].reshape(PEERS * PAD, width)
@@ -454,7 +447,7 @@
     )
     for half in range(2):
         span = slice(half * (tokens // 2), (half + 1) * (tokens // 2))
-        rows = near_ref[half]
+        rows = grads_ref[half, near, :]
         own = jnp.where(iota(rows.shape, 0) == at % 8, rows, 0.0)
         own = jnp.sum(own, axis=0, keepdims=True)
         out_ref[span, :] = (own + grad[span]).astype(bf16)
@@ -543,35 +536,37 @@
         scratch=[pltpu.VMEM((8 * PEERS, width), bf16), pltpu.VMEM((8 * PEERS, width), bf16)],
     )
 
-    pre75, p75 = backward((7, 5), block_rows, made, prod, w_in)
-    s75 = swap(p75)
-    pre64, p64 = backward((6, 4), block_rows, made, after(prod, p75), w_in)
+    def plus(x, y):
+        return call(plus_kernel, [shape_of(HALF, width)] * 2, [x, y])
+
     half = shape_of(HALF, width)
-    r6a, r6b, r4a, r4b = call(plus_kernel, [half] * 4, [p64, s75])
+    pre7, p7 = backward((7,), block_rows, made, prod, w_in)
+    s7 = swap(p7)
+    pre654, p6, p5, p4 = backward((6, 5, 4), block_rows, made, after(prod, p7), w_in)
+    s5 = swap(p5)
+    r6a, r6b = plus(p6, s7)
     from_below, from_above = up(r6a), down(r6b)
+    rest, p3, p1, p2, p0 = backward((3, 1, 2, 0), block_rows, made, after(prod, r6a), w_in)
+    r4a, r4b = plus(p4, after(s5, p2))
     low_b = up(r4b)
-    rest, p31, p20 = backward((3, 1, 2, 0), block_rows, made, after(prod, r6a), w_in)
-    s31 = swap(p31)
-    low_a = call(add_kernel, half, [after(r4a, p20), from_below], cost=DEAR)
-    r2a, r2b = call(below_kernel, [half, half], [p20, after(s31, low_a), from_above])
+    s3, s1 = swap(p3), swap(p1)
+    low_a = call(add_kernel, half, [after(r4a, p0), from_below], cost=DEAR)
+    r2a, r2b = call(below_kernel, [half, half], [p2, after(s3, low_a), from_above])
     high_a, high_b = down(r2a), down(r2b)
     grad_w_out = grad_out(pooled, after(rows, r2a), width, hidden)
     grad_w_in = grad_in(
-        block_rows, [pre75, pre64, after(rest, grad_w_out)], width, hidden
+        block_rows, [pre7, pre654, after(rest, grad_w_out)], width, hidden
     )
     low_a = up(low_a)
     settled = call(
         settle_kernel,
         shape_of(PEERS, PAD, width),
-        [after(p20, grad_w_in), s31, low_a, low_b, high_a, high_b],
+        [after(p0, grad_w_in), s1, low_a, low_b, high_a, high_b],
     )
     grad_flat = call(
         tail_kernel,
         shape_of(row_count, width),
         [ids, slot, flat, ln_gain, grad_pooled, exchange(settled)],
-        hbm=(0, 1, 2, 3, 4),
-        scratch=input_scratch(row_count, width)
-        + [pltpu.VMEM((2, 8, width), f32), pltpu.SemaphoreType.DMA],
     )
     return (grad_flat.reshape(tokens.shape), grad_w_in, grad_w_out)
 

time: 139 us -> 138 us (level)
  waiting for transfers between devices: 20.1 us -> 18 us
    ppermute x5, waiting for transfers between devices: 16 us -> 14.5 us  [up(): return lax.ppermute(x, 'dp', [(i, (i + 2) % 8) for i in range(8)])]
    ppermute x8 -> x10, waiting for transfers between devices: 4.11 us -> 3.22 us  [swap(): return lax.ppermute(x, 'dp', [(i, i ^ 1) for i in range(8)])]
    pallas_call x21 -> x22, Pallas kernels: 21.8 us -> 21.6 us  [call(): pl.pallas_call(kernel, out_shape=out, in_specs=[pl.BlockSpec(memory_space...]
  transfers between devices with their start and end apart: 18 -> 20, of which waited for: 7 -> 7; matrix products, arithmetic and copies ran while one was open for 0% -> 0% of each run, Pallas kernels for 14% -> 14%
where the time goes in v7:
time: 138 us; the launch traced here: 137 us
  blocking collectives  68.9 us (50%)
  Pallas kernels  30.7 us (22%)
  waiting for transfers between devices  18 us (13%)
  starting transfers between devices  16.6 us (12%)
  local copies, waits for them, and re-layouts  2.25 us (2%)
    all_to_all x2, blocking collectives, exchange(): return lax.all_to_all(x, 'expert', split_axis=0, concat_axis=0, tiled=True)  34.6 us
    all_to_all x2, blocking collectives, spread(): lax.all_to_all(x, everyone, split_axis=0, concat_axis=0, tiled=True, axis...  34.3 us
    pallas_call x22, Pallas kernels, call(): pl.pallas_call(kernel, out_shape=out, in_specs=[pl.BlockSpec(memory_space...  21.6 us
    ppermute x5, waiting for transfers between devices, up(): return lax.ppermute(x, 'dp', [(i, (i + 2) % 8) for i in range(8)])  14.5 us
    ppermute x5, starting transfers between devices, down(): return lax.ppermute(x, 'dp', [(i, (i + 6) % 8) for i in range(8)])  11.6 us
    pallas_call x1, Pallas kernels, grad_in(): pl.pallas_call(grad_in_kernel, grid=(HELD,), out_shape=shape_of(HELD, wid...  5.61 us
    pallas_call x1, Pallas kernels, grad_out(): pl.pallas_call(grad_out_kernel, grid=(HELD,), out_shape=shape_of(HELD, hi...  3.43 us
    ppermute x10, waiting for transfers between devices, swap(): return lax.ppermute(x, 'dp', [(i, i ^ 1) for i in range(8)])  3.22 us
  transfers between devices with their start and end apart: 20, of which 7 were waited for; matrix products, arithmetic and copies ran while one was open for 0% of the time, Pallas kernels for 14%

profile of v7, /device:TPU:0, one launch (start us, length us, event | category | flops | bytes accessed | tf_op | source)
XLA Modules:
  0.0 137.3 jit_solution(12552938969634954607)
XLA Ops:
  0.6 2.5 %shard_map.85 = (bf16[16,16,1280]{2,1,0:T(8,128)(2,1)}, f32[2,1280]{1,0:T(2,128)}) custom-call(s32[2,64]{1,0:T(2,128)} %bitcast.16, s32[2,64]{1,0:T(2,128)} %bitcast.18, bf16[128,1280]{1,0:T(8,128)(2,1)} %bitcast.13, f32[1280]{0:T(1024)} %gain_ref.1), custom_call_target="tpu_custom_call" | custom-call | flops 1 | bytes 1 | tf_op jit(solution)/shard_map/pallas_call | solution.py:68
  3.1 20.1 %all_to_all.20.in_ref = bf16[16,16,1280]{2,1,0:T(8,128)(2,1)S(1)} all-to-all(bf16[16,16,1280]{2,1,0:T(8,128)(2,1)} %get-tuple-element.52), channel_id=1, replica_groups=mesh['dp'=8,'expert'=16] {'expert'}, dimensions={0} | all-to-all | bytes 1310720 | tf_op jit(solution)/shard_map/all_to_all | solution.py:478
  23.2 0.4 shard_map.86.refs_0_.refs_3_
  23.6 2.0 %collective-permute-start.1 = (bf16[200,1280]{1,0:T(8,128)(2,1)S(1)}, bf16[200,1280]{1,0:T(8,128)(2,1)S(1)}, u32[]{:S(2)}, u32[]{:S(2)}) collective-permute-start(bf16[200,1280]{1,0:T(8,128)(2,1)S(1)} %shard_map.86.refs_0_.refs_3_), channel_id=1, source_target_pairs={{0,32},{16,48},{32,64},{48,80},{64,96},{80,112},{96,0},{112,16},{1... | collective-permute-start | bytes 1536008 | tf_op jit(solution)/shard_map/ppermute | solution.py:466
  25.6 2.2 %collective-permute-start.2 = (bf16[200,1280]{1,0:T(8,128)(2,1)S(1)}, bf16[200,1280]{1,0:T(8,128)(2,1)S(1)}, u32[]{:S(2)}, u32[]{:S(2)}) collective-permute-start(bf16[200,1280]{1,0:T(8,128)(2,1)S(1)} %shard_map.86.refs_0_.refs_3_), channel_id=1, source_target_pairs={{0,96},{16,112},{32,0},{48,16},{64,32},{80,48},{96,64},{112,80},{1... | collective-permute-start | bytes 1536008 | tf_op jit(solution)/shard_map/ppermute | solution.py:469
  27.8 0.0 collective-permute-start
  27.8 1.9 %copy-done = bf16[2,1280,640]{2,1,0:T(8,128)(2,1)S(1)} copy-done((bf16[2,1280,640]{2,1,0:T(8,128)(2,1)S(1)}, bf16[2,1280,640]{2,1,0:T(8,128)(2,1)}, u32[]{:S(2)}) %copy-start) | copy-done | bytes 3276824
  29.7 1.1 shard_map.87
  30.8 7.2 %collective-permute-done.1.x2_ref.refs_1_.refs_2_ = bf16[200,1280]{1,0:T(8,128)(2,1)S(1)} collective-permute-done((bf16[200,1280]{1,0:T(8,128)(2,1)S(1)}, bf16[200,1280]{1,0:T(8,128)(2,1)S(1)}, u32[]{:S(2)}, u32[]{:S(2)}) %collective-permute-start.1) | collective-permute-done | bytes 512032 | tf_op jit(solution)/shard_map/ppermute | solution.py:466
  37.9 0.0 collective-permute-done.2.x4_ref.refs_2_.refs_4_
  38.0 3.1 %collective-permute-start.5 = (bf16[104,1280]{1,0:T(8,128)(2,1)S(1)}, bf16[104,1280]{1,0:T(8,128)(2,1)S(1)}, u32[]{:S(2)}, u32[]{:S(2)}) collective-permute-start(bf16[104,1280]{1,0:T(8,128)(2,1)S(1)} %get-tuple-element.60), channel_id=1, source_target_pairs={{0,96},{16,112},{32,0},{48,16},{64,32},{80,48},{96,64},{112,80},{1... | collective-permute-start | bytes 798728 | tf_op jit(solution)/shard_map/ppermute | solution.py:469
  41.1 0.0 collective-permute-start.4
  41.1 2.4 %shard_map.89 = (bf16[3,2,32,640]{3,2,1,0:T(8,128)(2,1)S(1)}, bf16[3,2,96,640]{3,2,1,0:T(8,128)(2,1)S(1)}) custom-call(bf16[200,1280]{1,0:T(8,128)(2,1)S(1)} %collective-permute-done.refs_0_.refs_1_, bf16[200,1280]{1,0:T(8,128)(2,1)S(1)} %collective-permute-done.1.x2_ref.refs_1_.refs_2_, bf16[200,1280]{1,0:T(8,128)(2,1)S(1)} %collective-permute-done.2.x4_ref.refs_2_.refs_4_, ...), custom_call_target="tpu_custom_call" | custom-call | flops 1 | bytes 1 | tf_op jit(solution)/shard_map/pallas_call | solution.py:68
  43.5 0.1 collective-permute-start.3
  43.6 0.5 collective-permute-start.6
  44.1 4.4 %collective-permute-done.4.first_ref = bf16[96,1280]{1,0:T(8,128)(2,1)S(1)} collective-permute-done((bf16[96,1280]{1,0:T(8,128)(2,1)S(1)}, bf16[96,1280]{1,0:T(8,128)(2,1)S(1)}, u32[]{:S(2)}, u32[]{:S(2)}) %collective-permute-start.4) | collective-permute-done | bytes 245792 | tf_op jit(solution)/shard_map/ppermute | solution.py:466
  48.5 0.0 copy-start.2
  48.5 0.1 collective-permute-start.7
  48.6 0.0 collective-permute-done.3.refs_0_.refs_3_
  48.6 1.5 %shard_map.91 = (bf16[2,2,32,640]{3,2,1,0:T(8,128)(2,1)S(1)}, bf16[2,2,96,640]{3,2,1,0:T(8,128)(2,1)S(1)}) custom-call(bf16[200,1280]{1,0:T(8,128)(2,1)S(1)} %collective-permute-done.3.refs_0_.refs_3_, bf16[200,1280]{1,0:T(8,128)(2,1)S(1)} %collective-permute-done.6.refs_1_.refs_5_, bf16[2,1280,640]{2,1,0:T(8,128)(2,1)S(1)} %copy-done.1), custom_call_target="tpu_custom_call" | custom-call | flops 1 | bytes 1 | tf_op jit(solution)/shard_map/pallas_call | solution.py:68
  50.2 0.3 collective-permute-done.7.refs_1_.refs_0_.refs_7_
  50.5 1.5 %shard_map.92 = (bf16[2,2,32,640]{3,2,1,0:T(8,128)(2,1)S(1)}, bf16[2,2,96,640]{3,2,1,0:T(8,128)(2,1)S(1)}) custom-call(bf16[200,1280]{1,0:T(8,128)(2,1)S(1)} %shard_map.90.refs_0_.refs_6_, bf16[200,1280]{1,0:T(8,128)(2,1)S(1)} %collective-permute-done.7.refs_1_.refs_0_.refs_7_, bf16[2,1280,640]{2,1,0:T(8,128)(2,1)S(1)} %copy-done.1), custom_call_target="tpu_custom_call" | custom-call | flops 1 | bytes 1 | tf_op jit(solution)/shard_map/pallas_call | solution.py:68
  52.0 0.7 shard_map.93
  52.7 0.0 copy-start.5
  52.7 0.2 collective-permute-start.8
  53.0 0.7 shard_map.94.own_ref
  53.6 0.8 collective-permute-done.8.got_ref
  54.4 0.1 shard_map.95
  54.5 0.3 copy.11
  54.8 15.8 %all_to_all.21.part_ref = bf16[64,2,1280]{2,1,0:T(2,128)(2,1)S(1)} all-to-all(bf16[64,2,1280]{2,1,0:T(2,128)(2,1)S(1)} %bitcast.20), channel_id=1, replica_groups={{0,1,2,3,4,5,6,7,8,9,10,11,12,13,14,15,32,33,34,35,36,37,38,39,40,41,42..., dimensions={0} | all-to-all | bytes 655360 | tf_op jit(solution)/shard_map/all_to_all | solution.py:481
  70.6 0.3 shard_map.96
  70.9 18.5 %all_to_all.22 = f32[64,2,1280]{2,1,0:T(2,128)S(1)} all-to-all(f32[64,2,1280]{2,1,0:T(2,128)S(1)} %shard_map.96), channel_id=1, replica_groups={{0,1,2,3,4,5,6,7,8,9,10,11,12,13,14,15,32,33,34,35,36,37,38,39,40,41,42..., dimensions={0} | all-to-all | bytes 1310720 | tf_op jit(solution)/shard_map/all_to_all | solution.py:481
  89.5 0.1 collective-permute-start.9
  89.6 2.1 %collective-permute-done.9.other_ref = f32[2,64,1280]{2,1,0:T(8,128)S(1)} collective-permute-done((f32[2,64,1280]{2,1,0:T(8,128)S(1)}, f32[2,64,1280]{2,1,0:T(8,128)S(1)}, u32[]{:S(2)}, u32[]{:S(2)}) %collective-permute-start.9) | collective-permute-done | bytes 655392 | tf_op jit(solution)/shard_map/ppermute | solution.py:472
  91.7 2.9 %shard_map.97 = (f32[2,128,1280]{2,1,0:T(8,128)S(1)}, bf16[8,32,1280]{2,1,0:T(8,128)(2,1)S(1)}, bf16[2,256,640]{2,1,0:T(8,128)(2,1)S(1)}) custom-call(f32[2,64,1280]{2,1,0:T(8,128)S(1)} %bitcast.12, f32[2,64,1280]{2,1,0:T(8,128)S(1)} %collective-permute-done.9.other_ref, bf16[2,640,1280]{2,1,0:T(8,128)(2,1)S(1)} %copy-done.2), custom_call_target="tpu_custom_call" | custom-call | flops 1 | bytes 1 | tf_op jit(solution)/shard_map/pallas_call | solution.py:68
  94.6 1.2 shard_map.98
  95.8 0.2 collective-permute-start.10
  96.1 1.8 %shard_map.99 = (bf16[3,2,96,640]{3,2,1,0:T(8,128)(2,1)S(1)}, bf16[192,1280]{1,0:T(8,128)(2,1)S(1)}, bf16[192,1280]{1,0:T(8,128)(2,1)S(1)}, bf16[192,1280]{1,0:T(8,128)(2,1)S(1)}) custom-call(bf16[200,1280]{1,0:T(8,128)(2,1)S(1)} %shard_map.90.refs_0_.refs_6_, bf16[200,1280]{1,0:T(8,128)(2,1)S(1)} %collective-permute-done.6.refs_1_.refs_5_, ...), custom_call_target="tpu_custom_call" | custom-call | flops 1 | bytes 1 | tf_op jit(solution)/shard_map/pallas_call | solution.py:68
  97.8 0.5 collective-permute-start.12
  98.3 0.0 collective-permute-done.10.got_ref
  98.3 0.1 shard_map.100
  98.4 0.6 collective-permute-start.13
  99.0 2.8 %collective-permute-start.14 = (bf16[96,1280]{1,0:T(8,128)(2,1)S(1)}, bf16[96,1280]{1,0:T(8,128)(2,1)S(1)}, u32[]{:S(2)}, u32[]{:S(2)}) collective-permute-start(bf16[96,1280]{1,0:T(8,128)(2,1)S(1)} %get-tuple-element.93), channel_id=1, source_target_pairs={{0,96},{16,112},{32,0},{48,16},{64,32},{80,48},{96,64},{112,80},{1... | collective-permute-start | bytes 737288 | tf_op jit(solution)/shard_map/ppermute | solution.py:469
  101.7 2.3 %shard_map.101 = (bf16[4,2,96,640]{3,2,1,0:T(8,128)(2,1)S(1)}, bf16[192,1280]{1,0:T(8,128)(2,1)S(1)}, bf16[192,1280]{1,0:T(8,128)(2,1)S(1)}, bf16[192,1280]{1,0:T(8,128)(2,1)S(1)}, bf16[192,1280]{1,0:T(8,128)(2,1)S(1)}) custom-call(bf16[200,1280]{1,0:T(8,128)(2,1)S(1)} %collective-permute-done.3.refs_0_.refs_3_, ...), custom_call_target="tpu_custom_call" | custom-call | flops 1 | bytes 1 | tf_op jit(solution)/shard_map/pallas_call | solution.py:68
  104.0 0.0 collective-permute-done.12.got_ref
  104.0 0.1 shard_map.102
  104.1 0.1 collective-permute-start.17
  104.2 0.1 collective-permute-start.11
  104.3 0.5 collective-permute-start.15
  104.8 3.0 %collective-permute-done.13.y_ref = bf16[96,1280]{1,0:T(8,128)(2,1)S(1)} collective-permute-done((bf16[96,1280]{1,0:T(8,128)(2,1)S(1)}, bf16[96,1280]{1,0:T(8,128)(2,1)S(1)}, u32[]{:S(2)}, u32[]{:S(2)}) %collective-permute-start.13) | collective-permute-done | bytes 245792 | tf_op jit(solution)/shard_map/ppermute | solution.py:466
  107.8 0.1 shard_map.103
  107.8 0.1 collective-permute-start.16
  107.9 0.0 collective-permute-done.14.above_ref
  107.9 0.1 shard_map.104
  108.1 3.3 %collective-permute-start.19 = (bf16[96,1280]{1,0:T(8,128)(2,1)S(1)}, bf16[96,1280]{1,0:T(8,128)(2,1)S(1)}, u32[]{:S(2)}, u32[]{:S(2)}) collective-permute-start(bf16[96,1280]{1,0:T(8,128)(2,1)S(1)} %get-tuple-element.100), channel_id=1, source_target_pairs={{0,96},{16,112},{32,0},{48,16},{64,32},{80,48},{96,64},{112,80},{1... | collective-permute-start | bytes 737288 | tf_op jit(solution)/shard_map/ppermute | solution.py:469
  111.4 0.3 collective-permute-start.18
  111.7 3.4 %shard_map.105 = f32[2,640,1280]{2,1,0:T(8,128)} custom-call(bf16[1,2,32,640]{3,2,1,0:T(8,128)(2,1)S(1)} %get-tuple-element.53.refs_0_, bf16[3,2,32,640]{3,2,1,0:T(8,128)(2,1)S(1)} %get-tuple-element.57.refs_1_, bf16[2,2,32,640]{3,2,1,0:T(8,128)(2,1)S(1)} %get-tuple-element.63.refs_2_, bf16[2,2,32,640]{3,2,1,0:T(8,128)(2,1)S(1)} %get-tuple-element.65.refs_3_, ...), custom_call_target="tpu_custom_call" | custom-call | flops 1 | bytes 1 | tf_op jit(solution)/shard_map/pallas_call | solution.py:398
  115.1 5.6 %shard_map.106 = f32[2,1280,640]{2,1,0:T(8,128)} custom-call(bf16[200,1280]{1,0:T(8,128)(2,1)S(1)} %shard_map.86.refs_0_.refs_3_, bf16[200,1280]{1,0:T(8,128)(2,1)S(1)} %collective-permute-done.refs_0_.refs_1_, bf16[200,1280]{1,0:T(8,128)(2,1)S(1)} %collective-permute-done.1.x2_ref.refs_1_.refs_2_, ...), custom_call_target="tpu_custom_call" | custom-call | flops 1 | bytes 1 | tf_op jit(solution)/shard_map/pallas_call | solution.py:370
  120.7 0.0 collective-permute-done.15.got_ref
  120.7 0.0 collective-permute-done.19.hb_ref
  120.8 0.2 collective-permute-done.18.ha_ref
  121.0 0.5 shard_map.107
  121.5 14.5 %all_to_all.23.back_ref = bf16[16,16,1280]{2,1,0:T(8,128)(2,1)S(1)} all-to-all(bf16[16,16,1280]{2,1,0:T(8,128)(2,1)S(1)} %shard_map.107), channel_id=1, replica_groups=mesh['dp'=8,'expert'=16] {'expert'}, dimensions={0} | all-to-all | bytes 1310720 | tf_op jit(solution)/shard_map/all_to_all | solution.py:478
  136.0 1.3 shard_map.108
  (22 shorter events, 0.2 us)
Async XLA Ops:
  23.6 14.3 %collective-permute-start.1 = (bf16[200,1280]{1,0:T(8,128)(2,1)S(1)}, bf16[200,1280]{1,0:T(8,128)(2,1)S(1)}, u32[]{:S(2)}, u32[]{:S(2)}) collective-permute-start(bf16[200,1280]{1,0:T(8,128)(2,1)S(1)} %shard_map.86.refs_0_.refs_3_), channel_id=1, source_target_pairs={{0,32},{16,48},{32,64},{48,80},{64,96},{80,112},{96,0},{112,16},{1... | collective-permute-start | bytes 1536008 | tf_op jit(solution)/shard_map/ppermute | solution.py:466
  25.6 12.4 %collective-permute-start.2 = (bf16[200,1280]{1,0:T(8,128)(2,1)S(1)}, bf16[200,1280]{1,0:T(8,128)(2,1)S(1)}, u32[]{:S(2)}, u32[]{:S(2)}) collective-permute-start(bf16[200,1280]{1,0:T(8,128)(2,1)S(1)} %shard_map.86.refs_0_.refs_3_), channel_id=1, source_target_pairs={{0,96},{16,112},{32,0},{48,16},{64,32},{80,48},{96,64},{112,80},{1... | collective-permute-start | bytes 1536008 | tf_op jit(solution)/shard_map/ppermute | solution.py:469
  27.8 13.3 %collective-permute-start = (bf16[200,1280]{1,0:T(8,128)(2,1)S(1)}, bf16[200,1280]{1,0:T(8,128)(2,1)S(1)}, u32[]{:S(2)}, u32[]{:S(2)}) collective-permute-start(bf16[200,1280]{1,0:T(8,128)(2,1)S(1)} %shard_map.86.refs_0_.refs_3_), channel_id=1, source_target_pairs={{0,16},{16,0},{32,48},{48,32},{64,80},{80,64},{96,112},{112,96},{1... | collective-permute-start | bytes 1536008 | tf_op jit(solution)/shard_map/ppermute | solution.py:472
  27.8 1.9 %copy-start = (bf16[2,1280,640]{2,1,0:T(8,128)(2,1)S(1)}, bf16[2,1280,640]{2,1,0:T(8,128)(2,1)}, u32[]{:S(2)}) copy-start(bf16[2,1280,640]{2,1,0:T(8,128)(2,1)} %refs_9_.1) | copy-start | bytes 9830404
  29.7 11.4 %copy-start.1 = (bf16[2,1280,640]{2,1,0:T(8,128)(2,1)S(1)}, bf16[2,1280,640]{2,1,0:T(8,128)(2,1)}, u32[]{:S(2)}) copy-start(bf16[2,1280,640]{2,1,0:T(8,128)(2,1)} %refs_9_.1) | copy-start | bytes 9830404
  38.0 10.5 %collective-permute-start.5 = (bf16[104,1280]{1,0:T(8,128)(2,1)S(1)}, bf16[104,1280]{1,0:T(8,128)(2,1)S(1)}, u32[]{:S(2)}, u32[]{:S(2)}) collective-permute-start(bf16[104,1280]{1,0:T(8,128)(2,1)S(1)} %get-tuple-element.60), channel_id=1, source_target_pairs={{0,96},{16,112},{32,0},{48,16},{64,32},{80,48},{96,64},{112,80},{1... | collective-permute-start | bytes 798728 | tf_op jit(solution)/shard_map/ppermute | solution.py:469
  41.1 7.4 %collective-permute-start.4 = (bf16[96,1280]{1,0:T(8,128)(2,1)S(1)}, bf16[96,1280]{1,0:T(8,128)(2,1)S(1)}, u32[]{:S(2)}, u32[]{:S(2)}) collective-permute-start(bf16[96,1280]{1,0:T(8,128)(2,1)S(1)} %get-tuple-element.55), channel_id=1, source_target_pairs={{0,32},{16,48},{32,64},{48,80},{64,96},{80,112},{96,0},{112,16},{1... | collective-permute-start | bytes 737288 | tf_op jit(solution)/shard_map/ppermute | solution.py:466
  43.5 5.2 %collective-permute-start.3 = (bf16[200,1280]{1,0:T(8,128)(2,1)S(1)}, bf16[200,1280]{1,0:T(8,128)(2,1)S(1)}, u32[]{:S(2)}, u32[]{:S(2)}) collective-permute-start(bf16[200,1280]{1,0:T(8,128)(2,1)S(1)} %collective-permute-done.1.x2_ref.refs_1_.refs_2_), channel_id=1, source_target_pairs={{0,16},{16,0},{32,48},{48,32},{64,80},{80,64},{96,112},{112,96},{1... | collective-permute-start | bytes 1536008 | tf_op jit(solution)/shard_map/ppermute | solution.py:472
  43.6 5.1 %collective-permute-start.6 = (bf16[200,1280]{1,0:T(8,128)(2,1)S(1)}, bf16[200,1280]{1,0:T(8,128)(2,1)S(1)}, u32[]{:S(2)}, u32[]{:S(2)}) collective-permute-start(bf16[200,1280]{1,0:T(8,128)(2,1)S(1)} %collective-permute-done.2.x4_ref.refs_2_.refs_4_), channel_id=1, source_target_pairs={{0,16},{16,0},{32,48},{48,32},{64,80},{80,64},{96,112},{112,96},{1... | collective-permute-start | bytes 1536008 | tf_op jit(solution)/shard_map/ppermute | solution.py:472
  48.5 3.5 %copy-start.2 = (bf16[2,640,1280]{2,1,0:T(8,128)(2,1)S(1)}, bf16[2,640,1280]{2,1,0:T(8,128)(2,1)}, u32[]{:S(2)}) copy-start(bf16[2,640,1280]{2,1,0:T(8,128)(2,1)} %w_out.1) | copy-start | bytes 9830404
  48.5 2.0 %collective-permute-start.7 = (bf16[200,1280]{1,0:T(8,128)(2,1)S(1)}, bf16[200,1280]{1,0:T(8,128)(2,1)S(1)}, u32[]{:S(2)}, u32[]{:S(2)}) collective-permute-start(bf16[200,1280]{1,0:T(8,128)(2,1)S(1)} %shard_map.90.refs_0_.refs_6_), channel_id=1, source_target_pairs={{0,16},{16,0},{32,48},{48,32},{64,80},{80,64},{96,112},{112,96},{1... | collective-permute-start | bytes 1536008 | tf_op jit(solution)/shard_map/ppermute | solution.py:472
  52.7 17.9 %copy-start.5 = (f32[2,1280]{1,0:T(2,128)S(1)}, f32[2,1280]{1,0:T(2,128)}, u32[]{:S(2)}) copy-start(f32[2,1280]{1,0:T(2,128)} %get-tuple-element.68.sum_ref) | copy-start | bytes 30724
  52.7 1.7 %collective-permute-start.8 = (bf16[4,32,1280]{2,1,0:T(8,128)(2,1)S(1)}, bf16[4,32,1280]{2,1,0:T(8,128)(2,1)S(1)}, u32[]{:S(2)}, u32[]{:S(2)}) collective-permute-start(bf16[4,32,1280]{2,1,0:T(8,128)(2,1)S(1)} %shard_map.93), channel_id=1, source_target_pairs={{0,16},{16,0},{32,48},{48,32},{64,80},{80,64},{96,112},{112,96},{1... | collective-permute-start | bytes 983048 | tf_op jit(solution)/shard_map/ppermute | solution.py:472
  89.5 2.2 %collective-permute-start.9 = (f32[2,64,1280]{2,1,0:T(8,128)S(1)}, f32[2,64,1280]{2,1,0:T(8,128)S(1)}, u32[]{:S(2)}, u32[]{:S(2)}) collective-permute-start(f32[2,64,1280]{2,1,0:T(8,128)S(1)} %bitcast.11), channel_id=1, source_target_pairs={{0,16},{16,0},{32,48},{48,32},{64,80},{80,64},{96,112},{112,96},{1... | collective-permute-start | bytes 1966088 | tf_op jit(solution)/shard_map/ppermute | solution.py:472
  95.8 2.5 %collective-permute-start.10 = (bf16[192,1280]{1,0:T(8,128)(2,1)S(1)}, bf16[192,1280]{1,0:T(8,128)(2,1)S(1)}, u32[]{:S(2)}, u32[]{:S(2)}) collective-permute-start(bf16[192,1280]{1,0:T(8,128)(2,1)S(1)} %get-tuple-element.75), channel_id=1, source_target_pairs={{0,16},{16,0},{32,48},{48,32},{64,80},{80,64},{96,112},{112,96},{1... | collective-permute-start | bytes 1474568 | tf_op jit(solution)/shard_map/ppermute | solution.py:472
  97.8 6.2 %collective-permute-start.12 = (bf16[192,1280]{1,0:T(8,128)(2,1)S(1)}, bf16[192,1280]{1,0:T(8,128)(2,1)S(1)}, u32[]{:S(2)}, u32[]{:S(2)}) collective-permute-start(bf16[192,1280]{1,0:T(8,128)(2,1)S(1)} %get-tuple-element.88), channel_id=1, source_target_pairs={{0,16},{16,0},{32,48},{48,32},{64,80},{80,64},{96,112},{112,96},{1... | collective-permute-start | bytes 1474568 | tf_op jit(solution)/shard_map/ppermute | solution.py:472
  98.4 9.3 %collective-permute-start.13 = (bf16[96,1280]{1,0:T(8,128)(2,1)S(1)}, bf16[96,1280]{1,0:T(8,128)(2,1)S(1)}, u32[]{:S(2)}, u32[]{:S(2)}) collective-permute-start(bf16[96,1280]{1,0:T(8,128)(2,1)S(1)} %get-tuple-element.78), channel_id=1, source_target_pairs={{0,32},{16,48},{32,64},{48,80},{64,96},{80,112},{96,0},{112,16},{1... | collective-permute-start | bytes 737288 | tf_op jit(solution)/shard_map/ppermute | solution.py:466
  99.0 8.9 %collective-permute-start.14 = (bf16[96,1280]{1,0:T(8,128)(2,1)S(1)}, bf16[96,1280]{1,0:T(8,128)(2,1)S(1)}, u32[]{:S(2)}, u32[]{:S(2)}) collective-permute-start(bf16[96,1280]{1,0:T(8,128)(2,1)S(1)} %get-tuple-element.93), channel_id=1, source_target_pairs={{0,96},{16,112},{32,0},{48,16},{64,32},{80,48},{96,64},{112,80},{1... | collective-permute-start | bytes 737288 | tf_op jit(solution)/shard_map/ppermute | solution.py:469
  104.1 16.6 %collective-permute-start.17 = (bf16[96,1280]{1,0:T(8,128)(2,1)S(1)}, bf16[96,1280]{1,0:T(8,128)(2,1)S(1)}, u32[]{:S(2)}, u32[]{:S(2)}) collective-permute-start(bf16[96,1280]{1,0:T(8,128)(2,1)S(1)} %get-tuple-element.99), channel_id=1, source_target_pairs={{0,32},{16,48},{32,64},{48,80},{64,96},{80,112},{96,0},{112,16},{1... | collective-permute-start | bytes 737288 | tf_op jit(solution)/shard_map/ppermute | solution.py:466
  104.2 3.7 %collective-permute-start.11 = (bf16[192,1280]{1,0:T(8,128)(2,1)S(1)}, bf16[192,1280]{1,0:T(8,128)(2,1)S(1)}, u32[]{:S(2)}, u32[]{:S(2)}) collective-permute-start(bf16[192,1280]{1,0:T(8,128)(2,1)S(1)} %get-tuple-element.86), channel_id=1, source_target_pairs={{0,16},{16,0},{32,48},{48,32},{64,80},{80,64},{96,112},{112,96},{1... | collective-permute-start | bytes 1474568 | tf_op jit(solution)/shard_map/ppermute | solution.py:472
  104.3 16.4 %collective-permute-start.15 = (bf16[192,1280]{1,0:T(8,128)(2,1)S(1)}, bf16[192,1280]{1,0:T(8,128)(2,1)S(1)}, u32[]{:S(2)}, u32[]{:S(2)}) collective-permute-start(bf16[192,1280]{1,0:T(8,128)(2,1)S(1)} %get-tuple-element.98), channel_id=1, source_target_pairs={{0,16},{16,0},{32,48},{48,32},{64,80},{80,64},{96,112},{112,96},{1... | collective-permute-start | bytes 1474568 | tf_op jit(solution)/shard_map/ppermute | solution.py:472
  107.8 12.9 %collective-permute-start.16 = (bf16[96,1280]{1,0:T(8,128)(2,1)S(1)}, bf16[96,1280]{1,0:T(8,128)(2,1)S(1)}, u32[]{:S(2)}, u32[]{:S(2)}) collective-permute-start(bf16[96,1280]{1,0:T(8,128)(2,1)S(1)} %shard_map.103), channel_id=1, source_target_pairs={{0,32},{16,48},{32,64},{48,80},{64,96},{80,112},{96,0},{112,16},{1... | collective-permute-start | bytes 737288 | tf_op jit(solution)/shard_map/ppermute | solution.py:466
  108.1 12.7 %collective-permute-start.19 = (bf16[96,1280]{1,0:T(8,128)(2,1)S(1)}, bf16[96,1280]{1,0:T(8,128)(2,1)S(1)}, u32[]{:S(2)}, u32[]{:S(2)}) collective-permute-start(bf16[96,1280]{1,0:T(8,128)(2,1)S(1)} %get-tuple-element.100), channel_id=1, source_target_pairs={{0,96},{16,112},{32,0},{48,16},{64,32},{80,48},{96,64},{112,80},{1... | collective-permute-start | bytes 737288 | tf_op jit(solution)/shard_map/ppermute | solution.py:469
  111.4 9.6 %collective-permute-start.18 = (bf16[96,1280]{1,0:T(8,128)(2,1)S(1)}, bf16[96,1280]{1,0:T(8,128)(2,1)S(1)}, u32[]{:S(2)}, u32[]{:S(2)}) collective-permute-start(bf16[96,1280]{1,0:T(8,128)(2,1)S(1)} %get-tuple-element.94), channel_id=1, source_target_pairs={{0,96},{16,112},{32,0},{48,16},{64,32},{80,48},{96,64},{112,80},{1... | collective-permute-start | bytes 737288 | tf_op jit(solution)/shard_map/ppermute | solution.py:469
  120.7 15.3 %copy-start.3 = (bf16[1,2,64,1280]{3,2,1,0:T(8,128)(2,1)S(1)}, bf16[1,2,64,1280]{3,2,1,0:T(8,128)(2,1)}, u32[]{:S(2)}) copy-start(bf16[1,2,64,1280]{3,2,1,0:T(8,128)(2,1)} %param.6) | copy-start | bytes 983044
  120.7 15.3 %copy-start.4 = (f32[1280]{0:T(1024)S(1)}, f32[1280]{0:T(1024)}, u32[]{:S(2)}) copy-start(f32[1280]{0:T(1024)} %gain_ref.1) | copy-start | bytes 15364
  120.7 15.3 %copy-start.6 = (s32[1,2,64]{2,1,0:T(2,128)S(1)}, s32[1,2,64]{2,1,0:T(2,128)}, u32[]{:S(2)}) copy-start(s32[1,2,64]{2,1,0:T(2,128)} %param.7) | copy-start | bytes 1540
  120.7 15.3 %copy-start.7 = (s32[1,2,64]{2,1,0:T(2,128)S(1)}, s32[1,2,64]{2,1,0:T(2,128)}, u32[]{:S(2)}) copy-start(s32[1,2,64]{2,1,0:T(2,128)} %param.8) | copy-start | bytes 1540

commit v8 on v7

--- a/solution.py
+++ b/solution.py
@@ -20,7 +20,7 @@
 PAD = 16
 PEERS = 16
 HALF = PEERS * CAP
-KIND_ROWS = 8
+KIND_ROWS = 16
 POOLED = 2 * PEERS
 PAIR_TOKENS = 64
 LANES = 128
@@ -180,8 +180,8 @@
         pool_table(blocks, held, wide_ref)
         rows = [block[held * HALF : (held + 1) * HALF, :] for block in blocks]
         rows = jnp.concatenate(rows, axis=0)
-        for at in range(0, hidden, 256):
-            to = slice(at, min(at + 256, hidden))
+        for at in range(0, hidden, 640):
+            to = slice(at, min(at + 640, hidden))
             full = nn(rows, w_in[held, :, to])
             for k in range(count):
                 h = full[k * HALF : (k + 1) * HALF]

time: 138 us -> 138 us (level)
  no operation moved by 1% of the time
where the time goes in v8:
time: 138 us
  blocking collectives  68.9 us (50%)
  Pallas kernels  30.7 us (22%)
  waiting for transfers between devices  18.4 us (13%)
  starting transfers between devices  16.5 us (12%)
  local copies, waits for them, and re-layouts  2.25 us (2%)
    all_to_all x2, blocking collectives, exchange(): return lax.all_to_all(x, 'expert', split_axis=0, concat_axis=0, tiled=True)  34.6 us
    all_to_all x2, blocking collectives, spread(): lax.all_to_all(x, everyone, split_axis=0, concat_axis=0, tiled=True, axis...  34.3 us
    pallas_call x22, Pallas kernels, call(): pl.pallas_call(kernel, out_shape=out, in_specs=[pl.BlockSpec(memory_space...  21.6 us
    ppermute x5, waiting for transfers between devices, up(): return lax.ppermute(x, 'dp', [(i, (i + 2) % 8) for i in range(8)])  15 us
    ppermute x5, starting transfers between devices, down(): return lax.ppermute(x, 'dp', [(i, (i + 6) % 8) for i in range(8)])  11.6 us
    pallas_call x1, Pallas kernels, grad_in(): pl.pallas_call(grad_in_kernel, grid=(HELD,), out_shape=shape_of(HELD, wid...  5.62 us
    pallas_call x1, Pallas kernels, grad_out(): pl.pallas_call(grad_out_kernel, grid=(HELD,), out_shape=shape_of(HELD, hi...  3.43 us
    ppermute x10, waiting for transfers between devices, swap(): return lax.ppermute(x, 'dp', [(i, i ^ 1) for i in range(8)])  3.25 us
  transfers between devices with their start and end apart: 20, of which 7 were waited for; matrix products, arithmetic and copies ran while one was open for 0% of the time, Pallas kernels for 14%

profile of v8, /device:TPU:0, one launch (start us, length us, event | category | flops | bytes accessed | tf_op | source)
XLA Modules:
  0.0 137.7 jit_solution(8096651238479821298)
XLA Ops:
  0.6 2.5 %shard_map.85 = (bf16[16,16,1280]{2,1,0:T(8,128)(2,1)}, f32[2,1280]{1,0:T(2,128)}) custom-call(s32[2,64]{1,0:T(2,128)} %bitcast.16, s32[2,64]{1,0:T(2,128)} %bitcast.18, bf16[128,1280]{1,0:T(8,128)(2,1)} %bitcast.13, f32[1280]{0:T(1024)} %gain_ref.1), custom_call_target="tpu_custom_call" | custom-call | flops 1 | bytes 1 | tf_op jit(solution)/shard_map/pallas_call | solution.py:68
  3.1 20.1 %all_to_all.20.in_ref = bf16[16,16,1280]{2,1,0:T(8,128)(2,1)S(1)} all-to-all(bf16[16,16,1280]{2,1,0:T(8,128)(2,1)} %get-tuple-element.52), channel_id=1, replica_groups=mesh['dp'=8,'expert'=16] {'expert'}, dimensions={0} | all-to-all | bytes 1310720 | tf_op jit(solution)/shard_map/all_to_all | solution.py:478
  23.2 0.4 shard_map.86.refs_0_.refs_3_
  23.6 2.0 %collective-permute-start.1 = (bf16[208,1280]{1,0:T(8,128)(2,1)S(1)}, bf16[208,1280]{1,0:T(8,128)(2,1)S(1)}, u32[]{:S(2)}, u32[]{:S(2)}) collective-permute-start(bf16[208,1280]{1,0:T(8,128)(2,1)S(1)} %shard_map.86.refs_0_.refs_3_), channel_id=1, source_target_pairs={{0,32},{16,48},{32,64},{48,80},{64,96},{80,112},{96,0},{112,16},{1... | collective-permute-start | bytes 1597448 | tf_op jit(solution)/shard_map/ppermute | solution.py:466
  25.5 2.2 %collective-permute-start.2 = (bf16[208,1280]{1,0:T(8,128)(2,1)S(1)}, bf16[208,1280]{1,0:T(8,128)(2,1)S(1)}, u32[]{:S(2)}, u32[]{:S(2)}) collective-permute-start(bf16[208,1280]{1,0:T(8,128)(2,1)S(1)} %shard_map.86.refs_0_.refs_3_), channel_id=1, source_target_pairs={{0,96},{16,112},{32,0},{48,16},{64,32},{80,48},{96,64},{112,80},{1... | collective-permute-start | bytes 1597448 | tf_op jit(solution)/shard_map/ppermute | solution.py:469
  27.7 0.0 collective-permute-start
  27.8 1.9 %copy-done = bf16[2,1280,640]{2,1,0:T(8,128)(2,1)S(1)} copy-done((bf16[2,1280,640]{2,1,0:T(8,128)(2,1)S(1)}, bf16[2,1280,640]{2,1,0:T(8,128)(2,1)}, u32[]{:S(2)}) %copy-start) | copy-done | bytes 3276824
  29.7 1.1 shard_map.87
  30.8 7.6 %collective-permute-done.1.x2_ref.refs_1_.refs_2_ = bf16[208,1280]{1,0:T(8,128)(2,1)S(1)} collective-permute-done((bf16[208,1280]{1,0:T(8,128)(2,1)S(1)}, bf16[208,1280]{1,0:T(8,128)(2,1)S(1)}, u32[]{:S(2)}, u32[]{:S(2)}) %collective-permute-start.1) | collective-permute-done | bytes 532512 | tf_op jit(solution)/shard_map/ppermute | solution.py:466
  38.3 0.0 collective-permute-done.2.x4_ref.refs_2_.refs_4_
  38.4 3.1 %collective-permute-start.5 = (bf16[112,1280]{1,0:T(8,128)(2,1)S(1)}, bf16[112,1280]{1,0:T(8,128)(2,1)S(1)}, u32[]{:S(2)}, u32[]{:S(2)}) collective-permute-start(bf16[112,1280]{1,0:T(8,128)(2,1)S(1)} %get-tuple-element.60), channel_id=1, source_target_pairs={{0,96},{16,112},{32,0},{48,16},{64,32},{80,48},{96,64},{112,80},{1... | collective-permute-start | bytes 860168 | tf_op jit(solution)/shard_map/ppermute | solution.py:469
  41.5 0.0 collective-permute-start.4
  41.5 2.4 %shard_map.89 = (bf16[3,2,32,640]{3,2,1,0:T(8,128)(2,1)S(1)}, bf16[3,2,96,640]{3,2,1,0:T(8,128)(2,1)S(1)}) custom-call(bf16[208,1280]{1,0:T(8,128)(2,1)S(1)} %collective-permute-done.refs_0_.refs_1_, bf16[208,1280]{1,0:T(8,128)(2,1)S(1)} %collective-permute-done.1.x2_ref.refs_1_.refs_2_, bf16[208,1280]{1,0:T(8,128)(2,1)S(1)} %collective-permute-done.2.x4_ref.refs_2_.refs_4_, ...), custom_call_target="tpu_custom_call" | custom-call | flops 1 | bytes 1 | tf_op jit(solution)/shard_map/pallas_call | solution.py:68
  43.9 0.1 collective-permute-start.3
  44.0 0.5 collective-permute-start.6
  44.5 4.4 %collective-permute-done.4.first_ref = bf16[96,1280]{1,0:T(8,128)(2,1)S(1)} collective-permute-done((bf16[96,1280]{1,0:T(8,128)(2,1)S(1)}, bf16[96,1280]{1,0:T(8,128)(2,1)S(1)}, u32[]{:S(2)}, u32[]{:S(2)}) %collective-permute-start.4) | collective-permute-done | bytes 245792 | tf_op jit(solution)/shard_map/ppermute | solution.py:466
  48.9 0.0 copy-start.2
  49.0 0.1 collective-permute-start.7
  49.1 0.0 collective-permute-done.6.refs_1_.refs_5_
  49.1 1.5 %shard_map.91 = (bf16[2,2,32,640]{3,2,1,0:T(8,128)(2,1)S(1)}, bf16[2,2,96,640]{3,2,1,0:T(8,128)(2,1)S(1)}) custom-call(bf16[208,1280]{1,0:T(8,128)(2,1)S(1)} %collective-permute-done.3.refs_0_.refs_3_, bf16[208,1280]{1,0:T(8,128)(2,1)S(1)} %collective-permute-done.6.refs_1_.refs_5_, bf16[2,1280,640]{2,1,0:T(8,128)(2,1)S(1)} %copy-done.1), custom_call_target="tpu_custom_call" | custom-call | flops 1 | bytes 1 | tf_op jit(solution)/shard_map/pallas_call | solution.py:68
  50.6 0.3 collective-permute-done.7.refs_1_.refs_0_.refs_7_
  51.0 1.5 %shard_map.92 = (bf16[2,2,32,640]{3,2,1,0:T(8,128)(2,1)S(1)}, bf16[2,2,96,640]{3,2,1,0:T(8,128)(2,1)S(1)}) custom-call(bf16[208,1280]{1,0:T(8,128)(2,1)S(1)} %shard_map.90.refs_0_.refs_6_, bf16[208,1280]{1,0:T(8,128)(2,1)S(1)} %collective-permute-done.7.refs_1_.refs_0_.refs_7_, bf16[2,1280,640]{2,1,0:T(8,128)(2,1)S(1)} %copy-done.1), custom_call_target="tpu_custom_call" | custom-call | flops 1 | bytes 1 | tf_op jit(solution)/shard_map/pallas_call | solution.py:68
  52.5 0.7 shard_map.93
  53.2 0.0 copy-start.5
  53.2 0.2 collective-permute-start.8
  53.4 0.7 shard_map.94.own_ref
  54.1 0.8 collective-permute-done.8.got_ref
  54.9 0.1 shard_map.95
  55.0 0.3 copy.11
  55.2 15.8 %all_to_all.21.part_ref = bf16[64,2,1280]{2,1,0:T(2,128)(2,1)S(1)} all-to-all(bf16[64,2,1280]{2,1,0:T(2,128)(2,1)S(1)} %bitcast.20), channel_id=1, replica_groups={{0,1,2,3,4,5,6,7,8,9,10,11,12,13,14,15,32,33,34,35,36,37,38,39,40,41,42..., dimensions={0} | all-to-all | bytes 655360 | tf_op jit(solution)/shard_map/all_to_all | solution.py:481
  71.0 0.3 shard_map.96
  71.4 18.5 %all_to_all.22 = f32[64,2,1280]{2,1,0:T(2,128)S(1)} all-to-all(f32[64,2,1280]{2,1,0:T(2,128)S(1)} %shard_map.96), channel_id=1, replica_groups={{0,1,2,3,4,5,6,7,8,9,10,11,12,13,14,15,32,33,34,35,36,37,38,39,40,41,42..., dimensions={0} | all-to-all | bytes 1310720 | tf_op jit(solution)/shard_map/all_to_all | solution.py:481
  89.9 0.1 collective-permute-start.9
  90.0 2.1 %collective-permute-done.9.other_ref = f32[2,64,1280]{2,1,0:T(8,128)S(1)} collective-permute-done((f32[2,64,1280]{2,1,0:T(8,128)S(1)}, f32[2,64,1280]{2,1,0:T(8,128)S(1)}, u32[]{:S(2)}, u32[]{:S(2)}) %collective-permute-start.9) | collective-permute-done | bytes 655392 | tf_op jit(solution)/shard_map/ppermute | solution.py:472
  92.1 2.9 %shard_map.97 = (f32[2,128,1280]{2,1,0:T(8,128)S(1)}, bf16[8,32,1280]{2,1,0:T(8,128)(2,1)S(1)}, bf16[2,256,640]{2,1,0:T(8,128)(2,1)S(1)}) custom-call(f32[2,64,1280]{2,1,0:T(8,128)S(1)} %bitcast.12, f32[2,64,1280]{2,1,0:T(8,128)S(1)} %collective-permute-done.9.other_ref, bf16[2,640,1280]{2,1,0:T(8,128)(2,1)S(1)} %copy-done.2), custom_call_target="tpu_custom_call" | custom-call | flops 1 | bytes 1 | tf_op jit(solution)/shard_map/pallas_call | solution.py:68
  95.0 1.2 shard_map.98
  96.3 0.2 collective-permute-start.10
  96.5 1.8 %shard_map.99 = (bf16[3,2,96,640]{3,2,1,0:T(8,128)(2,1)S(1)}, bf16[192,1280]{1,0:T(8,128)(2,1)S(1)}, bf16[192,1280]{1,0:T(8,128)(2,1)S(1)}, bf16[192,1280]{1,0:T(8,128)(2,1)S(1)}) custom-call(bf16[208,1280]{1,0:T(8,128)(2,1)S(1)} %shard_map.90.refs_0_.refs_6_, bf16[208,1280]{1,0:T(8,128)(2,1)S(1)} %collective-permute-done.6.refs_1_.refs_5_, ...), custom_call_target="tpu_custom_call" | custom-call | flops 1 | bytes 1 | tf_op jit(solution)/shard_map/pallas_call | solution.py:68
  98.3 0.5 collective-permute-start.12
  98.7 0.0 collective-permute-done.10.got_ref
  98.7 0.1 shard_map.100
  98.8 0.6 collective-permute-start.13
  99.4 2.8 %collective-permute-start.14 = (bf16[96,1280]{1,0:T(8,128)(2,1)S(1)}, bf16[96,1280]{1,0:T(8,128)(2,1)S(1)}, u32[]{:S(2)}, u32[]{:S(2)}) collective-permute-start(bf16[96,1280]{1,0:T(8,128)(2,1)S(1)} %get-tuple-element.93), channel_id=1, source_target_pairs={{0,96},{16,112},{32,0},{48,16},{64,32},{80,48},{96,64},{112,80},{1... | collective-permute-start | bytes 737288 | tf_op jit(solution)/shard_map/ppermute | solution.py:469
  102.1 2.3 %shard_map.101 = (bf16[4,2,96,640]{3,2,1,0:T(8,128)(2,1)S(1)}, bf16[192,1280]{1,0:T(8,128)(2,1)S(1)}, bf16[192,1280]{1,0:T(8,128)(2,1)S(1)}, bf16[192,1280]{1,0:T(8,128)(2,1)S(1)}, bf16[192,1280]{1,0:T(8,128)(2,1)S(1)}) custom-call(bf16[208,1280]{1,0:T(8,128)(2,1)S(1)} %collective-permute-done.3.refs_0_.refs_3_, ...), custom_call_target="tpu_custom_call" | custom-call | flops 1 | bytes 1 | tf_op jit(solution)/shard_map/pallas_call | solution.py:68
  104.4 0.0 collective-permute-done.12.got_ref
  104.4 0.1 shard_map.102
  104.5 0.1 collective-permute-start.17
  104.6 0.1 collective-permute-start.11
  104.7 0.5 collective-permute-start.15
  105.2 3.0 %collective-permute-done.13.y_ref = bf16[96,1280]{1,0:T(8,128)(2,1)S(1)} collective-permute-done((bf16[96,1280]{1,0:T(8,128)(2,1)S(1)}, bf16[96,1280]{1,0:T(8,128)(2,1)S(1)}, u32[]{:S(2)}, u32[]{:S(2)}) %collective-permute-start.13) | collective-permute-done | bytes 245792 | tf_op jit(solution)/shard_map/ppermute | solution.py:466
  108.2 0.1 shard_map.103
  108.2 0.1 collective-permute-start.16
  108.3 0.0 collective-permute-done.11.got_ref
  108.3 0.1 shard_map.104
  108.5 3.3 %collective-permute-start.19 = (bf16[96,1280]{1,0:T(8,128)(2,1)S(1)}, bf16[96,1280]{1,0:T(8,128)(2,1)S(1)}, u32[]{:S(2)}, u32[]{:S(2)}) collective-permute-start(bf16[96,1280]{1,0:T(8,128)(2,1)S(1)} %get-tuple-element.100), channel_id=1, source_target_pairs={{0,96},{16,112},{32,0},{48,16},{64,32},{80,48},{96,64},{112,80},{1... | collective-permute-start | bytes 737288 | tf_op jit(solution)/shard_map/ppermute | solution.py:469
  111.8 0.3 collective-permute-start.18
  112.1 3.4 %shard_map.105 = f32[2,640,1280]{2,1,0:T(8,128)} custom-call(bf16[1,2,32,640]{3,2,1,0:T(8,128)(2,1)S(1)} %get-tuple-element.53.refs_0_, bf16[3,2,32,640]{3,2,1,0:T(8,128)(2,1)S(1)} %get-tuple-element.57.refs_1_, bf16[2,2,32,640]{3,2,1,0:T(8,128)(2,1)S(1)} %get-tuple-element.63.refs_2_, bf16[2,2,32,640]{3,2,1,0:T(8,128)(2,1)S(1)} %get-tuple-element.65.refs_3_, ...), custom_call_target="tpu_custom_call" | custom-call | flops 1 | bytes 1 | tf_op jit(solution)/shard_map/pallas_call | solution.py:398
  115.5 5.6 %shard_map.106 = f32[2,1280,640]{2,1,0:T(8,128)} custom-call(bf16[208,1280]{1,0:T(8,128)(2,1)S(1)} %shard_map.86.refs_0_.refs_3_, bf16[208,1280]{1,0:T(8,128)(2,1)S(1)} %collective-permute-done.refs_0_.refs_1_, bf16[208,1280]{1,0:T(8,128)(2,1)S(1)} %collective-permute-done.1.x2_ref.refs_1_.refs_2_, ...), custom_call_target="tpu_custom_call" | custom-call | flops 1 | bytes 1 | tf_op jit(solution)/shard_map/pallas_call | solution.py:370
  121.1 0.0 collective-permute-done.16.la_ref
  121.1 0.0 collective-permute-done.15.got_ref
  121.2 0.2 collective-permute-done.18.ha_ref
  121.4 0.5 shard_map.107
  121.9 14.5 %all_to_all.23.back_ref = bf16[16,16,1280]{2,1,0:T(8,128)(2,1)S(1)} all-to-all(bf16[16,16,1280]{2,1,0:T(8,128)(2,1)S(1)} %shard_map.107), channel_id=1, replica_groups=mesh['dp'=8,'expert'=16] {'expert'}, dimensions={0} | all-to-all | bytes 1310720 | tf_op jit(solution)/shard_map/all_to_all | solution.py:478
  136.4 1.3 shard_map.108
  (22 shorter events, 0.2 us)
Async XLA Ops:
  23.6 14.8 %collective-permute-start.1 = (bf16[208,1280]{1,0:T(8,128)(2,1)S(1)}, bf16[208,1280]{1,0:T(8,128)(2,1)S(1)}, u32[]{:S(2)}, u32[]{:S(2)}) collective-permute-start(bf16[208,1280]{1,0:T(8,128)(2,1)S(1)} %shard_map.86.refs_0_.refs_3_), channel_id=1, source_target_pairs={{0,32},{16,48},{32,64},{48,80},{64,96},{80,112},{96,0},{112,16},{1... | collective-permute-start | bytes 1597448 | tf_op jit(solution)/shard_map/ppermute | solution.py:466
  25.5 12.8 %collective-permute-start.2 = (bf16[208,1280]{1,0:T(8,128)(2,1)S(1)}, bf16[208,1280]{1,0:T(8,128)(2,1)S(1)}, u32[]{:S(2)}, u32[]{:S(2)}) collective-permute-start(bf16[208,1280]{1,0:T(8,128)(2,1)S(1)} %shard_map.86.refs_0_.refs_3_), channel_id=1, source_target_pairs={{0,96},{16,112},{32,0},{48,16},{64,32},{80,48},{96,64},{112,80},{1... | collective-permute-start | bytes 1597448 | tf_op jit(solution)/shard_map/ppermute | solution.py:469
  27.7 13.8 %collective-permute-start = (bf16[208,1280]{1,0:T(8,128)(2,1)S(1)}, bf16[208,1280]{1,0:T(8,128)(2,1)S(1)}, u32[]{:S(2)}, u32[]{:S(2)}) collective-permute-start(bf16[208,1280]{1,0:T(8,128)(2,1)S(1)} %shard_map.86.refs_0_.refs_3_), channel_id=1, source_target_pairs={{0,16},{16,0},{32,48},{48,32},{64,80},{80,64},{96,112},{112,96},{1... | collective-permute-start | bytes 1597448 | tf_op jit(solution)/shard_map/ppermute | solution.py:472
  27.7 1.9 %copy-start = (bf16[2,1280,640]{2,1,0:T(8,128)(2,1)S(1)}, bf16[2,1280,640]{2,1,0:T(8,128)(2,1)}, u32[]{:S(2)}) copy-start(bf16[2,1280,640]{2,1,0:T(8,128)(2,1)} %refs_9_.1) | copy-start | bytes 9830404
  29.7 11.8 %copy-start.1 = (bf16[2,1280,640]{2,1,0:T(8,128)(2,1)S(1)}, bf16[2,1280,640]{2,1,0:T(8,128)(2,1)}, u32[]{:S(2)}) copy-start(bf16[2,1280,640]{2,1,0:T(8,128)(2,1)} %refs_9_.1) | copy-start | bytes 9830404
  38.4 10.5 %collective-permute-start.5 = (bf16[112,1280]{1,0:T(8,128)(2,1)S(1)}, bf16[112,1280]{1,0:T(8,128)(2,1)S(1)}, u32[]{:S(2)}, u32[]{:S(2)}) collective-permute-start(bf16[112,1280]{1,0:T(8,128)(2,1)S(1)} %get-tuple-element.60), channel_id=1, source_target_pairs={{0,96},{16,112},{32,0},{48,16},{64,32},{80,48},{96,64},{112,80},{1... | collective-permute-start | bytes 860168 | tf_op jit(solution)/shard_map/ppermute | solution.py:469
  41.5 7.4 %collective-permute-start.4 = (bf16[96,1280]{1,0:T(8,128)(2,1)S(1)}, bf16[96,1280]{1,0:T(8,128)(2,1)S(1)}, u32[]{:S(2)}, u32[]{:S(2)}) collective-permute-start(bf16[96,1280]{1,0:T(8,128)(2,1)S(1)} %get-tuple-element.55), channel_id=1, source_target_pairs={{0,32},{16,48},{32,64},{48,80},{64,96},{80,112},{96,0},{112,16},{1... | collective-permute-start | bytes 737288 | tf_op jit(solution)/shard_map/ppermute | solution.py:466
  43.9 5.2 %collective-permute-start.3 = (bf16[208,1280]{1,0:T(8,128)(2,1)S(1)}, bf16[208,1280]{1,0:T(8,128)(2,1)S(1)}, u32[]{:S(2)}, u32[]{:S(2)}) collective-permute-start(bf16[208,1280]{1,0:T(8,128)(2,1)S(1)} %collective-permute-done.1.x2_ref.refs_1_.refs_2_), channel_id=1, source_target_pairs={{0,16},{16,0},{32,48},{48,32},{64,80},{80,64},{96,112},{112,96},{1... | collective-permute-start | bytes 1597448 | tf_op jit(solution)/shard_map/ppermute | solution.py:472
  44.0 5.1 %collective-permute-start.6 = (bf16[208,1280]{1,0:T(8,128)(2,1)S(1)}, bf16[208,1280]{1,0:T(8,128)(2,1)S(1)}, u32[]{:S(2)}, u32[]{:S(2)}) collective-permute-start(bf16[208,1280]{1,0:T(8,128)(2,1)S(1)} %collective-permute-done.2.x4_ref.refs_2_.refs_4_), channel_id=1, source_target_pairs={{0,16},{16,0},{32,48},{48,32},{64,80},{80,64},{96,112},{112,96},{1... | collective-permute-start | bytes 1597448 | tf_op jit(solution)/shard_map/ppermute | solution.py:472
  48.9 3.6 %copy-start.2 = (bf16[2,640,1280]{2,1,0:T(8,128)(2,1)S(1)}, bf16[2,640,1280]{2,1,0:T(8,128)(2,1)}, u32[]{:S(2)}) copy-start(bf16[2,640,1280]{2,1,0:T(8,128)(2,1)} %w_out.1) | copy-start | bytes 9830404
  49.0 2.0 %collective-permute-start.7 = (bf16[208,1280]{1,0:T(8,128)(2,1)S(1)}, bf16[208,1280]{1,0:T(8,128)(2,1)S(1)}, u32[]{:S(2)}, u32[]{:S(2)}) collective-permute-start(bf16[208,1280]{1,0:T(8,128)(2,1)S(1)} %shard_map.90.refs_0_.refs_6_), channel_id=1, source_target_pairs={{0,16},{16,0},{32,48},{48,32},{64,80},{80,64},{96,112},{112,96},{1... | collective-permute-start | bytes 1597448 | tf_op jit(solution)/shard_map/ppermute | solution.py:472
  53.2 17.9 %copy-start.5 = (f32[2,1280]{1,0:T(2,128)S(1)}, f32[2,1280]{1,0:T(2,128)}, u32[]{:S(2)}) copy-start(f32[2,1280]{1,0:T(2,128)} %get-tuple-element.68.sum_ref) | copy-start | bytes 30724
  53.2 1.7 %collective-permute-start.8 = (bf16[4,32,1280]{2,1,0:T(8,128)(2,1)S(1)}, bf16[4,32,1280]{2,1,0:T(8,128)(2,1)S(1)}, u32[]{:S(2)}, u32[]{:S(2)}) collective-permute-start(bf16[4,32,1280]{2,1,0:T(8,128)(2,1)S(1)} %shard_map.93), channel_id=1, source_target_pairs={{0,16},{16,0},{32,48},{48,32},{64,80},{80,64},{96,112},{112,96},{1... | collective-permute-start | bytes 983048 | tf_op jit(solution)/shard_map/ppermute | solution.py:472
  89.9 2.2 %collective-permute-start.9 = (f32[2,64,1280]{2,1,0:T(8,128)S(1)}, f32[2,64,1280]{2,1,0:T(8,128)S(1)}, u32[]{:S(2)}, u32[]{:S(2)}) collective-permute-start(f32[2,64,1280]{2,1,0:T(8,128)S(1)} %bitcast.11), channel_id=1, source_target_pairs={{0,16},{16,0},{32,48},{48,32},{64,80},{80,64},{96,112},{112,96},{1... | collective-permute-start | bytes 1966088 | tf_op jit(solution)/shard_map/ppermute | solution.py:472
  96.3 2.5 %collective-permute-start.10 = (bf16[192,1280]{1,0:T(8,128)(2,1)S(1)}, bf16[192,1280]{1,0:T(8,128)(2,1)S(1)}, u32[]{:S(2)}, u32[]{:S(2)}) collective-permute-start(bf16[192,1280]{1,0:T(8,128)(2,1)S(1)} %get-tuple-element.75), channel_id=1, source_target_pairs={{0,16},{16,0},{32,48},{48,32},{64,80},{80,64},{96,112},{112,96},{1... | collective-permute-start | bytes 1474568 | tf_op jit(solution)/shard_map/ppermute | solution.py:472
  98.3 6.1 %collective-permute-start.12 = (bf16[192,1280]{1,0:T(8,128)(2,1)S(1)}, bf16[192,1280]{1,0:T(8,128)(2,1)S(1)}, u32[]{:S(2)}, u32[]{:S(2)}) collective-permute-start(bf16[192,1280]{1,0:T(8,128)(2,1)S(1)} %get-tuple-element.88), channel_id=1, source_target_pairs={{0,16},{16,0},{32,48},{48,32},{64,80},{80,64},{96,112},{112,96},{1... | collective-permute-start | bytes 1474568 | tf_op jit(solution)/shard_map/ppermute | solution.py:472
  98.8 9.3 %collective-permute-start.13 = (bf16[96,1280]{1,0:T(8,128)(2,1)S(1)}, bf16[96,1280]{1,0:T(8,128)(2,1)S(1)}, u32[]{:S(2)}, u32[]{:S(2)}) collective-permute-start(bf16[96,1280]{1,0:T(8,128)(2,1)S(1)} %get-tuple-element.78), channel_id=1, source_target_pairs={{0,32},{16,48},{32,64},{48,80},{64,96},{80,112},{96,0},{112,16},{1... | collective-permute-start | bytes 737288 | tf_op jit(solution)/shard_map/ppermute | solution.py:466
  99.4 8.9 %collective-permute-start.14 = (bf16[96,1280]{1,0:T(8,128)(2,1)S(1)}, bf16[96,1280]{1,0:T(8,128)(2,1)S(1)}, u32[]{:S(2)}, u32[]{:S(2)}) collective-permute-start(bf16[96,1280]{1,0:T(8,128)(2,1)S(1)} %get-tuple-element.93), channel_id=1, source_target_pairs={{0,96},{16,112},{32,0},{48,16},{64,32},{80,48},{96,64},{112,80},{1... | collective-permute-start | bytes 737288 | tf_op jit(solution)/shard_map/ppermute | solution.py:469
  104.5 16.6 %collective-permute-start.17 = (bf16[96,1280]{1,0:T(8,128)(2,1)S(1)}, bf16[96,1280]{1,0:T(8,128)(2,1)S(1)}, u32[]{:S(2)}, u32[]{:S(2)}) collective-permute-start(bf16[96,1280]{1,0:T(8,128)(2,1)S(1)} %get-tuple-element.99), channel_id=1, source_target_pairs={{0,32},{16,48},{32,64},{48,80},{64,96},{80,112},{96,0},{112,16},{1... | collective-permute-start | bytes 737288 | tf_op jit(solution)/shard_map/ppermute | solution.py:466
  104.6 3.7 %collective-permute-start.11 = (bf16[192,1280]{1,0:T(8,128)(2,1)S(1)}, bf16[192,1280]{1,0:T(8,128)(2,1)S(1)}, u32[]{:S(2)}, u32[]{:S(2)}) collective-permute-start(bf16[192,1280]{1,0:T(8,128)(2,1)S(1)} %get-tuple-element.86), channel_id=1, source_target_pairs={{0,16},{16,0},{32,48},{48,32},{64,80},{80,64},{96,112},{112,96},{1... | collective-permute-start | bytes 1474568 | tf_op jit(solution)/shard_map/ppermute | solution.py:472
  104.7 16.4 %collective-permute-start.15 = (bf16[192,1280]{1,0:T(8,128)(2,1)S(1)}, bf16[192,1280]{1,0:T(8,128)(2,1)S(1)}, u32[]{:S(2)}, u32[]{:S(2)}) collective-permute-start(bf16[192,1280]{1,0:T(8,128)(2,1)S(1)} %get-tuple-element.98), channel_id=1, source_target_pairs={{0,16},{16,0},{32,48},{48,32},{64,80},{80,64},{96,112},{112,96},{1... | collective-permute-start | bytes 1474568 | tf_op jit(solution)/shard_map/ppermute | solution.py:472
  108.2 12.9 %collective-permute-start.16 = (bf16[96,1280]{1,0:T(8,128)(2,1)S(1)}, bf16[96,1280]{1,0:T(8,128)(2,1)S(1)}, u32[]{:S(2)}, u32[]{:S(2)}) collective-permute-start(bf16[96,1280]{1,0:T(8,128)(2,1)S(1)} %shard_map.103), channel_id=1, source_target_pairs={{0,32},{16,48},{32,64},{48,80},{64,96},{80,112},{96,0},{112,16},{1... | collective-permute-start | bytes 737288 | tf_op jit(solution)/shard_map/ppermute | solution.py:466
  108.5 12.7 %collective-permute-start.19 = (bf16[96,1280]{1,0:T(8,128)(2,1)S(1)}, bf16[96,1280]{1,0:T(8,128)(2,1)S(1)}, u32[]{:S(2)}, u32[]{:S(2)}) collective-permute-start(bf16[96,1280]{1,0:T(8,128)(2,1)S(1)} %get-tuple-element.100), channel_id=1, source_target_pairs={{0,96},{16,112},{32,0},{48,16},{64,32},{80,48},{96,64},{112,80},{1... | collective-permute-start | bytes 737288 | tf_op jit(solution)/shard_map/ppermute | solution.py:469
  111.8 9.6 %collective-permute-start.18 = (bf16[96,1280]{1,0:T(8,128)(2,1)S(1)}, bf16[96,1280]{1,0:T(8,128)(2,1)S(1)}, u32[]{:S(2)}, u32[]{:S(2)}) collective-permute-start(bf16[96,1280]{1,0:T(8,128)(2,1)S(1)} %get-tuple-element.94), channel_id=1, source_target_pairs={{0,96},{16,112},{32,0},{48,16},{64,32},{80,48},{96,64},{112,80},{1... | collective-permute-start | bytes 737288 | tf_op jit(solution)/shard_map/ppermute | solution.py:469
  121.1 15.3 %copy-start.3 = (bf16[1,2,64,1280]{3,2,1,0:T(8,128)(2,1)S(1)}, bf16[1,2,64,1280]{3,2,1,0:T(8,128)(2,1)}, u32[]{:S(2)}) copy-start(bf16[1,2,64,1280]{3,2,1,0:T(8,128)(2,1)} %param.6) | copy-start | bytes 983044
  121.1 15.3 %copy-start.4 = (f32[1280]{0:T(1024)S(1)}, f32[1280]{0:T(1024)}, u32[]{:S(2)}) copy-start(f32[1280]{0:T(1024)} %gain_ref.1) | copy-start | bytes 15364
  121.1 15.3 %copy-start.6 = (s32[1,2,64]{2,1,0:T(2,128)S(1)}, s32[1,2,64]{2,1,0:T(2,128)}, u32[]{:S(2)}) copy-start(s32[1,2,64]{2,1,0:T(2,128)} %param.7) | copy-start | bytes 1540
  121.1 15.3 %copy-start.7 = (s32[1,2,64]{2,1,0:T(2,128)S(1)}, s32[1,2,64]{2,1,0:T(2,128)}, u32[]{:S(2)}) copy-start(s32[1,2,64]{2,1,0:T(2,128)} %param.8) | copy-start | bytes 1540

commit v9 on v8

--- a/solution.py
+++ b/solution.py
@@ -95,27 +95,7 @@
     return one_hot((want == pos) & (row % PAD < GROUP))
 
 
-def fetch(sources, refs, sems):
-    copies = [pltpu.make_async_copy(a, b, sems.at[k]) for k, (a, b) in enumerate(zip(sources, refs))]
-    for copy in copies:
-        copy.start()
-    return copies
-
-
-def input_scratch(tokens, width):
-    return [
-        pltpu.VMEM((2, tokens // 2), i32),
-        pltpu.VMEM((2, tokens // 2), i32),
-        pltpu.VMEM((tokens, width), bf16),
-        pltpu.VMEM((width,), f32),
-        pltpu.SemaphoreType.DMA((4,)),
-    ]
-
-
-def dispatch_kernel(ids, slots, toks, gain, out_ref, sum_ref, ids_ref, slots_ref, tok_ref, gain_ref, sems):
-    copies = fetch((ids, slots, toks, gain), (ids_ref, slots_ref, tok_ref, gain_ref), sems)
-    copies[0].wait()
-    copies[1].wait()
+def dispatch_kernel(ids_ref, slots_ref, tok_ref, gain_ref, out_ref, sum_ref):
     pos = places(ids_ref, slots_ref)
     tokens, width = tok_ref.shape
     table = slot_table(pos)
@@ -126,8 +106,6 @@
     lane = iota((2 * LANES, tokens), 0)
     kind = jnp.where(iota((2 * LANES, tokens), 1) < tokens // 2, 1.0, 2.0)
     kinds = nt(goes, jnp.where(lane == column, kind, 0.0).astype(bf16))
-    copies[2].wait()
-    copies[3].wait()
     x = tok_ref[...].astype(f32)
     normed = normal_parts(x)[0] * gain_ref[...].reshape(1, -1)
     sent = nn(table, normed.astype(bf16))
@@ -486,8 +464,6 @@
         dispatch_kernel,
         [shape_of(PEERS, PAD, width), shape_of(2, width, dtype=f32)],
         [ids, slot, flat, ln_gain],
-        hbm=(0, 1, 2, 3),
-        scratch=input_scratch(row_count, width),
         vmem=60,
     )
     rows_shape = shape_of(2 * HALF + KIND_ROWS, width)

time: 138 us -> 138 us (level)
  no operation moved by 1% of the time
where the time goes in v9:
time: 138 us
  blocking collectives  68.9 us (50%)
  Pallas kernels  30.6 us (22%)
  waiting for transfers between devices  18.4 us (13%)
  starting transfers between devices  16.5 us (12%)
  local copies, waits for them, and re-layouts  2.25 us (2%)
    all_to_all x2, blocking collectives, exchange(): return lax.all_to_all(x, 'expert', split_axis=0, concat_axis=0, tiled=True)  34.6 us
    all_to_all x2, blocking collectives, spread(): lax.all_to_all(x, everyone, split_axis=0, concat_axis=0, tiled=True, axis...  34.3 us
    pallas_call x22, Pallas kernels, call(): pl.pallas_call(kernel, out_shape=out, in_specs=[pl.BlockSpec(memory_space...  21.6 us
    ppermute x5, waiting for transfers between devices, up(): return lax.ppermute(x, 'dp', [(i, (i + 2) % 8) for i in range(8)])  15 us
    ppermute x5, starting transfers between devices, down(): return lax.ppermute(x, 'dp', [(i, (i + 6) % 8) for i in range(8)])  11.6 us
    pallas_call x1, Pallas kernels, grad_in(): pl.pallas_call(grad_in_kernel, grid=(HELD,), out_shape=shape_of(HELD, wid...  5.62 us
    pallas_call x1, Pallas kernels, grad_out(): pl.pallas_call(grad_out_kernel, grid=(HELD,), out_shape=shape_of(HELD, hi...  3.43 us
    ppermute x10, waiting for transfers between devices, swap(): return lax.ppermute(x, 'dp', [(i, i ^ 1) for i in range(8)])  3.25 us
  transfers between devices with their start and end apart: 20, of which 7 were waited for; matrix products, arithmetic and copies ran while one was open for 0% of the time, Pallas kernels for 14%

profile of v9, /device:TPU:0, one launch (start us, length us, event | category | flops | bytes accessed | tf_op | source)
XLA Modules:
  0.0 137.7 jit_solution(18321693018504111770)
XLA Ops:
  0.6 2.4 %shard_map.85 = (bf16[16,16,1280]{2,1,0:T(8,128)(2,1)}, f32[2,1280]{1,0:T(2,128)}) custom-call(s32[2,64]{1,0:T(2,128)} %bitcast.16, s32[2,64]{1,0:T(2,128)} %bitcast.18, bf16[128,1280]{1,0:T(8,128)(2,1)} %bitcast.13, f32[1280]{0:T(1024)} %gain_ref.3), custom_call_target="tpu_custom_call" | custom-call | flops 1 | bytes 1 | tf_op jit(solution)/shard_map/pallas_call | solution.py:68
  3.1 20.1 %all_to_all.20.in_ref = bf16[16,16,1280]{2,1,0:T(8,128)(2,1)S(1)} all-to-all(bf16[16,16,1280]{2,1,0:T(8,128)(2,1)} %get-tuple-element.52), channel_id=1, replica_groups=mesh['dp'=8,'expert'=16] {'expert'}, dimensions={0} | all-to-all | bytes 1310720 | tf_op jit(solution)/shard_map/all_to_all | solution.py:456
  23.1 0.4 shard_map.86.refs_0_.refs_3_
  23.5 2.0 %collective-permute-start.1 = (bf16[208,1280]{1,0:T(8,128)(2,1)S(1)}, bf16[208,1280]{1,0:T(8,128)(2,1)S(1)}, u32[]{:S(2)}, u32[]{:S(2)}) collective-permute-start(bf16[208,1280]{1,0:T(8,128)(2,1)S(1)} %shard_map.86.refs_0_.refs_3_), channel_id=1, source_target_pairs={{0,32},{16,48},{32,64},{48,80},{64,96},{80,112},{96,0},{112,16},{1... | collective-permute-start | bytes 1597448 | tf_op jit(solution)/shard_map/ppermute | solution.py:444
  25.5 2.2 %collective-permute-start.2 = (bf16[208,1280]{1,0:T(8,128)(2,1)S(1)}, bf16[208,1280]{1,0:T(8,128)(2,1)S(1)}, u32[]{:S(2)}, u32[]{:S(2)}) collective-permute-start(bf16[208,1280]{1,0:T(8,128)(2,1)S(1)} %shard_map.86.refs_0_.refs_3_), channel_id=1, source_target_pairs={{0,96},{16,112},{32,0},{48,16},{64,32},{80,48},{96,64},{112,80},{1... | collective-permute-start | bytes 1597448 | tf_op jit(solution)/shard_map/ppermute | solution.py:447
  27.7 0.0 collective-permute-start
  27.7 1.9 %copy-done = bf16[2,1280,640]{2,1,0:T(8,128)(2,1)S(1)} copy-done((bf16[2,1280,640]{2,1,0:T(8,128)(2,1)S(1)}, bf16[2,1280,640]{2,1,0:T(8,128)(2,1)}, u32[]{:S(2)}) %copy-start) | copy-done | bytes 3276824
  29.6 1.1 shard_map.87
  30.7 7.6 %collective-permute-done.1.x2_ref.refs_1_.refs_2_ = bf16[208,1280]{1,0:T(8,128)(2,1)S(1)} collective-permute-done((bf16[208,1280]{1,0:T(8,128)(2,1)S(1)}, bf16[208,1280]{1,0:T(8,128)(2,1)S(1)}, u32[]{:S(2)}, u32[]{:S(2)}) %collective-permute-start.1) | collective-permute-done | bytes 532512 | tf_op jit(solution)/shard_map/ppermute | solution.py:444
  38.3 3.1 %collective-permute-start.5 = (bf16[112,1280]{1,0:T(8,128)(2,1)S(1)}, bf16[112,1280]{1,0:T(8,128)(2,1)S(1)}, u32[]{:S(2)}, u32[]{:S(2)}) collective-permute-start(bf16[112,1280]{1,0:T(8,128)(2,1)S(1)} %get-tuple-element.60), channel_id=1, source_target_pairs={{0,96},{16,112},{32,0},{48,16},{64,32},{80,48},{96,64},{112,80},{1... | collective-permute-start | bytes 860168 | tf_op jit(solution)/shard_map/ppermute | solution.py:447
  41.4 0.0 collective-permute-start.4
  41.4 0.0 collective-permute-done.refs_0_.refs_1_
  41.4 2.4 %shard_map.89 = (bf16[3,2,32,640]{3,2,1,0:T(8,128)(2,1)S(1)}, bf16[3,2,96,640]{3,2,1,0:T(8,128)(2,1)S(1)}) custom-call(bf16[208,1280]{1,0:T(8,128)(2,1)S(1)} %collective-permute-done.refs_0_.refs_1_, bf16[208,1280]{1,0:T(8,128)(2,1)S(1)} %collective-permute-done.1.x2_ref.refs_1_.refs_2_, bf16[208,1280]{1,0:T(8,128)(2,1)S(1)} %collective-permute-done.2.x4_ref.refs_2_.refs_4_, ...), custom_call_target="tpu_custom_call" | custom-call | flops 1 | bytes 1 | tf_op jit(solution)/shard_map/pallas_call | solution.py:68
  43.8 0.1 collective-permute-start.3
  43.9 0.5 collective-permute-start.6
  44.4 4.4 %collective-permute-done.4.first_ref = bf16[96,1280]{1,0:T(8,128)(2,1)S(1)} collective-permute-done((bf16[96,1280]{1,0:T(8,128)(2,1)S(1)}, bf16[96,1280]{1,0:T(8,128)(2,1)S(1)}, u32[]{:S(2)}, u32[]{:S(2)}) %collective-permute-start.4) | collective-permute-done | bytes 245792 | tf_op jit(solution)/shard_map/ppermute | solution.py:444
  48.9 0.0 copy-start.2
  48.9 0.1 collective-permute-start.7
  49.0 0.0 collective-permute-done.6.refs_1_.refs_5_
  49.0 1.5 %shard_map.91 = (bf16[2,2,32,640]{3,2,1,0:T(8,128)(2,1)S(1)}, bf16[2,2,96,640]{3,2,1,0:T(8,128)(2,1)S(1)}) custom-call(bf16[208,1280]{1,0:T(8,128)(2,1)S(1)} %collective-permute-done.3.refs_0_.refs_3_, bf16[208,1280]{1,0:T(8,128)(2,1)S(1)} %collective-permute-done.6.refs_1_.refs_5_, bf16[2,1280,640]{2,1,0:T(8,128)(2,1)S(1)} %copy-done.1), custom_call_target="tpu_custom_call" | custom-call | flops 1 | bytes 1 | tf_op jit(solution)/shard_map/pallas_call | solution.py:68
  50.5 0.3 collective-permute-done.7.refs_1_.refs_0_.refs_7_
  50.9 1.5 %shard_map.92 = (bf16[2,2,32,640]{3,2,1,0:T(8,128)(2,1)S(1)}, bf16[2,2,96,640]{3,2,1,0:T(8,128)(2,1)S(1)}) custom-call(bf16[208,1280]{1,0:T(8,128)(2,1)S(1)} %shard_map.90.refs_0_.refs_6_, bf16[208,1280]{1,0:T(8,128)(2,1)S(1)} %collective-permute-done.7.refs_1_.refs_0_.refs_7_, bf16[2,1280,640]{2,1,0:T(8,128)(2,1)S(1)} %copy-done.1), custom_call_target="tpu_custom_call" | custom-call | flops 1 | bytes 1 | tf_op jit(solution)/shard_map/pallas_call | solution.py:68
  52.4 0.7 shard_map.93
  53.1 0.0 copy-start.5
  53.1 0.2 collective-permute-start.8
  53.3 0.7 shard_map.94.own_ref
  54.0 0.8 collective-permute-done.8.got_ref
  54.8 0.1 shard_map.95
  54.9 0.3 copy.11
  55.2 15.8 %all_to_all.21.part_ref = bf16[64,2,1280]{2,1,0:T(2,128)(2,1)S(1)} all-to-all(bf16[64,2,1280]{2,1,0:T(2,128)(2,1)S(1)} %bitcast.20), channel_id=1, replica_groups={{0,1,2,3,4,5,6,7,8,9,10,11,12,13,14,15,32,33,34,35,36,37,38,39,40,41,42..., dimensions={0} | all-to-all | bytes 655360 | tf_op jit(solution)/shard_map/all_to_all | solution.py:459
  71.0 0.3 shard_map.96
  71.3 18.5 %all_to_all.22 = f32[64,2,1280]{2,1,0:T(2,128)S(1)} all-to-all(f32[64,2,1280]{2,1,0:T(2,128)S(1)} %shard_map.96), channel_id=1, replica_groups={{0,1,2,3,4,5,6,7,8,9,10,11,12,13,14,15,32,33,34,35,36,37,38,39,40,41,42..., dimensions={0} | all-to-all | bytes 1310720 | tf_op jit(solution)/shard_map/all_to_all | solution.py:459
  89.9 0.1 collective-permute-start.9
  89.9 2.1 %collective-permute-done.9.other_ref = f32[2,64,1280]{2,1,0:T(8,128)S(1)} collective-permute-done((f32[2,64,1280]{2,1,0:T(8,128)S(1)}, f32[2,64,1280]{2,1,0:T(8,128)S(1)}, u32[]{:S(2)}, u32[]{:S(2)}) %collective-permute-start.9) | collective-permute-done | bytes 655392 | tf_op jit(solution)/shard_map/ppermute | solution.py:450
  92.0 2.9 %shard_map.97 = (f32[2,128,1280]{2,1,0:T(8,128)S(1)}, bf16[8,32,1280]{2,1,0:T(8,128)(2,1)S(1)}, bf16[2,256,640]{2,1,0:T(8,128)(2,1)S(1)}) custom-call(f32[2,64,1280]{2,1,0:T(8,128)S(1)} %bitcast.12, f32[2,64,1280]{2,1,0:T(8,128)S(1)} %collective-permute-done.9.other_ref, bf16[2,640,1280]{2,1,0:T(8,128)(2,1)S(1)} %copy-done.2), custom_call_target="tpu_custom_call" | custom-call | flops 1 | bytes 1 | tf_op jit(solution)/shard_map/pallas_call | solution.py:68
  94.9 1.2 shard_map.98
  96.2 0.2 collective-permute-start.10
  96.4 1.8 %shard_map.99 = (bf16[3,2,96,640]{3,2,1,0:T(8,128)(2,1)S(1)}, bf16[192,1280]{1,0:T(8,128)(2,1)S(1)}, bf16[192,1280]{1,0:T(8,128)(2,1)S(1)}, bf16[192,1280]{1,0:T(8,128)(2,1)S(1)}) custom-call(bf16[208,1280]{1,0:T(8,128)(2,1)S(1)} %shard_map.90.refs_0_.refs_6_, bf16[208,1280]{1,0:T(8,128)(2,1)S(1)} %collective-permute-done.6.refs_1_.refs_5_, ...), custom_call_target="tpu_custom_call" | custom-call | flops 1 | bytes 1 | tf_op jit(solution)/shard_map/pallas_call | solution.py:68
  98.2 0.5 collective-permute-start.12
  98.6 0.0 collective-permute-done.10.got_ref
  98.7 0.1 shard_map.100
  98.8 0.6 collective-permute-start.13
  99.3 2.8 %collective-permute-start.14 = (bf16[96,1280]{1,0:T(8,128)(2,1)S(1)}, bf16[96,1280]{1,0:T(8,128)(2,1)S(1)}, u32[]{:S(2)}, u32[]{:S(2)}) collective-permute-start(bf16[96,1280]{1,0:T(8,128)(2,1)S(1)} %get-tuple-element.93), channel_id=1, source_target_pairs={{0,96},{16,112},{32,0},{48,16},{64,32},{80,48},{96,64},{112,80},{1... | collective-permute-start | bytes 737288 | tf_op jit(solution)/shard_map/ppermute | solution.py:447
  102.1 2.3 %shard_map.101 = (bf16[4,2,96,640]{3,2,1,0:T(8,128)(2,1)S(1)}, bf16[192,1280]{1,0:T(8,128)(2,1)S(1)}, bf16[192,1280]{1,0:T(8,128)(2,1)S(1)}, bf16[192,1280]{1,0:T(8,128)(2,1)S(1)}, bf16[192,1280]{1,0:T(8,128)(2,1)S(1)}) custom-call(bf16[208,1280]{1,0:T(8,128)(2,1)S(1)} %collective-permute-done.3.refs_0_.refs_3_, ...), custom_call_target="tpu_custom_call" | custom-call | flops 1 | bytes 1 | tf_op jit(solution)/shard_map/pallas_call | solution.py:68
  104.3 0.1 shard_map.102
  104.5 0.1 collective-permute-start.17
  104.6 0.1 collective-permute-start.11
  104.6 0.5 collective-permute-start.15
  105.1 3.0 %collective-permute-done.13.y_ref = bf16[96,1280]{1,0:T(8,128)(2,1)S(1)} collective-permute-done((bf16[96,1280]{1,0:T(8,128)(2,1)S(1)}, bf16[96,1280]{1,0:T(8,128)(2,1)S(1)}, u32[]{:S(2)}, u32[]{:S(2)}) %collective-permute-start.13) | collective-permute-done | bytes 245792 | tf_op jit(solution)/shard_map/ppermute | solution.py:444
  108.1 0.1 shard_map.103
  108.2 0.1 collective-permute-start.16
  108.3 0.0 collective-permute-done.14.above_ref
  108.3 0.1 shard_map.104
  108.4 3.3 %collective-permute-start.19 = (bf16[96,1280]{1,0:T(8,128)(2,1)S(1)}, bf16[96,1280]{1,0:T(8,128)(2,1)S(1)}, u32[]{:S(2)}, u32[]{:S(2)}) collective-permute-start(bf16[96,1280]{1,0:T(8,128)(2,1)S(1)} %get-tuple-element.100), channel_id=1, source_target_pairs={{0,96},{16,112},{32,0},{48,16},{64,32},{80,48},{96,64},{112,80},{1... | collective-permute-start | bytes 737288 | tf_op jit(solution)/shard_map/ppermute | solution.py:447
  111.7 0.3 collective-permute-start.18
  112.0 3.4 %shard_map.105 = f32[2,640,1280]{2,1,0:T(8,128)} custom-call(bf16[1,2,32,640]{3,2,1,0:T(8,128)(2,1)S(1)} %get-tuple-element.53.refs_0_, bf16[3,2,32,640]{3,2,1,0:T(8,128)(2,1)S(1)} %get-tuple-element.57.refs_1_, bf16[2,2,32,640]{3,2,1,0:T(8,128)(2,1)S(1)} %get-tuple-element.63.refs_2_, bf16[2,2,32,640]{3,2,1,0:T(8,128)(2,1)S(1)} %get-tuple-element.65.refs_3_, ...), custom_call_target="tpu_custom_call" | custom-call | flops 1 | bytes 1 | tf_op jit(solution)/shard_map/pallas_call | solution.py:376
  115.4 5.6 %shard_map.106 = f32[2,1280,640]{2,1,0:T(8,128)} custom-call(bf16[208,1280]{1,0:T(8,128)(2,1)S(1)} %shard_map.86.refs_0_.refs_3_, bf16[208,1280]{1,0:T(8,128)(2,1)S(1)} %collective-permute-done.refs_0_.refs_1_, bf16[208,1280]{1,0:T(8,128)(2,1)S(1)} %collective-permute-done.1.x2_ref.refs_1_.refs_2_, ...), custom_call_target="tpu_custom_call" | custom-call | flops 1 | bytes 1 | tf_op jit(solution)/shard_map/pallas_call | solution.py:348
  121.1 0.0 collective-permute-done.17.lb_ref
  121.1 0.0 collective-permute-done.15.got_ref
  121.1 0.0 collective-permute-done.19.hb_ref
  121.1 0.2 collective-permute-done.18.ha_ref
  121.3 0.5 shard_map.107
  121.8 14.5 %all_to_all.23.back_ref = bf16[16,16,1280]{2,1,0:T(8,128)(2,1)S(1)} all-to-all(bf16[16,16,1280]{2,1,0:T(8,128)(2,1)S(1)} %shard_map.107), channel_id=1, replica_groups=mesh['dp'=8,'expert'=16] {'expert'}, dimensions={0} | all-to-all | bytes 1310720 | tf_op jit(solution)/shard_map/all_to_all | solution.py:456
  136.3 1.3 shard_map.108
  (22 shorter events, 0.2 us)
Async XLA Ops:
  23.5 14.8 %collective-permute-start.1 = (bf16[208,1280]{1,0:T(8,128)(2,1)S(1)}, bf16[208,1280]{1,0:T(8,128)(2,1)S(1)}, u32[]{:S(2)}, u32[]{:S(2)}) collective-permute-start(bf16[208,1280]{1,0:T(8,128)(2,1)S(1)} %shard_map.86.refs_0_.refs_3_), channel_id=1, source_target_pairs={{0,32},{16,48},{32,64},{48,80},{64,96},{80,112},{96,0},{112,16},{1... | collective-permute-start | bytes 1597448 | tf_op jit(solution)/shard_map/ppermute | solution.py:444
  25.5 12.8 %collective-permute-start.2 = (bf16[208,1280]{1,0:T(8,128)(2,1)S(1)}, bf16[208,1280]{1,0:T(8,128)(2,1)S(1)}, u32[]{:S(2)}, u32[]{:S(2)}) collective-permute-start(bf16[208,1280]{1,0:T(8,128)(2,1)S(1)} %shard_map.86.refs_0_.refs_3_), channel_id=1, source_target_pairs={{0,96},{16,112},{32,0},{48,16},{64,32},{80,48},{96,64},{112,80},{1... | collective-permute-start | bytes 1597448 | tf_op jit(solution)/shard_map/ppermute | solution.py:447
  27.7 13.7 %collective-permute-start = (bf16[208,1280]{1,0:T(8,128)(2,1)S(1)}, bf16[208,1280]{1,0:T(8,128)(2,1)S(1)}, u32[]{:S(2)}, u32[]{:S(2)}) collective-permute-start(bf16[208,1280]{1,0:T(8,128)(2,1)S(1)} %shard_map.86.refs_0_.refs_3_), channel_id=1, source_target_pairs={{0,16},{16,0},{32,48},{48,32},{64,80},{80,64},{96,112},{112,96},{1... | collective-permute-start | bytes 1597448 | tf_op jit(solution)/shard_map/ppermute | solution.py:450
  27.7 1.9 %copy-start = (bf16[2,1280,640]{2,1,0:T(8,128)(2,1)S(1)}, bf16[2,1280,640]{2,1,0:T(8,128)(2,1)}, u32[]{:S(2)}) copy-start(bf16[2,1280,640]{2,1,0:T(8,128)(2,1)} %refs_9_.1) | copy-start | bytes 9830404
  29.6 11.8 %copy-start.1 = (bf16[2,1280,640]{2,1,0:T(8,128)(2,1)S(1)}, bf16[2,1280,640]{2,1,0:T(8,128)(2,1)}, u32[]{:S(2)}) copy-start(bf16[2,1280,640]{2,1,0:T(8,128)(2,1)} %refs_9_.1) | copy-start | bytes 9830404
  38.3 10.5 %collective-permute-start.5 = (bf16[112,1280]{1,0:T(8,128)(2,1)S(1)}, bf16[112,1280]{1,0:T(8,128)(2,1)S(1)}, u32[]{:S(2)}, u32[]{:S(2)}) collective-permute-start(bf16[112,1280]{1,0:T(8,128)(2,1)S(1)} %get-tuple-element.60), channel_id=1, source_target_pairs={{0,96},{16,112},{32,0},{48,16},{64,32},{80,48},{96,64},{112,80},{1... | collective-permute-start | bytes 860168 | tf_op jit(solution)/shard_map/ppermute | solution.py:447
  41.4 7.4 %collective-permute-start.4 = (bf16[96,1280]{1,0:T(8,128)(2,1)S(1)}, bf16[96,1280]{1,0:T(8,128)(2,1)S(1)}, u32[]{:S(2)}, u32[]{:S(2)}) collective-permute-start(bf16[96,1280]{1,0:T(8,128)(2,1)S(1)} %get-tuple-element.55), channel_id=1, source_target_pairs={{0,32},{16,48},{32,64},{48,80},{64,96},{80,112},{96,0},{112,16},{1... | collective-permute-start | bytes 737288 | tf_op jit(solution)/shard_map/ppermute | solution.py:444
  43.8 5.2 %collective-permute-start.3 = (bf16[208,1280]{1,0:T(8,128)(2,1)S(1)}, bf16[208,1280]{1,0:T(8,128)(2,1)S(1)}, u32[]{:S(2)}, u32[]{:S(2)}) collective-permute-start(bf16[208,1280]{1,0:T(8,128)(2,1)S(1)} %collective-permute-done.1.x2_ref.refs_1_.refs_2_), channel_id=1, source_target_pairs={{0,16},{16,0},{32,48},{48,32},{64,80},{80,64},{96,112},{112,96},{1... | collective-permute-start | bytes 1597448 | tf_op jit(solution)/shard_map/ppermute | solution.py:450
  43.9 5.1 %collective-permute-start.6 = (bf16[208,1280]{1,0:T(8,128)(2,1)S(1)}, bf16[208,1280]{1,0:T(8,128)(2,1)S(1)}, u32[]{:S(2)}, u32[]{:S(2)}) collective-permute-start(bf16[208,1280]{1,0:T(8,128)(2,1)S(1)} %collective-permute-done.2.x4_ref.refs_2_.refs_4_), channel_id=1, source_target_pairs={{0,16},{16,0},{32,48},{48,32},{64,80},{80,64},{96,112},{112,96},{1... | collective-permute-start | bytes 1597448 | tf_op jit(solution)/shard_map/ppermute | solution.py:450
  48.9 3.5 %copy-start.2 = (bf16[2,640,1280]{2,1,0:T(8,128)(2,1)S(1)}, bf16[2,640,1280]{2,1,0:T(8,128)(2,1)}, u32[]{:S(2)}) copy-start(bf16[2,640,1280]{2,1,0:T(8,128)(2,1)} %w_out.1) | copy-start | bytes 9830404
  48.9 2.0 %collective-permute-start.7 = (bf16[208,1280]{1,0:T(8,128)(2,1)S(1)}, bf16[208,1280]{1,0:T(8,128)(2,1)S(1)}, u32[]{:S(2)}, u32[]{:S(2)}) collective-permute-start(bf16[208,1280]{1,0:T(8,128)(2,1)S(1)} %shard_map.90.refs_0_.refs_6_), channel_id=1, source_target_pairs={{0,16},{16,0},{32,48},{48,32},{64,80},{80,64},{96,112},{112,96},{1... | collective-permute-start | bytes 1597448 | tf_op jit(solution)/shard_map/ppermute | solution.py:450
  53.1 17.9 %copy-start.5 = (f32[2,1280]{1,0:T(2,128)S(1)}, f32[2,1280]{1,0:T(2,128)}, u32[]{:S(2)}) copy-start(f32[2,1280]{1,0:T(2,128)} %get-tuple-element.68.sum_ref) | copy-start | bytes 30724
  53.1 1.7 %collective-permute-start.8 = (bf16[4,32,1280]{2,1,0:T(8,128)(2,1)S(1)}, bf16[4,32,1280]{2,1,0:T(8,128)(2,1)S(1)}, u32[]{:S(2)}, u32[]{:S(2)}) collective-permute-start(bf16[4,32,1280]{2,1,0:T(8,128)(2,1)S(1)} %shard_map.93), channel_id=1, source_target_pairs={{0,16},{16,0},{32,48},{48,32},{64,80},{80,64},{96,112},{112,96},{1... | collective-permute-start | bytes 983048 | tf_op jit(solution)/shard_map/ppermute | solution.py:450
  89.9 2.2 %collective-permute-start.9 = (f32[2,64,1280]{2,1,0:T(8,128)S(1)}, f32[2,64,1280]{2,1,0:T(8,128)S(1)}, u32[]{:S(2)}, u32[]{:S(2)}) collective-permute-start(f32[2,64,1280]{2,1,0:T(8,128)S(1)} %bitcast.11), channel_id=1, source_target_pairs={{0,16},{16,0},{32,48},{48,32},{64,80},{80,64},{96,112},{112,96},{1... | collective-permute-start | bytes 1966088 | tf_op jit(solution)/shard_map/ppermute | solution.py:450
  96.2 2.5 %collective-permute-start.10 = (bf16[192,1280]{1,0:T(8,128)(2,1)S(1)}, bf16[192,1280]{1,0:T(8,128)(2,1)S(1)}, u32[]{:S(2)}, u32[]{:S(2)}) collective-permute-start(bf16[192,1280]{1,0:T(8,128)(2,1)S(1)} %get-tuple-element.75), channel_id=1, source_target_pairs={{0,16},{16,0},{32,48},{48,32},{64,80},{80,64},{96,112},{112,96},{1... | collective-permute-start | bytes 1474568 | tf_op jit(solution)/shard_map/ppermute | solution.py:450
  98.2 6.1 %collective-permute-start.12 = (bf16[192,1280]{1,0:T(8,128)(2,1)S(1)}, bf16[192,1280]{1,0:T(8,128)(2,1)S(1)}, u32[]{:S(2)}, u32[]{:S(2)}) collective-permute-start(bf16[192,1280]{1,0:T(8,128)(2,1)S(1)} %get-tuple-element.88), channel_id=1, source_target_pairs={{0,16},{16,0},{32,48},{48,32},{64,80},{80,64},{96,112},{112,96},{1... | collective-permute-start | bytes 1474568 | tf_op jit(solution)/shard_map/ppermute | solution.py:450
  98.8 9.3 %collective-permute-start.13 = (bf16[96,1280]{1,0:T(8,128)(2,1)S(1)}, bf16[96,1280]{1,0:T(8,128)(2,1)S(1)}, u32[]{:S(2)}, u32[]{:S(2)}) collective-permute-start(bf16[96,1280]{1,0:T(8,128)(2,1)S(1)} %get-tuple-element.78), channel_id=1, source_target_pairs={{0,32},{16,48},{32,64},{48,80},{64,96},{80,112},{96,0},{112,16},{1... | collective-permute-start | bytes 737288 | tf_op jit(solution)/shard_map/ppermute | solution.py:444
  99.3 8.9 %collective-permute-start.14 = (bf16[96,1280]{1,0:T(8,128)(2,1)S(1)}, bf16[96,1280]{1,0:T(8,128)(2,1)S(1)}, u32[]{:S(2)}, u32[]{:S(2)}) collective-permute-start(bf16[96,1280]{1,0:T(8,128)(2,1)S(1)} %get-tuple-element.93), channel_id=1, source_target_pairs={{0,96},{16,112},{32,0},{48,16},{64,32},{80,48},{96,64},{112,80},{1... | collective-permute-start | bytes 737288 | tf_op jit(solution)/shard_map/ppermute | solution.py:447
  104.5 16.6 %collective-permute-start.17 = (bf16[96,1280]{1,0:T(8,128)(2,1)S(1)}, bf16[96,1280]{1,0:T(8,128)(2,1)S(1)}, u32[]{:S(2)}, u32[]{:S(2)}) collective-permute-start(bf16[96,1280]{1,0:T(8,128)(2,1)S(1)} %get-tuple-element.99), channel_id=1, source_target_pairs={{0,32},{16,48},{32,64},{48,80},{64,96},{80,112},{96,0},{112,16},{1... | collective-permute-start | bytes 737288 | tf_op jit(solution)/shard_map/ppermute | solution.py:444
  104.6 3.7 %collective-permute-start.11 = (bf16[192,1280]{1,0:T(8,128)(2,1)S(1)}, bf16[192,1280]{1,0:T(8,128)(2,1)S(1)}, u32[]{:S(2)}, u32[]{:S(2)}) collective-permute-start(bf16[192,1280]{1,0:T(8,128)(2,1)S(1)} %get-tuple-element.86), channel_id=1, source_target_pairs={{0,16},{16,0},{32,48},{48,32},{64,80},{80,64},{96,112},{112,96},{1... | collective-permute-start | bytes 1474568 | tf_op jit(solution)/shard_map/ppermute | solution.py:450
  104.6 16.4 %collective-permute-start.15 = (bf16[192,1280]{1,0:T(8,128)(2,1)S(1)}, bf16[192,1280]{1,0:T(8,128)(2,1)S(1)}, u32[]{:S(2)}, u32[]{:S(2)}) collective-permute-start(bf16[192,1280]{1,0:T(8,128)(2,1)S(1)} %get-tuple-element.98), channel_id=1, source_target_pairs={{0,16},{16,0},{32,48},{48,32},{64,80},{80,64},{96,112},{112,96},{1... | collective-permute-start | bytes 1474568 | tf_op jit(solution)/shard_map/ppermute | solution.py:450
  108.2 12.9 %collective-permute-start.16 = (bf16[96,1280]{1,0:T(8,128)(2,1)S(1)}, bf16[96,1280]{1,0:T(8,128)(2,1)S(1)}, u32[]{:S(2)}, u32[]{:S(2)}) collective-permute-start(bf16[96,1280]{1,0:T(8,128)(2,1)S(1)} %shard_map.103), channel_id=1, source_target_pairs={{0,32},{16,48},{32,64},{48,80},{64,96},{80,112},{96,0},{112,16},{1... | collective-permute-start | bytes 737288 | tf_op jit(solution)/shard_map/ppermute | solution.py:444
  108.4 12.7 %collective-permute-start.19 = (bf16[96,1280]{1,0:T(8,128)(2,1)S(1)}, bf16[96,1280]{1,0:T(8,128)(2,1)S(1)}, u32[]{:S(2)}, u32[]{:S(2)}) collective-permute-start(bf16[96,1280]{1,0:T(8,128)(2,1)S(1)} %get-tuple-element.100), channel_id=1, source_target_pairs={{0,96},{16,112},{32,0},{48,16},{64,32},{80,48},{96,64},{112,80},{1... | collective-permute-start | bytes 737288 | tf_op jit(solution)/shard_map/ppermute | solution.py:447
  111.7 9.6 %collective-permute-start.18 = (bf16[96,1280]{1,0:T(8,128)(2,1)S(1)}, bf16[96,1280]{1,0:T(8,128)(2,1)S(1)}, u32[]{:S(2)}, u32[]{:S(2)}) collective-permute-start(bf16[96,1280]{1,0:T(8,128)(2,1)S(1)} %get-tuple-element.94), channel_id=1, source_target_pairs={{0,96},{16,112},{32,0},{48,16},{64,32},{80,48},{96,64},{112,80},{1... | collective-permute-start | bytes 737288 | tf_op jit(solution)/shard_map/ppermute | solution.py:447
  121.0 15.3 %copy-start.3 = (bf16[1,2,64,1280]{3,2,1,0:T(8,128)(2,1)S(1)}, bf16[1,2,64,1280]{3,2,1,0:T(8,128)(2,1)}, u32[]{:S(2)}) copy-start(bf16[1,2,64,1280]{3,2,1,0:T(8,128)(2,1)} %param.6) | copy-start | bytes 983044
  121.0 15.3 %copy-start.4 = (f32[1280]{0:T(1024)S(1)}, f32[1280]{0:T(1024)}, u32[]{:S(2)}) copy-start(f32[1280]{0:T(1024)} %gain_ref.3) | copy-start | bytes 15364
  121.0 15.3 %copy-start.6 = (s32[1,2,64]{2,1,0:T(2,128)S(1)}, s32[1,2,64]{2,1,0:T(2,128)}, u32[]{:S(2)}) copy-start(s32[1,2,64]{2,1,0:T(2,128)} %param.7) | copy-start | bytes 1540
  121.1 15.3 %copy-start.7 = (s32[1,2,64]{2,1,0:T(2,128)S(1)}, s32[1,2,64]{2,1,0:T(2,128)}, u32[]{:S(2)}) copy-start(s32[1,2,64]{2,1,0:T(2,128)} %param.8) | copy-start | bytes 1540

commit v10 on v8

--- a/solution.py
+++ b/solution.py
@@ -20,7 +20,7 @@
 PAD = 16
 PEERS = 16
 HALF = PEERS * CAP
-KIND_ROWS = 16
+KIND_ROWS = 8
 POOLED = 2 * PEERS
 PAIR_TOKENS = 64
 LANES = 128
@@ -348,62 +348,53 @@
 PAIRED = {7: (0, 0), 6: (1, 0), 5: (1, 1), 4: (1, 2), 3: (2, 0), 1: (2, 1), 2: (2, 2), 0: (2, 3)}
 
 
-def grad_in_kernel(*refs):
-    rows, pres = refs[:8], refs[8:11]
-    out_ref, x_ref, p_ref = refs[11:]
-    held = pl.program_id(0)
-
-    def fill(which):
+def grads_kernel(*refs):
+    rows, pres, parts, grads = refs[:8], refs[8:11], refs[11:15], refs[15]
+    in_ref, out_ref, x_ref, p_ref = refs[16:]
+    step = pl.program_id(0)
+    width = in_ref.shape[1]
+
+    def inner(held):
         for k in range(8):
             span = slice(k * HALF, (k + 1) * HALF)
-            x_ref[span, :] = rows[k][which * HALF : (which + 1) * HALF, :]
+            x_ref[span, :] = rows[k][held * HALF : (held + 1) * HALF, :]
             pair, at = PAIRED[k]
-            p_ref[span, :] = pres[pair][at, which]
-
-    for which in range(HELD):
-        pl.when(held == which)(functools.partial(fill, which))
-    out_ref[0] = tn(x_ref[...], p_ref[...])
-
-
-def grad_in(rows, pres, width, hidden):
+            p_ref[span, :] = pres[pair][at, held]
+        in_ref[0] = tn(x_ref[...], p_ref[...])
+
+    def outer(held):
+        pooled = []
+        for k in range(8):
+            ref, at = part_of(parts, k)
+            pooled.append(ref[at, held])
+        out_ref[0] = tn(jnp.concatenate(pooled, axis=0), grads[...].reshape(8 * POOLED, width))
+
+    for held in range(HELD):
+        pl.when(step == held)(functools.partial(inner, held))
+        pl.when(step == HELD + held)(functools.partial(outer, held))
+
+
+def weight_grads(rows, pres, pooled, grads, width, hidden):
     whole = pl.BlockSpec(memory_space=pltpu.VMEM)
     return pl.pallas_call(
-        grad_in_kernel,
-        grid=(HELD,),
-        out_shape=shape_of(HELD, width, hidden, dtype=f32),
-        in_specs=[whole] * 11,
-        out_specs=pl.BlockSpec((1, width, hidden), lambda i: (i, 0, 0)),
+        grads_kernel,
+        grid=(2 * HELD,),
+        out_shape=[
+            shape_of(HELD, width, hidden, dtype=f32),
+            shape_of(HELD, hidden, width, dtype=f32),
+        ],
+        in_specs=[whole] * 16,
+        out_specs=[
+            pl.BlockSpec((1, width, hidden), lambda i: (jnp.minimum(i, HELD - 1), 0, 0)),
+            pl.BlockSpec((1, hidden, width), lambda i: (jnp.maximum(i - HELD, 0), 0, 0)),
+        ],
         scratch_shapes=[
             pltpu.VMEM((8 * HALF, width), bf16),
             pltpu.VMEM((8 * HALF, hidden), bf16),
         ],
-        compiler_params=pltpu.CompilerParams(vmem_limit_bytes=26 * 1024 * 1024),
+        compiler_params=pltpu.CompilerParams(vmem_limit_bytes=30 * 1024 * 1024),
         cost_estimate=FREE,
-    )(*rows, *pres)
-
-
-def grad_out_kernel(*refs):
-    parts, (rows_ref, out_ref) = refs[:4], refs[4:]
-    held = pl.program_id(0)
-    width = rows_ref.shape[2]
-    pooled = []
-    for k in range(8):
-        ref, at = part_of(parts, k)
-        pooled.append(ref[at, held])
-    out_ref[0] = tn(jnp.concatenate(pooled, axis=0), rows_ref[...].reshape(8 * POOLED, width))
-
-
-def grad_out(pooled, rows, width, hidden):
-    whole = pl.BlockSpec(memory_space=pltpu.VMEM)
-    return pl.pallas_call(
-        grad_out_kernel,
-        grid=(HELD,),
-        out_shape=shape_of(HELD, hidden, width, dtype=f32),
-        in_specs=[whole] * 5,
-        out_specs=pl.BlockSpec((1, hidden, width), lambda i: (i, 0, 0)),
-        compiler_params=pltpu.CompilerParams(vmem_limit_bytes=18 * 1024 * 1024),
-        cost_estimate=FREE,
-    )(*pooled, rows)
+    )(*rows, *pres, *pooled, grads)
 
 
 def plus_kernel(own_ref, got_ref, first_ref, second_ref):
@@ -553,9 +544,8 @@
     low_a = call(add_kernel, half, [after(r4a, p0), from_below], cost=DEAR)
     r2a, r2b = call(below_kernel, [half, half], [p2, after(s3, low_a), from_above])
     high_a, high_b = down(r2a), down(r2b)
-    grad_w_out = grad_out(pooled, after(rows, r2a), width, hidden)
-    grad_w_in = grad_in(
-        block_rows, [pre7, pre654, after(rest, grad_w_out)], width, hidden
+    grad_w_in, grad_w_out = weight_grads(
+        block_rows, [pre7, pre654, after(rest, r2a)], pooled, rows, width, hidden
     )
     low_a = up(low_a)
     settled = call(

time: 138 us -> 137 us (level)
    pallas_call x2 -> x1, Pallas kernels: 9.05 us -> 8.24 us  [weight_grads(): pl.pallas_call(grads_kernel, grid=(2 * HELD,), out_shape=[shape_of(HELD,...]
  transfers between devices with their start and end apart: 20 -> 20, of which waited for: 7 -> 7; matrix products, arithmetic and copies ran while one was open for 0% -> 0% of each run, Pallas kernels for 14% -> 13%
where the time goes in v10:
time: 137 us
  blocking collectives  68.5 us (50%)
  Pallas kernels  29.9 us (22%)
  waiting for transfers between devices  18.8 us (14%)
  starting transfers between devices  16.6 us (12%)
  local copies, waits for them, and re-layouts  2.25 us (2%)
    all_to_all x2, blocking collectives, spread(): lax.all_to_all(x, everyone, split_axis=0, concat_axis=0, tiled=True, axis...  34.4 us
    all_to_all x2, blocking collectives, exchange(): return lax.all_to_all(x, 'expert', split_axis=0, concat_axis=0, tiled=True)  34.1 us
    pallas_call x22, Pallas kernels, call(): pl.pallas_call(kernel, out_shape=out, in_specs=[pl.BlockSpec(memory_space...  21.7 us
    ppermute x5, waiting for transfers between devices, up(): return lax.ppermute(x, 'dp', [(i, (i + 2) % 8) for i in range(8)])  14.5 us
    ppermute x5, starting transfers between devices, down(): return lax.ppermute(x, 'dp', [(i, (i + 6) % 8) for i in range(8)])  11.6 us
    pallas_call x1, Pallas kernels, weight_grads(): pl.pallas_call(grads_kernel, grid=(2 * HELD,), out_shape=[shape_of(HELD,...  8.24 us
    ppermute x10, waiting for transfers between devices, swap(): return lax.ppermute(x, 'dp', [(i, i ^ 1) for i in range(8)])  3.2 us
  transfers between devices with their start and end apart: 20, of which 7 were waited for; matrix products, arithmetic and copies ran while one was open for 0% of the time, Pallas kernels for 13%

profile of v10, /device:TPU:0, one launch (start us, length us, event | category | flops | bytes accessed | tf_op | source)
XLA Modules:
  0.0 136.9 jit_solution(7743906168328593968)
XLA Ops:
  0.6 2.5 %shard_map.85 = (bf16[16,16,1280]{2,1,0:T(8,128)(2,1)}, f32[2,1280]{1,0:T(2,128)}) custom-call(s32[2,64]{1,0:T(2,128)} %bitcast.16, s32[2,64]{1,0:T(2,128)} %bitcast.18, bf16[128,1280]{1,0:T(8,128)(2,1)} %bitcast.13, f32[1280]{0:T(1024)} %gain_ref.1), custom_call_target="tpu_custom_call" | custom-call | flops 1 | bytes 1 | tf_op jit(solution)/shard_map/pallas_call | solution.py:68
  3.1 20.1 %all_to_all.20.in_ref = bf16[16,16,1280]{2,1,0:T(8,128)(2,1)S(1)} all-to-all(bf16[16,16,1280]{2,1,0:T(8,128)(2,1)} %get-tuple-element.53), channel_id=1, replica_groups=mesh['dp'=8,'expert'=16] {'expert'}, dimensions={0} | all-to-all | bytes 1310720 | tf_op jit(solution)/shard_map/all_to_all | solution.py:469
  23.2 0.4 shard_map.86.refs_0_.refs_3_
  23.6 2.0 %collective-permute-start.1 = (bf16[200,1280]{1,0:T(8,128)(2,1)S(1)}, bf16[200,1280]{1,0:T(8,128)(2,1)S(1)}, u32[]{:S(2)}, u32[]{:S(2)}) collective-permute-start(bf16[200,1280]{1,0:T(8,128)(2,1)S(1)} %shard_map.86.refs_0_.refs_3_), channel_id=1, source_target_pairs={{0,32},{16,48},{32,64},{48,80},{64,96},{80,112},{96,0},{112,16},{1... | collective-permute-start | bytes 1536008 | tf_op jit(solution)/shard_map/ppermute | solution.py:457
  25.6 2.2 %collective-permute-start.2 = (bf16[200,1280]{1,0:T(8,128)(2,1)S(1)}, bf16[200,1280]{1,0:T(8,128)(2,1)S(1)}, u32[]{:S(2)}, u32[]{:S(2)}) collective-permute-start(bf16[200,1280]{1,0:T(8,128)(2,1)S(1)} %shard_map.86.refs_0_.refs_3_), channel_id=1, source_target_pairs={{0,96},{16,112},{32,0},{48,16},{64,32},{80,48},{96,64},{112,80},{1... | collective-permute-start | bytes 1536008 | tf_op jit(solution)/shard_map/ppermute | solution.py:460
  27.8 0.0 collective-permute-start
  27.8 1.9 %copy-done = bf16[2,1280,640]{2,1,0:T(8,128)(2,1)S(1)} copy-done((bf16[2,1280,640]{2,1,0:T(8,128)(2,1)S(1)}, bf16[2,1280,640]{2,1,0:T(8,128)(2,1)}, u32[]{:S(2)}) %copy-start) | copy-done | bytes 3276824
  29.7 1.1 shard_map.87
  30.8 7.2 %collective-permute-done.1.x2_ref.refs_1_.refs_2_ = bf16[200,1280]{1,0:T(8,128)(2,1)S(1)} collective-permute-done((bf16[200,1280]{1,0:T(8,128)(2,1)S(1)}, bf16[200,1280]{1,0:T(8,128)(2,1)S(1)}, u32[]{:S(2)}, u32[]{:S(2)}) %collective-permute-start.1) | collective-permute-done | bytes 512032 | tf_op jit(solution)/shard_map/ppermute | solution.py:457
  38.0 3.1 %collective-permute-start.5 = (bf16[104,1280]{1,0:T(8,128)(2,1)S(1)}, bf16[104,1280]{1,0:T(8,128)(2,1)S(1)}, u32[]{:S(2)}, u32[]{:S(2)}) collective-permute-start(bf16[104,1280]{1,0:T(8,128)(2,1)S(1)} %get-tuple-element.61), channel_id=1, source_target_pairs={{0,96},{16,112},{32,0},{48,16},{64,32},{80,48},{96,64},{112,80},{1... | collective-permute-start | bytes 798728 | tf_op jit(solution)/shard_map/ppermute | solution.py:460
  41.1 0.0 collective-permute-start.4
  41.1 0.0 collective-permute-done.refs_0_.refs_1_
  41.1 2.4 %shard_map.89 = (bf16[3,2,32,640]{3,2,1,0:T(8,128)(2,1)S(1)}, bf16[3,2,96,640]{3,2,1,0:T(8,128)(2,1)S(1)}) custom-call(bf16[200,1280]{1,0:T(8,128)(2,1)S(1)} %collective-permute-done.refs_0_.refs_1_, bf16[200,1280]{1,0:T(8,128)(2,1)S(1)} %collective-permute-done.1.x2_ref.refs_1_.refs_2_, bf16[200,1280]{1,0:T(8,128)(2,1)S(1)} %collective-permute-done.2.x4_ref.refs_2_.refs_4_, ...), custom_call_target="tpu_custom_call" | custom-call | flops 1 | bytes 1 | tf_op jit(solution)/shard_map/pallas_call | solution.py:68
  43.5 0.1 collective-permute-start.3
  43.6 0.5 collective-permute-start.6
  44.1 4.4 %collective-permute-done.4.first_ref = bf16[96,1280]{1,0:T(8,128)(2,1)S(1)} collective-permute-done((bf16[96,1280]{1,0:T(8,128)(2,1)S(1)}, bf16[96,1280]{1,0:T(8,128)(2,1)S(1)}, u32[]{:S(2)}, u32[]{:S(2)}) %collective-permute-start.4) | collective-permute-done | bytes 245792 | tf_op jit(solution)/shard_map/ppermute | solution.py:457
  48.5 0.0 collective-permute-done.5.second_ref
  48.5 0.0 copy-start.2
  48.5 0.1 collective-permute-start.7
  48.6 0.0 collective-permute-done.6.refs_1_.refs_5_
  48.6 1.5 %shard_map.91 = (bf16[2,2,32,640]{3,2,1,0:T(8,128)(2,1)S(1)}, bf16[2,2,96,640]{3,2,1,0:T(8,128)(2,1)S(1)}) custom-call(bf16[200,1280]{1,0:T(8,128)(2,1)S(1)} %collective-permute-done.3.refs_0_.refs_3_, bf16[200,1280]{1,0:T(8,128)(2,1)S(1)} %collective-permute-done.6.refs_1_.refs_5_, bf16[2,1280,640]{2,1,0:T(8,128)(2,1)S(1)} %copy-done.1), custom_call_target="tpu_custom_call" | custom-call | flops 1 | bytes 1 | tf_op jit(solution)/shard_map/pallas_call | solution.py:68
  50.2 0.3 collective-permute-done.7.refs_1_.refs_0_.refs_7_
  50.5 1.5 %shard_map.92 = (bf16[2,2,32,640]{3,2,1,0:T(8,128)(2,1)S(1)}, bf16[2,2,96,640]{3,2,1,0:T(8,128)(2,1)S(1)}) custom-call(bf16[200,1280]{1,0:T(8,128)(2,1)S(1)} %shard_map.90.refs_0_.refs_6_, bf16[200,1280]{1,0:T(8,128)(2,1)S(1)} %collective-permute-done.7.refs_1_.refs_0_.refs_7_, bf16[2,1280,640]{2,1,0:T(8,128)(2,1)S(1)} %copy-done.1), custom_call_target="tpu_custom_call" | custom-call | flops 1 | bytes 1 | tf_op jit(solution)/shard_map/pallas_call | solution.py:68
  52.0 0.7 shard_map.93
  52.7 0.0 copy-start.5
  52.7 0.3 collective-permute-start.8
  53.0 0.7 shard_map.94.own_ref
  53.6 0.8 collective-permute-done.8.got_ref
  54.4 0.1 shard_map.95
  54.5 0.3 copy.11
  54.8 15.8 %all_to_all.21.part_ref = bf16[64,2,1280]{2,1,0:T(2,128)(2,1)S(1)} all-to-all(bf16[64,2,1280]{2,1,0:T(2,128)(2,1)S(1)} %bitcast.20), channel_id=1, replica_groups={{0,1,2,3,4,5,6,7,8,9,10,11,12,13,14,15,32,33,34,35,36,37,38,39,40,41,42..., dimensions={0} | all-to-all | bytes 655360 | tf_op jit(solution)/shard_map/all_to_all | solution.py:472
  70.6 0.3 shard_map.96
  70.9 18.5 %all_to_all.22 = f32[64,2,1280]{2,1,0:T(2,128)S(1)} all-to-all(f32[64,2,1280]{2,1,0:T(2,128)S(1)} %shard_map.96), channel_id=1, replica_groups={{0,1,2,3,4,5,6,7,8,9,10,11,12,13,14,15,32,33,34,35,36,37,38,39,40,41,42..., dimensions={0} | all-to-all | bytes 1310720 | tf_op jit(solution)/shard_map/all_to_all | solution.py:472
  89.5 0.1 collective-permute-start.9
  89.6 2.1 %collective-permute-done.9.other_ref = f32[2,64,1280]{2,1,0:T(8,128)S(1)} collective-permute-done((f32[2,64,1280]{2,1,0:T(8,128)S(1)}, f32[2,64,1280]{2,1,0:T(8,128)S(1)}, u32[]{:S(2)}, u32[]{:S(2)}) %collective-permute-start.9) | collective-permute-done | bytes 655392 | tf_op jit(solution)/shard_map/ppermute | solution.py:463
  91.7 2.9 %shard_map.97 = (f32[2,128,1280]{2,1,0:T(8,128)S(1)}, bf16[8,32,1280]{2,1,0:T(8,128)(2,1)S(1)}, bf16[2,256,640]{2,1,0:T(8,128)(2,1)S(1)}) custom-call(f32[2,64,1280]{2,1,0:T(8,128)S(1)} %bitcast.12, f32[2,64,1280]{2,1,0:T(8,128)S(1)} %collective-permute-done.9.other_ref, bf16[2,640,1280]{2,1,0:T(8,128)(2,1)S(1)} %copy-done.2), custom_call_target="tpu_custom_call" | custom-call | flops 1 | bytes 1 | tf_op jit(solution)/shard_map/pallas_call | solution.py:68
  94.6 1.2 shard_map.98
  95.9 0.2 collective-permute-start.10
  96.1 1.8 %shard_map.99 = (bf16[3,2,96,640]{3,2,1,0:T(8,128)(2,1)S(1)}, bf16[192,1280]{1,0:T(8,128)(2,1)S(1)}, bf16[192,1280]{1,0:T(8,128)(2,1)S(1)}, bf16[192,1280]{1,0:T(8,128)(2,1)S(1)}) custom-call(bf16[200,1280]{1,0:T(8,128)(2,1)S(1)} %shard_map.90.refs_0_.refs_6_, bf16[200,1280]{1,0:T(8,128)(2,1)S(1)} %collective-permute-done.6.refs_1_.refs_5_, ...), custom_call_target="tpu_custom_call" | custom-call | flops 1 | bytes 1 | tf_op jit(solution)/shard_map/pallas_call | solution.py:68
  97.9 0.4 collective-permute-start.12
  98.3 0.0 collective-permute-done.10.got_ref
  98.3 0.1 shard_map.100
  98.4 0.6 collective-permute-start.13
  99.0 2.8 %collective-permute-start.14 = (bf16[96,1280]{1,0:T(8,128)(2,1)S(1)}, bf16[96,1280]{1,0:T(8,128)(2,1)S(1)}, u32[]{:S(2)}, u32[]{:S(2)}) collective-permute-start(bf16[96,1280]{1,0:T(8,128)(2,1)S(1)} %get-tuple-element.93), channel_id=1, source_target_pairs={{0,96},{16,112},{32,0},{48,16},{64,32},{80,48},{96,64},{112,80},{1... | collective-permute-start | bytes 737288 | tf_op jit(solution)/shard_map/ppermute | solution.py:460
  101.8 2.3 %shard_map.101 = (bf16[4,2,96,640]{3,2,1,0:T(8,128)(2,1)S(1)}, bf16[192,1280]{1,0:T(8,128)(2,1)S(1)}, bf16[192,1280]{1,0:T(8,128)(2,1)S(1)}, bf16[192,1280]{1,0:T(8,128)(2,1)S(1)}, bf16[192,1280]{1,0:T(8,128)(2,1)S(1)}) custom-call(bf16[200,1280]{1,0:T(8,128)(2,1)S(1)} %collective-permute-done.3.refs_0_.refs_3_, ...), custom_call_target="tpu_custom_call" | custom-call | flops 1 | bytes 1 | tf_op jit(solution)/shard_map/pallas_call | solution.py:68
  104.0 0.0 collective-permute-done.12.got_ref
  104.0 0.1 shard_map.102
  104.1 0.1 collective-permute-start.17
  104.2 0.1 collective-permute-start.11
  104.3 0.5 collective-permute-start.15
  104.8 3.0 %collective-permute-done.13.y_ref = bf16[96,1280]{1,0:T(8,128)(2,1)S(1)} collective-permute-done((bf16[96,1280]{1,0:T(8,128)(2,1)S(1)}, bf16[96,1280]{1,0:T(8,128)(2,1)S(1)}, u32[]{:S(2)}, u32[]{:S(2)}) %collective-permute-start.13) | collective-permute-done | bytes 245792 | tf_op jit(solution)/shard_map/ppermute | solution.py:457
  107.8 0.1 shard_map.103
  107.8 0.1 collective-permute-start.16
  107.9 0.0 collective-permute-done.11.got_ref
  107.9 0.0 collective-permute-done.14.above_ref
  108.0 0.1 shard_map.104
  108.1 3.3 %collective-permute-start.19 = (bf16[96,1280]{1,0:T(8,128)(2,1)S(1)}, bf16[96,1280]{1,0:T(8,128)(2,1)S(1)}, u32[]{:S(2)}, u32[]{:S(2)}) collective-permute-start(bf16[96,1280]{1,0:T(8,128)(2,1)S(1)} %get-tuple-element.101), channel_id=1, source_target_pairs={{0,96},{16,112},{32,0},{48,16},{64,32},{80,48},{96,64},{112,80},{1... | collective-permute-start | bytes 737288 | tf_op jit(solution)/shard_map/ppermute | solution.py:460
  111.4 0.3 collective-permute-start.18
  111.7 8.2 %shard_map.105 = (f32[2,1280,640]{2,1,0:T(8,128)}, f32[2,640,1280]{2,1,0:T(8,128)}) custom-call(bf16[200,1280]{1,0:T(8,128)(2,1)S(1)} %shard_map.86.refs_0_.refs_3_, bf16[200,1280]{1,0:T(8,128)(2,1)S(1)} %collective-permute-done.refs_0_.refs_1_, bf16[200,1280]{1,0:T(8,128)(2,1)S(1)} %collective-permute-done.1.x2_ref.refs_1_.refs_2_, ...), custom_call_target="tpu_custom_call" | custom-call | flops 1 | bytes 1 | tf_op jit(solution)/shard_map/pallas_call | solution.py:379
  119.9 0.0 collective-permute-done.17.lb_ref
  120.0 1.0 collective-permute-done.18.ha_ref
  121.0 0.5 shard_map.106
  121.5 14.0 %all_to_all.23.back_ref = bf16[16,16,1280]{2,1,0:T(8,128)(2,1)S(1)} all-to-all(bf16[16,16,1280]{2,1,0:T(8,128)(2,1)S(1)} %shard_map.106), channel_id=1, replica_groups=mesh['dp'=8,'expert'=16] {'expert'}, dimensions={0} | all-to-all | bytes 1310720 | tf_op jit(solution)/shard_map/all_to_all | solution.py:469
  135.6 1.3 shard_map.107
  (21 shorter events, 0.1 us)
Async XLA Ops:
  23.6 14.3 %collective-permute-start.1 = (bf16[200,1280]{1,0:T(8,128)(2,1)S(1)}, bf16[200,1280]{1,0:T(8,128)(2,1)S(1)}, u32[]{:S(2)}, u32[]{:S(2)}) collective-permute-start(bf16[200,1280]{1,0:T(8,128)(2,1)S(1)} %shard_map.86.refs_0_.refs_3_), channel_id=1, source_target_pairs={{0,32},{16,48},{32,64},{48,80},{64,96},{80,112},{96,0},{112,16},{1... | collective-permute-start | bytes 1536008 | tf_op jit(solution)/shard_map/ppermute | solution.py:457
  25.6 12.4 %collective-permute-start.2 = (bf16[200,1280]{1,0:T(8,128)(2,1)S(1)}, bf16[200,1280]{1,0:T(8,128)(2,1)S(1)}, u32[]{:S(2)}, u32[]{:S(2)}) collective-permute-start(bf16[200,1280]{1,0:T(8,128)(2,1)S(1)} %shard_map.86.refs_0_.refs_3_), channel_id=1, source_target_pairs={{0,96},{16,112},{32,0},{48,16},{64,32},{80,48},{96,64},{112,80},{1... | collective-permute-start | bytes 1536008 | tf_op jit(solution)/shard_map/ppermute | solution.py:460
  27.8 13.3 %collective-permute-start = (bf16[200,1280]{1,0:T(8,128)(2,1)S(1)}, bf16[200,1280]{1,0:T(8,128)(2,1)S(1)}, u32[]{:S(2)}, u32[]{:S(2)}) collective-permute-start(bf16[200,1280]{1,0:T(8,128)(2,1)S(1)} %shard_map.86.refs_0_.refs_3_), channel_id=1, source_target_pairs={{0,16},{16,0},{32,48},{48,32},{64,80},{80,64},{96,112},{112,96},{1... | collective-permute-start | bytes 1536008 | tf_op jit(solution)/shard_map/ppermute | solution.py:463
  27.8 1.9 %copy-start = (bf16[2,1280,640]{2,1,0:T(8,128)(2,1)S(1)}, bf16[2,1280,640]{2,1,0:T(8,128)(2,1)}, u32[]{:S(2)}) copy-start(bf16[2,1280,640]{2,1,0:T(8,128)(2,1)} %refs_9_.1) | copy-start | bytes 9830404
  29.7 11.4 %copy-start.1 = (bf16[2,1280,640]{2,1,0:T(8,128)(2,1)S(1)}, bf16[2,1280,640]{2,1,0:T(8,128)(2,1)}, u32[]{:S(2)}) copy-start(bf16[2,1280,640]{2,1,0:T(8,128)(2,1)} %refs_9_.1) | copy-start | bytes 9830404
  38.0 10.5 %collective-permute-start.5 = (bf16[104,1280]{1,0:T(8,128)(2,1)S(1)}, bf16[104,1280]{1,0:T(8,128)(2,1)S(1)}, u32[]{:S(2)}, u32[]{:S(2)}) collective-permute-start(bf16[104,1280]{1,0:T(8,128)(2,1)S(1)} %get-tuple-element.61), channel_id=1, source_target_pairs={{0,96},{16,112},{32,0},{48,16},{64,32},{80,48},{96,64},{112,80},{1... | collective-permute-start | bytes 798728 | tf_op jit(solution)/shard_map/ppermute | solution.py:460
  41.1 7.4 %collective-permute-start.4 = (bf16[96,1280]{1,0:T(8,128)(2,1)S(1)}, bf16[96,1280]{1,0:T(8,128)(2,1)S(1)}, u32[]{:S(2)}, u32[]{:S(2)}) collective-permute-start(bf16[96,1280]{1,0:T(8,128)(2,1)S(1)} %get-tuple-element.56), channel_id=1, source_target_pairs={{0,32},{16,48},{32,64},{48,80},{64,96},{80,112},{96,0},{112,16},{1... | collective-permute-start | bytes 737288 | tf_op jit(solution)/shard_map/ppermute | solution.py:457
  43.5 5.1 %collective-permute-start.3 = (bf16[200,1280]{1,0:T(8,128)(2,1)S(1)}, bf16[200,1280]{1,0:T(8,128)(2,1)S(1)}, u32[]{:S(2)}, u32[]{:S(2)}) collective-permute-start(bf16[200,1280]{1,0:T(8,128)(2,1)S(1)} %collective-permute-done.1.x2_ref.refs_1_.refs_2_), channel_id=1, source_target_pairs={{0,16},{16,0},{32,48},{48,32},{64,80},{80,64},{96,112},{112,96},{1... | collective-permute-start | bytes 1536008 | tf_op jit(solution)/shard_map/ppermute | solution.py:463
  43.6 5.1 %collective-permute-start.6 = (bf16[200,1280]{1,0:T(8,128)(2,1)S(1)}, bf16[200,1280]{1,0:T(8,128)(2,1)S(1)}, u32[]{:S(2)}, u32[]{:S(2)}) collective-permute-start(bf16[200,1280]{1,0:T(8,128)(2,1)S(1)} %collective-permute-done.2.x4_ref.refs_2_.refs_4_), channel_id=1, source_target_pairs={{0,16},{16,0},{32,48},{48,32},{64,80},{80,64},{96,112},{112,96},{1... | collective-permute-start | bytes 1536008 | tf_op jit(solution)/shard_map/ppermute | solution.py:463
  48.5 3.5 %copy-start.2 = (bf16[2,640,1280]{2,1,0:T(8,128)(2,1)S(1)}, bf16[2,640,1280]{2,1,0:T(8,128)(2,1)}, u32[]{:S(2)}) copy-start(bf16[2,640,1280]{2,1,0:T(8,128)(2,1)} %w_out.1) | copy-start | bytes 9830404
  48.5 2.0 %collective-permute-start.7 = (bf16[200,1280]{1,0:T(8,128)(2,1)S(1)}, bf16[200,1280]{1,0:T(8,128)(2,1)S(1)}, u32[]{:S(2)}, u32[]{:S(2)}) collective-permute-start(bf16[200,1280]{1,0:T(8,128)(2,1)S(1)} %shard_map.90.refs_0_.refs_6_), channel_id=1, source_target_pairs={{0,16},{16,0},{32,48},{48,32},{64,80},{80,64},{96,112},{112,96},{1... | collective-permute-start | bytes 1536008 | tf_op jit(solution)/shard_map/ppermute | solution.py:463
  52.7 17.9 %copy-start.5 = (f32[2,1280]{1,0:T(2,128)S(1)}, f32[2,1280]{1,0:T(2,128)}, u32[]{:S(2)}) copy-start(f32[2,1280]{1,0:T(2,128)} %get-tuple-element.69.sum_ref) | copy-start | bytes 30724
  52.7 1.7 %collective-permute-start.8 = (bf16[4,32,1280]{2,1,0:T(8,128)(2,1)S(1)}, bf16[4,32,1280]{2,1,0:T(8,128)(2,1)S(1)}, u32[]{:S(2)}, u32[]{:S(2)}) collective-permute-start(bf16[4,32,1280]{2,1,0:T(8,128)(2,1)S(1)} %shard_map.93), channel_id=1, source_target_pairs={{0,16},{16,0},{32,48},{48,32},{64,80},{80,64},{96,112},{112,96},{1... | collective-permute-start | bytes 983048 | tf_op jit(solution)/shard_map/ppermute | solution.py:463
  89.5 2.2 %collective-permute-start.9 = (f32[2,64,1280]{2,1,0:T(8,128)S(1)}, f32[2,64,1280]{2,1,0:T(8,128)S(1)}, u32[]{:S(2)}, u32[]{:S(2)}) collective-permute-start(f32[2,64,1280]{2,1,0:T(8,128)S(1)} %bitcast.11), channel_id=1, source_target_pairs={{0,16},{16,0},{32,48},{48,32},{64,80},{80,64},{96,112},{112,96},{1... | collective-permute-start | bytes 1966088 | tf_op jit(solution)/shard_map/ppermute | solution.py:463
  95.9 2.5 %collective-permute-start.10 = (bf16[192,1280]{1,0:T(8,128)(2,1)S(1)}, bf16[192,1280]{1,0:T(8,128)(2,1)S(1)}, u32[]{:S(2)}, u32[]{:S(2)}) collective-permute-start(bf16[192,1280]{1,0:T(8,128)(2,1)S(1)} %get-tuple-element.76), channel_id=1, source_target_pairs={{0,16},{16,0},{32,48},{48,32},{64,80},{80,64},{96,112},{112,96},{1... | collective-permute-start | bytes 1474568 | tf_op jit(solution)/shard_map/ppermute | solution.py:463
  97.9 6.2 %collective-permute-start.12 = (bf16[192,1280]{1,0:T(8,128)(2,1)S(1)}, bf16[192,1280]{1,0:T(8,128)(2,1)S(1)}, u32[]{:S(2)}, u32[]{:S(2)}) collective-permute-start(bf16[192,1280]{1,0:T(8,128)(2,1)S(1)} %get-tuple-element.88), channel_id=1, source_target_pairs={{0,16},{16,0},{32,48},{48,32},{64,80},{80,64},{96,112},{112,96},{1... | collective-permute-start | bytes 1474568 | tf_op jit(solution)/shard_map/ppermute | solution.py:463
  98.4 9.3 %collective-permute-start.13 = (bf16[96,1280]{1,0:T(8,128)(2,1)S(1)}, bf16[96,1280]{1,0:T(8,128)(2,1)S(1)}, u32[]{:S(2)}, u32[]{:S(2)}) collective-permute-start(bf16[96,1280]{1,0:T(8,128)(2,1)S(1)} %get-tuple-element.79), channel_id=1, source_target_pairs={{0,32},{16,48},{32,64},{48,80},{64,96},{80,112},{96,0},{112,16},{1... | collective-permute-start | bytes 737288 | tf_op jit(solution)/shard_map/ppermute | solution.py:457
  99.0 8.9 %collective-permute-start.14 = (bf16[96,1280]{1,0:T(8,128)(2,1)S(1)}, bf16[96,1280]{1,0:T(8,128)(2,1)S(1)}, u32[]{:S(2)}, u32[]{:S(2)}) collective-permute-start(bf16[96,1280]{1,0:T(8,128)(2,1)S(1)} %get-tuple-element.93), channel_id=1, source_target_pairs={{0,96},{16,112},{32,0},{48,16},{64,32},{80,48},{96,64},{112,80},{1... | collective-permute-start | bytes 737288 | tf_op jit(solution)/shard_map/ppermute | solution.py:460
  104.1 15.8 %collective-permute-start.17 = (bf16[96,1280]{1,0:T(8,128)(2,1)S(1)}, bf16[96,1280]{1,0:T(8,128)(2,1)S(1)}, u32[]{:S(2)}, u32[]{:S(2)}) collective-permute-start(bf16[96,1280]{1,0:T(8,128)(2,1)S(1)} %get-tuple-element.100), channel_id=1, source_target_pairs={{0,32},{16,48},{32,64},{48,80},{64,96},{80,112},{96,0},{112,16},{1... | collective-permute-start | bytes 737288 | tf_op jit(solution)/shard_map/ppermute | solution.py:457
  104.2 3.7 %collective-permute-start.11 = (bf16[192,1280]{1,0:T(8,128)(2,1)S(1)}, bf16[192,1280]{1,0:T(8,128)(2,1)S(1)}, u32[]{:S(2)}, u32[]{:S(2)}) collective-permute-start(bf16[192,1280]{1,0:T(8,128)(2,1)S(1)} %get-tuple-element.86), channel_id=1, source_target_pairs={{0,16},{16,0},{32,48},{48,32},{64,80},{80,64},{96,112},{112,96},{1... | collective-permute-start | bytes 1474568 | tf_op jit(solution)/shard_map/ppermute | solution.py:463
  104.3 15.6 %collective-permute-start.15 = (bf16[192,1280]{1,0:T(8,128)(2,1)S(1)}, bf16[192,1280]{1,0:T(8,128)(2,1)S(1)}, u32[]{:S(2)}, u32[]{:S(2)}) collective-permute-start(bf16[192,1280]{1,0:T(8,128)(2,1)S(1)} %get-tuple-element.99), channel_id=1, source_target_pairs={{0,16},{16,0},{32,48},{48,32},{64,80},{80,64},{96,112},{112,96},{1... | collective-permute-start | bytes 1474568 | tf_op jit(solution)/shard_map/ppermute | solution.py:463
  107.8 12.1 %collective-permute-start.16 = (bf16[96,1280]{1,0:T(8,128)(2,1)S(1)}, bf16[96,1280]{1,0:T(8,128)(2,1)S(1)}, u32[]{:S(2)}, u32[]{:S(2)}) collective-permute-start(bf16[96,1280]{1,0:T(8,128)(2,1)S(1)} %shard_map.103), channel_id=1, source_target_pairs={{0,32},{16,48},{32,64},{48,80},{64,96},{80,112},{96,0},{112,16},{1... | collective-permute-start | bytes 737288 | tf_op jit(solution)/shard_map/ppermute | solution.py:457
  108.1 11.9 %collective-permute-start.19 = (bf16[96,1280]{1,0:T(8,128)(2,1)S(1)}, bf16[96,1280]{1,0:T(8,128)(2,1)S(1)}, u32[]{:S(2)}, u32[]{:S(2)}) collective-permute-start(bf16[96,1280]{1,0:T(8,128)(2,1)S(1)} %get-tuple-element.101), channel_id=1, source_target_pairs={{0,96},{16,112},{32,0},{48,16},{64,32},{80,48},{96,64},{112,80},{1... | collective-permute-start | bytes 737288 | tf_op jit(solution)/shard_map/ppermute | solution.py:460
  111.4 9.6 %collective-permute-start.18 = (bf16[96,1280]{1,0:T(8,128)(2,1)S(1)}, bf16[96,1280]{1,0:T(8,128)(2,1)S(1)}, u32[]{:S(2)}, u32[]{:S(2)}) collective-permute-start(bf16[96,1280]{1,0:T(8,128)(2,1)S(1)} %get-tuple-element.94), channel_id=1, source_target_pairs={{0,96},{16,112},{32,0},{48,16},{64,32},{80,48},{96,64},{112,80},{1... | collective-permute-start | bytes 737288 | tf_op jit(solution)/shard_map/ppermute | solution.py:460
  119.9 15.6 %copy-start.3 = (bf16[1,2,64,1280]{3,2,1,0:T(8,128)(2,1)S(1)}, bf16[1,2,64,1280]{3,2,1,0:T(8,128)(2,1)}, u32[]{:S(2)}) copy-start(bf16[1,2,64,1280]{3,2,1,0:T(8,128)(2,1)} %param.6) | copy-start | bytes 983044
  119.9 15.6 %copy-start.4 = (f32[1280]{0:T(1024)S(1)}, f32[1280]{0:T(1024)}, u32[]{:S(2)}) copy-start(f32[1280]{0:T(1024)} %gain_ref.1) | copy-start | bytes 15364
  119.9 15.6 %copy-start.6 = (s32[1,2,64]{2,1,0:T(2,128)S(1)}, s32[1,2,64]{2,1,0:T(2,128)}, u32[]{:S(2)}) copy-start(s32[1,2,64]{2,1,0:T(2,128)} %param.7) | copy-start | bytes 1540
  119.9 15.6 %copy-start.7 = (s32[1,2,64]{2,1,0:T(2,128)S(1)}, s32[1,2,64]{2,1,0:T(2,128)}, u32[]{:S(2)}) copy-start(s32[1,2,64]{2,1,0:T(2,128)} %param.8) | copy-start | bytes 1540

commit v11 on v10

--- a/solution.py
+++ b/solution.py
@@ -345,7 +345,7 @@
     )
 
 
-PAIRED = {7: (0, 0), 6: (1, 0), 5: (1, 1), 4: (1, 2), 3: (2, 0), 1: (2, 1), 2: (2, 2), 0: (2, 3)}
+PAIRED = {7: (0, 0), 6: (1, 0), 5: (1, 1), 4: (1, 2), 3: (1, 3), 2: (2, 0), 1: (2, 1), 0: (2, 2)}
 
 
 def grads_kernel(*refs):
@@ -403,14 +403,9 @@
     second_ref[...] = total[HALF:]
 
 
-def add_kernel(x_ref, y_ref, out_ref):
-    out_ref[...] = (x_ref[...].astype(f32) + y_ref[...].astype(f32)).astype(bf16)
-
-
-def below_kernel(own_ref, got_ref, above_ref, first_ref, second_ref):
-    total = own_ref[...].astype(f32) + got_ref[...].astype(f32)
-    first_ref[...] = total[:HALF].astype(bf16)
-    second_ref[...] = (total[HALF:] + above_ref[...].astype(f32)).astype(bf16)
+def turn_kernel(above_ref, low_ref, below_ref, high_ref, up_ref, down_ref):
+    up_ref[...] = (above_ref[...].astype(f32) + low_ref[...].astype(f32)).astype(bf16)
+    down_ref[...] = (below_ref[...].astype(f32) + high_ref[...].astype(f32)).astype(bf16)
 
 
 def settle_kernel(own_ref, got_ref, la_ref, lb_ref, ha_ref, hb_ref, out_ref):
@@ -533,21 +528,24 @@
     half = shape_of(HALF, width)
     pre7, p7 = backward((7,), block_rows, made, prod, w_in)
     s7 = swap(p7)
-    pre654, p6, p5, p4 = backward((6, 5, 4), block_rows, made, after(prod, p7), w_in)
-    s5 = swap(p5)
+    pre6543, p6, p5, p4, p3 = backward(
+        (6, 5, 4, 3), block_rows, made, after(prod, p7), w_in
+    )
+    s5, s3 = swap(p5), swap(p3)
     r6a, r6b = plus(p6, s7)
     from_below, from_above = up(r6a), down(r6b)
-    rest, p3, p1, p2, p0 = backward((3, 1, 2, 0), block_rows, made, after(prod, r6a), w_in)
+    pre210, p2, p1, p0 = backward((2, 1, 0), block_rows, made, after(prod, r6a), w_in)
+    s1 = swap(p1)
     r4a, r4b = plus(p4, after(s5, p2))
-    low_b = up(r4b)
-    s3, s1 = swap(p3), swap(p1)
-    low_a = call(add_kernel, half, [after(r4a, p0), from_below], cost=DEAR)
-    r2a, r2b = call(below_kernel, [half, half], [p2, after(s3, low_a), from_above])
-    high_a, high_b = down(r2a), down(r2b)
+    r2a, r2b = plus(p2, s3)
+    low_b, high_a = up(r4b), down(r2a)
+    low_a, high_b = call(
+        turn_kernel, [half, half], [r4a, from_below, r2b, from_above], cost=DEAR
+    )
     grad_w_in, grad_w_out = weight_grads(
-        block_rows, [pre7, pre654, after(rest, r2a)], pooled, rows, width, hidden
-    )
-    low_a = up(low_a)
+        block_rows, [pre7, pre6543, after(pre210, low_a)], pooled, rows, width, hidden
+    )
+    low_a, high_b = up(low_a), down(high_b)
     settled = call(
         settle_kernel,
         shape_of(PEERS, PAD, width),

time: 137 us -> 137 us (level)
    ppermute x5, starting transfers between devices: 2.68 us -> 5.71 us  [up(): return lax.ppermute(x, 'dp', [(i, (i + 2) % 8) for i in range(8)])]
    ppermute x5, starting transfers between devices: 11.6 us -> 9.15 us  [down(): return lax.ppermute(x, 'dp', [(i, (i + 6) % 8) for i in range(8)])]
  transfers between devices with their start and end apart: 20 -> 20, of which waited for: 7 -> 7; matrix products, arithmetic and copies ran while one was open for 0% -> 0% of each run, Pallas kernels for 13% -> 14%
where the time goes in v11:
time: 137 us
  blocking collectives  68.9 us (50%)
  Pallas kernels  30 us (22%)
  waiting for transfers between devices  18.2 us (13%)
  starting transfers between devices  16.7 us (12%)
  local copies, waits for them, and re-layouts  2.25 us (2%)
    all_to_all x2, blocking collectives, exchange(): return lax.all_to_all(x, 'expert', split_axis=0, concat_axis=0, tiled=True)  34.5 us
    all_to_all x2, blocking collectives, spread(): lax.all_to_all(x, everyone, split_axis=0, concat_axis=0, tiled=True, axis...  34.4 us
    pallas_call x22, Pallas kernels, call(): pl.pallas_call(kernel, out_shape=out, in_specs=[pl.BlockSpec(memory_space...  21.7 us
    ppermute x5, waiting for transfers between devices, up(): return lax.ppermute(x, 'dp', [(i, (i + 2) % 8) for i in range(8)])  13.7 us
    ppermute x5, starting transfers between devices, down(): return lax.ppermute(x, 'dp', [(i, (i + 6) % 8) for i in range(8)])  9.15 us
    pallas_call x1, Pallas kernels, weight_grads(): pl.pallas_call(grads_kernel, grid=(2 * HELD,), out_shape=[shape_of(HELD,...  8.24 us
    ppermute x5, starting transfers between devices, up(): return lax.ppermute(x, 'dp', [(i, (i + 2) % 8) for i in range(8)])  5.71 us
    ppermute x10, waiting for transfers between devices, swap(): return lax.ppermute(x, 'dp', [(i, i ^ 1) for i in range(8)])  3.19 us
  transfers between devices with their start and end apart: 20, of which 7 were waited for; matrix products, arithmetic and copies ran while one was open for 0% of the time, Pallas kernels for 14%

profile of v11, /device:TPU:0, one launch (start us, length us, event | category | flops | bytes accessed | tf_op | source)
XLA Modules:
  0.0 136.9 jit_solution(14497880039665012123)
XLA Ops:
  0.6 2.5 %shard_map.85 = (bf16[16,16,1280]{2,1,0:T(8,128)(2,1)}, f32[2,1280]{1,0:T(2,128)}) custom-call(s32[2,64]{1,0:T(2,128)} %bitcast.16, s32[2,64]{1,0:T(2,128)} %bitcast.18, bf16[128,1280]{1,0:T(8,128)(2,1)} %bitcast.13, f32[1280]{0:T(1024)} %gain_ref.1), custom_call_target="tpu_custom_call" | custom-call | flops 1 | bytes 1 | tf_op jit(solution)/shard_map/pallas_call | solution.py:68
  3.1 20.1 %all_to_all.20.in_ref = bf16[16,16,1280]{2,1,0:T(8,128)(2,1)S(1)} all-to-all(bf16[16,16,1280]{2,1,0:T(8,128)(2,1)} %get-tuple-element.53), channel_id=1, replica_groups=mesh['dp'=8,'expert'=16] {'expert'}, dimensions={0} | all-to-all | bytes 1310720 | tf_op jit(solution)/shard_map/all_to_all | solution.py:464
  23.2 0.4 shard_map.86.refs_0_.refs_2_
  23.6 2.0 %collective-permute-start.1 = (bf16[200,1280]{1,0:T(8,128)(2,1)S(1)}, bf16[200,1280]{1,0:T(8,128)(2,1)S(1)}, u32[]{:S(2)}, u32[]{:S(2)}) collective-permute-start(bf16[200,1280]{1,0:T(8,128)(2,1)S(1)} %shard_map.86.refs_0_.refs_2_), channel_id=1, source_target_pairs={{0,32},{16,48},{32,64},{48,80},{64,96},{80,112},{96,0},{112,16},{1... | collective-permute-start | bytes 1536008 | tf_op jit(solution)/shard_map/ppermute | solution.py:452
  25.6 2.2 %collective-permute-start.2 = (bf16[200,1280]{1,0:T(8,128)(2,1)S(1)}, bf16[200,1280]{1,0:T(8,128)(2,1)S(1)}, u32[]{:S(2)}, u32[]{:S(2)}) collective-permute-start(bf16[200,1280]{1,0:T(8,128)(2,1)S(1)} %shard_map.86.refs_0_.refs_2_), channel_id=1, source_target_pairs={{0,96},{16,112},{32,0},{48,16},{64,32},{80,48},{96,64},{112,80},{1... | collective-permute-start | bytes 1536008 | tf_op jit(solution)/shard_map/ppermute | solution.py:455
  27.8 0.0 collective-permute-start
  27.8 1.9 %copy-done = bf16[2,1280,640]{2,1,0:T(8,128)(2,1)S(1)} copy-done((bf16[2,1280,640]{2,1,0:T(8,128)(2,1)S(1)}, bf16[2,1280,640]{2,1,0:T(8,128)(2,1)}, u32[]{:S(2)}) %copy-start) | copy-done | bytes 3276824
  29.7 1.1 shard_map.87
  30.8 7.2 %collective-permute-done.1.x2_ref.refs_1_.refs_0_.refs_2_ = bf16[200,1280]{1,0:T(8,128)(2,1)S(1)} collective-permute-done((bf16[200,1280]{1,0:T(8,128)(2,1)S(1)}, bf16[200,1280]{1,0:T(8,128)(2,1)S(1)}, u32[]{:S(2)}, u32[]{:S(2)}) %collective-permute-start.1) | collective-permute-done | bytes 512032 | tf_op jit(solution)/shard_map/ppermute | solution.py:452
  37.9 0.0 collective-permute-done.2.x4_ref.refs_2_.refs_4_
  38.0 3.1 %collective-permute-start.5 = (bf16[104,1280]{1,0:T(8,128)(2,1)S(1)}, bf16[104,1280]{1,0:T(8,128)(2,1)S(1)}, u32[]{:S(2)}, u32[]{:S(2)}) collective-permute-start(bf16[104,1280]{1,0:T(8,128)(2,1)S(1)} %get-tuple-element.61), channel_id=1, source_target_pairs={{0,96},{16,112},{32,0},{48,16},{64,32},{80,48},{96,64},{112,80},{1... | collective-permute-start | bytes 798728 | tf_op jit(solution)/shard_map/ppermute | solution.py:455
  41.1 0.0 collective-permute-start.4
  41.1 0.0 collective-permute-done.refs_0_.refs_1_
  41.1 2.4 %shard_map.89 = (bf16[3,2,32,640]{3,2,1,0:T(8,128)(2,1)S(1)}, bf16[3,2,96,640]{3,2,1,0:T(8,128)(2,1)S(1)}) custom-call(bf16[200,1280]{1,0:T(8,128)(2,1)S(1)} %collective-permute-done.refs_0_.refs_1_, bf16[200,1280]{1,0:T(8,128)(2,1)S(1)} %collective-permute-done.1.x2_ref.refs_1_.refs_0_.refs_2_, ...), custom_call_target="tpu_custom_call" | custom-call | flops 1 | bytes 1 | tf_op jit(solution)/shard_map/pallas_call | solution.py:68
  43.5 0.1 collective-permute-start.3
  43.6 0.5 collective-permute-start.6
  44.1 4.4 %collective-permute-done.4.first_ref = bf16[96,1280]{1,0:T(8,128)(2,1)S(1)} collective-permute-done((bf16[96,1280]{1,0:T(8,128)(2,1)S(1)}, bf16[96,1280]{1,0:T(8,128)(2,1)S(1)}, u32[]{:S(2)}, u32[]{:S(2)}) %collective-permute-start.4) | collective-permute-done | bytes 245792 | tf_op jit(solution)/shard_map/ppermute | solution.py:452
  48.5 0.0 collective-permute-done.5.second_ref
  48.5 0.0 copy-start.2
  48.5 0.1 collective-permute-start.7
  48.6 0.0 collective-permute-done.3.refs_0_.refs_3_
  48.6 1.5 %shard_map.91 = (bf16[2,2,32,640]{3,2,1,0:T(8,128)(2,1)S(1)}, bf16[2,2,96,640]{3,2,1,0:T(8,128)(2,1)S(1)}) custom-call(bf16[200,1280]{1,0:T(8,128)(2,1)S(1)} %collective-permute-done.3.refs_0_.refs_3_, bf16[200,1280]{1,0:T(8,128)(2,1)S(1)} %collective-permute-done.6.refs_1_.refs_5_, bf16[2,1280,640]{2,1,0:T(8,128)(2,1)S(1)} %copy-done.1), custom_call_target="tpu_custom_call" | custom-call | flops 1 | bytes 1 | tf_op jit(solution)/shard_map/pallas_call | solution.py:68
  50.2 0.3 collective-permute-done.7.refs_1_.refs_0_.refs_7_
  50.5 1.5 %shard_map.92 = (bf16[2,2,32,640]{3,2,1,0:T(8,128)(2,1)S(1)}, bf16[2,2,96,640]{3,2,1,0:T(8,128)(2,1)S(1)}) custom-call(bf16[200,1280]{1,0:T(8,128)(2,1)S(1)} %shard_map.90.refs_0_.refs_6_, bf16[200,1280]{1,0:T(8,128)(2,1)S(1)} %collective-permute-done.7.refs_1_.refs_0_.refs_7_, bf16[2,1280,640]{2,1,0:T(8,128)(2,1)S(1)} %copy-done.1), custom_call_target="tpu_custom_call" | custom-call | flops 1 | bytes 1 | tf_op jit(solution)/shard_map/pallas_call | solution.py:68
  52.0 0.7 shard_map.93
  52.7 0.0 copy-start.5
  52.7 0.3 collective-permute-start.8
  53.0 0.7 shard_map.94.own_ref
  53.7 0.8 collective-permute-done.8.got_ref
  54.4 0.1 shard_map.95
  54.5 0.3 copy.11
  54.8 15.8 %all_to_all.21.part_ref = bf16[64,2,1280]{2,1,0:T(2,128)(2,1)S(1)} all-to-all(bf16[64,2,1280]{2,1,0:T(2,128)(2,1)S(1)} %bitcast.20), channel_id=1, replica_groups={{0,1,2,3,4,5,6,7,8,9,10,11,12,13,14,15,32,33,34,35,36,37,38,39,40,41,42..., dimensions={0} | all-to-all | bytes 655360 | tf_op jit(solution)/shard_map/all_to_all | solution.py:467
  70.6 0.3 shard_map.96
  71.0 18.5 %all_to_all.22 = f32[64,2,1280]{2,1,0:T(2,128)S(1)} all-to-all(f32[64,2,1280]{2,1,0:T(2,128)S(1)} %shard_map.96), channel_id=1, replica_groups={{0,1,2,3,4,5,6,7,8,9,10,11,12,13,14,15,32,33,34,35,36,37,38,39,40,41,42..., dimensions={0} | all-to-all | bytes 1310720 | tf_op jit(solution)/shard_map/all_to_all | solution.py:467
  89.5 0.1 collective-permute-start.9
  89.6 2.1 %collective-permute-done.9.other_ref = f32[2,64,1280]{2,1,0:T(8,128)S(1)} collective-permute-done((f32[2,64,1280]{2,1,0:T(8,128)S(1)}, f32[2,64,1280]{2,1,0:T(8,128)S(1)}, u32[]{:S(2)}, u32[]{:S(2)}) %collective-permute-start.9) | collective-permute-done | bytes 655392 | tf_op jit(solution)/shard_map/ppermute | solution.py:458
  91.7 2.9 %shard_map.97 = (f32[2,128,1280]{2,1,0:T(8,128)S(1)}, bf16[8,32,1280]{2,1,0:T(8,128)(2,1)S(1)}, bf16[2,256,640]{2,1,0:T(8,128)(2,1)S(1)}) custom-call(f32[2,64,1280]{2,1,0:T(8,128)S(1)} %bitcast.12, f32[2,64,1280]{2,1,0:T(8,128)S(1)} %collective-permute-done.9.other_ref, bf16[2,640,1280]{2,1,0:T(8,128)(2,1)S(1)} %copy-done.2), custom_call_target="tpu_custom_call" | custom-call | flops 1 | bytes 1 | tf_op jit(solution)/shard_map/pallas_call | solution.py:68
  94.6 1.3 shard_map.98
  95.9 0.2 collective-permute-start.10
  96.1 2.3 %shard_map.99 = (bf16[4,2,96,640]{3,2,1,0:T(8,128)(2,1)S(1)}, bf16[192,1280]{1,0:T(8,128)(2,1)S(1)}, bf16[192,1280]{1,0:T(8,128)(2,1)S(1)}, bf16[192,1280]{1,0:T(8,128)(2,1)S(1)}, bf16[192,1280]{1,0:T(8,128)(2,1)S(1)}) custom-call(bf16[200,1280]{1,0:T(8,128)(2,1)S(1)} %shard_map.90.refs_0_.refs_6_, ...), custom_call_target="tpu_custom_call" | custom-call | flops 1 | bytes 1 | tf_op jit(solution)/shard_map/pallas_call | solution.py:68
  98.4 0.5 collective-permute-start.11
  98.8 0.1 collective-permute-start.13
  99.0 0.1 shard_map.100
  99.1 1.0 collective-permute-start.14
  100.0 1.2 collective-permute-start.12
  101.2 1.8 %shard_map.101 = (bf16[3,2,96,640]{3,2,1,0:T(8,128)(2,1)S(1)}, bf16[192,1280]{1,0:T(8,128)(2,1)S(1)}, bf16[192,1280]{1,0:T(8,128)(2,1)S(1)}, bf16[192,1280]{1,0:T(8,128)(2,1)S(1)}) custom-call(bf16[200,1280]{1,0:T(8,128)(2,1)S(1)} %collective-permute-done.1.x2_ref.refs_1_.refs_0_.refs_2_, bf16[200,1280]{1,0:T(8,128)(2,1)S(1)} %collective-permute-done.refs_0_.refs_1_, ...), custom_call_target="tpu_custom_call" | custom-call | flops 1 | bytes 1 | tf_op jit(solution)/shard_map/pallas_call | solution.py:68
  103.0 0.1 shard_map.102
  103.1 0.6 collective-permute-start.17
  103.7 0.1 shard_map.103
  103.8 2.8 %collective-permute-start.18 = (bf16[96,1280]{1,0:T(8,128)(2,1)S(1)}, bf16[96,1280]{1,0:T(8,128)(2,1)S(1)}, u32[]{:S(2)}, u32[]{:S(2)}) collective-permute-start(bf16[96,1280]{1,0:T(8,128)(2,1)S(1)} %get-tuple-element.100), channel_id=1, source_target_pairs={{0,96},{16,112},{32,0},{48,16},{64,32},{80,48},{96,64},{112,80},{1... | collective-permute-start | bytes 737288 | tf_op jit(solution)/shard_map/ppermute | solution.py:455
  106.6 0.0 collective-permute-start.15
  106.6 1.3 collective-permute-done.14.high_ref
  107.9 2.1 %collective-permute-done.12.low_ref = bf16[96,1280]{1,0:T(8,128)(2,1)S(1)} collective-permute-done((bf16[96,1280]{1,0:T(8,128)(2,1)S(1)}, bf16[96,1280]{1,0:T(8,128)(2,1)S(1)}, u32[]{:S(2)}, u32[]{:S(2)}) %collective-permute-start.12) | collective-permute-done | bytes 245792 | tf_op jit(solution)/shard_map/ppermute | solution.py:452
  110.1 0.1 shard_map.104
  110.2 0.1 collective-permute-start.19
  110.3 2.0 %collective-permute-start.16 = (bf16[96,1280]{1,0:T(8,128)(2,1)S(1)}, bf16[96,1280]{1,0:T(8,128)(2,1)S(1)}, u32[]{:S(2)}, u32[]{:S(2)}) collective-permute-start(bf16[96,1280]{1,0:T(8,128)(2,1)S(1)} %get-tuple-element.93), channel_id=1, source_target_pairs={{0,32},{16,48},{32,64},{48,80},{64,96},{80,112},{96,0},{112,16},{1... | collective-permute-start | bytes 737288 | tf_op jit(solution)/shard_map/ppermute | solution.py:452
  112.3 8.2 %shard_map.105 = (f32[2,1280,640]{2,1,0:T(8,128)}, f32[2,640,1280]{2,1,0:T(8,128)}) custom-call(bf16[200,1280]{1,0:T(8,128)(2,1)S(1)} %shard_map.86.refs_0_.refs_2_, bf16[200,1280]{1,0:T(8,128)(2,1)S(1)} %collective-permute-done.refs_0_.refs_1_, bf16[200,1280]{1,0:T(8,128)(2,1)S(1)} %collective-permute-done.1.x2_ref.refs_1_.refs_0_.refs_2_, ...), custom_call_target="tpu_custom_call" | custom-call | flops 1 | bytes 1 | tf_op jit(solution)/shard_map/pallas_call | solution.py:379
  120.5 0.0 collective-permute-done.17.lb_ref
  120.5 0.0 collective-permute-done.18.ha_ref
  120.6 0.0 collective-permute-done.16.la_ref
  120.6 0.0 collective-permute-done.15.got_ref
  120.6 0.5 shard_map.106
  121.1 14.5 %all_to_all.23.back_ref = bf16[16,16,1280]{2,1,0:T(8,128)(2,1)S(1)} all-to-all(bf16[16,16,1280]{2,1,0:T(8,128)(2,1)S(1)} %shard_map.106), channel_id=1, replica_groups=mesh['dp'=8,'expert'=16] {'expert'}, dimensions={0} | all-to-all | bytes 1310720 | tf_op jit(solution)/shard_map/all_to_all | solution.py:464
  135.6 1.3 shard_map.107
  (21 shorter events, 0.1 us)
Async XLA Ops:
  23.6 14.3 %collective-permute-start.1 = (bf16[200,1280]{1,0:T(8,128)(2,1)S(1)}, bf16[200,1280]{1,0:T(8,128)(2,1)S(1)}, u32[]{:S(2)}, u32[]{:S(2)}) collective-permute-start(bf16[200,1280]{1,0:T(8,128)(2,1)S(1)} %shard_map.86.refs_0_.refs_2_), channel_id=1, source_target_pairs={{0,32},{16,48},{32,64},{48,80},{64,96},{80,112},{96,0},{112,16},{1... | collective-permute-start | bytes 1536008 | tf_op jit(solution)/shard_map/ppermute | solution.py:452
  25.6 12.4 %collective-permute-start.2 = (bf16[200,1280]{1,0:T(8,128)(2,1)S(1)}, bf16[200,1280]{1,0:T(8,128)(2,1)S(1)}, u32[]{:S(2)}, u32[]{:S(2)}) collective-permute-start(bf16[200,1280]{1,0:T(8,128)(2,1)S(1)} %shard_map.86.refs_0_.refs_2_), channel_id=1, source_target_pairs={{0,96},{16,112},{32,0},{48,16},{64,32},{80,48},{96,64},{112,80},{1... | collective-permute-start | bytes 1536008 | tf_op jit(solution)/shard_map/ppermute | solution.py:455
  27.8 13.3 %collective-permute-start = (bf16[200,1280]{1,0:T(8,128)(2,1)S(1)}, bf16[200,1280]{1,0:T(8,128)(2,1)S(1)}, u32[]{:S(2)}, u32[]{:S(2)}) collective-permute-start(bf16[200,1280]{1,0:T(8,128)(2,1)S(1)} %shard_map.86.refs_0_.refs_2_), channel_id=1, source_target_pairs={{0,16},{16,0},{32,48},{48,32},{64,80},{80,64},{96,112},{112,96},{1... | collective-permute-start | bytes 1536008 | tf_op jit(solution)/shard_map/ppermute | solution.py:458
  27.8 1.9 %copy-start = (bf16[2,1280,640]{2,1,0:T(8,128)(2,1)S(1)}, bf16[2,1280,640]{2,1,0:T(8,128)(2,1)}, u32[]{:S(2)}) copy-start(bf16[2,1280,640]{2,1,0:T(8,128)(2,1)} %refs_7_.1) | copy-start | bytes 9830404
  29.7 11.4 %copy-start.1 = (bf16[2,1280,640]{2,1,0:T(8,128)(2,1)S(1)}, bf16[2,1280,640]{2,1,0:T(8,128)(2,1)}, u32[]{:S(2)}) copy-start(bf16[2,1280,640]{2,1,0:T(8,128)(2,1)} %refs_7_.1) | copy-start | bytes 9830404
  38.0 10.5 %collective-permute-start.5 = (bf16[104,1280]{1,0:T(8,128)(2,1)S(1)}, bf16[104,1280]{1,0:T(8,128)(2,1)S(1)}, u32[]{:S(2)}, u32[]{:S(2)}) collective-permute-start(bf16[104,1280]{1,0:T(8,128)(2,1)S(1)} %get-tuple-element.61), channel_id=1, source_target_pairs={{0,96},{16,112},{32,0},{48,16},{64,32},{80,48},{96,64},{112,80},{1... | collective-permute-start | bytes 798728 | tf_op jit(solution)/shard_map/ppermute | solution.py:455
  41.1 7.4 %collective-permute-start.4 = (bf16[96,1280]{1,0:T(8,128)(2,1)S(1)}, bf16[96,1280]{1,0:T(8,128)(2,1)S(1)}, u32[]{:S(2)}, u32[]{:S(2)}) collective-permute-start(bf16[96,1280]{1,0:T(8,128)(2,1)S(1)} %get-tuple-element.56), channel_id=1, source_target_pairs={{0,32},{16,48},{32,64},{48,80},{64,96},{80,112},{96,0},{112,16},{1... | collective-permute-start | bytes 737288 | tf_op jit(solution)/shard_map/ppermute | solution.py:452
  43.5 5.1 %collective-permute-start.3 = (bf16[200,1280]{1,0:T(8,128)(2,1)S(1)}, bf16[200,1280]{1,0:T(8,128)(2,1)S(1)}, u32[]{:S(2)}, u32[]{:S(2)}) collective-permute-start(bf16[200,1280]{1,0:T(8,128)(2,1)S(1)} %collective-permute-done.1.x2_ref.refs_1_.refs_0_.refs_2_), channel_id=1, source_target_pairs={{0,16},{16,0},{32,48},{48,32},{64,80},{80,64},{96,112},{112,96},{1... | collective-permute-start | bytes 1536008 | tf_op jit(solution)/shard_map/ppermute | solution.py:458
  43.6 5.1 %collective-permute-start.6 = (bf16[200,1280]{1,0:T(8,128)(2,1)S(1)}, bf16[200,1280]{1,0:T(8,128)(2,1)S(1)}, u32[]{:S(2)}, u32[]{:S(2)}) collective-permute-start(bf16[200,1280]{1,0:T(8,128)(2,1)S(1)} %collective-permute-done.2.x4_ref.refs_2_.refs_4_), channel_id=1, source_target_pairs={{0,16},{16,0},{32,48},{48,32},{64,80},{80,64},{96,112},{112,96},{1... | collective-permute-start | bytes 1536008 | tf_op jit(solution)/shard_map/ppermute | solution.py:458
  48.5 3.5 %copy-start.2 = (bf16[2,640,1280]{2,1,0:T(8,128)(2,1)S(1)}, bf16[2,640,1280]{2,1,0:T(8,128)(2,1)}, u32[]{:S(2)}) copy-start(bf16[2,640,1280]{2,1,0:T(8,128)(2,1)} %w_out.1) | copy-start | bytes 9830404
  48.5 2.0 %collective-permute-start.7 = (bf16[200,1280]{1,0:T(8,128)(2,1)S(1)}, bf16[200,1280]{1,0:T(8,128)(2,1)S(1)}, u32[]{:S(2)}, u32[]{:S(2)}) collective-permute-start(bf16[200,1280]{1,0:T(8,128)(2,1)S(1)} %shard_map.90.refs_0_.refs_6_), channel_id=1, source_target_pairs={{0,16},{16,0},{32,48},{48,32},{64,80},{80,64},{96,112},{112,96},{1... | collective-permute-start | bytes 1536008 | tf_op jit(solution)/shard_map/ppermute | solution.py:458
  52.7 17.9 %copy-start.5 = (f32[2,1280]{1,0:T(2,128)S(1)}, f32[2,1280]{1,0:T(2,128)}, u32[]{:S(2)}) copy-start(f32[2,1280]{1,0:T(2,128)} %get-tuple-element.69.sum_ref) | copy-start | bytes 30724
  52.7 1.7 %collective-permute-start.8 = (bf16[4,32,1280]{2,1,0:T(8,128)(2,1)S(1)}, bf16[4,32,1280]{2,1,0:T(8,128)(2,1)S(1)}, u32[]{:S(2)}, u32[]{:S(2)}) collective-permute-start(bf16[4,32,1280]{2,1,0:T(8,128)(2,1)S(1)} %shard_map.93), channel_id=1, source_target_pairs={{0,16},{16,0},{32,48},{48,32},{64,80},{80,64},{96,112},{112,96},{1... | collective-permute-start | bytes 983048 | tf_op jit(solution)/shard_map/ppermute | solution.py:458
  89.5 2.2 %collective-permute-start.9 = (f32[2,64,1280]{2,1,0:T(8,128)S(1)}, f32[2,64,1280]{2,1,0:T(8,128)S(1)}, u32[]{:S(2)}, u32[]{:S(2)}) collective-permute-start(f32[2,64,1280]{2,1,0:T(8,128)S(1)} %bitcast.11), channel_id=1, source_target_pairs={{0,16},{16,0},{32,48},{48,32},{64,80},{80,64},{96,112},{112,96},{1... | collective-permute-start | bytes 1966088 | tf_op jit(solution)/shard_map/ppermute | solution.py:458
  95.9 3.1 %collective-permute-start.10 = (bf16[192,1280]{1,0:T(8,128)(2,1)S(1)}, bf16[192,1280]{1,0:T(8,128)(2,1)S(1)}, u32[]{:S(2)}, u32[]{:S(2)}) collective-permute-start(bf16[192,1280]{1,0:T(8,128)(2,1)S(1)} %get-tuple-element.76), channel_id=1, source_target_pairs={{0,16},{16,0},{32,48},{48,32},{64,80},{80,64},{96,112},{112,96},{1... | collective-permute-start | bytes 1474568 | tf_op jit(solution)/shard_map/ppermute | solution.py:458
  98.4 4.6 %collective-permute-start.11 = (bf16[192,1280]{1,0:T(8,128)(2,1)S(1)}, bf16[192,1280]{1,0:T(8,128)(2,1)S(1)}, u32[]{:S(2)}, u32[]{:S(2)}) collective-permute-start(bf16[192,1280]{1,0:T(8,128)(2,1)S(1)} %get-tuple-element.86), channel_id=1, source_target_pairs={{0,16},{16,0},{32,48},{48,32},{64,80},{80,64},{96,112},{112,96},{1... | collective-permute-start | bytes 1474568 | tf_op jit(solution)/shard_map/ppermute | solution.py:458
  98.8 4.9 %collective-permute-start.13 = (bf16[192,1280]{1,0:T(8,128)(2,1)S(1)}, bf16[192,1280]{1,0:T(8,128)(2,1)S(1)}, u32[]{:S(2)}, u32[]{:S(2)}) collective-permute-start(bf16[192,1280]{1,0:T(8,128)(2,1)S(1)} %get-tuple-element.90), channel_id=1, source_target_pairs={{0,16},{16,0},{32,48},{48,32},{64,80},{80,64},{96,112},{112,96},{1... | collective-permute-start | bytes 1474568 | tf_op jit(solution)/shard_map/ppermute | solution.py:458
  99.1 8.9 %collective-permute-start.14 = (bf16[96,1280]{1,0:T(8,128)(2,1)S(1)}, bf16[96,1280]{1,0:T(8,128)(2,1)S(1)}, u32[]{:S(2)}, u32[]{:S(2)}) collective-permute-start(bf16[96,1280]{1,0:T(8,128)(2,1)S(1)} %get-tuple-element.92), channel_id=1, source_target_pairs={{0,96},{16,112},{32,0},{48,16},{64,32},{80,48},{96,64},{112,80},{1... | collective-permute-start | bytes 737288 | tf_op jit(solution)/shard_map/ppermute | solution.py:455
  100.0 10.0 %collective-permute-start.12 = (bf16[96,1280]{1,0:T(8,128)(2,1)S(1)}, bf16[96,1280]{1,0:T(8,128)(2,1)S(1)}, u32[]{:S(2)}, u32[]{:S(2)}) collective-permute-start(bf16[96,1280]{1,0:T(8,128)(2,1)S(1)} %get-tuple-element.79), channel_id=1, source_target_pairs={{0,32},{16,48},{32,64},{48,80},{64,96},{80,112},{96,0},{112,16},{1... | collective-permute-start | bytes 737288 | tf_op jit(solution)/shard_map/ppermute | solution.py:452
  103.1 17.4 %collective-permute-start.17 = (bf16[96,1280]{1,0:T(8,128)(2,1)S(1)}, bf16[96,1280]{1,0:T(8,128)(2,1)S(1)}, u32[]{:S(2)}, u32[]{:S(2)}) collective-permute-start(bf16[96,1280]{1,0:T(8,128)(2,1)S(1)} %get-tuple-element.99), channel_id=1, source_target_pairs={{0,32},{16,48},{32,64},{48,80},{64,96},{80,112},{96,0},{112,16},{1... | collective-permute-start | bytes 737288 | tf_op jit(solution)/shard_map/ppermute | solution.py:452
  103.8 16.7 %collective-permute-start.18 = (bf16[96,1280]{1,0:T(8,128)(2,1)S(1)}, bf16[96,1280]{1,0:T(8,128)(2,1)S(1)}, u32[]{:S(2)}, u32[]{:S(2)}) collective-permute-start(bf16[96,1280]{1,0:T(8,128)(2,1)S(1)} %get-tuple-element.100), channel_id=1, source_target_pairs={{0,96},{16,112},{32,0},{48,16},{64,32},{80,48},{96,64},{112,80},{1... | collective-permute-start | bytes 737288 | tf_op jit(solution)/shard_map/ppermute | solution.py:455
  106.6 13.9 %collective-permute-start.15 = (bf16[192,1280]{1,0:T(8,128)(2,1)S(1)}, bf16[192,1280]{1,0:T(8,128)(2,1)S(1)}, u32[]{:S(2)}, u32[]{:S(2)}) collective-permute-start(bf16[192,1280]{1,0:T(8,128)(2,1)S(1)} %get-tuple-element.98), channel_id=1, source_target_pairs={{0,16},{16,0},{32,48},{48,32},{64,80},{80,64},{96,112},{112,96},{1... | collective-permute-start | bytes 1474568 | tf_op jit(solution)/shard_map/ppermute | solution.py:458
  110.2 10.4 %collective-permute-start.19 = (bf16[96,1280]{1,0:T(8,128)(2,1)S(1)}, bf16[96,1280]{1,0:T(8,128)(2,1)S(1)}, u32[]{:S(2)}, u32[]{:S(2)}) collective-permute-start(bf16[96,1280]{1,0:T(8,128)(2,1)S(1)} %get-tuple-element.101), channel_id=1, source_target_pairs={{0,96},{16,112},{32,0},{48,16},{64,32},{80,48},{96,64},{112,80},{1... | collective-permute-start | bytes 737288 | tf_op jit(solution)/shard_map/ppermute | solution.py:455
  110.3 10.3 %collective-permute-start.16 = (bf16[96,1280]{1,0:T(8,128)(2,1)S(1)}, bf16[96,1280]{1,0:T(8,128)(2,1)S(1)}, u32[]{:S(2)}, u32[]{:S(2)}) collective-permute-start(bf16[96,1280]{1,0:T(8,128)(2,1)S(1)} %get-tuple-element.93), channel_id=1, source_target_pairs={{0,32},{16,48},{32,64},{48,80},{64,96},{80,112},{96,0},{112,16},{1... | collective-permute-start | bytes 737288 | tf_op jit(solution)/shard_map/ppermute | solution.py:452
  120.5 15.0 %copy-start.3 = (bf16[1,2,64,1280]{3,2,1,0:T(8,128)(2,1)S(1)}, bf16[1,2,64,1280]{3,2,1,0:T(8,128)(2,1)}, u32[]{:S(2)}) copy-start(bf16[1,2,64,1280]{3,2,1,0:T(8,128)(2,1)} %param.6) | copy-start | bytes 983044
  120.5 15.0 %copy-start.4 = (f32[1280]{0:T(1024)S(1)}, f32[1280]{0:T(1024)}, u32[]{:S(2)}) copy-start(f32[1280]{0:T(1024)} %gain_ref.1) | copy-start | bytes 15364
  120.5 15.0 %copy-start.6 = (s32[1,2,64]{2,1,0:T(2,128)S(1)}, s32[1,2,64]{2,1,0:T(2,128)}, u32[]{:S(2)}) copy-start(s32[1,2,64]{2,1,0:T(2,128)} %param.7) | copy-start | bytes 1540
  120.5 15.0 %copy-start.7 = (s32[1,2,64]{2,1,0:T(2,128)S(1)}, s32[1,2,64]{2,1,0:T(2,128)}, u32[]{:S(2)}) copy-start(s32[1,2,64]{2,1,0:T(2,128)} %param.8) | copy-start | bytes 1540
